TPU v7x, 32 devices: a whole 2x2x4 slice. The times are simulated.
32 devices in a mesh: dp: 16 (over z, x, core), tensor: 2 (over y).
Axes of the slice: x: 2, y: 2, z: 4, core: 2. Of those that a mesh axis runs over, the one named last changes fastest.
Arguments:
- tokens: bfloat16 [2, 16384, 1024], P(None, ('dp', 'tensor')), may hold values from -6 to 6
- cotangent: bfloat16 [2, 16384, 1024], P(None, ('dp', 'tensor')), may hold values from -6 to 6
- piece_starts: int32 [2, 16, 2], P(None, 'dp'), may hold values from 0 to 768, as said below
- w_qkv: float32 [3, 1024, 1024], P(None, 'dp', 'tensor'), may hold values from -0.1875 to 0.1875
- w_out: float32 [1024, 1024], P('tensor', 'dp'), may hold values from -0.5 to 0.5
- w_up: float32 [1024, 4096], P('dp', 'tensor'), as said below
- w_down: float32 [4096, 1024], P('tensor', 'dp'), may hold values from -0.09375 to 0.09375
- vectors: float32 [12, 1024], replicated, as said below
- m_qkv: float32 [3, 1024, 1024], P(None, 'dp', 'tensor'), may hold values from -112 to 112
- m_out: float32 [1024, 1024], P('tensor', 'dp'), may hold values from -512 to 512
- m_up: float32 [1024, 4096], P('dp', 'tensor'), may hold values from -256 to 256
- m_down: float32 [4096, 1024], P('tensor', 'dp'), may hold values from -512 to 512
- m_vec: float32 [12, 1024], replicated, may hold values from -512 to 512
Outputs:
- block_output: bfloat16 [2, 16384, 1024], P(None, ('dp', 'tensor'))
- grad_tokens: float32 [2, 16384, 1024], P(None, ('dp', 'tensor'))
- grad_qkv: float32 [3, 1024, 1024], P(None, 'dp', 'tensor')
- grad_out: float32 [1024, 1024], P('tensor', 'dp')
- grad_up: float32 [1024, 4096], P('dp', 'tensor')
- grad_down: float32 [4096, 1024], P('tensor', 'dp')
- grad_vec: float32 [12, 1024], replicated
- moment_qkv: float32 [3, 1024, 1024], P(None, 'dp', 'tensor')
- moment_out: float32 [1024, 1024], P('tensor', 'dp')
- moment_up: float32 [1024, 4096], P('dp', 'tensor')
- moment_down: float32 [4096, 1024], P('tensor', 'dp')
- moment_vec: float32 [12, 1024], replicated
- new_qkv: float32 [3, 1024, 1024], P(None, 'dp', 'tensor')
- new_out: float32 [1024, 1024], P('tensor', 'dp')
- new_up: float32 [1024, 4096], P('dp', 'tensor')
- new_down: float32 [4096, 1024], P('tensor', 'dp')
- new_vec: float32 [12, 1024], replicated
Inputs may be any that keep to these rules, and one draw needn't show every extreme that they name: `piece_starts`: in each sequence piece k starts within [k * 512, (k + 1) * 512 - 256], so pieces lie inside the sequence and never intersect. `vectors`: rows 0 and 5 are gains near one. `w_up`: entries are at most six times 1024 to the power minus one half in magnitude.
All inputs are finite; a program needn't handle non-finite values.
Results may differ from a plain program's by a relative error of at most 0.019.
Values may be sent and summed in bfloat16 or wider, within the bound.
A program may use at most 320 MiB of HBM per device.

v0:
```python
import math

import jax
import jax.numpy as jnp
from jax import lax
from jax.sharding import PartitionSpec as P

D = 1024
H = 16
HD = 64
FF = 4096
LEN = 1024
PIECE = 256
NPIECE = 2
MB = 2
NS_ITERS = 3


NORM_EPSILON = 1e-05
SQUARE_EPSILON = 1e-06
MASKED_SCORE = -1e30
SCHULZ_FIRST = 3.4445
SCHULZ_SECOND = -4.775
SCHULZ_THIRD = 2.0315
MOMENTUM_DECAY = 0.5
MATRIX_RATE = 0.5
VECTOR_RATE = 0.05


def layer_norm(inputs, gain_row, shift_row):
    average = jnp.mean(inputs, axis=-1, keepdims=True)
    centered = inputs - average
    variance = jnp.mean(centered * centered, axis=-1, keepdims=True)
    return centered * lax.rsqrt(variance + NORM_EPSILON) * gain_row + shift_row


def gelu_tanh(inputs):
    return jax.nn.gelu(inputs, approximate=True)


def score_layout(starts, slopes):
    positions = jnp.arange(LEN, dtype=jnp.int32)
    inside = (positions[None, :] >= starts[:, None]) & (
        positions[None, :] < starts[:, None] + PIECE
    )
    labels = jnp.arange(1, NPIECE + 1, dtype=jnp.int32)
    piece_label = jnp.sum(jnp.where(inside, labels[:, None], 0), axis=0)
    same_piece = (piece_label[:, None] == piece_label[None, :]) & (piece_label[:, None] > 0)
    visible = (positions[None, :] <= positions[:, None]) | same_piece
    distance = jnp.abs(positions[:, None] - positions[None, :]).astype(jnp.float32)
    penalty = -slopes[:, None, None] * distance[None, :, :]
    return (visible, penalty)


def head_scores(query_heads, key_heads, starts, slopes):
    visible, penalty = score_layout(starts, slopes)
    raw_scores = jnp.einsum(
        "qhd,khd->hqk", query_heads, key_heads, preferred_element_type=jnp.float32
    )
    scores = raw_scores * (1.0 / math.sqrt(HD)) + penalty
    return jnp.where(visible[None, :, :], scores, MASKED_SCORE)


def attend_forward(element, slopes):
    query_seq, key_seq, value_seq, starts = element
    heads_here = slopes.shape[0]
    query_heads = query_seq.reshape(LEN, heads_here, HD)
    key_heads = key_seq.reshape(LEN, heads_here, HD)
    value_heads = value_seq.reshape(LEN, heads_here, HD)
    scores = head_scores(query_heads, key_heads, starts, slopes)
    maximum = jnp.max(scores, axis=-1, keepdims=True)
    weights_raw = jnp.exp(scores - maximum)
    denominator = jnp.sum(weights_raw, axis=-1, keepdims=True)
    probabilities = weights_raw / denominator
    context = jnp.einsum(
        "hqk,khd->qhd",
        probabilities.astype(jnp.bfloat16),
        value_heads,
        preferred_element_type=jnp.float32,
    )
    logsum = (maximum + jnp.log(denominator))[..., 0]
    return (context.reshape(LEN, heads_here * HD), logsum)


def attend_backward(element, slopes):
    query_seq, key_seq, value_seq, context_grad, logsum, starts = element
    heads_here = slopes.shape[0]
    query_heads = query_seq.reshape(LEN, heads_here, HD)
    key_heads = key_seq.reshape(LEN, heads_here, HD)
    value_heads = value_seq.reshape(LEN, heads_here, HD)
    grad_heads = context_grad.reshape(LEN, heads_here, HD)
    scores = head_scores(query_heads, key_heads, starts, slopes)
    probabilities = jnp.exp(scores - logsum[..., None])
    grad_probs = jnp.einsum(
        "qhd,khd->hqk", grad_heads, value_heads, preferred_element_type=jnp.float32
    )
    inner_sum = jnp.sum(probabilities * grad_probs, axis=-1, keepdims=True)
    grad_scores = (probabilities * (grad_probs - inner_sum)).astype(jnp.bfloat16)
    scale_factor = 1.0 / math.sqrt(HD)
    grad_query = (
        jnp.einsum("hqk,khd->qhd", grad_scores, key_heads, preferred_element_type=jnp.float32)
        * scale_factor
    )
    grad_key = (
        jnp.einsum("hqk,qhd->khd", grad_scores, query_heads, preferred_element_type=jnp.float32)
        * scale_factor
    )
    grad_value = jnp.einsum(
        "hqk,qhd->khd",
        probabilities.astype(jnp.bfloat16),
        grad_heads,
        preferred_element_type=jnp.float32,
    )
    width_here = heads_here * HD
    return (
        grad_query.astype(jnp.bfloat16).reshape(LEN, width_here),
        grad_key.astype(jnp.bfloat16).reshape(LEN, width_here),
        grad_value.astype(jnp.bfloat16).reshape(LEN, width_here),
    )


def placed(values, offset, length):
    return lax.dynamic_update_slice_in_dim(jnp.zeros((length,), jnp.float32), values, offset, 0)


def accumulate(totals, addend):
    if totals is None:
        return addend
    return tuple((former + latter for former, latter in zip(totals, addend)))


def gram_term(narrow_rows, wide_rows):
    part_narrow = jnp.einsum(
        "mrc,mrd->cmd", narrow_rows, narrow_rows, preferred_element_type=jnp.float32
    )
    part_wide = jnp.einsum("mrc,mrd->cmd", wide_rows, wide_rows, preferred_element_type=jnp.float32)
    return jnp.concatenate([part_narrow, part_wide], axis=1)


def schulz_step(state, gram_matrix):
    turned = jnp.einsum("mrc,cmd->mrd", state, gram_matrix, preferred_element_type=jnp.float32)
    mixed = (SCHULZ_SECOND * state.astype(jnp.float32) + SCHULZ_THIRD * turned).astype(jnp.bfloat16)
    return (
        SCHULZ_FIRST * state.astype(jnp.float32)
        + jnp.einsum("mrc,cmd->mrd", mixed, gram_matrix, preferred_element_type=jnp.float32)
    ).astype(jnp.bfloat16)


def slice_term(source, weights, pattern):
    return jnp.einsum(pattern, source, weights, preferred_element_type=jnp.float32)


def on_device(
    tokens,
    cotangent,
    piece_starts,
    w_qkv,
    w_out,
    w_up,
    w_down,
    vectors,
    m_qkv,
    m_out,
    m_up,
    m_down,
    m_vec,
):
    tensor_count = lax.axis_size("tensor")
    tensor_rank = lax.axis_index("tensor")
    shard_rank = lax.axis_index("dp")
    heads_here = H // tensor_count
    width_here = heads_here * HD
    hidden_here = FF // tensor_count
    rows_here = tokens.shape[1]
    group_rows = rows_here * tensor_count
    seqs_here = piece_starts.shape[1]
    shard_rows = w_qkv.shape[1]
    head_ids = tensor_rank * heads_here + jnp.arange(heads_here, dtype=jnp.int32) + 1
    slopes = jnp.exp2(-8.0 * head_ids.astype(jnp.float32) / H)
    query_shift = lax.dynamic_slice_in_dim(vectors[2], tensor_rank * width_here, width_here, 0)
    value_shift = lax.dynamic_slice_in_dim(vectors[3], tensor_rank * width_here, width_here, 0)
    up_shift = lax.dynamic_slice_in_dim(
        vectors[7:11].reshape(FF), tensor_rank * hidden_here, hidden_here, 0
    )
    low_qkv = w_qkv.astype(jnp.bfloat16)
    low_out = w_out.astype(jnp.bfloat16)
    low_up = w_up.astype(jnp.bfloat16)
    low_down = w_down.astype(jnp.bfloat16)
    outputs_list = []
    input_grads = []
    vector_total = jnp.zeros((12, D), jnp.float32)
    grad_total = None

    def forward_one(element):
        return attend_forward(element, slopes)

    def backward_one(element):
        return attend_backward(element, slopes)

    for batch_index in range(MB):
        full_qkv, full_out, full_up, full_down = (
            lax.all_gather(low_qkv, "dp", axis=1, tiled=True),
            lax.all_gather(low_out, "dp", axis=1, tiled=True),
            lax.all_gather(low_up, "dp", axis=0, tiled=True),
            lax.all_gather(low_down, "dp", axis=1, tiled=True),
        )
        token_rows = tokens[batch_index].astype(jnp.float32)
        cotangent_rows = cotangent[batch_index]
        normed_one = layer_norm(token_rows, vectors[0], vectors[1])
        normed_all, cotangent_all = (
            lax.all_gather(normed_one.astype(jnp.bfloat16), "tensor", axis=0, tiled=True),
            lax.all_gather(cotangent_rows, "tensor", axis=0, tiled=True),
        )
        projected = jnp.einsum(
            "td,cde->cte", normed_all, full_qkv, preferred_element_type=jnp.float32
        )
        query_low = (projected[0] + query_shift).astype(jnp.bfloat16)
        key_low = projected[1].astype(jnp.bfloat16)
        value_low = (projected[2] + value_shift).astype(jnp.bfloat16)
        query_seqs = query_low.reshape(seqs_here, LEN, width_here)
        key_seqs = key_low.reshape(seqs_here, LEN, width_here)
        value_seqs = value_low.reshape(seqs_here, LEN, width_here)
        starts_here = piece_starts[batch_index]
        context_seq, logsum = lax.map(forward_one, (query_seqs, key_seqs, value_seqs, starts_here))
        context_low = context_seq.reshape(group_rows, width_here).astype(jnp.bfloat16)
        attended = lax.psum_scatter(
            slice_term(context_low, full_out, "tc,cd->td").astype(jnp.bfloat16),
            "tensor",
            scatter_dimension=0,
            tiled=True,
        ).astype(jnp.float32)
        middle = token_rows + attended + vectors[4]
        normed_two = layer_norm(middle, vectors[5], vectors[6])
        normed_two_all = lax.all_gather(
            normed_two.astype(jnp.bfloat16), "tensor", axis=0, tiled=True
        )
        before = jnp.dot(normed_two_all, full_up, preferred_element_type=jnp.float32) + up_shift
        activated = gelu_tanh(before).astype(jnp.bfloat16)
        expanded = lax.psum_scatter(
            slice_term(activated, full_down, "tf,fd->td").astype(jnp.bfloat16),
            "tensor",
            scatter_dimension=0,
            tiled=True,
        ).astype(jnp.float32)
        outputs_list.append((middle + expanded + vectors[11]).astype(jnp.bfloat16))
        grad_down = jnp.einsum(
            "tf,td->fd", activated, cotangent_all, preferred_element_type=jnp.float32
        )
        grad_activated = jnp.einsum(
            "td,fd->tf", cotangent_all, full_down, preferred_element_type=jnp.float32
        )
        gelu_pull = jax.vjp(gelu_tanh, before)[1]
        grad_before = gelu_pull(grad_activated)[0].astype(jnp.bfloat16)
        grad_up = jnp.einsum(
            "td,tf->df", normed_two_all, grad_before, preferred_element_type=jnp.float32
        )
        grad_normed_two = lax.psum_scatter(
            slice_term(grad_before, full_up, "tf,df->td").astype(jnp.bfloat16),
            "tensor",
            scatter_dimension=0,
            tiled=True,
        ).astype(jnp.float32)
        second_pull = jax.vjp(layer_norm, middle, vectors[5], vectors[6])[1]
        middle_from_norm, gain_two_grad, shift_two_grad = second_pull(grad_normed_two)
        grad_middle = cotangent_rows.astype(jnp.float32) + middle_from_norm
        grad_middle_all = lax.all_gather(
            grad_middle.astype(jnp.bfloat16), "tensor", axis=0, tiled=True
        )
        grad_out = jnp.einsum(
            "tc,td->cd", context_low, grad_middle_all, preferred_element_type=jnp.float32
        )
        grad_context = jnp.einsum(
            "td,cd->tc", grad_middle_all, full_out, preferred_element_type=jnp.float32
        ).astype(jnp.bfloat16)
        grad_query, grad_key, grad_value = lax.map(
            backward_one,
            (
                query_seqs,
                key_seqs,
                value_seqs,
                grad_context.reshape(seqs_here, LEN, width_here),
                logsum,
                starts_here,
            ),
        )
        grad_stack = jnp.stack(
            [
                grad_query.reshape(group_rows, width_here),
                grad_key.reshape(group_rows, width_here),
                grad_value.reshape(group_rows, width_here),
            ]
        )
        grad_qkv = jnp.einsum(
            "td,cte->cde", normed_all, grad_stack, preferred_element_type=jnp.float32
        )
        grad_normed_one = lax.psum_scatter(
            slice_term(grad_stack, full_qkv, "cte,cde->td").astype(jnp.bfloat16),
            "tensor",
            scatter_dimension=0,
            tiled=True,
        ).astype(jnp.float32)
        first_pull = jax.vjp(layer_norm, token_rows, vectors[0], vectors[1])[1]
        token_from_norm, gain_one_grad, shift_one_grad = first_pull(grad_normed_one)
        input_grads.append(grad_middle + token_from_norm)
        query_bias = jnp.sum(grad_stack[0], axis=0, dtype=jnp.float32)
        value_bias = jnp.sum(grad_stack[2], axis=0, dtype=jnp.float32)
        up_bias = jnp.sum(grad_before, axis=0, dtype=jnp.float32)
        head_rows = jnp.stack(
            [
                gain_one_grad,
                shift_one_grad,
                placed(query_bias, tensor_rank * width_here, D),
                placed(value_bias, tensor_rank * width_here, D),
                jnp.sum(grad_middle, axis=0),
                gain_two_grad,
                shift_two_grad,
            ]
        )
        up_rows = placed(up_bias, tensor_rank * hidden_here, FF).reshape(4, D)
        tail_row = jnp.sum(cotangent_rows, axis=0, dtype=jnp.float32)[None, :]
        vector_total = vector_total + jnp.concatenate([head_rows, up_rows, tail_row], axis=0)
        shard_grads = (
            lax.psum_scatter(
                grad_qkv.astype(jnp.bfloat16), "dp", scatter_dimension=1, tiled=True
            ).astype(jnp.float32),
            lax.psum_scatter(
                grad_out.astype(jnp.bfloat16), "dp", scatter_dimension=1, tiled=True
            ).astype(jnp.float32),
            lax.psum_scatter(
                grad_up.astype(jnp.bfloat16), "dp", scatter_dimension=0, tiled=True
            ).astype(jnp.float32),
            lax.psum_scatter(
                grad_down.astype(jnp.bfloat16), "dp", scatter_dimension=1, tiled=True
            ).astype(jnp.float32),
        )
        grad_total = accumulate(grad_total, shard_grads)
    grad_qkv_shard, grad_out_shard, grad_up_shard, grad_down_shard = grad_total
    moment_qkv = MOMENTUM_DECAY * m_qkv + grad_qkv_shard
    moment_out = MOMENTUM_DECAY * m_out + grad_out_shard
    moment_up = MOMENTUM_DECAY * m_up + grad_up_shard
    moment_down = MOMENTUM_DECAY * m_down + grad_down_shard
    squares = jnp.concatenate(
        [
            jnp.sum(moment_qkv * moment_qkv, axis=(1, 2)),
            jnp.stack(
                [
                    jnp.sum(moment_out * moment_out),
                    jnp.sum(moment_up * moment_up),
                    jnp.sum(moment_down * moment_down),
                ]
            ),
        ]
    )
    vector_grad, square_total = lax.psum((vector_total, squares), ("dp", "tensor"))
    factors = lax.rsqrt(square_total + SQUARE_EPSILON)
    scaled_qkv = (moment_qkv * factors[0:3][:, None, None]).astype(jnp.bfloat16)
    scaled_out = (moment_out * factors[3]).astype(jnp.bfloat16)
    scaled_up = (moment_up * factors[4]).astype(jnp.bfloat16)
    scaled_down = (moment_down * factors[5]).astype(jnp.bfloat16)
    gathered_qkv, gathered_out, gathered_up, gathered_down = (
        lax.all_gather(scaled_qkv, "dp", axis=1, tiled=True),
        lax.all_gather(scaled_out, "dp", axis=1, tiled=True),
        lax.all_gather(scaled_up, "dp", axis=0, tiled=True),
        lax.all_gather(scaled_down, "dp", axis=1, tiled=True),
    )
    offset = shard_rank * shard_rows
    narrow_rows = jnp.concatenate([jnp.swapaxes(gathered_qkv, 1, 2), gathered_out[None]], axis=0)
    wide_rows = jnp.stack([gathered_up.T, gathered_down])
    for sweep_index in range(NS_ITERS):
        gram_share = lax.psum_scatter(
            gram_term(narrow_rows, wide_rows).astype(jnp.bfloat16),
            "tensor",
            scatter_dimension=0,
            tiled=True,
        )
        gram_matrix = lax.all_gather(gram_share, "tensor", axis=0, tiled=True)
        narrow_rows = schulz_step(narrow_rows, gram_matrix[:, 0:4])
        wide_rows = schulz_step(wide_rows, gram_matrix[:, 4:6])
    final_narrow = narrow_rows.astype(jnp.float32)
    final_wide = wide_rows.astype(jnp.float32)
    update_qkv = lax.dynamic_slice_in_dim(
        jnp.swapaxes(final_narrow[0:3], 1, 2), offset, shard_rows, 1
    )
    update_out = lax.dynamic_slice_in_dim(final_narrow[3], offset, shard_rows, 1)
    update_up = lax.dynamic_slice_in_dim(final_wide[0].T, offset, shard_rows, 0)
    update_down = lax.dynamic_slice_in_dim(final_wide[1], offset, shard_rows, 1)
    wide_factor = math.sqrt(FF / D)
    new_qkv = w_qkv - MATRIX_RATE * update_qkv
    new_out = w_out - MATRIX_RATE * update_out
    new_up = w_up - MATRIX_RATE * wide_factor * update_up
    new_down = w_down - MATRIX_RATE * wide_factor * update_down
    moment_vec = MOMENTUM_DECAY * m_vec + vector_grad
    new_vec = vectors - VECTOR_RATE * moment_vec * lax.rsqrt(
        jnp.mean(moment_vec * moment_vec, axis=1, keepdims=True) + SQUARE_EPSILON
    )
    return (
        jnp.stack(outputs_list),
        jnp.stack(input_grads),
        grad_qkv_shard,
        grad_out_shard,
        grad_up_shard,
        grad_down_shard,
        vector_grad,
        moment_qkv,
        moment_out,
        moment_up,
        moment_down,
        moment_vec,
        new_qkv,
        new_out,
        new_up,
        new_down,
        new_vec,
    )


def solution(mesh):
    in_specs = (
        P(None, ("dp", "tensor"), None),
        P(None, ("dp", "tensor"), None),
        P(None, "dp", None),
        P(None, "dp", "tensor"),
        P("tensor", "dp"),
        P("dp", "tensor"),
        P("tensor", "dp"),
        P(),
        P(None, "dp", "tensor"),
        P("tensor", "dp"),
        P("dp", "tensor"),
        P("tensor", "dp"),
        P(),
    )
    out_specs = (
        P(None, ("dp", "tensor"), None),
        P(None, ("dp", "tensor"), None),
        P(None, "dp", "tensor"),
        P("tensor", "dp"),
        P("dp", "tensor"),
        P("tensor", "dp"),
        P(),
        P(None, "dp", "tensor"),
        P("tensor", "dp"),
        P("dp", "tensor"),
        P("tensor", "dp"),
        P(),
        P(None, "dp", "tensor"),
        P("tensor", "dp"),
        P("dp", "tensor"),
        P("tensor", "dp"),
        P(),
    )
    return jax.shard_map(
        on_device, mesh=mesh, in_specs=in_specs, out_specs=out_specs, check_vma=False
    )
```

profile of v0, /device:TPU:9, one launch (start us, length us, event | category | flops | bytes accessed | tf_op | source)
XLA Modules:
  0.0 2852.6 jit_solution(16016373851216793956)
XLA Ops:
  22.9 26.8 all-gather.22.cloned.1.call-done
  49.6 48.8 %all-gather.24.cloned.1.call-done = bf16[3,1024,512]{2,1,0:T(8,128)(2,1)} async-done(((bf16[3,64,512]{2,1,0:T(8,128)(2,1)}), bf16[3,1024,512]{2,1,0:T(8,128)(2,1)}) %all-gather.24.cloned.1.call-update) | async-done | bytes 3145744 | tf_op jit(solution)/shard_map/all_gather | solution.py:202
  105.8 18.6 fusion.254
  124.5 13.1 fusion.2
  138.2 14.9 fusion.201
  157.6 29.9 %reduce-scatter.22.cloned.1.call-done = bf16[512,1024]{1,0:T(8,128)(2,1)} async-done(((bf16[1024,1024]{1,0:T(8,128)(2,1)}), bf16[512,1024]{1,0:T(8,128)(2,1)}) %reduce-scatter.22.cloned.1.call-update) | async-done | bytes 1048592 | tf_op jit(solution)/shard_map/reduce_scatter | solution.py:226
  190.9 33.2 %all-gather.34.cloned.1.call-done = bf16[1024,1024]{1,0:T(8,128)(2,1)} async-done(((bf16[512,1024]{1,0:T(8,128)(2,1)}), bf16[1024,1024]{1,0:T(8,128)(2,1)}) %all-gather.34.cloned.1.call-update) | async-done | bytes 2097168 | tf_op jit(solution)/shard_map/all_gather | solution.py:211
  232.2 18.4 fusion.255
  250.6 13.1 fusion.3
  263.7 14.9 fusion.200
  284.6 30.1 %reduce-scatter.26.cloned.1.call-done = bf16[512,1024]{1,0:T(8,128)(2,1)} async-done(((bf16[1024,1024]{1,0:T(8,128)(2,1)}), bf16[512,1024]{1,0:T(8,128)(2,1)}) %reduce-scatter.26.cloned.1.call-update) | async-done | bytes 1048592 | tf_op jit(solution)/shard_map/reduce_scatter | solution.py:226
  327.2 41.1 %all-gather.30.cloned.1.call-done = bf16[1024,2048]{1,0:T(8,128)(2,1)} async-done(((bf16[64,2048]{1,0:T(8,128)(2,1)}), bf16[1024,2048]{1,0:T(8,128)(2,1)}) %all-gather.30.cloned.1.call-update) | async-done | bytes 4194320 | tf_op jit(solution)/shard_map/all_gather | solution.py:204
  368.4 33.3 %all-gather.36.cloned.1.call-done = bf16[1024,1024]{1,0:T(8,128)(2,1)} async-done(((bf16[512,1024]{1,0:T(8,128)(2,1)}), bf16[1024,1024]{1,0:T(8,128)(2,1)}) %all-gather.36.cloned.1.call-update) | async-done | bytes 2097168 | tf_op jit(solution)/shard_map/all_gather | solution.py:234
  401.7 10.9 fusion.257
  412.6 23.8 all-gather.58.cloned.1.call-done
  436.4 53.8 %all-gather.32.cloned.1.call-done = bf16[2048,1024]{0,1:T(8,128)(2,1)} async-done(((bf16[2048,64]{0,1:T(8,128)(2,1)}), bf16[2048,1024]{0,1:T(8,128)(2,1)}) %all-gather.32.cloned.1.call-update) | async-done | bytes 4194320 | tf_op jit(solution)/shard_map/all_gather | solution.py:205
  490.2 13.7 convert_reduce_fusion
  512.0 10.9 all-gather.28.cloned.1.call-done
  540.3 17.2 all-gather.56.cloned.1.call-done
  557.5 13.7 convert_reduce_fusion.1
  579.5 11.4 convolution_convert_fusion.6
  591.6 34.1 %reduce-scatter.24.cloned.1.call-done = bf16[512,1024]{1,0:T(8,128)(2,1)} async-done(((bf16[1024,1024]{1,0:T(8,128)(2,1)}), bf16[512,1024]{1,0:T(8,128)(2,1)}) %reduce-scatter.24.cloned.1.call-update) | async-done | bytes 1048592 | tf_op jit(solution)/shard_map/reduce_scatter | solution.py:239
  625.7 33.9 %reduce-scatter.30.cloned.1.call-done = bf16[512,1024]{1,0:T(8,128)(2,1)} async-done(((bf16[1024,1024]{1,0:T(8,128)(2,1)}), bf16[512,1024]{1,0:T(8,128)(2,1)}) %reduce-scatter.30.cloned.1.call-update) | async-done | bytes 1048592 | tf_op jit(solution)/shard_map/reduce_scatter | solution.py:257
  664.6 29.1 %reduce-scatter.28.cloned.1.call-done = bf16[512,1024]{1,0:T(8,128)(2,1)} async-done(((bf16[1024,1024]{1,0:T(8,128)(2,1)}), bf16[512,1024]{1,0:T(8,128)(2,1)}) %reduce-scatter.28.cloned.1.call-update) | async-done | bytes 1048592 | tf_op jit(solution)/shard_map/reduce_scatter | solution.py:239
  708.1 10.8 convolution_convert_fusion
  720.5 10.3 convolution_convert_fusion.1
  754.9 15.3 convert_reduce_fusion.12
  770.2 22.1 multiply_reduce_fusion.1
  794.7 29.3 %multiply_convert_fusion.1 = bf16[8,1024,1024]{1,2,0:T(8,128)(2,1)} fusion(f32[8,1024,1024]{1,2,0:T(8,128)} %get-tuple-element.270, f32[8,1024,1024]{1,2,0:T(8,128)} %get-tuple-element.266, f32[8,1024]{1,0:T(8,128)S(1)} %get-tuple-element.269, f32[8,1024]{1,0:T(8,128)S(1)} %log_add_fusion.1), kind=kLoop, calls=%fused_computation.7 | loop fusion | flops 33554432 | bytes 83951616 | tf_op jit(solution)/shard_map/while/body/eval_jaxpr/convert_element_type | solution.py:98
  836.3 11.1 multiply_convert_fusion.6
  856.4 15.8 convert_reduce_fusion.10
  872.2 22.1 multiply_reduce_fusion
  894.4 29.3 %multiply_convert_fusion = bf16[8,1024,1024]{1,2,0:T(8,128)(2,1)} fusion(f32[8,1024,1024]{1,2,0:T(8,128)} %get-tuple-element.272, f32[8,1024,1024]{1,2,0:T(8,128)} %get-tuple-element.268, f32[8,1024]{1,0:T(8,128)S(1)} %get-tuple-element.271, f32[8,1024]{1,0:T(8,128)S(1)} %log_add_fusion), kind=kLoop, calls=%fused_computation.4 | loop fusion | flops 33554432 | bytes 83951616 | tf_op jit(solution)/shard_map/while/body/eval_jaxpr/convert_element_type | solution.py:98
  955.4 11.5 multiply_convert_fusion.4
  1004.4 71.9 %reduce-scatter.38.cloned.1.call-done = bf16[64,2048]{1,0:T(8,128)(2,1)} async-done(((bf16[1024,2048]{1,0:T(8,128)(2,1)}), bf16[64,2048]{1,0:T(8,128)(2,1)}) %reduce-scatter.38.cloned.1.call-update) | async-done | bytes 262160 | tf_op jit(solution)/shard_map/reduce_scatter | solution.py:329
  1079.1 57.2 %reduce-scatter.52.cloned.1.call-done = bf16[64,512]{1,0:T(8,128)(2,1)} async-done(((bf16[1024,512]{1,0:T(8,128)(2,1)}), bf16[64,512]{1,0:T(8,128)(2,1)}) %reduce-scatter.52.cloned.1.call-update) | async-done | bytes 65552
  1137.3 59.4 %reduce-scatter.54.cloned.1.call-done = bf16[64,512]{1,0:T(8,128)(2,1)} async-done(((bf16[1024,512]{1,0:T(8,128)(2,1)}), bf16[64,512]{1,0:T(8,128)(2,1)}) %reduce-scatter.54.cloned.1.call-update) | async-done | bytes 65552
  1199.0 173.1 %all-reduce.6.cloned.1.call-done = (bf16[3,1024,512]{2,0,1:T(4,128)(2,1)}, bf16[3,1024,512]{2,0,1:T(4,128)(2,1)}) async-done(((bf16[3,1024,512]{2,0,1:T(4,128)(2,1)}, bf16[3,1024,512]{2,0,1:T(4,128)(2,1)}), (bf16[3,1024,512]{2,0,1:T(4,128)(2,1)}, bf16[3,1024,512]{2,0,1:T(4,128)(2,1)})) %all-reduce.6.cloned.1.call-update) | async-done | bytes 6291472
  1376.9 30.0 %reduce-scatter.32.cloned.1.call-done = bf16[512,1024]{1,0:T(8,128)(2,1)} async-done(((bf16[1024,1024]{1,0:T(8,128)(2,1)}), bf16[512,1024]{1,0:T(8,128)(2,1)}) %reduce-scatter.32.cloned.1.call-update) | async-done | bytes 1048592 | tf_op jit(solution)/shard_map/reduce_scatter | solution.py:296
  1406.9 33.9 %reduce-scatter.36.cloned.1.call-done = bf16[512,1024]{1,0:T(8,128)(2,1)} async-done(((bf16[1024,1024]{1,0:T(8,128)(2,1)}), bf16[512,1024]{1,0:T(8,128)(2,1)}) %reduce-scatter.36.cloned.1.call-update) | async-done | bytes 1048592 | tf_op jit(solution)/shard_map/reduce_scatter | solution.py:296
  1447.5 39.6 %all-reduce.2 = (f32[12,1024]{1,0:T(8,128)}, f32[6]{0:T(128)S(1)}) all-reduce(f32[12,1024]{1,0:T(8,128)S(1)} %add.492, f32[6]{0:T(128)S(1)} %pad_maximum_fusion.23), channel_id=1, replica_groups=mesh['dp'=16,'tensor'=2] {'dp','tensor'}, use_global_device_ids=true, to_apply=%region_58.59 | all-reduce | flops 12294 | bytes 98352 | tf_op jit(solution)/shard_map/psum | solution.py:354
  1496.3 31.9 %all-gather.44.cloned.1.call-done = bf16[512,1024]{0,1:T(8,128)(2,1)} async-done(((bf16[512,64]{0,1:T(8,128)(2,1)}), bf16[512,1024]{0,1:T(8,128)(2,1)}) %all-gather.44.cloned.1.call-update) | async-done | bytes 1048592 | tf_op jit(solution)/shard_map/all_gather | solution.py:362
  1530.6 46.3 %all-gather.42.cloned.1.call-done = bf16[3,1024,512]{2,1,0:T(8,128)(2,1)} async-done(((bf16[3,64,512]{2,1,0:T(8,128)(2,1)}), bf16[3,1024,512]{2,1,0:T(8,128)(2,1)}) %all-gather.42.cloned.1.call-update) | async-done | bytes 3145744 | tf_op jit(solution)/shard_map/all_gather | solution.py:361
  1580.0 10.5 convert_bitcast_fusion.2
  1590.5 38.1 %all-gather.48.cloned.1.call-done = bf16[2048,1024]{0,1:T(8,128)(2,1)} async-done(((bf16[2048,64]{0,1:T(8,128)(2,1)}), bf16[2048,1024]{0,1:T(8,128)(2,1)}) %all-gather.48.cloned.1.call-update) | async-done | bytes 4194320 | tf_op jit(solution)/shard_map/all_gather | solution.py:364
  1628.6 51.5 %all-gather.46.cloned.1.call-done = bf16[1024,2048]{1,0:T(8,128)(2,1)} async-done(((bf16[64,2048]{1,0:T(8,128)(2,1)}), bf16[1024,2048]{1,0:T(8,128)(2,1)}) %all-gather.46.cloned.1.call-update) | async-done | bytes 4194320 | tf_op jit(solution)/shard_map/all_gather | solution.py:363
  1680.1 14.9 convert_bitcast_fusion.5
  1704.5 142.7 %reduce-scatter.46.cloned.1.call-done = bf16[512,6,1024]{0,2,1:T(8,128)(2,1)} async-done(((bf16[1024,6,1024]{0,2,1:T(8,128)(2,1)}), bf16[512,6,1024]{0,2,1:T(8,128)(2,1)}) %reduce-scatter.46.cloned.1.call-update) | async-done | bytes 6291472 | tf_op jit(solution)/shard_map/reduce_scatter | solution.py:370
  1847.4 153.7 %all-gather.50.cloned.1.call-done = bf16[1024,6,1024]{0,2,1:T(8,128)(2,1)} async-done(((bf16[512,6,1024]{0,2,1:T(8,128)(2,1)}), bf16[1024,6,1024]{0,2,1:T(8,128)(2,1)}) %all-gather.50.cloned.1.call-update) | async-done | bytes 12582928 | tf_op jit(solution)/shard_map/all_gather | solution.py:376
  2001.1 25.6 fusion.7
  2026.7 15.2 convert_bitcast_fusion.4
  2041.9 19.3 fusion.27
  2078.2 144.6 %reduce-scatter.48.cloned.1.call-done = bf16[512,6,1024]{0,2,1:T(8,128)(2,1)} async-done(((bf16[1024,6,1024]{0,2,1:T(8,128)(2,1)}), bf16[512,6,1024]{0,2,1:T(8,128)(2,1)}) %reduce-scatter.48.cloned.1.call-update) | async-done | bytes 6291472 | tf_op jit(solution)/shard_map/reduce_scatter | solution.py:370
  2222.9 154.1 %all-gather.52.cloned.1.call-done = bf16[1024,6,1024]{0,2,1:T(8,128)(2,1)} async-done(((bf16[512,6,1024]{0,2,1:T(8,128)(2,1)}), bf16[1024,6,1024]{0,2,1:T(8,128)(2,1)}) %all-gather.52.cloned.1.call-update) | async-done | bytes 12582928 | tf_op jit(solution)/shard_map/all_gather | solution.py:376
  2377.0 20.6 fusion.31
  2397.6 11.3 convert_bitcast_fusion
  2408.9 16.3 fusion.110
  2425.2 23.3 fusion.11
  2448.4 13.8 convert_bitcast_fusion.3
  2471.6 144.6 %reduce-scatter.50.cloned.1.call-done = bf16[512,6,1024]{0,2,1:T(8,128)(2,1)} async-done(((bf16[1024,6,1024]{0,2,1:T(8,128)(2,1)}), bf16[512,6,1024]{0,2,1:T(8,128)(2,1)}) %reduce-scatter.50.cloned.1.call-update) | async-done | bytes 6291472 | tf_op jit(solution)/shard_map/reduce_scatter | solution.py:370
  2637.2 132.9 %all-gather.54.cloned.1.call-done = bf16[1024,6,1024]{0,2,1:T(8,128)(2,1)} async-done(((bf16[512,6,1024]{0,2,1:T(8,128)(2,1)}), bf16[1024,6,1024]{0,2,1:T(8,128)(2,1)}) %all-gather.54.cloned.1.call-update) | async-done | bytes 12582928 | tf_op jit(solution)/shard_map/all_gather | solution.py:376
  2770.2 21.0 fusion.84
  2796.3 16.3 fusion.107
  2812.6 24.4 fusion.54
  (458 shorter events, 330.9 us)
Async XLA Ops:
  7.2 42.4 %all-gather.22.cloned.1.call-start = ((), (), s32[]{:S(2)}) async-start(), calls=%async_computation.17 | async-start | bytes 3145728 | tf_op jit(solution)/shard_map/all_gather | solution.py:211
  12.5 176.9 %copy-start.49 = (f32[1,1024]{1,0:T(1,128)}, f32[1,1024]{1,0:T(1,128)S(1)}, u32[]{:S(2)}) copy-start(f32[1,1024]{1,0:T(1,128)S(1)} %get-tuple-element.257) | copy-start | bytes 12292
  15.2 83.3 %all-gather.24.cloned.1.call-start = ((), (), s32[]{:S(2)}) async-start(), calls=%async_computation.18 | async-start | bytes 3342336 | tf_op jit(solution)/shard_map/all_gather | solution.py:202
  16.0 137.2 %all-gather.26.cloned.1.call-start = ((), (), s32[]{:S(2)}) async-start(), calls=%async_computation.19 | async-start | bytes 1114112 | tf_op jit(solution)/shard_map/all_gather | solution.py:203
  16.7 170.7 %reduce-scatter.22.cloned.1.call-start = ((), (), s32[]{:S(2)}) async-start(), calls=%async_computation.20 | async-start | bytes 3145728 | tf_op jit(solution)/shard_map/reduce_scatter | solution.py:226
  19.7 212.5 %copy-start.71 = (f32[8,64]{1,0:T(8,128)}, f32[8,64]{1,0:T(8,128)S(1)}, u32[]{:S(2)}) copy-start(f32[8,64]{1,0:T(8,128)S(1)} %add.443) | copy-start | bytes 6148
  19.8 243.9 %copy-start.45 = (f32[8,64]{1,0:T(8,128)}, f32[8,64]{1,0:T(8,128)S(1)}, u32[]{:S(2)}) copy-start(f32[8,64]{1,0:T(8,128)S(1)} %add.438) | copy-start | bytes 6148
  157.5 66.7 %all-gather.34.cloned.1.call-start = ((), (), s32[]{:S(2)}) async-start(), calls=%async_computation.25 | async-start | bytes 3145728 | tf_op jit(solution)/shard_map/all_gather | solution.py:211
  157.5 72.8 %copy-start.65 = (f32[512]{0:T(512)}, f32[512]{0:T(512)S(1)}, u32[]{:S(2)}) copy-start(f32[512]{0:T(512)S(1)} %broadcast_multiply_fusion.1) | copy-start | bytes 6148
  189.4 40.9 %copy-start.85 = (f32[512]{0:T(512)}, f32[512]{0:T(512)S(1)}, u32[]{:S(2)}) copy-start(f32[512]{0:T(512)S(1)} %get-tuple-element.203) | copy-start | bytes 6148
  189.4 40.9 %copy-start.76 = (f32[512]{0:T(512)}, f32[512]{0:T(512)S(1)}, u32[]{:S(2)}) copy-start(f32[512]{0:T(512)S(1)} %fusion.217) | copy-start | bytes 6148
  190.8 123.8 %reduce-scatter.26.cloned.1.call-start = ((), (), s32[]{:S(2)}) async-start(), calls=%async_computation.26 | async-start | bytes 3145728 | tf_op jit(solution)/shard_map/reduce_scatter | solution.py:226
  278.7 36.0 %copy-start.3 = (bf16[512,1024]{1,0:T(8,128)(2,1)S(1)}, bf16[512,1024]{1,0:T(8,128)(2,1)}, u32[]{:S(2)}) copy-start(bf16[512,1024]{1,0:T(8,128)(2,1)} %reduce-scatter.22.cloned.1.call-done) | copy-start | bytes 3145732
  282.6 85.7 %all-gather.30.cloned.1.call-start = ((), (), s32[]{:S(2)}) async-start(), calls=%async_computation.22 | async-start | bytes 4456448 | tf_op jit(solution)/shard_map/all_gather | solution.py:204
  284.5 117.2 %all-gather.36.cloned.1.call-start = ((), (), s32[]{:S(2)}) async-start(), calls=%async_computation.27 | async-start | bytes 3145728 | tf_op jit(solution)/shard_map/all_gather | solution.py:234
  319.9 116.5 %all-gather.58.cloned.1.call-start = ((), (), s32[]{:S(2)}) async-start(), calls=%async_computation.50 | async-start | bytes 3145728 | tf_op jit(solution)/shard_map/all_gather | solution.py:212
  323.2 167.0 %all-gather.32.cloned.1.call-start = ((), (), s32[]{:S(2)}) async-start(), calls=%async_computation.23 | async-start | bytes 4456448 | tf_op jit(solution)/shard_map/all_gather | solution.py:205
  325.0 197.9 %all-gather.28.cloned.1.call-start = ((), (), s32[]{:S(2)}) async-start(), calls=%async_computation.21 | async-start | bytes 3145728 | tf_op jit(solution)/shard_map/all_gather | solution.py:234
  325.7 231.8 %all-gather.56.cloned.1.call-start = ((), (), s32[]{:S(2)}) async-start(), calls=%async_computation.49 | async-start | bytes 3145728 | tf_op jit(solution)/shard_map/all_gather | solution.py:212
  326.3 265.3 %reduce-scatter.34.cloned.1.call-start = ((), (), s32[]{:S(2)}) async-start(), calls=%async_computation.32 | async-start | bytes 3145728 | tf_op jit(solution)/shard_map/reduce_scatter | solution.py:257
  511.8 113.9 %reduce-scatter.24.cloned.1.call-start = ((), (), s32[]{:S(2)}) async-start(), calls=%async_computation.24 | async-start | bytes 3145728 | tf_op jit(solution)/shard_map/reduce_scatter | solution.py:239
  540.2 119.4 %reduce-scatter.30.cloned.1.call-start = ((), (), s32[]{:S(2)}) async-start(), calls=%async_computation.29 | async-start | bytes 3145728 | tf_op jit(solution)/shard_map/reduce_scatter | solution.py:257
  579.1 80.6 %copy-start.70 = (f32[1,1024]{1,0:T(1,128)S(1)}, f32[1,1024]{1,0:T(1,128)}, u32[]{:S(2)}) copy-start(f32[1,1024]{1,0:T(1,128)} %get-tuple-element.250) | copy-start | bytes 12292
  579.1 114.6 %reduce-scatter.28.cloned.1.call-start = ((), (), s32[]{:S(2)}) async-start(), calls=%async_computation.28 | async-start | bytes 3145728 | tf_op jit(solution)/shard_map/reduce_scatter | solution.py:239
  591.0 159.8 %all-gather.38.cloned.1.call-start = ((), (), s32[]{:S(2)}) async-start(), calls=%async_computation.30 | async-start | bytes 3145728 | tf_op jit(solution)/shard_map/all_gather | solution.py:266
  706.6 146.9 %all-gather.40.cloned.1.call-start = ((), (), s32[]{:S(2)}) async-start(), calls=%async_computation.33 | async-start | bytes 3145728 | tf_op jit(solution)/shard_map/all_gather | solution.py:266
  707.9 293.8 %reduce-scatter.44.cloned.1.call-start = ((), (), s32[]{:S(2)}) async-start(), calls=%async_computation.38 | async-start | bytes 4456448 | tf_op jit(solution)/shard_map/reduce_scatter | solution.py:332
  719.0 282.7 %reduce-scatter.42.cloned.1.call-start = ((), (), s32[]{:S(2)}) async-start(), calls=%async_computation.37 | async-start | bytes 4456448 | tf_op jit(solution)/shard_map/reduce_scatter | solution.py:332
  730.8 273.6 %reduce-scatter.40.cloned.1.call-start = ((), (), s32[]{:S(2)}) async-start(), calls=%async_computation.36 | async-start | bytes 4456448 | tf_op jit(solution)/shard_map/reduce_scatter | solution.py:329
  740.7 335.6 %reduce-scatter.38.cloned.1.call-start = ((), (), s32[]{:S(2)}) async-start(), calls=%async_computation.35 | async-start | bytes 4456448 | tf_op jit(solution)/shard_map/reduce_scatter | solution.py:329
  750.7 385.7 %reduce-scatter.52.cloned.1.call-start = ((), (), s32[]{:S(2)}) async-start(), calls=%async_computation.51 | async-start | bytes 1114112
  894.3 302.4 %reduce-scatter.54.cloned.1.call-start = ((), (), s32[]{:S(2)}) async-start(), calls=%async_computation.52 | async-start | bytes 1114112
  955.1 417.0 %all-reduce.6.cloned.1.call-start = ((), (), s32[]{:S(2)}) async-start(), calls=%async_computation.53 | async-start | bytes 16777216
  980.1 426.8 %reduce-scatter.32.cloned.1.call-start = ((), (), s32[]{:S(2)}) async-start(), calls=%async_computation.31 | async-start | bytes 3145728 | tf_op jit(solution)/shard_map/reduce_scatter | solution.py:296
  988.5 452.3 %reduce-scatter.36.cloned.1.call-start = ((), (), s32[]{:S(2)}) async-start(), calls=%async_computation.34 | async-start | bytes 3145728 | tf_op jit(solution)/shard_map/reduce_scatter | solution.py:296
  996.3 80.1 %copy-start.42 = (f32[64,2048]{1,0:T(8,128)S(1)}, f32[64,2048]{1,0:T(8,128)}, u32[]{:S(2)}) copy-start(f32[64,2048]{1,0:T(8,128)} %param.23) | copy-start | bytes 1572868
  996.4 531.9 %all-gather.44.cloned.1.call-start = ((), (), s32[]{:S(2)}) async-start(), calls=%async_computation.40 | async-start | bytes 1114112 | tf_op jit(solution)/shard_map/all_gather | solution.py:362
  999.2 441.6 %copy-start.1 = (bf16[2,512,1024]{2,1,0:T(8,128)(2,1)S(1)}, bf16[2,512,1024]{2,1,0:T(8,128)(2,1)}, u32[]{:S(2)}) copy-start(bf16[2,512,1024]{2,1,0:T(8,128)(2,1)} %param.13) | copy-start | bytes 6291460
  999.2 441.6 %copy-start.50 = (f32[1,1024]{1,0:T(1,128)S(1)}, f32[1,1024]{1,0:T(1,128)}, u32[]{:S(2)}) copy-start(f32[1,1024]{1,0:T(1,128)} %copy-done.49) | copy-start | bytes 12292
  999.2 441.6 %copy-start.63 = (f32[512]{0:T(512)S(1)}, f32[512]{0:T(512)}, u32[]{:S(2)}) copy-start(f32[512]{0:T(512)} %copy-done.62) | copy-start | bytes 6148
  999.2 441.6 %copy-start.66 = (f32[512]{0:T(512)S(1)}, f32[512]{0:T(512)}, u32[]{:S(2)}) copy-start(f32[512]{0:T(512)} %copy-done.65) | copy-start | bytes 6148
  1079.1 364.7 %copy-start.84 = (f32[512]{0:T(512)S(1)}, f32[512]{0:T(512)}, u32[]{:S(2)}) copy-start(f32[512]{0:T(512)} %copy-done.83) | copy-start | bytes 6148
  1079.1 364.8 %copy-start.86 = (f32[512]{0:T(512)S(1)}, f32[512]{0:T(512)}, u32[]{:S(2)}) copy-start(f32[512]{0:T(512)} %copy-done.85) | copy-start | bytes 6148
  1079.1 364.8 %copy-start.74 = (f32[512]{0:T(512)S(1)}, f32[512]{0:T(512)}, u32[]{:S(2)}) copy-start(f32[512]{0:T(512)} %copy-done.73) | copy-start | bytes 6148
  1079.1 364.8 %copy-start.77 = (f32[512]{0:T(512)S(1)}, f32[512]{0:T(512)}, u32[]{:S(2)}) copy-start(f32[512]{0:T(512)} %copy-done.76) | copy-start | bytes 6148
  1199.0 288.6 %copy-start.30 = (f32[512,64]{1,0:T(8,128)}, f32[512,64]{1,0:T(8,128)S(1)}, u32[]{:S(2)}) copy-start(f32[512,64]{1,0:T(8,128)S(1)} %get-tuple-element.222) | copy-start | bytes 393220
  1376.8 70.2 %copy-start.88 = (f32[1024]{0:T(1024)S(1)}, f32[1024]{0:T(1024)}, u32[]{:S(2)}) copy-start(f32[1024]{0:T(1024)} %get-tuple-element.208) | copy-start | bytes 12292
  1376.8 70.2 %copy-start.91 = (f32[1024]{0:T(1024)S(1)}, f32[1024]{0:T(1024)}, u32[]{:S(2)}) copy-start(f32[1024]{0:T(1024)} %get-tuple-element.184) | copy-start | bytes 12292
  1376.8 70.2 %copy-start.92 = (f32[1024]{0:T(1024)S(1)}, f32[1024]{0:T(1024)}, u32[]{:S(2)}) copy-start(f32[1024]{0:T(1024)} %get-tuple-element.231) | copy-start | bytes 12292
  1376.8 70.4 %copy-start.87 = (f32[1024]{0:T(1024)S(1)}, f32[1024]{0:T(1024)}, u32[]{:S(2)}) copy-start(f32[1024]{0:T(1024)} %get-tuple-element.207) | copy-start | bytes 12292
  1376.8 70.4 %copy-start.89 = (f32[1024]{0:T(1024)S(1)}, f32[1024]{0:T(1024)}, u32[]{:S(2)}) copy-start(f32[1024]{0:T(1024)} %get-tuple-element.191) | copy-start | bytes 12292
  1376.9 70.4 %copy-start.90 = (f32[1024]{0:T(1024)S(1)}, f32[1024]{0:T(1024)}, u32[]{:S(2)}) copy-start(f32[1024]{0:T(1024)} %get-tuple-element.239) | copy-start | bytes 12292
  1406.9 37.0 %copy-start.10 = (bf16[512,1024]{1,0:T(8,128)(2,1)S(1)}, bf16[512,1024]{1,0:T(8,128)(2,1)}, u32[]{:S(2)}) copy-start(bf16[512,1024]{1,0:T(8,128)(2,1)} %reduce-scatter.32.cloned.1.call-done) | copy-start | bytes 3145732
  1489.1 87.7 %all-gather.42.cloned.1.call-start = ((), (), s32[]{:S(2)}) async-start(), calls=%async_computation.39 | async-start | bytes 3342336 | tf_op jit(solution)/shard_map/all_gather | solution.py:361
  1491.1 137.5 %all-gather.48.cloned.1.call-start = ((), (), s32[]{:S(2)}) async-start(), calls=%async_computation.42 | async-start | bytes 4456448 | tf_op jit(solution)/shard_map/all_gather | solution.py:364
  1493.6 186.5 %all-gather.46.cloned.1.call-start = ((), (), s32[]{:S(2)}) async-start(), calls=%async_computation.41 | async-start | bytes 4456448 | tf_op jit(solution)/shard_map/all_gather | solution.py:363
  1496.1 351.0 %reduce-scatter.46.cloned.1.call-start = ((), (), s32[]{:S(2)}) async-start(), calls=%async_computation.43 | async-start | bytes 18874368 | tf_op jit(solution)/shard_map/reduce_scatter | solution.py:370
  1704.4 296.7 %all-gather.50.cloned.1.call-start = ((), (), s32[]{:S(2)}) async-start(), calls=%async_computation.44 | async-start | bytes 18874368 | tf_op jit(solution)/shard_map/all_gather | solution.py:376
  1847.1 375.7 %reduce-scatter.48.cloned.1.call-start = ((), (), s32[]{:S(2)}) async-start(), calls=%async_computation.45 | async-start | bytes 18874368 | tf_op jit(solution)/shard_map/reduce_scatter | solution.py:370
  2078.2 298.8 %all-gather.52.cloned.1.call-start = ((), (), s32[]{:S(2)}) async-start(), calls=%async_computation.46 | async-start | bytes 18874368 | tf_op jit(solution)/shard_map/all_gather | solution.py:376
  2222.9 393.3 %reduce-scatter.50.cloned.1.call-start = ((), (), s32[]{:S(2)}) async-start(), calls=%async_computation.47 | async-start | bytes 18874368 | tf_op jit(solution)/shard_map/reduce_scatter | solution.py:370
  2471.5 144.7 %copy-start.44 = (f32[512,64]{0,1:T(8,128)S(1)}, f32[512,64]{0,1:T(8,128)}, u32[]{:S(2)}) copy-start(f32[512,64]{0,1:T(8,128)} %param.17) | copy-start | bytes 393220
  2471.5 298.6 %all-gather.54.cloned.1.call-start = ((), (), s32[]{:S(2)}) async-start(), calls=%async_computation.48 | async-start | bytes 18874368 | tf_op jit(solution)/shard_map/all_gather | solution.py:376
  2636.5 154.7 %copy-start.47 = (f32[12,1024]{1,0:T(8,128)}, f32[12,1024]{1,0:T(8,128)S(1)}, u32[]{:S(2)}) copy-start(f32[12,1024]{1,0:T(8,128)S(1)} %get-tuple-element.217) | copy-start | bytes 147460
  (86 other events, 834.7 us)
Sparse Core Ops, SparseCore 0:
  15.3 34.2 all-gather.21
  52.4 46.0 all-gather.23
  101.2 35.3 all-gather.25
  157.6 29.7 reduce-scatter.21
  191.0 33.1 all-gather.33
  282.7 31.8 reduce-scatter.25
  317.4 50.9 all-gather.29
  370.5 31.1 all-gather.35
  403.3 33.1 all-gather.57
  439.0 51.1 all-gather.31
  491.7 31.1 all-gather.27
  524.4 33.1 all-gather.55
  559.7 31.8 reduce-scatter.33
  593.8 31.8 reduce-scatter.23
  627.7 31.8 reduce-scatter.29
  661.8 31.8 reduce-scatter.27
  706.7 33.1 all-gather.37
  741.3 33.1 all-gather.39
  778.3 70.5 reduce-scatter.43
  853.0 71.5 reduce-scatter.41
  928.5 71.7 reduce-scatter.39
  1004.6 71.7 reduce-scatter.37
  1080.0 56.3 reduce-scatter.51
  1140.3 56.3 reduce-scatter.53
  1201.1 171.0 all-reduce.5
  1374.9 31.9 reduce-scatter.31
  1409.0 31.8 reduce-scatter.35
  1489.2 39.0 all-gather.43
  1531.3 45.4 all-gather.41
  1579.6 48.9 all-gather.47
  1631.0 49.0 all-gather.45
  1704.5 142.5 reduce-scatter.45
  1848.6 152.4 all-gather.49
  2078.3 144.4 reduce-scatter.47
  2224.5 152.4 all-gather.51
  2471.6 144.4 reduce-scatter.49
  2617.6 152.5 all-gather.53
where the time goes:
time: 2870 us; the launch traced here: 2850 us
  waiting for transfers between devices  1910 us (67%)
  matrix products  600 us (21%)
  other arithmetic  193 us (7%)
  local copies, waits for them, and re-layouts  84.7 us (3%)
  blocking collectives  39.6 us (1%)
    all_gather x3, waiting for transfers between devices, on_device(): gram_matrix = lax.all_gather(gram_share, 'tensor', axis=0, tiled=True)  441 us
    reduce_scatter x3, waiting for transfers between devices, on_device(): lax.psum_scatter(gram_term(narrow_rows, wide_rows).astype(jnp.bfloat16),...  432 us
    unnamed x40, waiting for transfers between devices  292 us
    dot_general x6, matrix products, schulz_step(): jnp.einsum('mrc,cmd->mrd', mixed, gram_matrix, preferred_element_type=jnp...  134 us
    reduce_scatter x2, waiting for transfers between devices, on_device(): lax.psum_scatter(grad_up.astype(jnp.bfloat16), 'dp', scatter_dimension=0,...  71.9 us
    reduce_scatter x2, waiting for transfers between devices, on_device(): lax.psum_scatter(slice_term(grad_stack, full_qkv, 'cte,cde->td').astype(j...  64 us
    reduce_scatter x2, waiting for transfers between devices, on_device(): lax.psum_scatter(slice_term(activated, full_down, 'tf,fd->td').astype(jnp...  63.1 us
    all_gather x2, waiting for transfers between devices, on_device(): lax.all_gather(normed_one.astype(jnp.bfloat16), 'tensor', axis=0, tiled=T...  60 us
  transfers between devices with their start and end apart: 37, of which 31 were waited for; matrix products, arithmetic and copies ran while one was open for 17% of the time, Pallas kernels for 0%

commit v1 on v0

--- a/solution.py
+++ b/solution.py
@@ -3,6 +3,8 @@
 import jax
 import jax.numpy as jnp
 from jax import lax
+from jax.experimental import pallas as pl
+from jax.experimental.pallas import tpu as pltpu
 from jax.sharding import PartitionSpec as P
 
 D = 1024
@@ -414,6 +416,345 @@
     )
 
 
+def layout_grid(starts_ref, dist_ref):
+    key_pos = lax.broadcasted_iota(jnp.int32, (LEN, LEN), 0)
+    query_pos = lax.broadcasted_iota(jnp.int32, (LEN, LEN), 1)
+    gap = query_pos - key_pos
+    visible = gap >= 0
+    for piece in range(NPIECE):
+        start = starts_ref[piece]
+        inside_key = (key_pos >= start) & (key_pos < start + PIECE)
+        inside_query = (query_pos >= start) & (query_pos < start + PIECE)
+        visible = visible | (inside_key & inside_query)
+    dist_ref[...] = jnp.where(visible, jnp.abs(gap).astype(jnp.float32), -MASKED_SCORE)
+
+
+def attend_fwd_kernel(starts_ref, slopes_ref, q_ref, k_ref, v_ref, ctx_ref, exps_ref, stat_ref, dist_ref):
+    head = pl.program_id(0)
+
+    @pl.when(head == 0)
+    def _():
+        layout_grid(starts_ref, dist_ref)
+
+    slope = slopes_ref[head]
+    keys = k_ref[0, 0, 0].T
+    queries = q_ref[0, 0, 0] * (1.0 / math.sqrt(HD))
+    for block in range(LEN // QB):
+        span = min(LEN, QB * block + QB + PIECE)
+        cols = slice(block * QB, block * QB + QB)
+        scores = jnp.dot(keys[:span], queries[:, cols], preferred_element_type=jnp.float32)
+        scores = scores - slope * dist_ref[:span, cols]
+        top = jnp.max(scores, axis=0, keepdims=True)
+        raw = jnp.exp(scores - top)
+        inverse = 1.0 / jnp.sum(raw, axis=0, keepdims=True)
+        low = raw.astype(jnp.bfloat16)
+        exps_ref[0, :span, cols] = low
+        context = jnp.dot(v_ref[0, 0, 0, :, :span], low, preferred_element_type=jnp.float32)
+        ctx_ref[0, :, cols] = (context * inverse).astype(jnp.bfloat16)
+        stat_ref[0, :, cols] = inverse
+
+
+def attend_bwd_kernel(q_ref, k_ref, v_ref, ctx_ref, grad_ref, exps_ref, stat_ref, dq_ref, dk_ref, dv_ref, dk_sum, dv_sum):
+    scale = 1.0 / math.sqrt(HD)
+    keys_t = k_ref[0, 0, 0]
+    values = v_ref[0, 0, 0].T
+    queries = q_ref[0, 0, 0].T
+    dk_sum[...] = jnp.zeros_like(dk_sum)
+    dv_sum[...] = jnp.zeros_like(dv_sum)
+    for block in reversed(range(LEN // QB)):
+        span = min(LEN, QB * block + QB + PIECE)
+        cols = slice(block * QB, block * QB + QB)
+        grad = grad_ref[0, :, cols].astype(jnp.float32) * stat_ref[0, :, cols]
+        inner = jnp.sum(grad * ctx_ref[0, :, cols].astype(jnp.float32), axis=0, keepdims=True)
+        grad_low = grad.astype(jnp.bfloat16)
+        exps = exps_ref[0, :span, cols]
+        grad_probs = jnp.dot(values[:span], grad_low, preferred_element_type=jnp.float32)
+        grad_scores = (exps.astype(jnp.float32) * (grad_probs - inner)).astype(jnp.bfloat16)
+        dv_sum[:span, :] += jnp.dot(exps, grad_low.T, preferred_element_type=jnp.float32)
+        dk_sum[:span, :] += jnp.dot(grad_scores, queries[cols], preferred_element_type=jnp.float32)
+        dq = jnp.dot(keys_t[:, :span], grad_scores, preferred_element_type=jnp.float32)
+        dq_ref[0, :, cols] = (dq * scale).astype(jnp.bfloat16)
+    dk_ref[0] = (dk_sum[...] * scale).T.astype(jnp.bfloat16)
+    dv_ref[0] = dv_sum[...].T.astype(jnp.bfloat16)
+
+
+QB = 256
+
+
+def part_spec(part, heads_each):
+    return pl.BlockSpec((1, 1, 1, HD, LEN), lambda h: (h // heads_each, part, h % heads_each, 0, 0))
+
+
+HEAD_ROWS = pl.BlockSpec((1, HD, LEN), lambda h: (h, 0, 0))
+HEAD_GRID = pl.BlockSpec((1, LEN, LEN), lambda h: (h, 0, 0))
+HEAD_STAT = pl.BlockSpec((1, 1, LEN), lambda h: (h, 0, 0))
+SCALARS = pl.BlockSpec(memory_space=pltpu.SMEM)
+VMEM_LIMIT = 56 * 1024 * 1024
+
+
+def attention_forward(starts, slopes, packed):
+    heads_each = packed.shape[2]
+    return pl.pallas_call(
+        attend_fwd_kernel,
+        grid=(H,),
+        in_specs=[SCALARS, SCALARS] + [part_spec(part, heads_each) for part in range(3)],
+        out_specs=[HEAD_ROWS, HEAD_GRID, HEAD_STAT],
+        out_shape=[
+            jax.ShapeDtypeStruct((H, HD, LEN), jnp.bfloat16),
+            jax.ShapeDtypeStruct((H, LEN, LEN), jnp.bfloat16),
+            jax.ShapeDtypeStruct((H, 1, LEN), jnp.float32),
+        ],
+        scratch_shapes=[pltpu.VMEM((LEN, LEN), jnp.float32)],
+        compiler_params=pltpu.CompilerParams(vmem_limit_bytes=VMEM_LIMIT),
+        cost_estimate=pl.CostEstimate(flops=4 * LEN * LEN * D * 4, bytes_accessed=44 * 1024 * 1024, transcendentals=H * LEN * LEN),
+    )(starts, slopes, packed, packed, packed)
+
+
+def attention_backward(packed, context, grad_context, exps, stats):
+    heads_each = packed.shape[2]
+    return pl.pallas_call(
+        attend_bwd_kernel,
+        grid=(H,),
+        in_specs=[part_spec(part, heads_each) for part in range(3)]
+        + [HEAD_ROWS, HEAD_ROWS, HEAD_GRID, HEAD_STAT],
+        out_specs=[HEAD_ROWS, HEAD_ROWS, HEAD_ROWS],
+        out_shape=[jax.ShapeDtypeStruct((H, HD, LEN), jnp.bfloat16)] * 3,
+        scratch_shapes=[pltpu.VMEM((LEN, HD), jnp.float32), pltpu.VMEM((LEN, HD), jnp.float32)],
+        compiler_params=pltpu.CompilerParams(vmem_limit_bytes=VMEM_LIMIT),
+        cost_estimate=pl.CostEstimate(flops=8 * LEN * LEN * D * 4, bytes_accessed=50 * 1024 * 1024, transcendentals=0),
+    )(packed, packed, packed, context, grad_context, exps, stats)
+
+
+BOTH = ("tensor", "dp")
+SWAP = [(0, 1), (1, 0)]
+
+
+def narrow(rows):
+    return rows.astype(jnp.bfloat16)
+
+
+def contract(left, right, left_dim, right_dim):
+    return lax.dot_general(
+        left, right, (((left_dim,), (right_dim,)), ((), ())), preferred_element_type=jnp.float32
+    )
+
+
+def swap_halves(mine, rank):
+    rows = mine.shape[0] // 2
+    kept = lax.dynamic_slice_in_dim(mine, rank * rows, rows, 0)
+    sent = lax.dynamic_slice_in_dim(mine, (1 - rank) * rows, rows, 0)
+    got = lax.ppermute(sent, "tensor", SWAP)
+    return jnp.where(rank == 0, jnp.stack([kept, got]), jnp.stack([got, kept]))
+
+
+def join_halves(pair, rank):
+    kept = lax.dynamic_index_in_dim(pair, rank, 0, keepdims=False)
+    sent = lax.dynamic_index_in_dim(pair, 1 - rank, 0, keepdims=False)
+    got = lax.ppermute(sent, "tensor", SWAP)
+    return jnp.where(rank == 0, jnp.concatenate([kept, got]), jnp.concatenate([got, kept]))
+
+
+def sequence_step(
+    tokens,
+    cotangent,
+    piece_starts,
+    w_qkv,
+    w_out,
+    w_up,
+    w_down,
+    vectors,
+    m_qkv,
+    m_out,
+    m_up,
+    m_down,
+    m_vec,
+):
+    rank = lax.axis_index("tensor")
+    parts = lax.axis_size("tensor")
+    width = D // parts
+    hidden = FF // parts
+    shard_rows = w_qkv.shape[1]
+    slopes = jnp.exp2(-8.0 * jnp.arange(1, H + 1, dtype=jnp.float32) / H)
+
+    def spread(rows):
+        whole = lax.all_gather(rows, BOTH, axis=0, tiled=True)
+        return whole.reshape(parts, D, rows.shape[1])
+
+    def collect(grads):
+        return lax.psum_scatter(
+            grads.reshape(parts * D, -1), BOTH, scatter_dimension=0, tiled=True
+        ).astype(jnp.float32)
+
+    full_qkv = spread(narrow(jnp.swapaxes(w_qkv, 0, 1)).reshape(shard_rows, 3 * width))
+    token_rows = join_halves(tokens, rank).astype(jnp.float32)
+    full_out = spread(narrow(w_out.T))
+    full_up = spread(narrow(w_up))
+    full_down = spread(narrow(w_down.T))
+    cotangent_low = join_halves(cotangent, rank)
+    cotangent_rows = cotangent_low.astype(jnp.float32)
+    starts = lax.dynamic_slice_in_dim(piece_starts[:, 0], rank, 1, 0)[0]
+
+    normed_one = narrow(layer_norm(token_rows, vectors[0], vectors[1]))
+    shifts = jnp.stack([vectors[2], jnp.zeros((D,), jnp.float32), vectors[3]])
+    shifts = jnp.swapaxes(shifts.reshape(3, parts, width), 0, 1).reshape(parts, 3 * width, 1)
+    packed = jnp.stack(
+        [narrow(contract(full_qkv[part], normed_one, 0, 1) + shifts[part]) for part in range(parts)]
+    )
+    packed = packed.reshape(parts, 3, width // HD, HD, LEN)
+    context, exps, stats = attention_forward(starts, slopes, packed)
+    context_rows = context.reshape(parts, width, LEN)
+    attended = sum(contract(context_rows[part], full_out[part], 0, 1) for part in range(parts))
+    middle = token_rows + attended + vectors[4]
+    normed_two = narrow(layer_norm(middle, vectors[5], vectors[6]))
+    up_shift = vectors[7:11].reshape(parts, hidden)
+    before = [contract(normed_two, full_up[part], 1, 0) + up_shift[part] for part in range(parts)]
+    activated = [narrow(gelu_tanh(rows)) for rows in before]
+    expanded = sum(contract(activated[part], full_down[part], 1, 1) for part in range(parts))
+    block_rows = narrow(middle + expanded + vectors[11])
+
+    grad_down = jnp.stack([narrow(contract(cotangent_low, rows, 0, 0)) for rows in activated])
+    grad_before = []
+    for part in range(parts):
+        grad_activated = contract(cotangent_low, full_down[part], 1, 0)
+        gelu_pull = jax.vjp(gelu_tanh, before[part])[1]
+        grad_before.append(narrow(gelu_pull(grad_activated)[0]))
+    grad_up = jnp.stack([narrow(contract(normed_two, rows, 0, 0)) for rows in grad_before])
+    grad_down_shard = collect(grad_down)
+    grad_up_shard = collect(grad_up)
+    grad_normed_two = sum(contract(grad_before[part], full_up[part], 1, 1) for part in range(parts))
+    second_pull = jax.vjp(layer_norm, middle, vectors[5], vectors[6])[1]
+    middle_from_norm, gain_two_grad, shift_two_grad = second_pull(grad_normed_two)
+    grad_middle = cotangent_rows + middle_from_norm
+    grad_middle_low = narrow(grad_middle)
+    grad_out = jnp.stack(
+        [narrow(contract(grad_middle_low, context_rows[part], 0, 1)) for part in range(parts)]
+    )
+    grad_out_shard = collect(grad_out)
+    grad_context = jnp.stack(
+        [narrow(contract(full_out[part], grad_middle_low, 0, 1)) for part in range(parts)]
+    ).reshape(H, HD, LEN)
+    grad_parts = attention_backward(packed, context, grad_context, exps, stats)
+    grad_packed = jnp.stack([rows.reshape(parts, width, LEN) for rows in grad_parts], axis=1)
+    grad_packed = grad_packed.reshape(parts, 3 * width, LEN)
+    grad_qkv = jnp.stack([narrow(contract(normed_one, grad_packed[part], 0, 1)) for part in range(parts)])
+    grad_qkv_shard = collect(grad_qkv)
+    grad_normed_one = sum(contract(grad_packed[part], full_qkv[part], 0, 1) for part in range(parts))
+    first_pull = jax.vjp(layer_norm, token_rows, vectors[0], vectors[1])[1]
+    token_from_norm, gain_one_grad, shift_one_grad = first_pull(grad_normed_one)
+    grad_token_rows = grad_middle + token_from_norm
+    output_pair = swap_halves(block_rows, rank)
+    token_pair = swap_halves(narrow(grad_token_rows), rank).astype(jnp.float32)
+
+    row_sums = [
+        jnp.sum(rows.astype(jnp.float32), axis=2).reshape(D) for rows in (grad_parts[0], grad_parts[2])
+    ]
+    up_bias = jnp.concatenate([jnp.sum(rows, axis=0, dtype=jnp.float32) for rows in grad_before])
+    vector_total = jnp.concatenate(
+        [
+            jnp.stack(
+                [
+                    gain_one_grad,
+                    shift_one_grad,
+                    row_sums[0],
+                    row_sums[1],
+                    jnp.sum(grad_middle, axis=0),
+                    gain_two_grad,
+                    shift_two_grad,
+                ]
+            ),
+            up_bias.reshape(4, D),
+            jnp.sum(cotangent_rows, axis=0)[None],
+        ]
+    )
+    grad_qkv_shard = jnp.swapaxes(grad_qkv_shard.reshape(shard_rows, 3, width), 0, 1)
+    shards = (grad_qkv_shard, grad_out_shard.T, grad_up_shard, grad_down_shard.T)
+    outputs = muon_step(shards, vector_total, w_qkv, w_out, w_up, w_down, vectors, m_qkv, m_out, m_up, m_down, m_vec)
+    return (output_pair, token_pair) + outputs
+
+
+def muon_step(
+    shards, vector_total, w_qkv, w_out, w_up, w_down, vectors, m_qkv, m_out, m_up, m_down, m_vec
+):
+    shard_rank = lax.axis_index("dp")
+    shard_rows = w_qkv.shape[1]
+    grad_qkv_shard, grad_out_shard, grad_up_shard, grad_down_shard = shards
+    moment_qkv = MOMENTUM_DECAY * m_qkv + grad_qkv_shard
+    moment_out = MOMENTUM_DECAY * m_out + grad_out_shard
+    moment_up = MOMENTUM_DECAY * m_up + grad_up_shard
+    moment_down = MOMENTUM_DECAY * m_down + grad_down_shard
+    squares = jnp.concatenate(
+        [
+            jnp.sum(moment_qkv * moment_qkv, axis=(1, 2)),
+            jnp.stack(
+                [
+                    jnp.sum(moment_out * moment_out),
+                    jnp.sum(moment_up * moment_up),
+                    jnp.sum(moment_down * moment_down),
+                ]
+            ),
+        ]
+    )
+    vector_grad, square_total = lax.psum((vector_total, squares), ("dp", "tensor"))
+    factors = lax.rsqrt(square_total + SQUARE_EPSILON)
+    scaled_qkv = (moment_qkv * factors[0:3][:, None, None]).astype(jnp.bfloat16)
+    scaled_out = (moment_out * factors[3]).astype(jnp.bfloat16)
+    scaled_up = (moment_up * factors[4]).astype(jnp.bfloat16)
+    scaled_down = (moment_down * factors[5]).astype(jnp.bfloat16)
+    gathered_qkv, gathered_out, gathered_up, gathered_down = (
+        lax.all_gather(scaled_qkv, "dp", axis=1, tiled=True),
+        lax.all_gather(scaled_out, "dp", axis=1, tiled=True),
+        lax.all_gather(scaled_up, "dp", axis=0, tiled=True),
+        lax.all_gather(scaled_down, "dp", axis=1, tiled=True),
+    )
+    offset = shard_rank * shard_rows
+    narrow_rows = jnp.concatenate([jnp.swapaxes(gathered_qkv, 1, 2), gathered_out[None]], axis=0)
+    wide_rows = jnp.stack([gathered_up.T, gathered_down])
+    for sweep_index in range(NS_ITERS):
+        gram_share = lax.psum_scatter(
+            gram_term(narrow_rows, wide_rows).astype(jnp.bfloat16),
+            "tensor",
+            scatter_dimension=0,
+            tiled=True,
+        )
+        gram_matrix = lax.all_gather(gram_share, "tensor", axis=0, tiled=True)
+        narrow_rows = schulz_step(narrow_rows, gram_matrix[:, 0:4])
+        wide_rows = schulz_step(wide_rows, gram_matrix[:, 4:6])
+    final_narrow = narrow_rows.astype(jnp.float32)
+    final_wide = wide_rows.astype(jnp.float32)
+    update_qkv = lax.dynamic_slice_in_dim(
+        jnp.swapaxes(final_narrow[0:3], 1, 2), offset, shard_rows, 1
+    )
+    update_out = lax.dynamic_slice_in_dim(final_narrow[3], offset, shard_rows, 1)
+    update_up = lax.dynamic_slice_in_dim(final_wide[0].T, offset, shard_rows, 0)
+    update_down = lax.dynamic_slice_in_dim(final_wide[1], offset, shard_rows, 1)
+    wide_factor = math.sqrt(FF / D)
+    new_qkv = w_qkv - MATRIX_RATE * update_qkv
+    new_out = w_out - MATRIX_RATE * update_out
+    new_up = w_up - MATRIX_RATE * wide_factor * update_up
+    new_down = w_down - MATRIX_RATE * wide_factor * update_down
+    moment_vec = MOMENTUM_DECAY * m_vec + vector_grad
+    new_vec = vectors - VECTOR_RATE * moment_vec * lax.rsqrt(
+        jnp.mean(moment_vec * moment_vec, axis=1, keepdims=True) + SQUARE_EPSILON
+    )
+    return (
+        grad_qkv_shard,
+        grad_out_shard,
+        grad_up_shard,
+        grad_down_shard,
+        vector_grad,
+        moment_qkv,
+        moment_out,
+        moment_up,
+        moment_down,
+        moment_vec,
+        new_qkv,
+        new_out,
+        new_up,
+        new_down,
+        new_vec,
+    )
+
+
 def solution(mesh):
     in_specs = (
         P(None, ("dp", "tensor"), None),
@@ -449,6 +790,13 @@
         P("tensor", "dp"),
         P(),
     )
+    groups_fit = mesh.shape["tensor"] == MB
+
+    def pick(*arrays):
+        if groups_fit and arrays[2].shape[1] == 1:
+            return sequence_step(*arrays)
+        return on_device(*arrays)
+
     return jax.shard_map(
-        on_device, mesh=mesh, in_specs=in_specs, out_specs=out_specs, check_vma=False
-    )
+        pick, mesh=mesh, in_specs=in_specs, out_specs=out_specs, check_vma=False
+    )

time: 2870 us -> 2400 us (0.84)
  waiting for transfers between devices: 1910 us -> 1610 us
  matrix products: 600 us -> 423 us
  other arithmetic: 193 us -> 103 us
  Pallas kernels: 0 us -> 81.9 us
    all_gather x19 -> x11, waiting for transfers between devices: 898 us -> 688 us  [the longest x3 369 us: muon_step(): gram_matrix = lax.all_gather(gram_share, 'tensor', axis=0, tiled=True)]
    reduce_scatter x15 -> x4, waiting for transfers between devices: 725 us -> 543 us  [the longest x3 432 us: muon_step(): lax.psum_scatter(gram_term(narrow_rows, wide_rows).astype(jnp.bfloat16),...]
    dot_general x36 -> x24, matrix products: 359 us -> 179 us  [contract(): lax.dot_general(left, right, (((left_dim,), (right_dim,)), ((), ())), pre...]
    ppermute x0 -> x4, waiting for transfers between devices: none -> 98.3 us  [the longest x2 77.1 us: swap_halves(): got = lax.ppermute(sent, 'tensor', SWAP)]
    pallas_call x0 -> x2, Pallas kernels: none -> 81.9 us  [the longest x1 47 us: attention_forward(): pl.pallas_call(attend_fwd_kernel, grid=(H,), in_specs=[SCALARS, SCALARS]...]
    convert_element_type x16 -> x10, other arithmetic: 81.7 us -> 18 us  [the longest x5 11.5 us: narrow(): return rows.astype(jnp.bfloat16)]
    unnamed x40 -> x21, waiting for transfers between devices: 292 us -> 280 us
  transfers between devices with their start and end apart: 37 -> 22, of which waited for: 31 -> 19; matrix products, arithmetic and copies ran while one was open for 17% -> 11% of each run, Pallas kernels for 0% -> 3%
where the time goes in v1:
time: 2400 us; the launch traced here: 2390 us
  waiting for transfers between devices  1610 us (67%)
  matrix products  423 us (18%)
  other arithmetic  103 us (4%)
  local copies, waits for them, and re-layouts  94.2 us (4%)
  Pallas kernels  81.9 us (3%)
  blocking collectives  52.5 us (2%)
    reduce_scatter x3, waiting for transfers between devices, muon_step(): lax.psum_scatter(gram_term(narrow_rows, wide_rows).astype(jnp.bfloat16),...  432 us
    all_gather x3, waiting for transfers between devices, muon_step(): gram_matrix = lax.all_gather(gram_share, 'tensor', axis=0, tiled=True)  369 us
    unnamed x21, waiting for transfers between devices  280 us
    dot_general x24, matrix products, contract(): lax.dot_general(left, right, (((left_dim,), (right_dim,)), ((), ())), pre...  179 us
    all_gather x4, waiting for transfers between devices, spread(): whole = lax.all_gather(rows, BOTH, axis=0, tiled=True)  156 us
    dot_general x6, matrix products, schulz_step(): jnp.einsum('mrc,cmd->mrd', mixed, gram_matrix, preferred_element_type=jnp...  124 us
    reduce_scatter x1, waiting for transfers between devices, collect(): lax.psum_scatter(grads.reshape(parts * D, -1), BOTH, scatter_dimension=0,...  112 us
    ppermute x2, waiting for transfers between devices, swap_halves(): got = lax.ppermute(sent, 'tensor', SWAP)  77.1 us
  transfers between devices with their start and end apart: 22, of which 19 were waited for; matrix products, arithmetic and copies ran while one was open for 11% of the time, Pallas kernels for 3%

profile of v1, /device:TPU:9, one launch (start us, length us, event | category | flops | bytes accessed | tf_op | source)
XLA Modules:
  0.0 2385.8 jit_solution(15037329704174027756)
XLA Ops:
  26.8 21.2 collective-permute-done
  49.5 44.6 %all-gather.12.cloned.1.call-done = bf16[2048,1536]{1,0:T(8,128)(2,1)} async-done(((bf16[64,1536]{1,0:T(8,128)(2,1)}), bf16[2048,1536]{1,0:T(8,128)(2,1)}) %all-gather.12.cloned.1.call-update) | async-done | bytes 6291472 | tf_op jit(solution)/shard_map/all_gather | solution.py:580
  94.2 7.5 fusion.139
  101.6 4.7 copy.187
  106.4 7.5 fusion.138
  118.5 6.1 pad_maximum_fusion.6.q_ref.k_ref.v_ref
  124.6 47.0 %shard_map.260 = (bf16[16,64,1024]{2,1,0:T(8,128)(2,1)}, bf16[16,1024,1024]{2,1,0:T(8,128)(2,1)}, f32[16,1,1024]{2,1,0:T(1,128)}) custom-call(s32[2]{0:T(128)} %fusion.184.starts_ref, f32[16]{0:T(128)} %multiply_exponential_fusion.slopes_ref, bf16[2,3,8,64,1024]{4,3,2,1,0:T(8,128)(2,1)} %pad_maximum_fusion.6.q_ref.k_ref.v_ref, ...), custom_call_target="tpu_custom_call" | custom-call | flops 17179869184 | bytes 46137344 | tf_op jit(solution)/shard_map/pallas_call | solution.py:497
  183.2 50.0 %all-gather.16.cloned.1.call-done = bf16[2048,2048]{1,0:T(8,128)(2,1)} async-done(((bf16[64,2048]{1,0:T(8,128)(2,1)}), bf16[2048,2048]{1,0:T(8,128)(2,1)}) %all-gather.16.cloned.1.call-update) | async-done | bytes 8388624 | tf_op jit(solution)/shard_map/all_gather | solution.py:580
  233.2 10.8 fusion.118
  244.0 7.2 fusion.126
  251.3 61.3 %all-gather.18.cloned.1.call-done = bf16[2048,2048]{1,0:T(8,128)(2,1)} async-done(((bf16[64,2048]{1,0:T(8,128)(2,1)}), bf16[2048,2048]{1,0:T(8,128)(2,1)}) %all-gather.18.cloned.1.call-update) | async-done | bytes 8388624 | tf_op jit(solution)/shard_map/all_gather | solution.py:580
  312.6 15.4 convert_reduce_fusion
  328.0 9.9 fusion.116
  337.9 14.4 convert_reduce_fusion.1
  352.4 10.8 multiply_reduce_fusion
  379.8 35.0 %shard_map.261 = (bf16[16,64,1024]{2,1,0:T(8,128)(2,1)}, bf16[16,64,1024]{2,1,0:T(8,128)(2,1)}, bf16[16,64,1024]{2,1,0:T(8,128)(2,1)}) custom-call(bf16[2,3,8,64,1024]{4,3,2,1,0:T(8,128)(2,1)} %pad_maximum_fusion.6.q_ref.k_ref.v_ref, bf16[2,3,8,64,1024]{4,3,2,1,0:T(8,128)(2,1)} %pad_maximum_fusion.6.q_ref.k_ref.v_ref, ...), custom_call_target="tpu_custom_call" | custom-call | flops 34359738368 | bytes 52428800 | tf_op jit(solution)/shard_map/pallas_call | solution.py:515
  432.1 11.1 convert_bitcast_fusion.6
  443.2 11.1 convert_bitcast_fusion.7
  454.3 7.6 pad_maximum_fusion.4
  462.1 9.6 convert_bitcast_fusion.8
  471.7 6.0 convert_bitcast_fusion.9
  477.7 7.6 pad_maximum_fusion.3
  494.6 6.4 fusion.154
  501.0 5.9 fusion.207
  512.1 111.6 %reduce-scatter.14.cloned.1.call-done = bf16[64,1536]{1,0:T(8,128)(2,1)} async-done(((bf16[2048,1536]{1,0:T(8,128)(2,1)}), bf16[64,1536]{1,0:T(8,128)(2,1)}) %reduce-scatter.14.cloned.1.call-update) | async-done | bytes 196624 | tf_op jit(solution)/shard_map/reduce_scatter | solution.py:584
  625.5 136.1 %reduce-scatter.26.cloned.1.call-done = bf16[64,2048]{1,0:T(8,128)(2,1)} async-done(((bf16[2048,2048]{1,0:T(8,128)(2,1)}), bf16[64,2048]{1,0:T(8,128)(2,1)}) %reduce-scatter.26.cloned.1.call-update) | async-done | bytes 262160
  765.2 143.8 %reduce-scatter.24.cloned.1.call-done = bf16[64,2048]{1,0:T(8,128)(2,1)} async-done(((bf16[2048,2048]{1,0:T(8,128)(2,1)}), bf16[64,2048]{1,0:T(8,128)(2,1)}) %reduce-scatter.24.cloned.1.call-update) | async-done | bytes 262160
  914.5 52.5 %all-reduce = (f32[12,1024]{1,0:T(8,128)}, f32[6]{0:T(128)S(1)}) all-reduce(f32[12,1024]{1,0:T(8,128)S(1)} %concatenate.47, f32[6]{0:T(128)S(1)} %pad_maximum_fusion.19), channel_id=1, replica_groups=mesh['dp'=16,'tensor'=2] {'dp','tensor'}, use_global_device_ids=true, to_apply=%region_22.23 | all-reduce | flops 12294 | bytes 98352 | tf_op jit(solution)/shard_map/psum | solution.py:697
  973.7 33.1 %all-gather.22.cloned.1.call-done = bf16[512,1024]{0,1:T(8,128)(2,1)} async-done(((bf16[512,64]{0,1:T(8,128)(2,1)}), bf16[512,1024]{0,1:T(8,128)(2,1)}) %all-gather.22.cloned.1.call-update) | async-done | bytes 1048592 | tf_op jit(solution)/shard_map/all_gather | solution.py:705
  1009.0 45.9 %all-gather.20.cloned.1.call-done = bf16[3,1024,512]{2,1,0:T(8,128)(2,1)} async-done(((bf16[3,64,512]{2,1,0:T(8,128)(2,1)}), bf16[3,1024,512]{2,1,0:T(8,128)(2,1)}) %all-gather.20.cloned.1.call-update) | async-done | bytes 3145744 | tf_op jit(solution)/shard_map/all_gather | solution.py:704
  1058.1 9.4 convert_bitcast_fusion.2
  1067.5 39.1 %all-gather.26.cloned.1.call-done = bf16[2048,1024]{0,1:T(8,128)(2,1)} async-done(((bf16[2048,64]{0,1:T(8,128)(2,1)}), bf16[2048,1024]{0,1:T(8,128)(2,1)}) %all-gather.26.cloned.1.call-update) | async-done | bytes 4194320 | tf_op jit(solution)/shard_map/all_gather | solution.py:707
  1106.6 6.4 copy.211
  1113.1 45.2 %all-gather.24.cloned.1.call-done = bf16[1024,2048]{1,0:T(8,128)(2,1)} async-done(((bf16[64,2048]{1,0:T(8,128)(2,1)}), bf16[1024,2048]{1,0:T(8,128)(2,1)}) %all-gather.24.cloned.1.call-update) | async-done | bytes 4194320 | tf_op jit(solution)/shard_map/all_gather | solution.py:706
  1158.3 6.4 copy.209
  1164.8 13.7 convert_bitcast_fusion.5
  1178.5 9.3 pad_maximum_fusion
  1187.9 142.6 %reduce-scatter.16.cloned.1.call-done = bf16[512,6,1024]{0,2,1:T(8,128)(2,1)} async-done(((bf16[1024,6,1024]{0,2,1:T(8,128)(2,1)}), bf16[512,6,1024]{0,2,1:T(8,128)(2,1)}) %reduce-scatter.16.cloned.1.call-update) | async-done | bytes 6291472 | tf_op jit(solution)/shard_map/reduce_scatter | solution.py:713
  1331.0 153.5 %all-gather.28.cloned.1.call-done = bf16[1024,6,1024]{0,2,1:T(8,128)(2,1)} async-done(((bf16[512,6,1024]{0,2,1:T(8,128)(2,1)}), bf16[1024,6,1024]{0,2,1:T(8,128)(2,1)}) %all-gather.28.cloned.1.call-update) | async-done | bytes 12582928 | tf_op jit(solution)/shard_map/all_gather | solution.py:719
  1484.5 19.2 fusion.13
  1503.8 11.5 convert_bitcast_fusion.1
  1515.2 15.3 fusion.110
  1530.5 19.3 fusion.1
  1549.8 13.9 convert_bitcast_fusion.4
  1563.7 7.2 pad_maximum_fusion.1
  1571.0 144.6 %reduce-scatter.18.cloned.1.call-done = bf16[512,6,1024]{0,2,1:T(8,128)(2,1)} async-done(((bf16[1024,6,1024]{0,2,1:T(8,128)(2,1)}), bf16[512,6,1024]{0,2,1:T(8,128)(2,1)}) %reduce-scatter.18.cloned.1.call-update) | async-done | bytes 6291472 | tf_op jit(solution)/shard_map/reduce_scatter | solution.py:713
  1715.7 153.9 %all-gather.30.cloned.1.call-done = bf16[1024,6,1024]{0,2,1:T(8,128)(2,1)} async-done(((bf16[512,6,1024]{0,2,1:T(8,128)(2,1)}), bf16[1024,6,1024]{0,2,1:T(8,128)(2,1)}) %all-gather.30.cloned.1.call-update) | async-done | bytes 12582928 | tf_op jit(solution)/shard_map/all_gather | solution.py:719
  1869.6 21.1 fusion.17
  1890.6 11.3 convert_bitcast_fusion
  1902.0 15.8 fusion.107
  1917.8 20.0 fusion.5
  1937.7 13.9 convert_bitcast_fusion.3
  1951.6 7.2 pad_maximum_fusion.2
  1959.1 144.4 %reduce-scatter.20.cloned.1.call-done = bf16[512,6,1024]{0,2,1:T(8,128)(2,1)} async-done(((bf16[1024,6,1024]{0,2,1:T(8,128)(2,1)}), bf16[512,6,1024]{0,2,1:T(8,128)(2,1)}) %reduce-scatter.20.cloned.1.call-update) | async-done | bytes 6291472 | tf_op jit(solution)/shard_map/reduce_scatter | solution.py:713
  2103.6 12.1 fusion.114
  2115.7 13.2 add_convert_fusion.3
  2140.1 36.6 %collective-permute-done.1 = bf16[512,1024]{0,1:T(8,128)(2,1)} collective-permute-done((bf16[512,1024]{0,1:T(8,128)(2,1)S(1)}, bf16[512,1024]{0,1:T(8,128)(2,1)}, u32[]{:S(2)}, u32[]{:S(2)}) %collective-permute-start.1) | collective-permute-done | bytes 1048608 | tf_op jit(solution)/shard_map/ppermute | solution.py:546
  2181.2 40.5 %collective-permute-done.3 = bf16[512,1024]{0,1:T(8,128)(2,1)} collective-permute-done((bf16[512,1024]{0,1:T(8,128)(2,1)}, bf16[512,1024]{0,1:T(8,128)(2,1)}, u32[]{:S(2)}, u32[]{:S(2)}) %collective-permute-start.3) | collective-permute-done | bytes 1048608 | tf_op jit(solution)/shard_map/ppermute | solution.py:546
  2225.9 5.5 copy.234
  2241.0 61.4 %all-gather.32.cloned.1.call-done = bf16[1024,6,1024]{0,2,1:T(8,128)(2,1)} async-done(((bf16[512,6,1024]{0,2,1:T(8,128)(2,1)}), bf16[1024,6,1024]{0,2,1:T(8,128)(2,1)}) %all-gather.32.cloned.1.call-update) | async-done | bytes 12582928 | tf_op jit(solution)/shard_map/all_gather | solution.py:719
  2302.4 21.4 fusion.82
  2329.0 16.0 fusion.104
  2345.0 22.6 fusion.40
  2367.7 6.7 fusion.210
  (344 shorter events, 147.8 us)
Async XLA Ops:
  7.2 19.0 copy-start
  7.2 87.0 %all-gather.12.cloned.1.call-start = ((), (), s32[]{:S(2)}) async-start(), calls=%async_computation.7 | async-start | bytes 6488064 | tf_op jit(solution)/shard_map/all_gather | solution.py:580
  9.0 165.7 %all-gather.14.cloned.1.call-start = ((), (), s32[]{:S(2)}) async-start(), calls=%async_computation.8 | async-start | bytes 2162688 | tf_op jit(solution)/shard_map/all_gather | solution.py:580
  10.6 222.6 %all-gather.16.cloned.1.call-start = ((), (), s32[]{:S(2)}) async-start(), calls=%async_computation.9 | async-start | bytes 8650752 | tf_op jit(solution)/shard_map/all_gather | solution.py:580
  12.5 300.1 %all-gather.18.cloned.1.call-start = ((), (), s32[]{:S(2)}) async-start(), calls=%async_computation.10 | async-start | bytes 8650752 | tf_op jit(solution)/shard_map/all_gather | solution.py:580
  14.3 496.2 %reduce-scatter.22.cloned.1.call-start = ((), (), s32[]{:S(2)}) async-start(), calls=%async_computation.22 | async-start | bytes 2162688
  19.5 28.5 %collective-permute-start = (bf16[512,1024]{0,1:T(8,128)(2,1)}, bf16[512,1024]{0,1:T(8,128)(2,1)S(1)}, u32[]{:S(2)}, u32[]{:S(2)}) collective-permute-start(bf16[512,1024]{0,1:T(8,128)(2,1)} %bitcast.207), channel_id=1, source_target_pairs={{0,1},{1,0},{2,3},{3,2},{4,5},{5,4},{6,7},{7,6},{8,9},{9,8},{10,11... | collective-permute-start | bytes 3145736 | tf_op jit(solution)/shard_map/ppermute | solution.py:553
  22.1 229.2 %collective-permute-start.2 = (bf16[512,1024]{0,1:T(8,128)(2,1)}, bf16[512,1024]{0,1:T(8,128)(2,1)}, u32[]{:S(2)}, u32[]{:S(2)}) collective-permute-start(bf16[512,1024]{0,1:T(8,128)(2,1)} %bitcast.206), channel_id=1, source_target_pairs={{0,1},{1,0},{2,3},{3,2},{4,5},{5,4},{6,7},{7,6},{8,9},{9,8},{10,11... | collective-permute-start | bytes 3145736 | tf_op jit(solution)/shard_map/ppermute | solution.py:553
  22.9 83.4 %copy-start.61 = (f32[1,1024]{1,0:T(1,128)}, f32[1,1024]{1,0:T(1,128)S(1)}, u32[]{:S(2)}) copy-start(f32[1,1024]{1,0:T(1,128)S(1)} %get-tuple-element.146) | copy-start | bytes 12292
  22.9 83.4 %copy-start.81 = (f32[1,1024]{1,0:T(1,128)}, f32[1,1024]{1,0:T(1,128)S(1)}, u32[]{:S(2)}) copy-start(f32[1,1024]{1,0:T(1,128)S(1)} %get-tuple-element.145) | copy-start | bytes 12292
  23.7 419.5 %copy-start.13 = (bf16[1,512,1024]{1,2,0:T(8,128)(2,1)}, bf16[1,512,1024]{1,2,0:T(8,128)(2,1)S(1)}, u32[]{:S(2)}) copy-start(bf16[1,512,1024]{1,2,0:T(8,128)(2,1)S(1)} %copy.190) | copy-start | bytes 3145732
  25.6 481.5 %copy-start.7 = (bf16[1,512,1024]{1,2,0:T(8,128)(2,1)}, bf16[1,512,1024]{1,2,0:T(8,128)(2,1)S(1)}, u32[]{:S(2)}) copy-start(bf16[1,512,1024]{1,2,0:T(8,128)(2,1)S(1)} %copy.183) | copy-start | bytes 3145732
  26.7 405.3 %copy-start.78 = (f32[2048]{0:T(1024)}, f32[2048]{0:T(1024)S(1)}, u32[]{:S(2)}) copy-start(f32[2048]{0:T(1024)S(1)} %get-tuple-element.160) | copy-start | bytes 24580
  26.7 416.4 %copy-start.76 = (f32[2048]{0:T(1024)}, f32[2048]{0:T(1024)S(1)}, u32[]{:S(2)}) copy-start(f32[2048]{0:T(1024)S(1)} %get-tuple-element.161) | copy-start | bytes 24580
  47.9 459.1 %copy-start.9 = (bf16[512,1024]{0,1:T(8,128)(2,1)}, bf16[512,1024]{0,1:T(8,128)(2,1)S(1)}, u32[]{:S(2)}) copy-start(bf16[512,1024]{0,1:T(8,128)(2,1)S(1)} %collective-permute-done) | copy-start | bytes 3145732
  48.6 57.7 %copy-start.56 = (f32[1024]{0:T(1024)}, f32[1024]{0:T(1024)S(1)}, u32[]{:S(2)}) copy-start(f32[1024]{0:T(1024)S(1)} %broadcast_multiply_fusion.1) | copy-start | bytes 12292
  49.5 52.1 %copy-start.71 = (f32[1024]{0:T(1024)}, f32[1024]{0:T(1024)S(1)}, u32[]{:S(2)}) copy-start(f32[1024]{0:T(1024)S(1)} %fusion.78) | copy-start | bytes 12292
  49.5 56.8 %copy-start.66 = (f32[1024]{0:T(1024)}, f32[1024]{0:T(1024)S(1)}, u32[]{:S(2)}) copy-start(f32[1024]{0:T(1024)S(1)} %fusion.182) | copy-start | bytes 12292
  233.2 10.8 copy-start.36
  233.2 10.8 copy-start.86
  328.0 9.9 copy-start.91
  328.0 9.9 copy-start.85
  337.9 14.4 copy-start.5
  352.4 10.8 copy-start.89
  373.5 250.2 %reduce-scatter.14.cloned.1.call-start = ((), (), s32[]{:S(2)}) async-start(), calls=%async_computation.11 | async-start | bytes 6488064 | tf_op jit(solution)/shard_map/reduce_scatter | solution.py:584
  431.6 330.1 %reduce-scatter.26.cloned.1.call-start = ((), (), s32[]{:S(2)}) async-start(), calls=%async_computation.24 | async-start | bytes 8650752
  461.9 447.1 %reduce-scatter.24.cloned.1.call-start = ((), (), s32[]{:S(2)}) async-start(), calls=%async_computation.23 | async-start | bytes 8650752
  485.4 521.4 %all-gather.22.cloned.1.call-start = ((), (), s32[]{:S(2)}) async-start(), calls=%async_computation.13 | async-start | bytes 1114112 | tf_op jit(solution)/shard_map/all_gather | solution.py:705
  507.0 118.0 %copy-start.51 = (f32[3,64,512]{2,1,0:T(8,128)S(1)}, f32[3,64,512]{2,1,0:T(8,128)}, u32[]{:S(2)}) copy-start(f32[3,64,512]{2,1,0:T(8,128)} %param.21) | copy-start | bytes 1179652
  507.1 116.7 %copy-start.64 = (f32[1024]{0:T(1024)}, f32[1024]{0:T(1024)S(1)}, u32[]{:S(2)}) copy-start(f32[1024]{0:T(1024)S(1)} %multiply_multiply_fusion.4) | copy-start | bytes 12292
  512.1 455.5 %copy-start.34 = (f32[512,64]{1,0:T(8,128)}, f32[512,64]{1,0:T(8,128)S(1)}, u32[]{:S(2)}) copy-start(f32[512,64]{1,0:T(8,128)S(1)} %get-tuple-element.115) | copy-start | bytes 393220
  625.0 136.6 %copy-start.21 = (f32[64,3,512]{2,1,0:T(4,128)}, f32[64,3,512]{2,1,0:T(4,128)S(1)}, u32[]{:S(2)}) copy-start(f32[64,3,512]{2,1,0:T(4,128)S(1)} %reshape.208) | copy-start | bytes 1179652
  625.5 344.5 %copy-start.23 = (f32[3,64,512]{2,0,1:T(4,128)}, f32[3,64,512]{2,0,1:T(4,128)S(1)}, u32[]{:S(2)}) copy-start(f32[3,64,512]{2,0,1:T(4,128)S(1)} %get-tuple-element.113) | copy-start | bytes 1179652
  762.9 146.1 %copy-start.25 = (bf16[64,2048]{0,1:T(8,128)(2,1)}, bf16[64,2048]{0,1:T(8,128)(2,1)S(1)}, u32[]{:S(2)}) copy-start(bf16[64,2048]{0,1:T(8,128)(2,1)S(1)} %copy.274) | copy-start | bytes 786436
  765.2 207.3 %copy-start.15 = (f32[2048,64]{1,0:T(8,128)}, f32[2048,64]{1,0:T(8,128)S(1)}, u32[]{:S(2)}) copy-start(f32[2048,64]{1,0:T(8,128)S(1)} %get-tuple-element.119) | copy-start | bytes 1572868
  910.2 62.3 %copy-start.27 = (bf16[64,2048]{0,1:T(8,128)(2,1)}, bf16[64,2048]{0,1:T(8,128)(2,1)S(1)}, u32[]{:S(2)}) copy-start(bf16[64,2048]{0,1:T(8,128)(2,1)S(1)} %copy.272) | copy-start | bytes 786436
  912.5 96.5 %copy-start.17 = (f32[64,2048]{0,1:T(8,128)}, f32[64,2048]{0,1:T(8,128)S(1)}, u32[]{:S(2)}) copy-start(f32[64,2048]{0,1:T(8,128)S(1)} %get-tuple-element.117) | copy-start | bytes 1572868
  969.0 85.9 %all-gather.20.cloned.1.call-start = ((), (), s32[]{:S(2)}) async-start(), calls=%async_computation.12 | async-start | bytes 3342336 | tf_op jit(solution)/shard_map/all_gather | solution.py:704
  970.0 136.7 %all-gather.26.cloned.1.call-start = ((), (), s32[]{:S(2)}) async-start(), calls=%async_computation.15 | async-start | bytes 4456448 | tf_op jit(solution)/shard_map/all_gather | solution.py:707
  971.7 186.6 %all-gather.24.cloned.1.call-start = ((), (), s32[]{:S(2)}) async-start(), calls=%async_computation.14 | async-start | bytes 4456448 | tf_op jit(solution)/shard_map/all_gather | solution.py:706
  973.4 357.2 %reduce-scatter.16.cloned.1.call-start = ((), (), s32[]{:S(2)}) async-start(), calls=%async_computation.16 | async-start | bytes 18874368 | tf_op jit(solution)/shard_map/reduce_scatter | solution.py:713
  1187.9 296.7 %all-gather.28.cloned.1.call-start = ((), (), s32[]{:S(2)}) async-start(), calls=%async_computation.17 | async-start | bytes 18874368 | tf_op jit(solution)/shard_map/all_gather | solution.py:719
  1330.6 385.0 %reduce-scatter.18.cloned.1.call-start = ((), (), s32[]{:S(2)}) async-start(), calls=%async_computation.18 | async-start | bytes 18874368 | tf_op jit(solution)/shard_map/reduce_scatter | solution.py:713
  1503.7 11.5 copy-start.29
  1549.8 13.9 copy-start.19
  1571.0 298.6 %all-gather.30.cloned.1.call-start = ((), (), s32[]{:S(2)}) async-start(), calls=%async_computation.19 | async-start | bytes 18874368 | tf_op jit(solution)/shard_map/all_gather | solution.py:719
  1715.7 387.9 %reduce-scatter.20.cloned.1.call-start = ((), (), s32[]{:S(2)}) async-start(), calls=%async_computation.20 | async-start | bytes 18874368 | tf_op jit(solution)/shard_map/reduce_scatter | solution.py:713
  1937.7 13.9 copy-start.20
  1958.9 144.6 %copy-start.79 = (f32[2048]{0:T(1024)S(1)}, f32[2048]{0:T(1024)}, u32[]{:S(2)}) copy-start(f32[2048]{0:T(1024)} %copy-done.78) | copy-start | bytes 24580
  1958.9 343.5 %all-gather.32.cloned.1.call-start = ((), (), s32[]{:S(2)}) async-start(), calls=%async_computation.21 | async-start | bytes 18874368 | tf_op jit(solution)/shard_map/all_gather | solution.py:719
  2103.6 12.1 copy-start.6
  2103.6 12.1 copy-start.77
  2103.6 12.1 copy-start.80
  2115.7 14.1 copy-start.75
  2115.7 14.1 copy-start.8
  2115.7 14.1 copy-start.10
  2115.7 14.1 copy-start.12
  2115.7 14.1 copy-start.14
  2115.7 14.1 copy-start.68
  2115.7 14.1 copy-start.70
  2129.3 47.4 %collective-permute-start.1 = (bf16[512,1024]{0,1:T(8,128)(2,1)S(1)}, bf16[512,1024]{0,1:T(8,128)(2,1)}, u32[]{:S(2)}, u32[]{:S(2)}) collective-permute-start(bf16[512,1024]{0,1:T(8,128)(2,1)S(1)} %get-tuple-element.132), channel_id=1, source_target_pairs={{0,1},{1,0},{2,3},{3,2},{4,5},{5,4},{6,7},{7,6},{8,9},{9,8},{10,11... | collective-permute-start | bytes 3145736 | tf_op jit(solution)/shard_map/ppermute | solution.py:546
  2137.4 84.2 %collective-permute-start.3 = (bf16[512,1024]{0,1:T(8,128)(2,1)}, bf16[512,1024]{0,1:T(8,128)(2,1)}, u32[]{:S(2)}, u32[]{:S(2)}) collective-permute-start(bf16[512,1024]{0,1:T(8,128)(2,1)} %get-tuple-element.128), channel_id=1, source_target_pairs={{0,1},{1,0},{2,3},{3,2},{4,5},{5,4},{6,7},{7,6},{8,9},{9,8},{10,11... | collective-permute-start | bytes 3145736 | tf_op jit(solution)/shard_map/ppermute | solution.py:546
  2178.8 42.9 %copy-start.28 = (bf16[1,512,1024]{1,2,0:T(8,128)(2,1)S(1)}, bf16[1,512,1024]{1,2,0:T(8,128)(2,1)}, u32[]{:S(2)}) copy-start(bf16[1,512,1024]{1,2,0:T(8,128)(2,1)} %get-tuple-element.127) | copy-start | bytes 3145732
  2240.3 83.6 %copy-start.52 = (f32[12,1024]{1,0:T(8,128)}, f32[12,1024]{1,0:T(8,128)S(1)}, u32[]{:S(2)}) copy-start(f32[12,1024]{1,0:T(8,128)S(1)} %get-tuple-element.111) | copy-start | bytes 147460
  (52 other events, 203.8 us)
Sparse Core Ops, SparseCore 0:
  11.5 82.6 all-gather.11
  97.6 55.0 all-gather.13
  156.1 77.1 all-gather.15
  236.5 76.0 all-gather.17
  373.7 119.5 reduce-scatter.21
  499.6 124.0 reduce-scatter.13
  626.0 135.5 reduce-scatter.25
  763.9 144.9 reduce-scatter.23
  969.1 37.5 all-gather.21
  1009.4 45.4 all-gather.19
  1057.6 48.9 all-gather.25
  1109.2 49.0 all-gather.23
  1188.0 142.5 reduce-scatter.15
  1332.0 152.5 all-gather.27
  1571.1 144.4 reduce-scatter.17
  1717.0 152.5 all-gather.29
  1959.0 144.4 reduce-scatter.19
  2104.9 197.4 all-gather.31

commit v2 on v1

--- a/solution.py
+++ b/solution.py
@@ -525,6 +525,364 @@
     )(packed, packed, packed, context, grad_context, exps, stats)
 
 
+SLOTS = 12
+SLOT = 512
+TILE = 256
+MESH_IDS = pl.DeviceIdType.MESH
+
+
+def handler_of(slot):
+    wide = slot - 4
+    square = slot < 4
+    dp_index = jnp.where(square, jnp.where(slot < 2, 2, 12), 4 + 6 * (wide // 4) + wide % 2)
+    tensor_index = jnp.where(square, slot % 2, (wide // 2) % 2)
+    return dp_index, tensor_index
+
+
+def muon_kernel(
+    moments_ref,
+    vec_ref,
+    updates_ref,
+    vec_out_ref,
+    pieces,
+    turned,
+    vec_pieces,
+    vec_sum,
+    gram,
+    gram_low,
+    poly_low,
+    half_low,
+    chain_low,
+    chain_next,
+    out_half,
+    in_half,
+    local_sem,
+    send_sem,
+    recv_sem,
+    half_send,
+    half_recv,
+):
+    groups = lax.axis_size("dp")
+    parts = lax.axis_size("tensor")
+    count = groups * parts
+    dp_me = lax.axis_index("dp")
+    t_me = lax.axis_index("tensor")
+    me = t_me * groups + dp_me
+    is_square = (dp_me == 2) | (dp_me == 12)
+    is_up = (dp_me == 4) | (dp_me == 5)
+    is_down = (dp_me == 10) | (dp_me == 11)
+    is_wide = is_up | is_down
+    is_handler = is_square | is_wide
+    wide_slot = jnp.where(is_up, 4 + (dp_me - 4), 8 + (dp_me - 10)) + 2 * t_me
+    slot_me = jnp.where(is_square, t_me + jnp.where(dp_me == 12, 2, 0), wide_slot)
+    slot_me = jnp.where(is_handler, slot_me, 0)
+
+    barrier = pltpu.get_barrier_semaphore()
+
+    def greet(step, carry):
+        other = lax.rem(me + step, count)
+        pl.semaphore_signal(
+            barrier, inc=1, device_id=(lax.rem(other, groups), other // groups), device_id_type=MESH_IDS
+        )
+        return carry
+
+    lax.fori_loop(1, count, greet, 0)
+    pl.semaphore_wait(barrier, count - 1)
+
+    def give(step, carry):
+        slot = lax.rem(me + step, SLOTS)
+        dp_to, t_to = handler_of(slot)
+        away = (dp_to != dp_me) | (t_to != t_me)
+
+        @pl.when(away)
+        def _():
+            pltpu.make_async_remote_copy(
+                src_ref=vec_ref.at[slot],
+                dst_ref=vec_pieces.at[me],
+                send_sem=send_sem.at[1],
+                recv_sem=recv_sem.at[1],
+                device_id=(dp_to, t_to),
+                device_id_type=MESH_IDS,
+            ).start()
+            pltpu.make_async_remote_copy(
+                src_ref=moments_ref.at[slot],
+                dst_ref=pieces.at[me],
+                send_sem=send_sem.at[0],
+                recv_sem=recv_sem.at[0],
+                device_id=(dp_to, t_to),
+                device_id_type=MESH_IDS,
+            ).start()
+
+        return carry
+
+    lax.fori_loop(0, SLOTS, give, 0)
+
+    def give_back(source, sem, target):
+        def one(step, carry):
+            other = lax.rem(me + step, count)
+            pltpu.make_async_remote_copy(
+                src_ref=source.at[other] if source is turned else source,
+                dst_ref=target.at[slot_me],
+                send_sem=send_sem.at[sem],
+                recv_sem=recv_sem.at[sem],
+                device_id=(lax.rem(other, groups), other // groups),
+                device_id_type=MESH_IDS,
+            ).start()
+            return carry
+
+        lax.fori_loop(1, count, one, 0)
+
+    @pl.when(is_handler)
+    def _():
+        own = [
+            pltpu.make_async_copy(vec_ref.at[slot_me], vec_pieces.at[me], local_sem.at[0]),
+            pltpu.make_async_copy(moments_ref.at[slot_me], pieces.at[me], local_sem.at[1]),
+        ]
+        for copy in own:
+            copy.start()
+        for copy in own:
+            copy.wait()
+        rest = pl.ds(0, count - 1)
+        pltpu.make_async_copy(vec_pieces.at[rest], vec_pieces.at[rest], recv_sem.at[1]).wait()
+        vec_sum[...] = jnp.sum(vec_pieces[...], axis=0)
+        give_back(vec_sum, 2, vec_out_ref)
+        own_vec = pltpu.make_async_copy(vec_sum, vec_out_ref.at[slot_me], local_sem.at[0])
+        own_vec.start()
+        own_vec.wait()
+        pltpu.make_async_copy(pieces.at[rest], pieces.at[rest], recv_sem.at[0]).wait()
+
+        rows_of = TILE // 64
+
+        def gram_tile(tile, carry):
+            rows = pl.ds(pl.multiple_of(tile * TILE, TILE), TILE)
+            total = jnp.zeros((TILE, D), jnp.float32)
+            for part in range(parts):
+                left = pieces[pl.ds(part * groups + tile * rows_of, rows_of)].reshape(TILE, SLOT)
+                right = pieces[part * groups : (part + 1) * groups].reshape(D, SLOT)
+                total += lax.dot_general(
+                    left, right, (((1,), (1,)), ((), ())), preferred_element_type=jnp.float32
+                )
+            gram[rows, :] = total
+            return carry
+
+        lax.fori_loop(0, D // TILE, gram_tile, 0)
+
+        @pl.when(is_wide)
+        def _():
+            core = lax.rem(dp_me, 2)
+            half = D // 2
+            mine = pl.ds(pl.multiple_of(core * half, half), half)
+            theirs = pl.ds(pl.multiple_of((1 - core) * half, half), half)
+            sibling = (dp_me + 1 - 2 * core, t_me)
+            across = (dp_me, 1 - t_me)
+
+            def exchange(stage, place):
+                copy = pltpu.make_async_remote_copy(
+                    src_ref=out_half.at[stage],
+                    dst_ref=in_half.at[stage],
+                    send_sem=half_send.at[stage],
+                    recv_sem=half_recv.at[stage],
+                    device_id=place,
+                    device_id_type=MESH_IDS,
+                )
+                copy.start()
+                copy.wait()
+
+            out_half[0] = gram[theirs, :].astype(jnp.bfloat16)
+            exchange(0, sibling)
+            out_half[1] = (gram[mine, :] + in_half[0].astype(jnp.float32)).astype(jnp.bfloat16)
+            exchange(1, across)
+            total = out_half[1].astype(jnp.float32) + in_half[1].astype(jnp.float32)
+            out_half[2] = total.astype(jnp.bfloat16)
+            exchange(2, sibling)
+            gram[mine, :] = out_half[2].astype(jnp.float32)
+            gram[theirs, :] = in_half[2].astype(jnp.float32)
+
+        def trace_tile(tile, total):
+            rows = pl.ds(pl.multiple_of(tile * TILE, TILE), TILE)
+            row_ids = lax.broadcasted_iota(jnp.int32, (TILE, D), 0) + tile * TILE
+            col_ids = lax.broadcasted_iota(jnp.int32, (TILE, D), 1)
+            diagonal = jnp.where(row_ids == col_ids, gram[rows, :], 0.0)
+            return total + jnp.sum(jnp.sum(diagonal, axis=0, keepdims=True), axis=1, keepdims=True)
+
+        square_total = lax.fori_loop(0, D // TILE, trace_tile, jnp.zeros((1, 1), jnp.float32))
+        factor = lax.rsqrt(square_total + SQUARE_EPSILON)
+        gram_low[...] = (gram[...] * (factor * factor)).astype(jnp.bfloat16)
+
+        first, second, third = SCHULZ_FIRST, SCHULZ_SECOND, SCHULZ_THIRD
+
+        def tiles(body):
+            def one(tile, carry):
+                body(pl.ds(pl.multiple_of(tile * TILE, TILE), TILE))
+                return carry
+
+            lax.fori_loop(0, D // TILE, one, 0)
+
+        def mul(left, right):
+            return jnp.dot(left, right, preferred_element_type=jnp.float32)
+
+        chain = chain_low
+        other = chain_next
+        for sweep in range(NS_ITERS):
+            target = chain if sweep == 0 else poly_low
+
+            def poly(rows):
+                square = mul(gram_low[rows, :], gram_low[...])
+                grown = (second / first) * gram_low[rows, :].astype(jnp.float32) + (third / first) * square
+                target[rows, :] = grown.astype(jnp.bfloat16)
+
+            tiles(poly)
+            if sweep > 0:
+
+                def join(rows, chain=chain, other=other):
+                    total = chain[rows, :].astype(jnp.float32) + poly_low[rows, :].astype(jnp.float32)
+                    other[rows, :] = (total + mul(chain[rows, :], poly_low[...])).astype(jnp.bfloat16)
+
+                tiles(join)
+                chain, other = other, chain
+            if sweep < NS_ITERS - 1:
+
+                def half(rows):
+                    grown = gram_low[rows, :].astype(jnp.float32) + mul(gram_low[rows, :], target[...])
+                    half_low[rows, :] = grown.astype(jnp.bfloat16)
+
+                def full(rows):
+                    grown = half_low[rows, :].astype(jnp.float32) + mul(half_low[rows, :], target[...])
+                    gram_low[rows, :] = (grown * (first * first)).astype(jnp.bfloat16)
+
+                tiles(half)
+                tiles(full)
+
+        scale = factor * (first**NS_ITERS)
+
+        def turn_tile(tile, carry):
+            rows = pl.ds(pl.multiple_of(tile * TILE, TILE), TILE)
+            for part in range(parts):
+                at = pl.ds(part * groups + tile * rows_of, rows_of)
+                whole = pieces[part * groups : (part + 1) * groups].reshape(D, SLOT)
+                kept = pieces[at].reshape(TILE, SLOT).astype(jnp.float32)
+                fresh = (kept + mul(chain[rows, :], whole)) * scale
+                turned[at] = fresh.astype(jnp.bfloat16).reshape(rows_of, 64, SLOT)
+            return carry
+
+        lax.fori_loop(0, D // TILE, turn_tile, 0)
+        give_back(turned, 3, updates_ref)
+        own_turned = pltpu.make_async_copy(turned.at[me], updates_ref.at[slot_me], local_sem.at[1])
+        own_turned.start()
+        own_turned.wait()
+
+    def finish(length):
+        here = pl.ds(0, length)
+        pltpu.make_async_copy(vec_ref.at[here], vec_ref.at[here], send_sem.at[1]).wait()
+        pltpu.make_async_copy(moments_ref.at[here], moments_ref.at[here], send_sem.at[0]).wait()
+        pltpu.make_async_copy(vec_out_ref.at[here], vec_out_ref.at[here], recv_sem.at[2]).wait()
+        pltpu.make_async_copy(updates_ref.at[here], updates_ref.at[here], recv_sem.at[3]).wait()
+
+    @pl.when(is_handler)
+    def _():
+        finish(SLOTS - 1)
+        rest = pl.ds(0, count - 1)
+        pltpu.make_async_copy(vec_pieces.at[rest], vec_pieces.at[rest], send_sem.at[2]).wait()
+        pltpu.make_async_copy(turned.at[rest], turned.at[rest], send_sem.at[3]).wait()
+
+    @pl.when(jnp.logical_not(is_handler))
+    def _():
+        finish(SLOTS)
+
+
+def muon_call(moments, vec_parts):
+    count = lax.axis_size("dp") * lax.axis_size("tensor")
+    rows = moments.shape[1]
+    vmem = pl.BlockSpec(memory_space=pltpu.VMEM)
+    low = pltpu.VMEM((D, D), jnp.bfloat16)
+    return pl.pallas_call(
+        muon_kernel,
+        in_specs=[vmem, vmem],
+        out_specs=[vmem, vmem],
+        out_shape=[
+            jax.ShapeDtypeStruct(moments.shape, jnp.bfloat16),
+            jax.ShapeDtypeStruct(vec_parts.shape, jnp.float32),
+        ],
+        scratch_shapes=[
+            pltpu.VMEM((count, rows, SLOT), jnp.bfloat16),
+            pltpu.VMEM((count, rows, SLOT), jnp.bfloat16),
+            pltpu.VMEM((count,) + vec_parts.shape[1:], jnp.float32),
+            pltpu.VMEM(vec_parts.shape[1:], jnp.float32),
+            pltpu.VMEM((D, D), jnp.float32),
+            low,
+            low,
+            low,
+            low,
+            low,
+            pltpu.VMEM((3, D // 2, D), jnp.bfloat16),
+            pltpu.VMEM((3, D // 2, D), jnp.bfloat16),
+            pltpu.SemaphoreType.DMA((2,)),
+            pltpu.SemaphoreType.DMA((4,)),
+            pltpu.SemaphoreType.DMA((4,)),
+            pltpu.SemaphoreType.DMA((3,)),
+            pltpu.SemaphoreType.DMA((3,)),
+        ],
+        compiler_params=pltpu.CompilerParams(
+            collective_id=1, has_side_effects=True, vmem_limit_bytes=VMEM_LIMIT
+        ),
+        cost_estimate=pl.CostEstimate(flops=12 * 2 * D**3, bytes_accessed=4 * 1024 * 1024, transcendentals=0),
+    )(moments, vec_parts)
+
+
+def by_slots(rows):
+    return jnp.swapaxes(rows.reshape(rows.shape[0], -1, SLOT), 0, 1)
+
+
+def from_slots(rows):
+    return jnp.swapaxes(rows, 0, 1).reshape(rows.shape[1], -1)
+
+
+def muon_step(
+    shards, vector_total, w_qkv, w_out, w_up, w_down, vectors, m_qkv, m_out, m_up, m_down, m_vec
+):
+    grad_qkv_shard, grad_out_shard, grad_up_shard, grad_down_shard = shards
+    moment_qkv = MOMENTUM_DECAY * m_qkv + grad_qkv_shard
+    moment_out = MOMENTUM_DECAY * m_out + grad_out_shard
+    moment_up = MOMENTUM_DECAY * m_up + grad_up_shard
+    moment_down = MOMENTUM_DECAY * m_down + grad_down_shard
+    slots = jnp.concatenate(
+        [
+            narrow(moment_qkv),
+            narrow(moment_out).T[None],
+            by_slots(narrow(moment_up)),
+            by_slots(narrow(moment_down).T),
+        ]
+    )
+    updates, vector_rows = muon_call(slots, vector_total.reshape(SLOTS, 8, 128))
+    vector_grad = vector_rows.reshape(12, D)
+    wide_factor = math.sqrt(FF / D)
+    new_qkv = w_qkv - MATRIX_RATE * updates[0:3].astype(jnp.float32)
+    new_out = w_out - MATRIX_RATE * updates[3].T.astype(jnp.float32)
+    new_up = w_up - MATRIX_RATE * wide_factor * from_slots(updates[4:8]).astype(jnp.float32)
+    new_down = w_down - MATRIX_RATE * wide_factor * from_slots(updates[8:12]).T.astype(jnp.float32)
+    moment_vec = MOMENTUM_DECAY * m_vec + vector_grad
+    new_vec = vectors - VECTOR_RATE * moment_vec * lax.rsqrt(
+        jnp.mean(moment_vec * moment_vec, axis=1, keepdims=True) + SQUARE_EPSILON
+    )
+    return (
+        grad_qkv_shard,
+        grad_out_shard,
+        grad_up_shard,
+        grad_down_shard,
+        vector_grad,
+        moment_qkv,
+        moment_out,
+        moment_up,
+        moment_down,
+        moment_vec,
+        new_qkv,
+        new_out,
+        new_up,
+        new_down,
+        new_vec,
+    )
+
+
 BOTH = ("tensor", "dp")
 SWAP = [(0, 1), (1, 0)]
 
@@ -672,89 +1030,6 @@
     return (output_pair, token_pair) + outputs
 
 
-def muon_step(
-    shards, vector_total, w_qkv, w_out, w_up, w_down, vectors, m_qkv, m_out, m_up, m_down, m_vec
-):
-    shard_rank = lax.axis_index("dp")
-    shard_rows = w_qkv.shape[1]
-    grad_qkv_shard, grad_out_shard, grad_up_shard, grad_down_shard = shards
-    moment_qkv = MOMENTUM_DECAY * m_qkv + grad_qkv_shard
-    moment_out = MOMENTUM_DECAY * m_out + grad_out_shard
-    moment_up = MOMENTUM_DECAY * m_up + grad_up_shard
-    moment_down = MOMENTUM_DECAY * m_down + grad_down_shard
-    squares = jnp.concatenate(
-        [
-            jnp.sum(moment_qkv * moment_qkv, axis=(1, 2)),
-            jnp.stack(
-                [
-                    jnp.sum(moment_out * moment_out),
-                    jnp.sum(moment_up * moment_up),
-                    jnp.sum(moment_down * moment_down),
-                ]
-            ),
-        ]
-    )
-    vector_grad, square_total = lax.psum((vector_total, squares), ("dp", "tensor"))
-    factors = lax.rsqrt(square_total + SQUARE_EPSILON)
-    scaled_qkv = (moment_qkv * factors[0:3][:, None, None]).astype(jnp.bfloat16)
-    scaled_out = (moment_out * factors[3]).astype(jnp.bfloat16)
-    scaled_up = (moment_up * factors[4]).astype(jnp.bfloat16)
-    scaled_down = (moment_down * factors[5]).astype(jnp.bfloat16)
-    gathered_qkv, gathered_out, gathered_up, gathered_down = (
-        lax.all_gather(scaled_qkv, "dp", axis=1, tiled=True),
-        lax.all_gather(scaled_out, "dp", axis=1, tiled=True),
-        lax.all_gather(scaled_up, "dp", axis=0, tiled=True),
-        lax.all_gather(scaled_down, "dp", axis=1, tiled=True),
-    )
-    offset = shard_rank * shard_rows
-    narrow_rows = jnp.concatenate([jnp.swapaxes(gathered_qkv, 1, 2), gathered_out[None]], axis=0)
-    wide_rows = jnp.stack([gathered_up.T, gathered_down])
-    for sweep_index in range(NS_ITERS):
-        gram_share = lax.psum_scatter(
-            gram_term(narrow_rows, wide_rows).astype(jnp.bfloat16),
-            "tensor",
-            scatter_dimension=0,
-            tiled=True,
-        )
-        gram_matrix = lax.all_gather(gram_share, "tensor", axis=0, tiled=True)
-        narrow_rows = schulz_step(narrow_rows, gram_matrix[:, 0:4])
-        wide_rows = schulz_step(wide_rows, gram_matrix[:, 4:6])
-    final_narrow = narrow_rows.astype(jnp.float32)
-    final_wide = wide_rows.astype(jnp.float32)
-    update_qkv = lax.dynamic_slice_in_dim(
-        jnp.swapaxes(final_narrow[0:3], 1, 2), offset, shard_rows, 1
-    )
-    update_out = lax.dynamic_slice_in_dim(final_narrow[3], offset, shard_rows, 1)
-    update_up = lax.dynamic_slice_in_dim(final_wide[0].T, offset, shard_rows, 0)
-    update_down = lax.dynamic_slice_in_dim(final_wide[1], offset, shard_rows, 1)
-    wide_factor = math.sqrt(FF / D)
-    new_qkv = w_qkv - MATRIX_RATE * update_qkv
-    new_out = w_out - MATRIX_RATE * update_out
-    new_up = w_up - MATRIX_RATE * wide_factor * update_up
-    new_down = w_down - MATRIX_RATE * wide_factor * update_down
-    moment_vec = MOMENTUM_DECAY * m_vec + vector_grad
-    new_vec = vectors - VECTOR_RATE * moment_vec * lax.rsqrt(
-        jnp.mean(moment_vec * moment_vec, axis=1, keepdims=True) + SQUARE_EPSILON
-    )
-    return (
-        grad_qkv_shard,
-        grad_out_shard,
-        grad_up_shard,
-        grad_down_shard,
-        vector_grad,
-        moment_qkv,
-        moment_out,
-        moment_up,
-        moment_down,
-        moment_vec,
-        new_qkv,
-        new_out,
-        new_up,
-        new_down,
-        new_vec,
-    )
-
-
 def solution(mesh):
     in_specs = (
         P(None, ("dp", "tensor"), None),
@@ -790,7 +1065,7 @@
         P("tensor", "dp"),
         P(),
     )
-    groups_fit = mesh.shape["tensor"] == MB
+    groups_fit = mesh.shape["tensor"] == MB and mesh.shape["dp"] == 16
 
     def pick(*arrays):
         if groups_fit and arrays[2].shape[1] == 1:

time: 2400 us -> 1070 us (0.45)
  waiting for transfers between devices: 1610 us -> 537 us
  matrix products: 423 us -> 172 us
  Pallas kernels: 81.9 us -> 216 us
  local copies, waits for them, and re-layouts: 94.2 us -> 38.3 us
  blocking collectives: 52.5 us -> 0 us
  other arithmetic: 103 us -> 78.8 us
    all_gather x7 -> x0, waiting for transfers between devices: 532 us -> none  [the longest x3 369 us: muon_step(): gram_matrix = lax.all_gather(gram_share, 'tensor', axis=0, tiled=True)]
    reduce_scatter x3 -> x0, waiting for transfers between devices: 432 us -> none  [muon_step(): lax.psum_scatter(gram_term(narrow_rows, wide_rows).astype(jnp.bfloat16),...]
    unnamed x21 -> x8, waiting for transfers between devices: 280 us -> 0.13 us
    dot_general x15 -> x0, matrix products: 244 us -> none  [the longest x6 124 us: schulz_step(): jnp.einsum('mrc,cmd->mrd', mixed, gram_matrix, preferred_element_type=jnp...]
    reduce_scatter x1 -> x4, waiting for transfers between devices: 112 us -> 340 us  [collect(): lax.psum_scatter(grads.reshape(parts * D, -1), BOTH, scatter_dimension=0,...]
    pallas_call x0 -> x1, Pallas kernels: none -> 134 us  [muon_call(): pl.pallas_call(muon_kernel, in_specs=[vmem, vmem], out_specs=[vmem, vmem]...]
    ppermute x2, waiting for transfers between devices: 77.1 us -> 19.1 us  [swap_halves(): got = lax.ppermute(sent, 'tensor', SWAP)]
    psum x1 -> x0, blocking collectives: 52.5 us -> none  [muon_step(): lax.psum((vector_total, squares), ('dp', 'tensor'))]
  transfers between devices with their start and end apart: 22 -> 12, of which waited for: 19 -> 8; matrix products, arithmetic and copies ran while one was open for 11% -> 20% of each run, Pallas kernels for 3% -> 8%
where the time goes in v2:
time: 1070 us; the launch traced here: 1060 us
  waiting for transfers between devices  537 us (50%)
  Pallas kernels  216 us (20%)
  matrix products  172 us (16%)
  other arithmetic  78.8 us (7%)
  local copies, waits for them, and re-layouts  38.3 us (4%)
  between operations  15.5 us (1%)
    reduce_scatter x4, waiting for transfers between devices, collect(): lax.psum_scatter(grads.reshape(parts * D, -1), BOTH, scatter_dimension=0,...  340 us
    dot_general x24, matrix products, contract(): lax.dot_general(left, right, (((left_dim,), (right_dim,)), ((), ())), pre...  172 us
    all_gather x4, waiting for transfers between devices, spread(): whole = lax.all_gather(rows, BOTH, axis=0, tiled=True)  156 us
    pallas_call x1, Pallas kernels, muon_call(): pl.pallas_call(muon_kernel, in_specs=[vmem, vmem], out_specs=[vmem, vmem]...  134 us
    pallas_call x1, Pallas kernels, attention_forward(): pl.pallas_call(attend_fwd_kernel, grid=(H,), in_specs=[SCALARS, SCALARS]...  46.9 us
    pallas_call x1, Pallas kernels, attention_backward(): pl.pallas_call(attend_bwd_kernel, grid=(H,), in_specs=[part_spec(part, he...  35 us
    ppermute x2, waiting for transfers between devices, join_halves(): got = lax.ppermute(sent, 'tensor', SWAP)  21.8 us
  transfers between devices with their start and end apart: 12, of which 8 were waited for; matrix products, arithmetic and copies ran while one was open for 20% of the time, Pallas kernels for 8%

profile of v2, /device:TPU:9, one launch (start us, length us, event | category | flops | bytes accessed | tf_op | source)
XLA Modules:
  0.0 1061.7 jit_solution(17483573074848797826)
XLA Ops:
  9.0 1.5 convert_bitcast_fusion.11
  10.7 1.8 convert_element_type.175
  12.5 1.8 convert_bitcast_fusion.7
  14.4 3.6 constant_dynamic-slice_fusion.2
  23.5 1.5 copy.44
  26.0 21.8 %collective-permute-done = bf16[512,1024]{0,1:T(8,128)(2,1)S(1)} collective-permute-done((bf16[512,1024]{0,1:T(8,128)(2,1)}, bf16[512,1024]{0,1:T(8,128)(2,1)S(1)}, u32[]{:S(2)}, u32[]{:S(2)}) %collective-permute-start) | collective-permute-done | bytes 1048608 | tf_op jit(solution)/shard_map/ppermute | solution.py:911
  49.4 44.5 %all-gather.5.cloned.1.call-done = bf16[2048,1536]{1,0:T(8,128)(2,1)} async-done(((bf16[64,1536]{1,0:T(8,128)(2,1)}), bf16[2048,1536]{1,0:T(8,128)(2,1)}) %all-gather.5.cloned.1.call-update) | async-done | bytes 6291472 | tf_op jit(solution)/shard_map/all_gather | solution.py:938
  94.0 7.5 fusion.47
  101.4 4.7 copy.48
  106.1 7.5 fusion.46
  113.6 4.7 copy.47
  118.2 6.1 pad_maximum_fusion.2.q_ref.k_ref.v_ref
  124.3 46.9 %shard_map.260 = (bf16[16,64,1024]{2,1,0:T(8,128)(2,1)}, bf16[16,1024,1024]{2,1,0:T(8,128)(2,1)}, f32[16,1,1024]{2,1,0:T(1,128)}) custom-call(s32[2]{0:T(128)} %fusion.79.starts_ref, f32[16]{0:T(128)} %multiply_exponential_fusion.slopes_ref, bf16[2,3,8,64,1024]{4,3,2,1,0:T(8,128)(2,1)} %pad_maximum_fusion.2.q_ref.k_ref.v_ref, ...), custom_call_target="tpu_custom_call" | custom-call | flops 17179869184 | bytes 46137344 | tf_op jit(solution)/shard_map/pallas_call | solution.py:497
  171.3 3.2 fusion.90
  174.4 2.9 fusion.74
  177.4 1.6 fusion.92
  179.5 1.5 copy-done.4
  181.0 2.0 add_convert_fusion.4
  183.0 50.1 %all-gather.9.cloned.1.call-done = bf16[2048,2048]{1,0:T(8,128)(2,1)} async-done(((bf16[64,2048]{1,0:T(8,128)(2,1)}), bf16[2048,2048]{1,0:T(8,128)(2,1)}) %all-gather.9.cloned.1.call-update) | async-done | bytes 8388624 | tf_op jit(solution)/shard_map/all_gather | solution.py:938
  233.1 10.8 %fusion.32 = f32[1024,2048]{1,0:T(8,128)} fusion(bf16[1024,1024]{0,1:T(8,128)(2,1)} %add_convert_fusion.4, bf16[2048,2048]{1,0:T(8,128)(2,1)} %all-gather.9.cloned.1.call-done), kind=kOutput, calls=%fused_computation.68 | convolution fusion | flops 4294967296 | bytes 14680064 | tf_op jit(solution)/shard_map/dot_general | solution.py:895
  243.9 7.2 fusion.40
  251.2 61.3 %all-gather.11.cloned.1.call-done = bf16[2048,2048]{1,0:T(8,128)(2,1)} async-done(((bf16[64,2048]{1,0:T(8,128)(2,1)}), bf16[2048,2048]{1,0:T(8,128)(2,1)}) %all-gather.11.cloned.1.call-update) | async-done | bytes 8388624 | tf_op jit(solution)/shard_map/all_gather | solution.py:938
  312.5 15.4 %convert_reduce_fusion = (f32[2048]{0:T(1024)}, bf16[1024,2048]{1,0:T(8,128)(2,1)S(1)}) fusion(f32[1024,2048]{1,0:T(8,128)} %fusion.32, f32[2048]{0:T(1024)S(1)} %get-tuple-element.129, bf16[2048,2048]{1,0:T(8,128)(2,1)} %all-gather.11.cloned.1.call-done, bf16[512,1024]{0,1:T(8,128)(2,1)} %collective-permute-done.2, bf16[512,1024]{0,1:T(8,128)(2,1)S(1)} %bitcast.178, ...), kind=kOutput, calls=%fused_computation.20 | convolution fusion | flops 4352636928 | bytes 18890752 | tf_op jit(solution)/shard_map/dot_general | solution.py:895
  327.9 9.9 fusion.30
  337.8 14.4 %convert_reduce_fusion.1 = (f32[2048]{0:T(1024)}, bf16[1024,2048]{1,0:T(8,128)(2,1)S(1)}) fusion(f32[1024,2048]{1,0:T(8,128)} %fusion.40, f32[2048]{0:T(1024)S(1)} %get-tuple-element.130, bf16[2048,2048]{1,0:T(8,128)(2,1)S(1)} %copy-done.52, bf16[512,1024]{0,1:T(8,128)(2,1)} %collective-permute-done.2, bf16[512,1024]{0,1:T(8,128)(2,1)S(1)} %bitcast.179, ...), kind=kOutput, calls=%fused_computation.21 | convolution fusion | flops 4352636928 | bytes 18890752 | tf_op jit(solution)/shard_map/dot_general | solution.py:895
  352.2 10.8 %multiply_reduce_fusion = (f32[1024]{0:T(1024)}, f32[1024]{0:T(1024)S(1)}, f32[1024]{0:T(1024)}, f32[1024,1024]{0,1:T(8,128)S(1)}) fusion(f32[1024,1024]{0,1:T(8,128)S(1)} %copy-done.5, f32[1024]{0:T(1024)S(1)} %fusion.78, f32[1024]{0:T(1024)S(1)} %broadcast_multiply_fusion, f32[1024]{0:T(1024)S(1)} %bitcast.219, f32[1024,1024]{0,1:T(8,128)} %fusion.30, ...), kind=kOutput, calls=%fused_computation.48 | convolution fusion | flops 4304401408 | bytes 20996096 | tf_op jit(solution)/shard_map/dot_general | solution.py:895
  364.1 4.5 convert_reduce_fusion.3
  371.9 1.5 pad_maximum_fusion.6
  373.5 3.3 fusion.64
  378.1 1.6 pad_maximum_fusion.5
  379.7 35.0 %shard_map.261 = (bf16[16,64,1024]{2,1,0:T(8,128)(2,1)}, bf16[16,64,1024]{2,1,0:T(8,128)(2,1)}, bf16[16,64,1024]{2,1,0:T(8,128)(2,1)}) custom-call(bf16[2,3,8,64,1024]{4,3,2,1,0:T(8,128)(2,1)} %pad_maximum_fusion.2.q_ref.k_ref.v_ref, bf16[2,3,8,64,1024]{4,3,2,1,0:T(8,128)(2,1)} %pad_maximum_fusion.2.q_ref.k_ref.v_ref, ...), custom_call_target="tpu_custom_call" | custom-call | flops 34359738368 | bytes 52428800 | tf_op jit(solution)/shard_map/pallas_call | solution.py:515
  414.6 3.7 pad_maximum_fusion.3
  418.4 1.4 fusion.89
  419.8 4.2 fusion.49
  424.1 4.2 fusion.48
  428.3 3.2 pad_maximum_fusion.4
  432.0 11.0 %convert_bitcast_fusion = bf16[1,1024,2048]{2,1,0:T(8,128)(2,1)} fusion(f32[1024,2048]{1,0:T(8,128)} %fusion.32, f32[2048]{0:T(1024)S(1)} %get-tuple-element.129, bf16[512,1024]{0,1:T(8,128)(2,1)} %collective-permute-done.2, bf16[512,1024]{0,1:T(8,128)(2,1)S(1)} %bitcast.181, pred[]{:T(512)S(6)} %eq.2), kind=kOutput, calls=%fused_computation.51 | convolution fusion | flops 4327473152 | bytes 14688257 | tf_op jit(solution)/shard_map/dot_general | solution.py:895
  443.0 11.0 %convert_bitcast_fusion.1 = bf16[1,1024,2048]{2,1,0:T(8,128)(2,1)} fusion(f32[1024,2048]{1,0:T(8,128)} %fusion.40, f32[2048]{0:T(1024)S(1)} %get-tuple-element.130, bf16[512,1024]{0,1:T(8,128)(2,1)} %collective-permute-done.2, bf16[512,1024]{0,1:T(8,128)(2,1)S(1)} %bitcast.182, pred[]{:T(512)S(6)} %eq.2), kind=kOutput, calls=%fused_computation.52 | convolution fusion | flops 4327473152 | bytes 14688257 | tf_op jit(solution)/shard_map/dot_general | solution.py:895
  453.9 7.5 pad_maximum_fusion.1
  461.7 9.5 convert_bitcast_fusion.2
  471.2 6.0 convert_bitcast_fusion.3
  477.2 7.5 pad_maximum_fusion
  484.8 8.9 fusion.28
  493.6 9.5 add_convert_fusion.3
  503.1 1.6 dynamic-slice_bitcast_fusion.1
  506.3 1.9 convert_reduce_fusion.4
  508.3 6.4 fusion.50
  514.7 5.9 fusion.84
  520.7 2.6 fusion.22
  523.3 4.8 add_convert_fusion.2
  530.4 2.0 maximum_select_fusion.1
  532.4 2.4 copy.62
  534.8 19.1 %collective-permute-done.3 = bf16[512,1024]{0,1:T(8,128)(2,1)} collective-permute-done((bf16[512,1024]{0,1:T(8,128)(2,1)}, bf16[512,1024]{0,1:T(8,128)(2,1)}, u32[]{:S(2)}, u32[]{:S(2)}) %collective-permute-start.3) | collective-permute-done | bytes 1048608 | tf_op jit(solution)/shard_map/ppermute | solution.py:904
  553.9 4.1 fusion.56
  558.0 5.5 copy.63
  563.5 1.6 convert_bitcast_fusion.10
  565.1 58.7 %reduce-scatter.5.cloned.1.call-done = bf16[64,1536]{1,0:T(8,128)(2,1)} async-done(((bf16[2048,1536]{1,0:T(8,128)(2,1)}), bf16[64,1536]{1,0:T(8,128)(2,1)}) %reduce-scatter.5.cloned.1.call-update) | async-done | bytes 196624 | tf_op jit(solution)/shard_map/reduce_scatter | solution.py:942
  625.7 135.7 %reduce-scatter.11.cloned.1.call-done = bf16[64,2048]{1,0:T(8,128)(2,1)} async-done(((bf16[2048,2048]{1,0:T(8,128)(2,1)}), bf16[64,2048]{1,0:T(8,128)(2,1)}) %reduce-scatter.11.cloned.1.call-update) | async-done | bytes 262160 | tf_op jit(solution)/shard_map/reduce_scatter | solution.py:942
  761.4 2.0 fusion.87
  763.5 145.4 %reduce-scatter.9.cloned.1.call-done = bf16[64,2048]{1,0:T(8,128)(2,1)} async-done(((bf16[2048,2048]{1,0:T(8,128)(2,1)}), bf16[64,2048]{1,0:T(8,128)(2,1)}) %reduce-scatter.9.cloned.1.call-update) | async-done | bytes 262160 | tf_op jit(solution)/shard_map/reduce_scatter | solution.py:942
  908.9 2.0 fusion.86
  912.0 134.4 %shard_map.262 = (bf16[12,64,512]{2,1,0:T(8,128)(2,1)}, f32[12,8,128]{2,1,0:T(8,128)}) custom-call(bf16[12,64,512]{2,1,0:T(8,128)(2,1)} %pad_maximum_fusion.7.moments_ref, f32[12,8,128]{2,1,0:T(8,128)} %copy-done.51), custom_call_target="tpu_custom_call" | custom-call | flops 25769803776 | bytes 4194304 | tf_op jit(solution)/shard_map/pallas_call | solution.py:798
  1046.4 1.6 bitcast_subtract_fusion.1
  1048.0 1.8 multiply_subtract_fusion
  (201 shorter events, 28.5 us)
Async XLA Ops:
  7.2 18.3 %copy-start = (s32[2,1,2]{2,1,0:T(1,128)S(1)}, s32[2,1,2]{2,1,0:T(1,128)}, u32[]{:S(2)}) copy-start(s32[2,1,2]{2,1,0:T(1,128)} %param.15) | copy-start | bytes 52
  7.2 86.8 %all-gather.5.cloned.1.call-start = ((), (), s32[]{:S(2)}) async-start(), calls=%async_computation.4 | async-start | bytes 6488064 | tf_op jit(solution)/shard_map/all_gather | solution.py:938
  9.0 165.4 %all-gather.7.cloned.1.call-start = ((), (), s32[]{:S(2)}) async-start(), calls=%async_computation.5 | async-start | bytes 2162688 | tf_op jit(solution)/shard_map/all_gather | solution.py:938
  10.6 222.5 %all-gather.9.cloned.1.call-start = ((), (), s32[]{:S(2)}) async-start(), calls=%async_computation.6 | async-start | bytes 8650752 | tf_op jit(solution)/shard_map/all_gather | solution.py:938
  12.5 300.0 %all-gather.11.cloned.1.call-start = ((), (), s32[]{:S(2)}) async-start(), calls=%async_computation.7 | async-start | bytes 8650752 | tf_op jit(solution)/shard_map/all_gather | solution.py:938
  14.3 549.2 %reduce-scatter.7.cloned.1.call-start = ((), (), s32[]{:S(2)}) async-start(), calls=%async_computation.9 | async-start | bytes 2162688 | tf_op jit(solution)/shard_map/reduce_scatter | solution.py:942
  18.0 4.1 copy-start.28
  19.3 28.6 %collective-permute-start = (bf16[512,1024]{0,1:T(8,128)(2,1)}, bf16[512,1024]{0,1:T(8,128)(2,1)S(1)}, u32[]{:S(2)}, u32[]{:S(2)}) collective-permute-start(bf16[512,1024]{0,1:T(8,128)(2,1)} %bitcast.197), channel_id=1, source_target_pairs={{0,1},{1,0},{2,3},{3,2},{4,5},{5,4},{6,7},{7,6},{8,9},{9,8},{10,11... | collective-permute-start | bytes 3145736 | tf_op jit(solution)/shard_map/ppermute | solution.py:911
  21.8 229.3 %collective-permute-start.2 = (bf16[512,1024]{0,1:T(8,128)(2,1)}, bf16[512,1024]{0,1:T(8,128)(2,1)}, u32[]{:S(2)}, u32[]{:S(2)}) collective-permute-start(bf16[512,1024]{0,1:T(8,128)(2,1)} %bitcast.196), channel_id=1, source_target_pairs={{0,1},{1,0},{2,3},{3,2},{4,5},{5,4},{6,7},{7,6},{8,9},{9,8},{10,11... | collective-permute-start | bytes 3145736 | tf_op jit(solution)/shard_map/ppermute | solution.py:911
  22.7 83.4 %copy-start.34 = (f32[1,1024]{1,0:T(1,128)}, f32[1,1024]{1,0:T(1,128)S(1)}, u32[]{:S(2)}) copy-start(f32[1,1024]{1,0:T(1,128)S(1)} %get-tuple-element.118) | copy-start | bytes 12292
  22.7 83.4 %copy-start.47 = (f32[1,1024]{1,0:T(1,128)}, f32[1,1024]{1,0:T(1,128)S(1)}, u32[]{:S(2)}) copy-start(f32[1,1024]{1,0:T(1,128)S(1)} %get-tuple-element.117) | copy-start | bytes 12292
  48.5 57.6 %copy-start.31 = (f32[1024]{0:T(1024)}, f32[1024]{0:T(1024)S(1)}, u32[]{:S(2)}) copy-start(f32[1024]{0:T(1024)S(1)} %broadcast_multiply_fusion.1) | copy-start | bytes 12292
  49.4 52.0 %copy-start.40 = (f32[1024]{0:T(1024)}, f32[1024]{0:T(1024)S(1)}, u32[]{:S(2)}) copy-start(f32[1024]{0:T(1024)S(1)} %fusion.23) | copy-start | bytes 12292
  49.4 56.7 %copy-start.36 = (f32[1024]{0:T(1024)}, f32[1024]{0:T(1024)S(1)}, u32[]{:S(2)}) copy-start(f32[1024]{0:T(1024)S(1)} %fusion.77) | copy-start | bytes 12292
  174.4 3.0 copy-start.20
  174.4 3.0 copy-start.54
  233.1 10.8 %copy-start.12 = (bf16[1024,1024]{0,1:T(8,128)(2,1)S(1)}, bf16[1024,1024]{0,1:T(8,128)(2,1)}, u32[]{:S(2)}) copy-start(bf16[1024,1024]{0,1:T(8,128)(2,1)} %add_convert_fusion.4) | copy-start | bytes 6291460
  233.1 10.8 %copy-start.53 = (bf16[2048,2048]{1,0:T(8,128)(2,1)S(1)}, bf16[2048,2048]{1,0:T(8,128)(2,1)}, u32[]{:S(2)}) copy-start(bf16[2048,2048]{1,0:T(8,128)(2,1)} %all-gather.9.cloned.1.call-done) | copy-start | bytes 25165828
  327.9 9.9 copy-start.58
  327.9 9.9 copy-start.52
  337.8 14.4 %copy-start.5 = (f32[1024,1024]{0,1:T(8,128)S(1)}, f32[1024,1024]{0,1:T(8,128)}, u32[]{:S(2)}) copy-start(f32[1024,1024]{0,1:T(8,128)} %copy-done.4) | copy-start | bytes 12582916
  352.2 10.8 %copy-start.56 = (bf16[1024,2048]{1,0:T(8,128)(2,1)}, bf16[1024,2048]{1,0:T(8,128)(2,1)S(1)}, u32[]{:S(2)}) copy-start(bf16[1024,2048]{1,0:T(8,128)(2,1)S(1)} %get-tuple-element.124) | copy-start | bytes 12582916
  364.0 4.6 copy-start.2
  364.0 4.6 copy-start.38
  364.1 4.6 copy-start.21
  373.4 250.4 %reduce-scatter.5.cloned.1.call-start = ((), (), s32[]{:S(2)}) async-start(), calls=%async_computation.8 | async-start | bytes 6488064 | tf_op jit(solution)/shard_map/reduce_scatter | solution.py:942
  373.5 3.3 copy-start.15
  373.5 3.3 copy-start.55
  419.8 4.3 copy-start.11
  419.8 4.3 copy-start.9
  431.5 329.9 %reduce-scatter.11.cloned.1.call-start = ((), (), s32[]{:S(2)}) async-start(), calls=%async_computation.11 | async-start | bytes 8650752 | tf_op jit(solution)/shard_map/reduce_scatter | solution.py:942
  461.5 447.4 %reduce-scatter.9.cloned.1.call-start = ((), (), s32[]{:S(2)}) async-start(), calls=%async_computation.10 | async-start | bytes 8650752 | tf_op jit(solution)/shard_map/reduce_scatter | solution.py:942
  461.7 9.5 copy-start.13
  461.7 9.5 copy-start.57
  484.7 8.9 copy-start.6
  484.7 8.9 copy-start.46
  503.1 2.8 copy-start.7
  504.7 25.7 %collective-permute-start.1 = (bf16[512,1024]{0,1:T(8,128)(2,1)}, bf16[512,1024]{0,1:T(8,128)(2,1)}, u32[]{:S(2)}, u32[]{:S(2)}) collective-permute-start(bf16[512,1024]{0,1:T(8,128)(2,1)} %get-tuple-element.102), channel_id=1, source_target_pairs={{0,1},{1,0},{2,3},{3,2},{4,5},{5,4},{6,7},{7,6},{8,9},{9,8},{10,11... | collective-permute-start | bytes 3145736 | tf_op jit(solution)/shard_map/ppermute | solution.py:904
  508.3 6.4 copy-start.10
  514.7 6.0 copy-start.41
  520.7 2.6 copy-start.3
  520.7 2.6 copy-start.39
  528.1 2.1 copy-start.43
  528.1 2.1 copy-start.50
  528.1 2.1 copy-start.49
  528.1 2.1 copy-start.45
  528.1 2.1 copy-start.44
  528.2 2.1 copy-start.42
  528.2 2.2 copy-start.8
  529.4 24.5 %collective-permute-start.3 = (bf16[512,1024]{0,1:T(8,128)(2,1)}, bf16[512,1024]{0,1:T(8,128)(2,1)}, u32[]{:S(2)}, u32[]{:S(2)}) collective-permute-start(bf16[512,1024]{0,1:T(8,128)(2,1)} %get-tuple-element.98), channel_id=1, source_target_pairs={{0,1},{1,0},{2,3},{3,2},{4,5},{5,4},{6,7},{7,6},{8,9},{9,8},{10,11... | collective-permute-start | bytes 3145736 | tf_op jit(solution)/shard_map/ppermute | solution.py:904
  530.3 4.4 copy-start.51
  558.0 5.5 copy-start.30
  558.0 66.8 %copy-start.25 = (f32[3,64,512]{2,1,0:T(8,128)S(1)}, f32[3,64,512]{2,1,0:T(8,128)}, u32[]{:S(2)}) copy-start(f32[3,64,512]{2,1,0:T(8,128)} %param.21) | copy-start | bytes 1179652
  558.0 203.4 %copy-start.23 = (f32[2048,64]{0,1:T(8,128)S(1)}, f32[2048,64]{0,1:T(8,128)}, u32[]{:S(2)}) copy-start(f32[2048,64]{0,1:T(8,128)} %param.24) | copy-start | bytes 1572868
  563.5 345.5 %copy-start.24 = (f32[64,2048]{1,0:T(8,128)S(1)}, f32[64,2048]{1,0:T(8,128)}, u32[]{:S(2)}) copy-start(f32[64,2048]{1,0:T(8,128)} %param.23) | copy-start | bytes 1572868
  912.0 134.4 %copy-start.22 = (f32[512,64]{0,1:T(8,128)S(1)}, f32[512,64]{0,1:T(8,128)}, u32[]{:S(2)}) copy-start(f32[512,64]{0,1:T(8,128)} %param.17) | copy-start | bytes 393220
  912.0 136.0 %copy-start.18 = (f32[3,64,512]{2,1,0:T(8,128)S(1)}, f32[3,64,512]{2,1,0:T(8,128)}, u32[]{:S(2)}) copy-start(f32[3,64,512]{2,1,0:T(8,128)} %param.16) | copy-start | bytes 1179652
  912.0 139.8 %copy-start.33 = (f32[12,1024]{1,0:T(8,128)S(1)}, f32[12,1024]{1,0:T(8,128)}, u32[]{:S(2)}) copy-start(f32[12,1024]{1,0:T(8,128)} %param.25) | copy-start | bytes 147460
  1046.4 5.6 copy-start.16
  1046.4 6.5 copy-start.17
  1046.4 8.1 copy-start.1
  1048.0 5.7 copy-start.29
  1051.8 2.7 copy-start.27
  1051.9 2.6 copy-start.26
  (7 other events, 11.2 us)
Sparse Core Ops, SparseCore 0:
  11.5 82.4 all-gather.4
  97.4 54.9 all-gather.6
  155.8 77.2 all-gather.8
  236.4 76.0 all-gather.10
  373.5 119.4 reduce-scatter.6
  499.4 124.3 reduce-scatter.4
  626.1 135.2 reduce-scatter.10
  763.7 145.1 reduce-scatter.8

commit v3 on v2

--- a/solution.py
+++ b/solution.py
@@ -416,6 +416,12 @@
     )
 
 
+QB = 256
+PAIR = 2 * HD
+PAIRS = D // PAIR
+VMEM_LIMIT = 56 * 1024 * 1024
+
+
 def layout_grid(starts_ref, dist_ref):
     key_pos = lax.broadcasted_iota(jnp.int32, (LEN, LEN), 0)
     query_pos = lax.broadcasted_iota(jnp.int32, (LEN, LEN), 1)
@@ -429,104 +435,130 @@
     dist_ref[...] = jnp.where(visible, jnp.abs(gap).astype(jnp.float32), -MASKED_SCORE)
 
 
-def attend_fwd_kernel(starts_ref, slopes_ref, q_ref, k_ref, v_ref, ctx_ref, exps_ref, stat_ref, dist_ref):
-    head = pl.program_id(0)
-
-    @pl.when(head == 0)
+def only_rows(pair, half):
+    rows = lax.broadcasted_iota(jnp.int32, pair.shape, 0)
+    return jnp.where((rows >= HD) if half else (rows < HD), pair, jnp.zeros_like(pair))
+
+
+def only_cols(pair, half):
+    cols = lax.broadcasted_iota(jnp.int32, pair.shape, 1)
+    return jnp.where((cols >= HD) if half else (cols < HD), pair, jnp.zeros_like(pair))
+
+
+def mul(left, right):
+    return jnp.dot(left, right, preferred_element_type=jnp.float32)
+
+
+def attend_fwd_kernel(starts_ref, slopes_ref, packed_ref, ctx_ref, exps_ref, stat_ref, dist_ref, ctx_t):
+    pair = pl.program_id(0)
+
+    @pl.when(pair == 0)
     def _():
         layout_grid(starts_ref, dist_ref)
 
-    slope = slopes_ref[head]
-    keys = k_ref[0, 0, 0].T
-    queries = q_ref[0, 0, 0] * (1.0 / math.sqrt(HD))
-    for block in range(LEN // QB):
-        span = min(LEN, QB * block + QB + PIECE)
-        cols = slice(block * QB, block * QB + QB)
-        scores = jnp.dot(keys[:span], queries[:, cols], preferred_element_type=jnp.float32)
-        scores = scores - slope * dist_ref[:span, cols]
-        top = jnp.max(scores, axis=0, keepdims=True)
-        raw = jnp.exp(scores - top)
-        inverse = 1.0 / jnp.sum(raw, axis=0, keepdims=True)
-        low = raw.astype(jnp.bfloat16)
-        exps_ref[0, :span, cols] = low
-        context = jnp.dot(v_ref[0, 0, 0, :, :span], low, preferred_element_type=jnp.float32)
-        ctx_ref[0, :, cols] = (context * inverse).astype(jnp.bfloat16)
-        stat_ref[0, :, cols] = inverse
-
-
-def attend_bwd_kernel(q_ref, k_ref, v_ref, ctx_ref, grad_ref, exps_ref, stat_ref, dq_ref, dk_ref, dv_ref, dk_sum, dv_sum):
+    keys = packed_ref[:, PAIR : 2 * PAIR]
+    values_t = packed_ref[:, 2 * PAIR :].T
+    queries_t = (packed_ref[:, :PAIR] * (1.0 / math.sqrt(HD))).T
+    for half in (0, 1):
+        slope = slopes_ref[2 * pair + half]
+        queries = only_rows(queries_t, half)
+        heads = slice(half * HD, half * HD + HD)
+        for block in range(LEN // QB):
+            span = min(LEN, QB * block + QB + PIECE)
+            cols = slice(block * QB, block * QB + QB)
+            scores = mul(keys[:span], queries[:, cols]) - slope * dist_ref[:span, cols]
+            top = jnp.max(scores, axis=0, keepdims=True)
+            raw = jnp.exp(scores - top)
+            inverse = 1.0 / jnp.sum(raw, axis=0, keepdims=True)
+            low = raw.astype(jnp.bfloat16)
+            exps_ref[half, :span, cols] = low
+            ctx_t[heads, cols] = mul(values_t[heads, :span], low) * inverse
+            stat_ref[0, half : half + 1, cols] = inverse
+    ctx_ref[...] = ctx_t[...].T.astype(jnp.bfloat16)
+
+
+def attend_bwd_kernel(packed_ref, ctx_ref, grad_ref, exps_ref, stat_ref, out_ref, dq_t, dk_sum, dv_sum):
     scale = 1.0 / math.sqrt(HD)
-    keys_t = k_ref[0, 0, 0]
-    values = v_ref[0, 0, 0].T
-    queries = q_ref[0, 0, 0].T
+    queries = packed_ref[:, :PAIR]
+    keys_t = packed_ref[:, PAIR : 2 * PAIR].T
+    values = packed_ref[:, 2 * PAIR :]
+    grads_t = grad_ref[...].T.astype(jnp.float32)
+    context_t = ctx_ref[...].T.astype(jnp.float32)
+    scaled = []
+    inner_rows = []
+    for half in (0, 1):
+        heads = slice(half * HD, half * HD + HD)
+        scaled.append(grads_t[heads] * stat_ref[0, half : half + 1, :])
+        inner_rows.append(jnp.sum(scaled[half] * context_t[heads], axis=0, keepdims=True))
+    scaled_t = jnp.concatenate(scaled, axis=0).astype(jnp.bfloat16)
+    scaled_rows = scaled_t.T
     dk_sum[...] = jnp.zeros_like(dk_sum)
     dv_sum[...] = jnp.zeros_like(dv_sum)
-    for block in reversed(range(LEN // QB)):
-        span = min(LEN, QB * block + QB + PIECE)
-        cols = slice(block * QB, block * QB + QB)
-        grad = grad_ref[0, :, cols].astype(jnp.float32) * stat_ref[0, :, cols]
-        inner = jnp.sum(grad * ctx_ref[0, :, cols].astype(jnp.float32), axis=0, keepdims=True)
-        grad_low = grad.astype(jnp.bfloat16)
-        exps = exps_ref[0, :span, cols]
-        grad_probs = jnp.dot(values[:span], grad_low, preferred_element_type=jnp.float32)
-        grad_scores = (exps.astype(jnp.float32) * (grad_probs - inner)).astype(jnp.bfloat16)
-        dv_sum[:span, :] += jnp.dot(exps, grad_low.T, preferred_element_type=jnp.float32)
-        dk_sum[:span, :] += jnp.dot(grad_scores, queries[cols], preferred_element_type=jnp.float32)
-        dq = jnp.dot(keys_t[:, :span], grad_scores, preferred_element_type=jnp.float32)
-        dq_ref[0, :, cols] = (dq * scale).astype(jnp.bfloat16)
-    dk_ref[0] = (dk_sum[...] * scale).T.astype(jnp.bfloat16)
-    dv_ref[0] = dv_sum[...].T.astype(jnp.bfloat16)
-
-
-QB = 256
-
-
-def part_spec(part, heads_each):
-    return pl.BlockSpec((1, 1, 1, HD, LEN), lambda h: (h // heads_each, part, h % heads_each, 0, 0))
-
-
-HEAD_ROWS = pl.BlockSpec((1, HD, LEN), lambda h: (h, 0, 0))
-HEAD_GRID = pl.BlockSpec((1, LEN, LEN), lambda h: (h, 0, 0))
-HEAD_STAT = pl.BlockSpec((1, 1, LEN), lambda h: (h, 0, 0))
+    for half in (0, 1):
+        heads = slice(half * HD, half * HD + HD)
+        half_t = only_rows(scaled_t, half)
+        half_rows = only_cols(scaled_rows, half)
+        half_queries = only_cols(queries, half)
+        for block in range(LEN // QB):
+            span = min(LEN, QB * block + QB + PIECE)
+            cols = slice(block * QB, block * QB + QB)
+            exps = exps_ref[half, :span, cols]
+            grad_probs = mul(values[:span], half_t[:, cols])
+            grad_scores = (exps.astype(jnp.float32) * (grad_probs - inner_rows[half][:, cols])).astype(jnp.bfloat16)
+            dv_sum[:span, :] += mul(exps, half_rows[cols])
+            dk_sum[:span, :] += mul(grad_scores, half_queries[cols])
+            dq_t[heads, cols] = mul(keys_t[heads, :span], grad_scores)
+    out_ref[:, :PAIR] = (dq_t[...] * scale).T.astype(jnp.bfloat16)
+    out_ref[:, PAIR : 2 * PAIR] = (dk_sum[...] * scale).astype(jnp.bfloat16)
+    out_ref[:, 2 * PAIR :] = dv_sum[...].astype(jnp.bfloat16)
+
+
+PACKED_COLS = pl.BlockSpec((LEN, 3 * PAIR), lambda p: (0, p))
+PAIR_COLS = pl.BlockSpec((LEN, PAIR), lambda p: (0, p))
+PAIR_GRID = pl.BlockSpec((2, LEN, LEN), lambda p: (p, 0, 0))
+PAIR_STAT = pl.BlockSpec((1, 2, LEN), lambda p: (p, 0, 0))
 SCALARS = pl.BlockSpec(memory_space=pltpu.SMEM)
-VMEM_LIMIT = 56 * 1024 * 1024
 
 
 def attention_forward(starts, slopes, packed):
-    heads_each = packed.shape[2]
     return pl.pallas_call(
         attend_fwd_kernel,
-        grid=(H,),
-        in_specs=[SCALARS, SCALARS] + [part_spec(part, heads_each) for part in range(3)],
-        out_specs=[HEAD_ROWS, HEAD_GRID, HEAD_STAT],
+        grid=(PAIRS,),
+        in_specs=[SCALARS, SCALARS, PACKED_COLS],
+        out_specs=[PAIR_COLS, PAIR_GRID, PAIR_STAT],
         out_shape=[
-            jax.ShapeDtypeStruct((H, HD, LEN), jnp.bfloat16),
+            jax.ShapeDtypeStruct((LEN, D), jnp.bfloat16),
             jax.ShapeDtypeStruct((H, LEN, LEN), jnp.bfloat16),
-            jax.ShapeDtypeStruct((H, 1, LEN), jnp.float32),
+            jax.ShapeDtypeStruct((PAIRS, 2, LEN), jnp.float32),
         ],
-        scratch_shapes=[pltpu.VMEM((LEN, LEN), jnp.float32)],
+        scratch_shapes=[pltpu.VMEM((LEN, LEN), jnp.float32), pltpu.VMEM((PAIR, LEN), jnp.float32)],
         compiler_params=pltpu.CompilerParams(vmem_limit_bytes=VMEM_LIMIT),
-        cost_estimate=pl.CostEstimate(flops=4 * LEN * LEN * D * 4, bytes_accessed=44 * 1024 * 1024, transcendentals=H * LEN * LEN),
-    )(starts, slopes, packed, packed, packed)
+        cost_estimate=pl.CostEstimate(
+            flops=16 * LEN * LEN * D, bytes_accessed=44 * 1024 * 1024, transcendentals=H * LEN * LEN
+        ),
+    )(starts, slopes, packed)
 
 
 def attention_backward(packed, context, grad_context, exps, stats):
-    heads_each = packed.shape[2]
     return pl.pallas_call(
         attend_bwd_kernel,
-        grid=(H,),
-        in_specs=[part_spec(part, heads_each) for part in range(3)]
-        + [HEAD_ROWS, HEAD_ROWS, HEAD_GRID, HEAD_STAT],
-        out_specs=[HEAD_ROWS, HEAD_ROWS, HEAD_ROWS],
-        out_shape=[jax.ShapeDtypeStruct((H, HD, LEN), jnp.bfloat16)] * 3,
-        scratch_shapes=[pltpu.VMEM((LEN, HD), jnp.float32), pltpu.VMEM((LEN, HD), jnp.float32)],
+        grid=(PAIRS,),
+        in_specs=[PACKED_COLS, PAIR_COLS, PAIR_COLS, PAIR_GRID, PAIR_STAT],
+        out_specs=PACKED_COLS,
+        out_shape=jax.ShapeDtypeStruct((LEN, 3 * D), jnp.bfloat16),
+        scratch_shapes=[
+            pltpu.VMEM((PAIR, LEN), jnp.float32),
+            pltpu.VMEM((LEN, PAIR), jnp.float32),
+            pltpu.VMEM((LEN, PAIR), jnp.float32),
+        ],
         compiler_params=pltpu.CompilerParams(vmem_limit_bytes=VMEM_LIMIT),
-        cost_estimate=pl.CostEstimate(flops=8 * LEN * LEN * D * 4, bytes_accessed=50 * 1024 * 1024, transcendentals=0),
-    )(packed, packed, packed, context, grad_context, exps, stats)
+        cost_estimate=pl.CostEstimate(flops=32 * LEN * LEN * D, bytes_accessed=50 * 1024 * 1024, transcendentals=0),
+    )(packed, context, grad_context, exps, stats)
 
 
 SLOTS = 12
 SLOT = 512
+HALF_SLOT = SLOT // 2
 TILE = 256
 MESH_IDS = pl.DeviceIdType.MESH
 
@@ -718,9 +750,6 @@
 
             lax.fori_loop(0, D // TILE, one, 0)
 
-        def mul(left, right):
-            return jnp.dot(left, right, preferred_element_type=jnp.float32)
-
         chain = chain_low
         other = chain_next
         for sweep in range(NS_ITERS):
@@ -883,8 +912,365 @@
     )
 
 
-BOTH = ("tensor", "dp")
-SWAP = [(0, 1), (1, 0)]
+def neighbours():
+    dp_me = lax.axis_index("dp")
+    y = lax.axis_index("tensor")
+    core = lax.rem(dp_me, 2)
+    x = lax.rem(dp_me // 2, 2)
+    z = dp_me // 4
+    sibling = (dp_me + 1 - 2 * core, y)
+    beside = (dp_me + 2 - 4 * x, y)
+    across = (dp_me, 1 - y)
+    stations = [(lax.rem(dp_me + 4 * hop, 16), y) for hop in (1, 2, 3)]
+    return (z, x, core, y), sibling, beside, across, stations
+
+
+def greet_neighbours(places):
+    barrier = pltpu.get_barrier_semaphore()
+    for place in places:
+        pl.semaphore_signal(barrier, inc=1, device_id=place, device_id_type=MESH_IDS)
+    pl.semaphore_wait(barrier, len(places))
+
+
+SWAP_AT = 2
+SPREAD_LAG = 1
+
+
+class Spread:
+    def __init__(self, slots_ref, table, local_sem, send_sem, recv_sem):
+        self.slots_ref, self.table = slots_ref, table
+        self.local_sem, self.send_sem, self.recv_sem = local_sem, send_sem, recv_sem
+        (self.z, self.x, self.core, self.y), self.sibling, self.beside, self.across, self.stations = neighbours()
+
+    def remote(self, source, target, stage, slot, place):
+        return pltpu.make_async_remote_copy(
+            src_ref=source,
+            dst_ref=target,
+            send_sem=self.send_sem.at[stage, slot],
+            recv_sem=self.recv_sem.at[stage, slot],
+            device_id=place,
+            device_id_type=MESH_IDS,
+        )
+
+    def cols(self, slot, part, start=0, size=SLOT):
+        _, column, distance, _ = self.table[slot]
+        if isinstance(part, int):
+            return pl.ds(column + part * distance + start, size)
+        return pl.ds(pl.multiple_of(column + part * distance + start, 128), size)
+
+    def own(self, slot):
+        here = self.table[slot][0].at[self.z, self.x, self.core, :, self.cols(slot, self.y)]
+        return pltpu.make_async_copy(self.slots_ref.at[slot], here, self.local_sem.at[slot])
+
+    def along_z(self, slot):
+        here = self.table[slot][0].at[self.z, self.x, self.core, :, self.cols(slot, self.y)]
+        return [
+            self.remote(self.slots_ref.at[slot], here, hop, slot, place)
+            for hop, place in enumerate(self.stations)
+        ]
+
+    def second(self, slot):
+        whole, _, _, size = self.table[slot]
+        copies = []
+        if size:
+            part = whole.at[:, self.x, self.core, :, self.cols(slot, self.y, 0, size)]
+            copies.append(self.remote(part, part, 3, slot, self.beside))
+        if size < SLOT:
+            part = whole.at[:, self.x, self.core, :, self.cols(slot, self.y, size, SLOT - size)]
+            copies.append(self.remote(part, part, 4, slot, self.across))
+        return copies
+
+    def third(self, slot):
+        whole, _, _, size = self.table[slot]
+        copies = []
+        if size:
+            part = whole.at[:, :, self.core, :, self.cols(slot, self.y, 0, size)]
+            copies.append(self.remote(part, part, 5, slot, self.across))
+        if size < SLOT:
+            for index in (0, 1):
+                part = whole.at[:, self.x, self.core, :, self.cols(slot, index, size, SLOT - size)]
+                copies.append(self.remote(part, part, 6 + index, slot, self.beside))
+        return copies
+
+    def fourth(self, slot):
+        whole = self.table[slot][0]
+        copies = []
+        for index in (0, 1):
+            part = whole.at[:, :, self.core, :, self.cols(slot, index)]
+            copies.append(self.remote(part, part, 8 + index, slot, self.sibling))
+        return copies
+
+    def begin(self):
+        for slot in range(len(self.table)):
+            self.own(slot).start()
+            for copy in self.along_z(slot):
+                copy.start()
+
+    def tick(self, index):
+        count = len(self.table)
+        if index < count:
+            self.own(index).wait()
+            for copy in self.along_z(index):
+                copy.wait_recv()
+            for copy in self.second(index):
+                copy.start()
+        if 0 <= index - SPREAD_LAG < count:
+            for copy in self.second(index - SPREAD_LAG):
+                copy.wait_recv()
+            for copy in self.third(index - SPREAD_LAG):
+                copy.start()
+        if 0 <= index - 2 * SPREAD_LAG < count:
+            for copy in self.third(index - 2 * SPREAD_LAG):
+                copy.wait_recv()
+            for copy in self.fourth(index - 2 * SPREAD_LAG):
+                copy.start()
+
+    def ticks(self):
+        return len(self.table) + 2 * SPREAD_LAG
+
+    def finish(self):
+        for slot in range(len(self.table)):
+            for copy in self.along_z(slot) + self.second(slot) + self.third(slot):
+                copy.wait_send()
+            for copy in self.fourth(slot):
+                copy.wait()
+
+
+def spread_semaphores(count):
+    return [
+        pltpu.SemaphoreType.DMA((count,)),
+        pltpu.SemaphoreType.DMA((10, count)),
+        pltpu.SemaphoreType.DMA((10, count)),
+    ]
+
+
+def first_spread_kernel(slots_ref, tokens_ref, whole_ref, got_ref, local_sem, send_sem, recv_sem, token_sem):
+    table = [(whole_ref, index * SLOT, 3 * SLOT, 0) for index in range(3)]
+    spread = Spread(slots_ref, table, local_sem, send_sem, recv_sem)
+    greet_neighbours([spread.sibling, spread.beside, spread.across] + spread.stations)
+    swap = pltpu.make_async_remote_copy(
+        src_ref=tokens_ref.at[1 - spread.y],
+        dst_ref=got_ref,
+        send_sem=token_sem.at[0],
+        recv_sem=token_sem.at[1],
+        device_id=spread.across,
+        device_id_type=MESH_IDS,
+    )
+    spread.begin()
+    for index in range(spread.ticks()):
+        spread.tick(index)
+        if index == SWAP_AT:
+            swap.start()
+    spread.finish()
+    swap.wait()
+
+
+def second_spread_kernel(
+    slots_ref, cotangent_ref, out_ref, up_ref, down_ref, got_ref, local_sem, send_sem, recv_sem, token_sem
+):
+    table = [(out_ref, 0, SLOT, 0)]
+    table += [(up_ref, index * SLOT, 4 * SLOT, HALF_SLOT if index % 2 else 0) for index in range(4)]
+    table += [(down_ref, index * SLOT, 4 * SLOT, HALF_SLOT if index % 2 else 0) for index in range(4)]
+    spread = Spread(slots_ref, table, local_sem, send_sem, recv_sem)
+    greet_neighbours([spread.sibling, spread.beside, spread.across] + spread.stations)
+    swap = pltpu.make_async_remote_copy(
+        src_ref=cotangent_ref.at[1 - spread.y],
+        dst_ref=got_ref,
+        send_sem=token_sem.at[0],
+        recv_sem=token_sem.at[1],
+        device_id=spread.across,
+        device_id_type=MESH_IDS,
+    )
+    spread.begin()
+    for index in range(spread.ticks()):
+        spread.tick(index)
+        if index == SWAP_AT:
+            swap.start()
+    spread.finish()
+    swap.wait()
+
+
+def whole_shape(columns):
+    return jax.ShapeDtypeStruct((4, 2, 2, 64, columns), jnp.bfloat16)
+
+
+def first_spread(slots, tokens):
+    anywhere = pl.BlockSpec(memory_space=pl.ANY)
+    whole, got = pl.pallas_call(
+        first_spread_kernel,
+        in_specs=[anywhere] * 2,
+        out_specs=[anywhere] * 2,
+        out_shape=[whole_shape(3 * D), jax.ShapeDtypeStruct(tokens.shape[1:], tokens.dtype)],
+        scratch_shapes=spread_semaphores(3) + [pltpu.SemaphoreType.DMA((2,))],
+        compiler_params=pltpu.CompilerParams(collective_id=3, has_side_effects=True),
+    )(slots, tokens)
+    return whole.reshape(D, 3 * D), got
+
+
+def second_spread(slots, cotangent):
+    anywhere = pl.BlockSpec(memory_space=pl.ANY)
+    out, up, down, got = pl.pallas_call(
+        second_spread_kernel,
+        in_specs=[anywhere] * 2,
+        out_specs=[anywhere] * 4,
+        out_shape=[
+            whole_shape(D),
+            whole_shape(FF),
+            whole_shape(FF),
+            jax.ShapeDtypeStruct(cotangent.shape[1:], cotangent.dtype),
+        ],
+        scratch_shapes=spread_semaphores(9) + [pltpu.SemaphoreType.DMA((2,))],
+        compiler_params=pltpu.CompilerParams(collective_id=4, has_side_effects=True),
+    )(slots, cotangent)
+    return out.reshape(D, D), up.reshape(D, FF), down.reshape(D, FF), got
+
+
+GROUP_SLOTS = (3, 1, 4, 4)
+LAG = 2
+
+
+def sum_kernel(
+    qkv_ref,
+    out_ref,
+    up_ref,
+    down_ref,
+    total_ref,
+    mine,
+    first,
+    second_y,
+    second_x,
+    third,
+    fourth,
+    load_sem,
+    send_sem,
+    recv_sem,
+):
+    (z, x, core, y), sibling, beside, across, stations = neighbours()
+    low_cols = pl.ds(0, HALF_SLOT)
+    high_cols = pl.ds(HALF_SLOT, HALF_SLOT)
+
+    greet_neighbours([sibling, beside, across] + stations)
+
+    def remote(source, target, stage, slot, place):
+        return pltpu.make_async_remote_copy(
+            src_ref=source,
+            dst_ref=target,
+            send_sem=send_sem.at[stage, slot],
+            recv_sem=recv_sem.at[stage, slot],
+            device_id=place,
+            device_id_type=MESH_IDS,
+        )
+
+    slot = 0
+    for ref, number in zip((qkv_ref, out_ref, up_ref, down_ref), GROUP_SLOTS):
+        for index in range(number):
+            for part in (0, 1):
+                cols = pl.ds((part * number + index) * SLOT, SLOT)
+                remote(ref.at[:, :, 1 - core, :, cols], first.at[slot, part], 0, slot, sibling).start()
+                pltpu.make_async_copy(
+                    ref.at[:, :, core, :, cols], mine.at[slot, part], load_sem.at[slot]
+                ).start()
+            slot += 1
+
+    def second_copies(slot):
+        return (
+            remote(first.at[slot, 1 - y, :, :, :, low_cols], second_y.at[slot], 1, slot, across),
+            remote(first.at[slot, :, :, 1 - x, :, high_cols], second_x.at[slot], 2, slot, beside),
+        )
+
+    def third_copies(slot):
+        return (
+            remote(second_y.at[slot, :, 1 - x], third.at[slot, :, :, low_cols], 3, slot, beside),
+            remote(second_x.at[slot, 1 - y], third.at[slot, :, :, high_cols], 4, slot, across),
+        )
+
+    def fourth_copies(slot):
+        return [
+            remote(third.at[slot, lax.rem(z + hop, 4)], fourth.at[slot, hop - 1], 4 + hop, slot, place)
+            for hop, place in zip((1, 2, 3), stations)
+        ]
+
+    def landed(ref, stage, slot):
+        pltpu.make_async_copy(ref, ref, recv_sem.at[stage, slot]).wait()
+
+    def step(index, carry):
+        @pl.when(index < SLOTS)
+        def _():
+            slot = index
+            pltpu.make_async_copy(mine.at[slot], mine.at[slot], load_sem.at[slot]).wait()
+            landed(first.at[slot], 0, slot)
+            first[slot] = first[slot] + mine[slot]
+            for copy in second_copies(slot):
+                copy.start()
+
+        @pl.when((index >= LAG) & (index < SLOTS + LAG))
+        def _():
+            slot = index - LAG
+            landed(second_y.at[slot], 1, slot)
+            second_y[slot] = second_y[slot] + first[slot, y, :, :, :, :HALF_SLOT]
+            landed(second_x.at[slot], 2, slot)
+            second_x[slot] = second_x[slot] + first[slot, :, :, x, :, HALF_SLOT:]
+            for copy in third_copies(slot):
+                copy.start()
+
+        @pl.when((index >= 2 * LAG) & (index < SLOTS + 2 * LAG))
+        def _():
+            slot = index - 2 * LAG
+            landed(third.at[slot, :, :, low_cols], 3, slot)
+            landed(third.at[slot, :, :, high_cols], 4, slot)
+            third[slot, :, :, :HALF_SLOT] = third[slot, :, :, :HALF_SLOT] + second_y[slot, :, x]
+            third[slot, :, :, HALF_SLOT:] = third[slot, :, :, HALF_SLOT:] + second_x[slot, y]
+            for copy in fourth_copies(slot):
+                copy.start()
+
+        @pl.when(index >= 3 * LAG)
+        def _():
+            slot = index - 3 * LAG
+            total = third[slot, z].astype(jnp.float32)
+            for hop in (1, 2, 3):
+                landed(fourth.at[slot, hop - 1], 4 + hop, slot)
+                total = total + fourth[slot, hop - 1].astype(jnp.float32)
+            total_ref[slot] = total
+
+        return carry
+
+    lax.fori_loop(0, SLOTS + 3 * LAG, step, 0)
+
+    def sent(slot, carry):
+        pltpu.make_async_copy(mine.at[slot], mine.at[slot], send_sem.at[0, slot]).wait()
+        for copy in second_copies(slot) + third_copies(slot) + tuple(fourth_copies(slot)):
+            copy.wait_send()
+        return carry
+
+    lax.fori_loop(0, SLOTS, sent, 0)
+
+
+def sum_over_devices(grads):
+    rows = 64
+    refs = [grad.reshape(4, 2, 2, rows, grad.shape[-1]) for grad in grads]
+    part = (SLOTS, 2, 4, 2, rows, SLOT)
+    anywhere = pl.BlockSpec(memory_space=pl.ANY)
+    return pl.pallas_call(
+        sum_kernel,
+        in_specs=[anywhere] * 4,
+        out_specs=pl.BlockSpec(memory_space=pltpu.VMEM),
+        out_shape=jax.ShapeDtypeStruct((SLOTS, rows, SLOT), jnp.float32),
+        scratch_shapes=[
+            pltpu.VMEM(part, jnp.bfloat16),
+            pltpu.VMEM(part, jnp.bfloat16),
+            pltpu.VMEM((SLOTS, 4, 2, rows, HALF_SLOT), jnp.bfloat16),
+            pltpu.VMEM((SLOTS, 2, 4, rows, HALF_SLOT), jnp.bfloat16),
+            pltpu.VMEM((SLOTS, 4, rows, SLOT), jnp.bfloat16),
+            pltpu.VMEM((SLOTS, 3, rows, SLOT), jnp.bfloat16),
+            pltpu.SemaphoreType.DMA((SLOTS,)),
+            pltpu.SemaphoreType.DMA((8, SLOTS)),
+            pltpu.SemaphoreType.DMA((8, SLOTS)),
+        ],
+        compiler_params=pltpu.CompilerParams(
+            collective_id=2, has_side_effects=True, vmem_limit_bytes=VMEM_LIMIT
+        ),
+        cost_estimate=pl.CostEstimate(flops=0, bytes_accessed=300 * 1024 * 1024, transcendentals=0),
+    )(*refs)
 
 
 def narrow(rows):
@@ -895,21 +1281,28 @@
     return lax.dot_general(
         left, right, (((left_dim,), (right_dim,)), ((), ())), preferred_element_type=jnp.float32
     )
+
+
+def in_order(rank, own, got):
+    return jnp.where(rank == 0, jnp.concatenate([own, got]), jnp.concatenate([got, own]))
 
 
 def swap_halves(mine, rank):
     rows = mine.shape[0] // 2
     kept = lax.dynamic_slice_in_dim(mine, rank * rows, rows, 0)
     sent = lax.dynamic_slice_in_dim(mine, (1 - rank) * rows, rows, 0)
-    got = lax.ppermute(sent, "tensor", SWAP)
+    got = lax.ppermute(sent, "tensor", [(0, 1), (1, 0)])
     return jnp.where(rank == 0, jnp.stack([kept, got]), jnp.stack([got, kept]))
 
 
-def join_halves(pair, rank):
-    kept = lax.dynamic_index_in_dim(pair, rank, 0, keepdims=False)
-    sent = lax.dynamic_index_in_dim(pair, 1 - rank, 0, keepdims=False)
-    got = lax.ppermute(sent, "tensor", SWAP)
-    return jnp.where(rank == 0, jnp.concatenate([kept, got]), jnp.concatenate([got, kept]))
+def by_pairs(rows):
+    count, height, width = rows.shape
+    return jnp.transpose(rows.reshape(count, height, width // PAIR, PAIR), (1, 2, 0, 3)).reshape(height, -1)
+
+
+def from_pairs(rows):
+    height = rows.shape[0]
+    return jnp.transpose(rows.reshape(height, -1, 3, PAIR), (2, 0, 1, 3)).reshape(3, height, -1)
 
 
 def sequence_step(
@@ -928,104 +1321,74 @@
     m_vec,
 ):
     rank = lax.axis_index("tensor")
-    parts = lax.axis_size("tensor")
-    width = D // parts
-    hidden = FF // parts
-    shard_rows = w_qkv.shape[1]
     slopes = jnp.exp2(-8.0 * jnp.arange(1, H + 1, dtype=jnp.float32) / H)
-
-    def spread(rows):
-        whole = lax.all_gather(rows, BOTH, axis=0, tiled=True)
-        return whole.reshape(parts, D, rows.shape[1])
-
-    def collect(grads):
-        return lax.psum_scatter(
-            grads.reshape(parts * D, -1), BOTH, scatter_dimension=0, tiled=True
-        ).astype(jnp.float32)
-
-    full_qkv = spread(narrow(jnp.swapaxes(w_qkv, 0, 1)).reshape(shard_rows, 3 * width))
-    token_rows = join_halves(tokens, rank).astype(jnp.float32)
-    full_out = spread(narrow(w_out.T))
-    full_up = spread(narrow(w_up))
-    full_down = spread(narrow(w_down.T))
-    cotangent_low = join_halves(cotangent, rank)
+    starts = lax.dynamic_slice_in_dim(piece_starts[:, 0], rank, 1, 0)[0]
+    own_tokens = lax.dynamic_index_in_dim(tokens, rank, 0, keepdims=False)
+    own_cotangent = lax.dynamic_index_in_dim(cotangent, rank, 0, keepdims=False)
+
+    full_qkv, other_tokens = first_spread(by_slots(by_pairs(narrow(w_qkv))), tokens)
+    token_rows = in_order(rank, own_tokens, other_tokens).astype(jnp.float32)
+    normed_one = narrow(layer_norm(token_rows, vectors[0], vectors[1]))
+    shifts = by_pairs(jnp.stack([vectors[2], jnp.zeros((D,), jnp.float32), vectors[3]])[:, None])
+    packed = narrow(contract(normed_one, full_qkv, 1, 0) + shifts)
+    context, exps, stats = attention_forward(starts, slopes, packed)
+
+    later_slots = jnp.concatenate(
+        [narrow(w_out).T[None], by_slots(narrow(w_up)), by_slots(narrow(w_down).T)]
+    )
+    full_out, full_up, full_down, other_cotangent = second_spread(later_slots, cotangent)
+    cotangent_low = in_order(rank, own_cotangent, other_cotangent)
     cotangent_rows = cotangent_low.astype(jnp.float32)
-    starts = lax.dynamic_slice_in_dim(piece_starts[:, 0], rank, 1, 0)[0]
-
-    normed_one = narrow(layer_norm(token_rows, vectors[0], vectors[1]))
-    shifts = jnp.stack([vectors[2], jnp.zeros((D,), jnp.float32), vectors[3]])
-    shifts = jnp.swapaxes(shifts.reshape(3, parts, width), 0, 1).reshape(parts, 3 * width, 1)
-    packed = jnp.stack(
-        [narrow(contract(full_qkv[part], normed_one, 0, 1) + shifts[part]) for part in range(parts)]
-    )
-    packed = packed.reshape(parts, 3, width // HD, HD, LEN)
-    context, exps, stats = attention_forward(starts, slopes, packed)
-    context_rows = context.reshape(parts, width, LEN)
-    attended = sum(contract(context_rows[part], full_out[part], 0, 1) for part in range(parts))
-    middle = token_rows + attended + vectors[4]
+
+    middle = token_rows + contract(context, full_out, 1, 1) + vectors[4]
     normed_two = narrow(layer_norm(middle, vectors[5], vectors[6]))
-    up_shift = vectors[7:11].reshape(parts, hidden)
-    before = [contract(normed_two, full_up[part], 1, 0) + up_shift[part] for part in range(parts)]
-    activated = [narrow(gelu_tanh(rows)) for rows in before]
-    expanded = sum(contract(activated[part], full_down[part], 1, 1) for part in range(parts))
-    block_rows = narrow(middle + expanded + vectors[11])
-
-    grad_down = jnp.stack([narrow(contract(cotangent_low, rows, 0, 0)) for rows in activated])
-    grad_before = []
-    for part in range(parts):
-        grad_activated = contract(cotangent_low, full_down[part], 1, 0)
-        gelu_pull = jax.vjp(gelu_tanh, before[part])[1]
-        grad_before.append(narrow(gelu_pull(grad_activated)[0]))
-    grad_up = jnp.stack([narrow(contract(normed_two, rows, 0, 0)) for rows in grad_before])
-    grad_down_shard = collect(grad_down)
-    grad_up_shard = collect(grad_up)
-    grad_normed_two = sum(contract(grad_before[part], full_up[part], 1, 1) for part in range(parts))
+    before = contract(normed_two, full_up, 1, 0) + vectors[7:11].reshape(FF)
+    activated = narrow(gelu_tanh(before))
+    block_rows = narrow(middle + contract(activated, full_down, 1, 1) + vectors[11])
+    output_pair = swap_halves(block_rows, rank)
+
+    grad_down = narrow(contract(cotangent_low, activated, 0, 0))
+    gelu_pull = jax.vjp(gelu_tanh, before)[1]
+    grad_before = narrow(gelu_pull(contract(cotangent_low, full_down, 1, 0))[0])
+    grad_up = narrow(contract(normed_two, grad_before, 0, 0))
     second_pull = jax.vjp(layer_norm, middle, vectors[5], vectors[6])[1]
-    middle_from_norm, gain_two_grad, shift_two_grad = second_pull(grad_normed_two)
+    middle_from_norm, gain_two_grad, shift_two_grad = second_pull(contract(grad_before, full_up, 1, 1))
     grad_middle = cotangent_rows + middle_from_norm
     grad_middle_low = narrow(grad_middle)
-    grad_out = jnp.stack(
-        [narrow(contract(grad_middle_low, context_rows[part], 0, 1)) for part in range(parts)]
-    )
-    grad_out_shard = collect(grad_out)
-    grad_context = jnp.stack(
-        [narrow(contract(full_out[part], grad_middle_low, 0, 1)) for part in range(parts)]
-    ).reshape(H, HD, LEN)
-    grad_parts = attention_backward(packed, context, grad_context, exps, stats)
-    grad_packed = jnp.stack([rows.reshape(parts, width, LEN) for rows in grad_parts], axis=1)
-    grad_packed = grad_packed.reshape(parts, 3 * width, LEN)
-    grad_qkv = jnp.stack([narrow(contract(normed_one, grad_packed[part], 0, 1)) for part in range(parts)])
-    grad_qkv_shard = collect(grad_qkv)
-    grad_normed_one = sum(contract(grad_packed[part], full_qkv[part], 0, 1) for part in range(parts))
+    grad_out = narrow(contract(grad_middle_low, context, 0, 0))
+    grad_context = narrow(contract(grad_middle_low, full_out, 1, 0))
+    grad_packed = attention_backward(packed, context, grad_context, exps, stats)
+    grad_qkv = narrow(contract(normed_one, grad_packed, 0, 0))
+    sums = sum_over_devices((grad_qkv, grad_out, grad_up, grad_down))
     first_pull = jax.vjp(layer_norm, token_rows, vectors[0], vectors[1])[1]
-    token_from_norm, gain_one_grad, shift_one_grad = first_pull(grad_normed_one)
+    token_from_norm, gain_one_grad, shift_one_grad = first_pull(contract(grad_packed, full_qkv, 1, 1))
     grad_token_rows = grad_middle + token_from_norm
-    output_pair = swap_halves(block_rows, rank)
     token_pair = swap_halves(narrow(grad_token_rows), rank).astype(jnp.float32)
 
-    row_sums = [
-        jnp.sum(rows.astype(jnp.float32), axis=2).reshape(D) for rows in (grad_parts[0], grad_parts[2])
-    ]
-    up_bias = jnp.concatenate([jnp.sum(rows, axis=0, dtype=jnp.float32) for rows in grad_before])
+    packed_sums = from_pairs(jnp.sum(grad_packed, axis=0, dtype=jnp.float32)[None])[:, 0]
     vector_total = jnp.concatenate(
         [
             jnp.stack(
                 [
                     gain_one_grad,
                     shift_one_grad,
-                    row_sums[0],
-                    row_sums[1],
+                    packed_sums[0],
+                    packed_sums[2],
                     jnp.sum(grad_middle, axis=0),
                     gain_two_grad,
                     shift_two_grad,
                 ]
             ),
-            up_bias.reshape(4, D),
+            jnp.sum(grad_before, axis=0, dtype=jnp.float32).reshape(4, D),
             jnp.sum(cotangent_rows, axis=0)[None],
         ]
     )
-    grad_qkv_shard = jnp.swapaxes(grad_qkv_shard.reshape(shard_rows, 3, width), 0, 1)
-    shards = (grad_qkv_shard, grad_out_shard.T, grad_up_shard, grad_down_shard.T)
+    shards = (
+        from_pairs(from_slots(sums[0:3])),
+        sums[3].T,
+        from_slots(sums[4:8]),
+        from_slots(sums[8:12]).T,
+    )
     outputs = muon_step(shards, vector_total, w_qkv, w_out, w_up, w_down, vectors, m_qkv, m_out, m_up, m_down, m_vec)
     return (output_pair, token_pair) + outputs
 

time: 1070 us -> 755 us (0.71)
  waiting for transfers between devices: 537 us -> 0.01 us
  Pallas kernels: 216 us -> 506 us
  other arithmetic: 78.8 us -> 52.4 us
  local copies, waits for them, and re-layouts: 38.3 us -> 23.3 us
  between operations: 15.5 us -> 1.78 us
  matrix products: 172 us -> 159 us
    reduce_scatter x4 -> x0, waiting for transfers between devices: 340 us -> none  [collect(): lax.psum_scatter(grads.reshape(parts * D, -1), BOTH, scatter_dimension=0,...]
    pallas_call x2 -> x5, Pallas kernels: 81.9 us -> 384 us  [the longest x1 129 us: sum_over_devices(): pl.pallas_call(sum_kernel, in_specs=[anywhere] * 4, out_specs=pl.BlockSpe...]
    all_gather x4 -> x0, waiting for transfers between devices: 156 us -> none  [spread(): whole = lax.all_gather(rows, BOTH, axis=0, tiled=True)]
    ppermute x4 -> x2, waiting for transfers between devices: 40.9 us -> 0.01 us  [swap_halves(): got = lax.ppermute(sent, 'tensor', [(0, 1), (1, 0)])]
    another operation x8 -> x0, other arithmetic: 31.1 us -> none  [the longest x1 7.5 us: sequence_step(): jnp.stack([narrow(contract(cotangent_low, rows, 0, 0)) for rows in activa...]
    dot_general x24 -> x12, matrix products: 172 us -> 159 us  [contract(): lax.dot_general(left, right, (((left_dim,), (right_dim,)), ((), ())), pre...]
    pallas_call x1, Pallas kernels: 134 us -> 123 us  [muon_call(): pl.pallas_call(muon_kernel, in_specs=[vmem, vmem], out_specs=[vmem, vmem]...]
  transfers between devices with their start and end apart: 12 -> 2, of which waited for: 8 -> 0; matrix products, arithmetic and copies ran while one was open for 20% -> 14% of each run, Pallas kernels for 8% -> 34%
where the time goes in v3:
time: 755 us; the launch traced here: 744 us
  Pallas kernels  506 us (67%)
  matrix products  159 us (21%)
  other arithmetic  52.4 us (7%)
  local copies, waits for them, and re-layouts  23.3 us (3%)
    dot_general x12, matrix products, contract(): lax.dot_general(left, right, (((left_dim,), (right_dim,)), ((), ())), pre...  159 us
    pallas_call x1, Pallas kernels, sum_over_devices(): pl.pallas_call(sum_kernel, in_specs=[anywhere] * 4, out_specs=pl.BlockSpe...  129 us
    pallas_call x1, Pallas kernels, muon_call(): pl.pallas_call(muon_kernel, in_specs=[vmem, vmem], out_specs=[vmem, vmem]...  123 us
    pallas_call x1, Pallas kernels, second_spread(): pl.pallas_call(second_spread_kernel, in_specs=[anywhere] * 2, out_specs=[...  119 us
    pallas_call x1, Pallas kernels, first_spread(): pl.pallas_call(first_spread_kernel, in_specs=[anywhere] * 2, out_specs=[a...  57.3 us
    pallas_call x1, Pallas kernels, attention_forward(): pl.pallas_call(attend_fwd_kernel, grid=(PAIRS,), in_specs=[SCALARS, SCALA...  46.2 us
    pallas_call x1, Pallas kernels, attention_backward(): pl.pallas_call(attend_bwd_kernel, grid=(PAIRS,), in_specs=[PACKED_COLS, P...  33 us
  transfers between devices with their start and end apart: 2, of which 0 were waited for; matrix products, arithmetic and copies ran while one was open for 14% of the time, Pallas kernels for 34%

profile of v3, /device:TPU:9, one launch (start us, length us, event | category | flops | bytes accessed | tf_op | source)
XLA Modules:
  0.0 743.9 jit_solution(11557336806157419739)
XLA Ops:
  0.7 0.5 multiply_exponential_fusion.slopes_ref
  1.2 0.9 slice_bitcast_fusion.4
  2.2 1.6 fusion.36
  4.0 0.9 convert_bitcast_fusion.3
  4.9 1.0 convert_element_type.107
  6.4 0.7 copy.68
  7.1 1.1 convert_element_type.112
  8.2 1.8 convert_element_type.113
  10.4 2.5 dynamic-slice_bitcast_fusion.1
  12.9 57.3 %shard_map.260 = (bf16[4,2,2,64,3072]{4,3,2,1,0:T(8,128)(2,1)}, bf16[512,1024]{1,0:T(8,128)(2,1)}) custom-call(bf16[3,64,512]{2,1,0:T(8,128)(2,1)} %bitcast.168, bf16[2,512,1024]{2,1,0:T(8,128)(2,1)} %tokens_ref.1), custom_call_target="tpu_custom_call" | custom-call | tf_op jit(solution)/shard_map/pallas_call | solution.py:1099
  70.2 2.3 convert_reduce_fusion.2
  72.6 2.4 fusion.16
  75.0 0.9 pad_maximum_fusion.1.slots_ref
  75.9 118.7 %shard_map.262 = (bf16[4,2,2,64,1024]{4,3,2,1,0:T(8,128)(2,1)}, bf16[4,2,2,64,4096]{4,3,2,1,0:T(8,128)(2,1)}, bf16[4,2,2,64,4096]{4,3,2,1,0:T(8,128)(2,1)}, bf16[512,1024]{1,0:T(8,128)(2,1)}) custom-call(bf16[9,64,512]{2,1,0:T(8,128)(2,1)} %pad_maximum_fusion.1.slots_ref, bf16[2,512,1024]{2,1,0:T(8,128)(2,1)} %cotangent_ref.1), custom_call_target="tpu_custom_call" | custom-call | tf_op jit(solution)/shard_map/pallas_call | solution.py:1112
  194.6 13.5 %add_convert_fusion.packed_ref = bf16[1024,3072]{1,0:T(8,128)(2,1)} fusion(f32[3072]{0:T(1024)S(1)} %add.149, bf16[1024,3072]{1,0:T(8,128)(2,1)} %bitcast.196, f32[1024]{0:T(1024)S(1)} %bitcast.186, f32[1024]{0:T(1024)S(1)} %bitcast.172, f32[1024]{0:T(1024)S(1)} %fusion.22, f32[1024]{0:T(1024)S(1)} %broadcast_multiply_fusion.1, ...), kind=kOutput, calls=%fused_computation.12 | convolution fusion | flops 6464471040 | bytes 14708737 | tf_op jit(solution)/shard_map/dot_general | solution.py:1281
  208.1 46.2 %shard_map.261 = (bf16[1024,1024]{1,0:T(8,128)(2,1)}, bf16[16,1024,1024]{2,1,0:T(8,128)(2,1)}, f32[8,2,1024]{2,1,0:T(2,128)}) custom-call(s32[2]{0:T(128)} %fusion.24.starts_ref, f32[16]{0:T(128)} %multiply_exponential_fusion.slopes_ref, bf16[1024,3072]{1,0:T(8,128)(2,1)} %add_convert_fusion.packed_ref), custom_call_target="tpu_custom_call" | custom-call | flops 17179869184 | bytes 46137344 | tf_op jit(solution)/shard_map/pallas_call | solution.py:524
  254.3 5.5 fusion.37
  259.9 0.6 multiply_reduce_fusion.2
  260.5 15.9 %fusion.28 = f32[1024,4096]{1,0:T(8,128)} fusion(bf16[1024,4096]{1,0:T(8,128)(2,1)} %bitcast.194, f32[1024,1024]{1,0:T(8,128)S(1)} %get-tuple-element.79, f32[1024]{0:T(1024)S(1)} %bitcast.188, f32[1024]{0:T(1024)S(1)} %bitcast.179, f32[1024]{0:T(1024)S(1)} %fusion.23, f32[1024]{0:T(1024)S(1)} %broadcast_multiply_fusion), kind=kOutput, calls=%fused_computation.112 | convolution fusion | flops 8595177472 | bytes 29376512 | tf_op jit(solution)/shard_map/dot_general | solution.py:1281
  276.4 27.6 %convert_reduce_fusion = (f32[4096]{0:T(1024)}, bf16[1024,4096]{1,0:T(8,128)(2,1)}) fusion(f32[1024,4096]{1,0:T(8,128)} %fusion.28, f32[4096]{0:T(1024)S(1)} %bitcast.183, bf16[1024,4096]{1,0:T(8,128)(2,1)} %bitcast.192, bf16[512,1024]{1,0:T(8,128)(2,1)S(1)} %copy-done.18, bf16[512,1024]{1,0:T(8,128)(2,1)S(1)} %copy-done.9, pred[]{:T(512)S(6)} %eq.2), kind=kOutput, calls=%fused_computation.9 | convolution fusion | flops 8695836672 | bytes 35684352 | tf_op jit(solution)/shard_map/dot_general | solution.py:1281
  303.9 15.6 %multiply_reduce_fusion = (f32[1024]{0:T(1024)}, f32[1024]{0:T(1024)S(1)}, f32[1024]{0:T(1024)}, f32[1024,1024]{1,0:T(8,128)S(1)}) fusion(f32[1024,1024]{1,0:T(8,128)S(1)} %get-tuple-element.79, f32[1024]{0:T(1024)S(1)} %fusion.23, f32[1024]{0:T(1024)S(1)} %broadcast_multiply_fusion, f32[1024]{0:T(1024)S(1)} %bitcast.180, ...), kind=kOutput, calls=%fused_computation.35 | convolution fusion | flops 8598320128 | bytes 25190400 | tf_op jit(solution)/shard_map/dot_general | solution.py:1281
  319.5 1.7 fusion.35
  321.3 3.9 fusion.31
  325.3 3.7 convolution_convert_fusion.4.grad_ref
  329.0 33.0 %shard_map.263 = bf16[1024,3072]{1,0:T(8,128)(2,1)} custom-call(bf16[1024,3072]{1,0:T(8,128)(2,1)} %add_convert_fusion.packed_ref, bf16[1024,1024]{1,0:T(8,128)(2,1)} %get-tuple-element.30.ctx_ref, bf16[1024,1024]{1,0:T(8,128)(2,1)} %convolution_convert_fusion.4.grad_ref, bf16[16,1024,1024]{2,1,0:T(8,128)(2,1)} %get-tuple-element.35.exps_ref, ...), custom_call_target="tpu_custom_call" | custom-call | flops 34359738368 | bytes 52428800 | tf_op jit(solution)/shard_map/pallas_call | solution.py:543
  361.9 11.4 %fusion.30 = (f32[1024]{0:T(1024)S(1)}, f32[1024]{0:T(1024)S(1)}, f32[1024,1024]{1,0:T(8,128)S(1)}) fusion(f32[1024]{0:T(1024)S(1)} %bitcast.173, f32[1024]{0:T(1024)S(1)} %copy-done.28, bf16[512,1024]{1,0:T(8,128)(2,1)S(1)} %get-tuple-element.85, bf16[512,1024]{1,0:T(8,128)(2,1)S(1)} %copy-done.2, pred[]{:T(512)S(6)} %eq.2, ...), kind=kOutput, calls=%fused_computation.114 | convolution fusion | flops 6458177536 | bytes 18890752 | tf_op jit(solution)/shard_map/dot_general | solution.py:1281
  373.4 4.0 fusion.15
  377.4 4.3 add_convert_fusion.1
  381.7 2.7 dynamic-slice_bitcast_fusion
  384.4 1.8 collective-permute-start.1
  386.2 18.5 %add_convert_fusion.2 = bf16[1024,1024]{1,0:T(8,128)(2,1)} fusion(f32[1024,1024]{1,0:T(8,128)} %copy-done.3, f32[1024]{0:T(1024)S(1)} %bitcast.190, bf16[1024,4096]{1,0:T(8,128)(2,1)} %bitcast.193, f32[1024,4096]{1,0:T(8,128)} %fusion.28, f32[4096]{0:T(1024)S(1)} %bitcast.184), kind=kOutput, calls=%fused_computation.38 | convolution fusion | flops 8635023360 | bytes 31477760 | tf_op jit(solution)/shard_map/dot_general | solution.py:1281
  404.6 3.2 dynamic-slice_bitcast_fusion.2
  407.9 15.8 %convolution_convert_fusion = bf16[1024,4096]{1,0:T(8,128)(2,1)} fusion(bf16[512,1024]{1,0:T(8,128)(2,1)S(1)} %copy-done.20, bf16[512,1024]{1,0:T(8,128)(2,1)S(1)} %copy-done.10, pred[]{:T(512)S(6)} %eq.2, f32[1024,4096]{1,0:T(8,128)} %fusion.28, f32[4096]{0:T(1024)S(1)} %bitcast.185), kind=kOutput, calls=%fused_computation.13 | convolution fusion | flops 8645509120 | bytes 27279360 | tf_op jit(solution)/shard_map/dot_general | solution.py:1281
  423.7 15.2 %convolution_convert_fusion.1 = bf16[1024,4096]{1,0:T(8,128)(2,1)} fusion(bf16[1024,4096]{1,0:T(8,128)(2,1)} %get-tuple-element.83, f32[1024,1024]{1,0:T(8,128)S(1)} %copy-done.4, f32[1024]{0:T(1024)S(1)} %bitcast.189, f32[1024]{0:T(1024)S(1)} %bitcast.182, f32[1024]{0:T(1024)S(1)} %fusion.23, f32[1024]{0:T(1024)S(1)} %broadcast_multiply_fusion), kind=kOutput, calls=%fused_computation.14 | convolution fusion | flops 8599371776 | bytes 20987904 | tf_op jit(solution)/shard_map/dot_general | solution.py:1281
  439.0 3.7 convolution_convert_fusion.3
  442.7 3.7 convert_reduce_fusion.1
  446.4 12.2 %convolution_convert_fusion.2 = bf16[1024,3072]{1,0:T(8,128)(2,1)} fusion(bf16[1024,3072]{1,0:T(8,128)(2,1)} %shard_map.263, f32[1024]{0:T(1024)S(1)} %bitcast.187, f32[1024]{0:T(1024)S(1)} %bitcast.176, f32[1024]{0:T(1024)S(1)} %copy-done.33, f32[1024]{0:T(1024)S(1)} %copy-done.28, bf16[512,1024]{1,0:T(8,128)(2,1)S(1)} %copy-done.2, ...), kind=kOutput, calls=%fused_computation.24 | convolution fusion | flops 6461325312 | bytes 14696449 | tf_op jit(solution)/shard_map/dot_general | solution.py:1281
  458.6 128.5 %shard_map.264 = f32[12,64,512]{2,1,0:T(8,128)} custom-call(bf16[4,2,2,64,3072]{4,3,2,1,0:T(8,128)(2,1)} %bitcast.152, bf16[4,2,2,64,1024]{4,3,2,1,0:T(8,128)(2,1)} %bitcast.153, bf16[4,2,2,64,4096]{4,3,2,1,0:T(8,128)(2,1)} %bitcast.151, bf16[4,2,2,64,4096]{4,3,2,1,0:T(8,128)(2,1)} %bitcast.150), custom_call_target="tpu_custom_call" | custom-call | bytes 314572800 | tf_op jit(solution)/shard_map/pallas_call | solution.py:1253
  587.1 1.0 slice_bitcast_fusion.2
  588.2 1.3 slice_bitcast_fusion
  589.5 0.6 constant_dynamic-update-slice_fusion.8
  590.1 0.6 constant_dynamic-update-slice_fusion.7
  590.7 0.6 constant_dynamic-update-slice_fusion.6
  591.3 0.6 constant_dynamic-update-slice_fusion.5
  591.9 1.7 convert_bitcast_fusion.2
  594.6 2.2 fusion.33
  596.9 2.0 fusion.34
  598.8 0.6 constant_dynamic-update-slice_fusion.4
  599.4 0.6 constant_dynamic-update-slice_fusion.3
  600.0 0.6 constant_dynamic-update-slice_fusion.2
  600.6 1.3 constant_dynamic-update-slice_fusion.1
  602.0 0.6 constant_dynamic-update-slice_fusion.vec_ref
  602.5 1.8 fusion.32
  604.4 1.0 pad_maximum_fusion.moments_ref
  605.4 122.6 %shard_map.265 = (bf16[12,64,512]{2,1,0:T(8,128)(2,1)}, f32[12,8,128]{2,1,0:T(8,128)}) custom-call(bf16[12,64,512]{2,1,0:T(8,128)(2,1)} %pad_maximum_fusion.moments_ref, f32[12,8,128]{2,1,0:T(8,128)} %constant_dynamic-update-slice_fusion.vec_ref), custom_call_target="tpu_custom_call" | custom-call | flops 25769803776 | bytes 4194304 | tf_op jit(solution)/shard_map/pallas_call | solution.py:827
  728.0 1.6 bitcast_subtract_fusion.1
  729.6 1.2 convert_bitcast_fusion
  730.8 0.8 pad.26
  731.8 0.7 multiply_subtract_fusion.1
  732.6 0.9 sub.54
  733.5 1.7 multiply_subtract_fusion
  735.2 0.8 bitcast_subtract_fusion
  736.1 3.3 maximum_select_fusion.1
  739.4 4.1 fusion.19
  (127 shorter events, 2.7 us)
Async XLA Ops:
  0.7 9.3 %copy-start = (s32[2,1,2]{2,1,0:T(1,128)S(1)}, s32[2,1,2]{2,1,0:T(1,128)}, u32[]{:S(2)}) copy-start(s32[2,1,2]{2,1,0:T(1,128)} %param.15) | copy-start | bytes 52
  0.7 9.8 %copy-start.7 = (bf16[2,512,1024]{2,1,0:T(8,128)(2,1)S(1)}, bf16[2,512,1024]{2,1,0:T(8,128)(2,1)}, u32[]{:S(2)}) copy-start(bf16[2,512,1024]{2,1,0:T(8,128)(2,1)} %tokens_ref.1) | copy-start | bytes 6291460
  3.8 190.8 %copy-start.30 = (f32[1,1024]{1,0:T(1,128)}, f32[1,1024]{1,0:T(1,128)S(1)}, u32[]{:S(2)}) copy-start(f32[1,1024]{1,0:T(1,128)S(1)} %get-tuple-element.76) | copy-start | bytes 12292
  3.8 190.8 %copy-start.36 = (f32[1,1024]{1,0:T(1,128)}, f32[1,1024]{1,0:T(1,128)S(1)}, u32[]{:S(2)}) copy-start(f32[1,1024]{1,0:T(1,128)S(1)} %get-tuple-element.75) | copy-start | bytes 12292
  3.8 256.7 %copy-start.38 = (f32[1,1024]{1,0:T(1,128)}, f32[1,1024]{1,0:T(1,128)S(1)}, u32[]{:S(2)}) copy-start(f32[1,1024]{1,0:T(1,128)S(1)} %get-tuple-element.71) | copy-start | bytes 12292
  12.9 62.0 %copy-start.17 = (bf16[2048,64]{0,1:T(8,128)(2,1)S(1)}, bf16[2048,64]{0,1:T(8,128)(2,1)}, u32[]{:S(2)}) copy-start(bf16[2048,64]{0,1:T(8,128)(2,1)} %convert_element_type.113) | copy-start | bytes 786436
  70.2 124.4 %copy-start.2 = (bf16[512,1024]{1,0:T(8,128)(2,1)S(1)}, bf16[512,1024]{1,0:T(8,128)(2,1)}, u32[]{:S(2)}) copy-start(bf16[512,1024]{1,0:T(8,128)(2,1)} %get-tuple-element.28) | copy-start | bytes 3145732
  72.6 135.6 %copy-start.27 = (f32[1024]{0:T(1024)}, f32[1024]{0:T(1024)S(1)}, u32[]{:S(2)}) copy-start(f32[1024]{0:T(1024)S(1)} %broadcast_multiply_fusion.1) | copy-start | bytes 12292
  74.9 133.2 %copy-start.34 = (f32[1024]{0:T(1024)}, f32[1024]{0:T(1024)S(1)}, u32[]{:S(2)}) copy-start(f32[1024]{0:T(1024)S(1)} %fusion.16) | copy-start | bytes 12292
  75.0 133.2 %copy-start.32 = (f32[1024]{0:T(1024)}, f32[1024]{0:T(1024)S(1)}, u32[]{:S(2)}) copy-start(f32[1024]{0:T(1024)S(1)} %fusion.22) | copy-start | bytes 12292
  208.1 46.2 %copy-start.43 = (bf16[4,2,2,64,1024]{4,3,2,1,0:T(8,128)(2,1)S(1)}, bf16[4,2,2,64,1024]{4,3,2,1,0:T(8,128)(2,1)}, u32[]{:S(2)}) copy-start(bf16[4,2,2,64,1024]{4,3,2,1,0:T(8,128)(2,1)} %get-tuple-element.31) | copy-start | bytes 6291460
  259.9 59.6 %copy-start.3 = (f32[1024,1024]{1,0:T(8,128)}, f32[1024,1024]{1,0:T(8,128)S(1)}, u32[]{:S(2)}) copy-start(f32[1024,1024]{1,0:T(8,128)S(1)} %get-tuple-element.79) | copy-start | bytes 12582916
  260.5 15.9 %copy-start.9 = (bf16[512,1024]{1,0:T(8,128)(2,1)S(1)}, bf16[512,1024]{1,0:T(8,128)(2,1)}, u32[]{:S(2)}) copy-start(bf16[512,1024]{1,0:T(8,128)(2,1)} %get-tuple-element.84) | copy-start | bytes 3145732
  260.5 15.9 %copy-start.18 = (bf16[512,1024]{1,0:T(8,128)(2,1)S(1)}, bf16[512,1024]{1,0:T(8,128)(2,1)}, u32[]{:S(2)}) copy-start(bf16[512,1024]{1,0:T(8,128)(2,1)} %get-tuple-element.34) | copy-start | bytes 3145732
  319.5 1.8 copy-start.19
  321.3 4.0 copy-start.44
  325.2 52.2 %copy-start.5 = (f32[1024,1024]{1,0:T(8,128)}, f32[1024,1024]{1,0:T(8,128)S(1)}, u32[]{:S(2)}) copy-start(f32[1024,1024]{1,0:T(8,128)S(1)} %get-tuple-element.49) | copy-start | bytes 12582916
  328.9 33.0 %copy-start.28 = (f32[1024]{0:T(1024)S(1)}, f32[1024]{0:T(1024)}, u32[]{:S(2)}) copy-start(f32[1024]{0:T(1024)} %copy-done.27) | copy-start | bytes 12292
  328.9 33.0 %copy-start.31 = (f32[1,1024]{1,0:T(1,128)S(1)}, f32[1,1024]{1,0:T(1,128)}, u32[]{:S(2)}) copy-start(f32[1,1024]{1,0:T(1,128)} %copy-done.30) | copy-start | bytes 12292
  361.9 11.4 %copy-start.35 = (f32[1024]{0:T(1024)S(1)}, f32[1024]{0:T(1024)}, u32[]{:S(2)}) copy-start(f32[1024]{0:T(1024)} %copy-done.34) | copy-start | bytes 12292
  361.9 11.5 %copy-start.33 = (f32[1024]{0:T(1024)S(1)}, f32[1024]{0:T(1024)}, u32[]{:S(2)}) copy-start(f32[1024]{0:T(1024)} %copy-done.32) | copy-start | bytes 12292
  381.7 4.5 copy-start.40
  384.4 355.0 %collective-permute-start.1 = (bf16[512,1024]{1,0:T(8,128)(2,1)}, bf16[512,1024]{1,0:T(8,128)(2,1)}, u32[]{:S(2)}, u32[]{:S(2)}) collective-permute-start(bf16[512,1024]{1,0:T(8,128)(2,1)} %get-tuple-element.63), channel_id=1, source_target_pairs={{0,1},{1,0},{2,3},{3,2},{4,5},{5,4},{6,7},{7,6},{8,9},{9,8},{10,11... | collective-permute-start | bytes 3145736 | tf_op jit(solution)/shard_map/ppermute | solution.py:1294
  404.6 3.2 copy-start.10
  404.6 3.2 copy-start.20
  407.8 15.9 %copy-start.4 = (f32[1024,1024]{1,0:T(8,128)S(1)}, f32[1024,1024]{1,0:T(8,128)}, u32[]{:S(2)}) copy-start(f32[1024,1024]{1,0:T(8,128)} %copy-done.3) | copy-start | bytes 12582916
  407.8 15.9 %copy-start.39 = (f32[1,1024]{1,0:T(1,128)S(1)}, f32[1,1024]{1,0:T(1,128)}, u32[]{:S(2)}) copy-start(f32[1,1024]{1,0:T(1,128)} %copy-done.38) | copy-start | bytes 12292
  407.8 328.3 %collective-permute-start = (bf16[512,1024]{1,0:T(8,128)(2,1)}, bf16[512,1024]{1,0:T(8,128)(2,1)}, u32[]{:S(2)}, u32[]{:S(2)}) collective-permute-start(bf16[512,1024]{1,0:T(8,128)(2,1)} %get-tuple-element.65), channel_id=1, source_target_pairs={{0,1},{1,0},{2,3},{3,2},{4,5},{5,4},{6,7},{7,6},{8,9},{9,8},{10,11... | collective-permute-start | bytes 3145736 | tf_op jit(solution)/shard_map/ppermute | solution.py:1294
  423.7 15.2 %copy-start.6 = (f32[1024,1024]{1,0:T(8,128)S(1)}, f32[1024,1024]{1,0:T(8,128)}, u32[]{:S(2)}) copy-start(f32[1024,1024]{1,0:T(8,128)} %copy-done.5) | copy-start | bytes 12582916
  423.7 15.2 %copy-start.45 = (bf16[1024,1024]{1,0:T(8,128)(2,1)S(1)}, bf16[1024,1024]{1,0:T(8,128)(2,1)}, u32[]{:S(2)}) copy-start(bf16[1024,1024]{1,0:T(8,128)(2,1)} %get-tuple-element.30.ctx_ref) | copy-start | bytes 6291460
  442.7 3.7 copy-start.37
  458.6 133.3 %copy-start.26 = (f32[512,64]{0,1:T(8,128)S(1)}, f32[512,64]{0,1:T(8,128)}, u32[]{:S(2)}) copy-start(f32[512,64]{0,1:T(8,128)} %param.22) | copy-start | bytes 393220
  593.6 5.2 copy-start.13
  593.9 5.6 copy-start.42
  593.9 6.1 copy-start.41
  594.5 10.8 %copy-start.16 = (f32[3,64,512]{2,1,0:T(8,128)}, f32[3,64,512]{2,1,0:T(8,128)S(1)}, u32[]{:S(2)}) copy-start(f32[3,64,512]{2,1,0:T(8,128)S(1)} %reshape.200) | copy-start | bytes 1179652
  594.5 9.9 %copy-start.23 = (bf16[1,64,512]{2,1,0:T(8,128)(2,1)S(1)}, bf16[1,64,512]{2,1,0:T(8,128)(2,1)}, u32[]{:S(2)}) copy-start(bf16[1,64,512]{2,1,0:T(8,128)(2,1)} %get-tuple-element.52) | copy-start | bytes 196612
  594.6 133.3 %copy-start.14 = (f32[4,8,8,512]{3,2,0,1:T(8,128)}, f32[4,8,8,512]{3,2,0,1:T(8,128)S(1)}, u32[]{:S(2)}) copy-start(f32[4,8,8,512]{3,2,0,1:T(8,128)S(1)} %copy.51) | copy-start | bytes 1572868
  605.4 122.6 %copy-start.21 = (f32[512,64]{0,1:T(8,128)S(1)}, f32[512,64]{0,1:T(8,128)}, u32[]{:S(2)}) copy-start(f32[512,64]{0,1:T(8,128)} %param.17) | copy-start | bytes 393220
  605.4 126.3 %copy-start.29 = (f32[12,1024]{1,0:T(8,128)S(1)}, f32[12,1024]{1,0:T(8,128)}, u32[]{:S(2)}) copy-start(f32[12,1024]{1,0:T(8,128)} %param.25) | copy-start | bytes 147460
  605.4 126.5 %copy-start.25 = (f32[12,1024]{1,0:T(8,128)S(1)}, f32[12,1024]{1,0:T(8,128)}, u32[]{:S(2)}) copy-start(f32[12,1024]{1,0:T(8,128)} %param.20) | copy-start | bytes 147460
  727.9 4.7 copy-start.11
  727.9 5.6 copy-start.15
  728.0 7.3 copy-start.12
  729.6 6.5 copy-start.8
  731.7 7.7 %copy-start.24 = (f32[2,8,8,128]{3,1,2,0:T(8,128)}, f32[2,8,8,128]{3,1,2,0:T(8,128)S(1)}, u32[]{:S(2)}) copy-start(f32[2,8,8,128]{3,1,2,0:T(8,128)S(1)} %copy.56) | copy-start | bytes 196612
  731.8 7.6 %copy-start.22 = (f32[12,1024]{1,0:T(8,128)}, f32[12,1024]{1,0:T(8,128)S(1)}, u32[]{:S(2)}) copy-start(f32[12,1024]{1,0:T(8,128)S(1)} %get-tuple-element.47) | copy-start | bytes 147460
  736.1 7.4 copy-start.1

commit v4 on v3

--- a/solution.py
+++ b/solution.py
@@ -449,16 +449,10 @@
     return jnp.dot(left, right, preferred_element_type=jnp.float32)
 
 
-def attend_fwd_kernel(starts_ref, slopes_ref, packed_ref, ctx_ref, exps_ref, stat_ref, dist_ref, ctx_t):
-    pair = pl.program_id(0)
-
-    @pl.when(pair == 0)
-    def _():
-        layout_grid(starts_ref, dist_ref)
-
-    keys = packed_ref[:, PAIR : 2 * PAIR]
-    values_t = packed_ref[:, 2 * PAIR :].T
-    queries_t = (packed_ref[:, :PAIR] * (1.0 / math.sqrt(HD))).T
+def attend_pair(pair, slopes_ref, packed, dist_ref, ctx_ref, exps_ref, stat_ref, ctx_t):
+    keys = packed[:, PAIR : 2 * PAIR]
+    values_t = packed[:, 2 * PAIR :].T
+    queries_t = (packed[:, :PAIR] * (1.0 / math.sqrt(HD))).T
     for half in (0, 1):
         slope = slopes_ref[2 * pair + half]
         queries = only_rows(queries_t, half)
@@ -518,25 +512,6 @@
 PAIR_GRID = pl.BlockSpec((2, LEN, LEN), lambda p: (p, 0, 0))
 PAIR_STAT = pl.BlockSpec((1, 2, LEN), lambda p: (p, 0, 0))
 SCALARS = pl.BlockSpec(memory_space=pltpu.SMEM)
-
-
-def attention_forward(starts, slopes, packed):
-    return pl.pallas_call(
-        attend_fwd_kernel,
-        grid=(PAIRS,),
-        in_specs=[SCALARS, SCALARS, PACKED_COLS],
-        out_specs=[PAIR_COLS, PAIR_GRID, PAIR_STAT],
-        out_shape=[
-            jax.ShapeDtypeStruct((LEN, D), jnp.bfloat16),
-            jax.ShapeDtypeStruct((H, LEN, LEN), jnp.bfloat16),
-            jax.ShapeDtypeStruct((PAIRS, 2, LEN), jnp.float32),
-        ],
-        scratch_shapes=[pltpu.VMEM((LEN, LEN), jnp.float32), pltpu.VMEM((PAIR, LEN), jnp.float32)],
-        compiler_params=pltpu.CompilerParams(vmem_limit_bytes=VMEM_LIMIT),
-        cost_estimate=pl.CostEstimate(
-            flops=16 * LEN * LEN * D, bytes_accessed=44 * 1024 * 1024, transcendentals=H * LEN * LEN
-        ),
-    )(starts, slopes, packed)
 
 
 def attention_backward(packed, context, grad_context, exps, stats):
@@ -1065,14 +1040,34 @@
     swap.wait()
 
 
-def second_spread_kernel(
-    slots_ref, cotangent_ref, out_ref, up_ref, down_ref, got_ref, local_sem, send_sem, recv_sem, token_sem
+def attend_spread_kernel(
+    starts_ref,
+    slopes_ref,
+    normed_ref,
+    weights_ref,
+    shifts_ref,
+    slots_ref,
+    cotangent_ref,
+    packed_ref,
+    ctx_ref,
+    exps_ref,
+    stat_ref,
+    out_ref,
+    up_ref,
+    down_ref,
+    got_ref,
+    dist_ref,
+    ctx_t,
+    local_sem,
+    send_sem,
+    recv_sem,
+    token_sem,
 ):
+    pair = pl.program_id(0)
     table = [(out_ref, 0, SLOT, 0)]
     table += [(up_ref, index * SLOT, 4 * SLOT, HALF_SLOT if index % 2 else 0) for index in range(4)]
     table += [(down_ref, index * SLOT, 4 * SLOT, HALF_SLOT if index % 2 else 0) for index in range(4)]
     spread = Spread(slots_ref, table, local_sem, send_sem, recv_sem)
-    greet_neighbours([spread.sibling, spread.beside, spread.across] + spread.stations)
     swap = pltpu.make_async_remote_copy(
         src_ref=cotangent_ref.at[1 - spread.y],
         dst_ref=got_ref,
@@ -1081,13 +1076,31 @@
         device_id=spread.across,
         device_id_type=MESH_IDS,
     )
-    spread.begin()
-    for index in range(spread.ticks()):
-        spread.tick(index)
-        if index == SWAP_AT:
-            swap.start()
-    spread.finish()
-    swap.wait()
+
+    @pl.when(pair == 0)
+    def _():
+        greet_neighbours([spread.sibling, spread.beside, spread.across] + spread.stations)
+        spread.begin()
+        layout_grid(starts_ref, dist_ref)
+
+    for index in range(1, PAIRS):
+
+        @pl.when(pair == index)
+        def _(index=index):
+            spread.tick(index - 1)
+            if index == 5:
+                swap.start()
+
+    packed = (mul(normed_ref[...], weights_ref[...]) + shifts_ref[...]).astype(jnp.bfloat16)
+    packed_ref[...] = packed
+    attend_pair(pair, slopes_ref, packed, dist_ref, ctx_ref, exps_ref, stat_ref, ctx_t)
+
+    @pl.when(pair == PAIRS - 1)
+    def _():
+        for index in range(PAIRS - 1, spread.ticks()):
+            spread.tick(index)
+        spread.finish()
+        swap.wait()
 
 
 def whole_shape(columns):
@@ -1107,22 +1120,43 @@
     return whole.reshape(D, 3 * D), got
 
 
-def second_spread(slots, cotangent):
+def attend_spread(starts, slopes, normed, weights, shifts, slots, cotangent):
     anywhere = pl.BlockSpec(memory_space=pl.ANY)
-    out, up, down, got = pl.pallas_call(
-        second_spread_kernel,
-        in_specs=[anywhere] * 2,
-        out_specs=[anywhere] * 4,
+    packed, context, exps, stats, out, up, down, got = pl.pallas_call(
+        attend_spread_kernel,
+        grid=(PAIRS,),
+        in_specs=[
+            SCALARS,
+            SCALARS,
+            pl.BlockSpec((LEN, D), lambda p: (0, 0)),
+            PACKED_COLS,
+            pl.BlockSpec((1, 3 * PAIR), lambda p: (0, p)),
+            anywhere,
+            anywhere,
+        ],
+        out_specs=[PACKED_COLS, PAIR_COLS, PAIR_GRID, PAIR_STAT] + [anywhere] * 4,
         out_shape=[
+            jax.ShapeDtypeStruct((LEN, 3 * D), jnp.bfloat16),
+            jax.ShapeDtypeStruct((LEN, D), jnp.bfloat16),
+            jax.ShapeDtypeStruct((H, LEN, LEN), jnp.bfloat16),
+            jax.ShapeDtypeStruct((PAIRS, 2, LEN), jnp.float32),
             whole_shape(D),
             whole_shape(FF),
             whole_shape(FF),
             jax.ShapeDtypeStruct(cotangent.shape[1:], cotangent.dtype),
         ],
-        scratch_shapes=spread_semaphores(9) + [pltpu.SemaphoreType.DMA((2,))],
-        compiler_params=pltpu.CompilerParams(collective_id=4, has_side_effects=True),
-    )(slots, cotangent)
-    return out.reshape(D, D), up.reshape(D, FF), down.reshape(D, FF), got
+        scratch_shapes=[pltpu.VMEM((LEN, LEN), jnp.float32), pltpu.VMEM((PAIR, LEN), jnp.float32)]
+        + spread_semaphores(9)
+        + [pltpu.SemaphoreType.DMA((2,))],
+        compiler_params=pltpu.CompilerParams(
+            collective_id=4, has_side_effects=True, vmem_limit_bytes=VMEM_LIMIT
+        ),
+        cost_estimate=pl.CostEstimate(
+            flops=16 * LEN * LEN * D, bytes_accessed=90 * 1024 * 1024, transcendentals=H * LEN * LEN
+        ),
+    )(starts, slopes, normed, weights, shifts, slots, cotangent)
+    wholes = out.reshape(D, D), up.reshape(D, FF), down.reshape(D, FF)
+    return packed, context, exps, stats, wholes, got
 
 
 GROUP_SLOTS = (3, 1, 4, 4)
@@ -1330,13 +1364,13 @@
     token_rows = in_order(rank, own_tokens, other_tokens).astype(jnp.float32)
     normed_one = narrow(layer_norm(token_rows, vectors[0], vectors[1]))
     shifts = by_pairs(jnp.stack([vectors[2], jnp.zeros((D,), jnp.float32), vectors[3]])[:, None])
-    packed = narrow(contract(normed_one, full_qkv, 1, 0) + shifts)
-    context, exps, stats = attention_forward(starts, slopes, packed)
-
     later_slots = jnp.concatenate(
         [narrow(w_out).T[None], by_slots(narrow(w_up)), by_slots(narrow(w_down).T)]
     )
-    full_out, full_up, full_down, other_cotangent = second_spread(later_slots, cotangent)
+    packed, context, exps, stats, wholes, other_cotangent = attend_spread(
+        starts, slopes, normed_one, full_qkv, shifts, later_slots, cotangent
+    )
+    full_out, full_up, full_down = wholes
     cotangent_low = in_order(rank, own_cotangent, other_cotangent)
     cotangent_rows = cotangent_low.astype(jnp.float32)
 

time: 755 us -> 710 us (0.940)
  Pallas kernels: 506 us -> 469 us
  matrix products: 159 us -> 145 us
    pallas_call x2 -> x1, Pallas kernels: 165 us -> 129 us  [attend_spread(): pl.pallas_call(attend_spread_kernel, grid=(PAIRS,), in_specs=[SCALARS, SC...]
    dot_general x12 -> x11, matrix products: 159 us -> 145 us  [contract(): lax.dot_general(left, right, (((left_dim,), (right_dim,)), ((), ())), pre...]
    convert_element_type x7 -> x8, other arithmetic: 14.2 us -> 15.6 us  [narrow(): return rows.astype(jnp.bfloat16)]
  transfers between devices with their start and end apart: 2 -> 2, of which waited for: 0 -> 0; matrix products, arithmetic and copies ran while one was open for 14% -> 15% of each run, Pallas kernels for 34% -> 36%
where the time goes in v4:
time: 710 us; the launch traced here: 699 us
  Pallas kernels  469 us (66%)
  matrix products  145 us (20%)
  other arithmetic  56.2 us (8%)
  local copies, waits for them, and re-layouts  25.8 us (4%)
    dot_general x11, matrix products, contract(): lax.dot_general(left, right, (((left_dim,), (right_dim,)), ((), ())), pre...  145 us
    pallas_call x1, Pallas kernels, attend_spread(): pl.pallas_call(attend_spread_kernel, grid=(PAIRS,), in_specs=[SCALARS, SC...  129 us
    pallas_call x1, Pallas kernels, sum_over_devices(): pl.pallas_call(sum_kernel, in_specs=[anywhere] * 4, out_specs=pl.BlockSpe...  126 us
    pallas_call x1, Pallas kernels, muon_call(): pl.pallas_call(muon_kernel, in_specs=[vmem, vmem], out_specs=[vmem, vmem]...  123 us
    pallas_call x1, Pallas kernels, first_spread(): pl.pallas_call(first_spread_kernel, in_specs=[anywhere] * 2, out_specs=[a...  57.3 us
    pallas_call x1, Pallas kernels, attention_backward(): pl.pallas_call(attend_bwd_kernel, grid=(PAIRS,), in_specs=[PACKED_COLS, P...  33 us
    convert_element_type x8, other arithmetic, narrow(): return rows.astype(jnp.bfloat16)  15.6 us
  transfers between devices with their start and end apart: 2, of which 0 were waited for; matrix products, arithmetic and copies ran while one was open for 15% of the time, Pallas kernels for 36%

profile of v4, /device:TPU:9, one launch (start us, length us, event | category | flops | bytes accessed | tf_op | source)
XLA Modules:
  0.0 699.3 jit_solution(7953781348149981597)
XLA Ops:
  1.2 0.9 slice_bitcast_fusion.4
  2.2 1.7 fusion.34
  4.0 0.6 reshape.192.shifts_ref
  4.6 0.9 convert_bitcast_fusion.3
  5.5 1.0 convert_element_type.104
  7.0 0.7 copy.69
  7.7 1.1 convert_element_type.108
  8.8 1.8 convert_element_type.109
  11.1 2.6 dynamic-slice_bitcast_fusion.1
  13.7 57.3 %shard_map.260 = (bf16[4,2,2,64,3072]{4,3,2,1,0:T(8,128)(2,1)}, bf16[512,1024]{1,0:T(8,128)(2,1)}) custom-call(bf16[3,64,512]{2,1,0:T(8,128)(2,1)} %bitcast.168, bf16[2,512,1024]{2,1,0:T(8,128)(2,1)} %tokens_ref.1), custom_call_target="tpu_custom_call" | custom-call | tf_op jit(solution)/shard_map/pallas_call | solution.py:1112
  70.9 2.3 convert_reduce_fusion.2
  73.3 2.3 fusion.16
  76.3 0.9 pad_maximum_fusion.1.slots_ref
  77.2 3.5 fusion.14.normed_ref
  80.6 129.4 %shard_map.261 = (bf16[1024,3072]{1,0:T(8,128)(2,1)}, bf16[1024,1024]{1,0:T(8,128)(2,1)}, bf16[16,1024,1024]{2,1,0:T(8,128)(2,1)}, f32[8,2,1024]{2,1,0:T(2,128)}...) custom-call(s32[2]{0:T(128)} %fusion.24.starts_ref, ...), custom_call_target="tpu_custom_call" | custom-call | flops 17179869184 | bytes 94371840 | tf_op jit(solution)/shard_map/pallas_call | solution.py:1125
  210.1 4.9 fusion.35
  215.7 16.1 %fusion.26 = f32[1024,4096]{1,0:T(8,128)} fusion(bf16[1024,4096]{1,0:T(8,128)(2,1)} %bitcast.194, f32[1024,1024]{1,0:T(8,128)S(1)} %get-tuple-element.81, f32[1024]{0:T(1024)S(1)} %bitcast.186, f32[1024]{0:T(1024)S(1)} %bitcast.178, f32[1024]{0:T(1024)S(1)} %fusion.23, f32[1024]{0:T(1024)S(1)} %broadcast_multiply_fusion), kind=kOutput, calls=%fused_computation.111 | convolution fusion | flops 8595177472 | bytes 29376512 | tf_op jit(solution)/shard_map/dot_general | solution.py:1315
  231.7 27.6 %convert_reduce_fusion = (f32[4096]{0:T(1024)}, bf16[1024,4096]{1,0:T(8,128)(2,1)}) fusion(f32[1024,4096]{1,0:T(8,128)} %fusion.26, f32[4096]{0:T(1024)S(1)} %bitcast.182, bf16[1024,4096]{1,0:T(8,128)(2,1)} %bitcast.192, bf16[512,1024]{1,0:T(8,128)(2,1)S(1)} %copy-done.19, bf16[512,1024]{1,0:T(8,128)(2,1)S(1)} %copy-done.9, pred[]{:T(512)S(6)} %eq.2), kind=kOutput, calls=%fused_computation.9 | convolution fusion | flops 8695836672 | bytes 35684352 | tf_op jit(solution)/shard_map/dot_general | solution.py:1315
  259.4 16.8 %multiply_reduce_fusion = (f32[1024]{0:T(1024)}, f32[1024]{0:T(1024)S(1)}, f32[1024]{0:T(1024)}, f32[1024,1024]{1,0:T(8,128)}) fusion(f32[1024,1024]{1,0:T(8,128)S(1)} %get-tuple-element.81, f32[1024]{0:T(1024)S(1)} %fusion.23, f32[1024]{0:T(1024)S(1)} %broadcast_multiply_fusion, f32[1024]{0:T(1024)S(1)} %bitcast.179, ...), kind=kOutput, calls=%fused_computation.34 | convolution fusion | flops 8598320128 | bytes 25190400 | tf_op jit(solution)/shard_map/dot_general | solution.py:1315
  276.2 3.4 fusion.33
  279.6 4.5 fusion.29
  284.1 3.7 convolution_convert_fusion.4.grad_ref
  287.8 33.0 %shard_map.262 = bf16[1024,3072]{1,0:T(8,128)(2,1)} custom-call(bf16[1024,3072]{1,0:T(8,128)(2,1)} %get-tuple-element.36.packed_ref, bf16[1024,1024]{1,0:T(8,128)(2,1)} %get-tuple-element.31.ctx_ref, bf16[1024,1024]{1,0:T(8,128)(2,1)} %convolution_convert_fusion.4.grad_ref, bf16[16,1024,1024]{2,1,0:T(8,128)(2,1)} %get-tuple-element.37.exps_ref, ...), custom_call_target="tpu_custom_call" | custom-call | flops 34359738368 | bytes 52428800 | tf_op jit(solution)/shard_map/pallas_call | solution.py:518
  320.8 11.4 %fusion.28 = (f32[1024]{0:T(1024)S(1)}, f32[1024]{0:T(1024)S(1)}, f32[1024,1024]{1,0:T(8,128)S(1)}) fusion(f32[1024]{0:T(1024)S(1)} %bitcast.173, f32[1024]{0:T(1024)S(1)} %copy-done.29, bf16[512,1024]{1,0:T(8,128)(2,1)S(1)} %get-tuple-element.87, bf16[512,1024]{1,0:T(8,128)(2,1)S(1)} %copy-done.2, pred[]{:T(512)S(6)} %eq.2, ...), kind=kOutput, calls=%fused_computation.113 | convolution fusion | flops 6458177536 | bytes 18890752 | tf_op jit(solution)/shard_map/dot_general | solution.py:1315
  332.3 4.0 fusion.15
  336.4 3.4 add_convert_fusion
  339.7 1.2 dynamic-slice_bitcast_fusion
  340.9 18.5 %add_convert_fusion.1 = bf16[1024,1024]{1,0:T(8,128)(2,1)} fusion(f32[1024,1024]{1,0:T(8,128)} %copy-done.3, f32[1024]{0:T(1024)S(1)} %bitcast.188, bf16[1024,4096]{1,0:T(8,128)(2,1)} %bitcast.193, f32[1024,4096]{1,0:T(8,128)} %fusion.26, f32[4096]{0:T(1024)S(1)} %bitcast.183), kind=kOutput, calls=%fused_computation.37 | convolution fusion | flops 8635023360 | bytes 31477760 | tf_op jit(solution)/shard_map/dot_general | solution.py:1315
  359.4 2.8 dynamic-slice_bitcast_fusion.2
  362.2 1.4 collective-permute-start
  363.7 15.6 %convolution_convert_fusion = bf16[1024,4096]{1,0:T(8,128)(2,1)} fusion(bf16[512,1024]{1,0:T(8,128)(2,1)S(1)} %copy-done.20, bf16[512,1024]{1,0:T(8,128)(2,1)S(1)} %copy-done.10, pred[]{:T(512)S(6)} %eq.2, f32[1024,4096]{1,0:T(8,128)} %fusion.26, f32[4096]{0:T(1024)S(1)} %bitcast.184), kind=kOutput, calls=%fused_computation.12 | convolution fusion | flops 8645509120 | bytes 27279360 | tf_op jit(solution)/shard_map/dot_general | solution.py:1315
  379.4 15.2 %convolution_convert_fusion.1 = bf16[1024,4096]{1,0:T(8,128)(2,1)} fusion(bf16[1024,4096]{1,0:T(8,128)(2,1)} %get-tuple-element.85, f32[1024,1024]{1,0:T(8,128)S(1)} %copy-done.4, f32[1024]{0:T(1024)S(1)} %bitcast.187, f32[1024]{0:T(1024)S(1)} %bitcast.181, f32[1024]{0:T(1024)S(1)} %fusion.23, f32[1024]{0:T(1024)S(1)} %broadcast_multiply_fusion), kind=kOutput, calls=%fused_computation.13 | convolution fusion | flops 8599371776 | bytes 20987904 | tf_op jit(solution)/shard_map/dot_general | solution.py:1315
  394.6 3.7 convolution_convert_fusion.3
  398.3 3.8 convert_reduce_fusion.1
  402.1 11.5 %convolution_convert_fusion.2 = bf16[1024,3072]{1,0:T(8,128)(2,1)} fusion(bf16[1024,1024]{1,0:T(8,128)(2,1)S(1)} %copy-done.15, bf16[1024,3072]{1,0:T(8,128)(2,1)} %shard_map.262), kind=kOutput, calls=%fused_computation.23 | convolution fusion | flops 6445596672 | bytes 14680064 | tf_op jit(solution)/shard_map/dot_general | solution.py:1315
  413.7 126.4 %shard_map.263 = f32[12,64,512]{2,1,0:T(8,128)} custom-call(bf16[4,2,2,64,3072]{4,3,2,1,0:T(8,128)(2,1)} %bitcast.152, bf16[4,2,2,64,1024]{4,3,2,1,0:T(8,128)(2,1)} %bitcast.153, bf16[4,2,2,64,4096]{4,3,2,1,0:T(8,128)(2,1)} %bitcast.151, bf16[4,2,2,64,4096]{4,3,2,1,0:T(8,128)(2,1)} %bitcast.150), custom_call_target="tpu_custom_call" | custom-call | bytes 314572800 | tf_op jit(solution)/shard_map/pallas_call | solution.py:1287
  540.1 1.0 slice_bitcast_fusion.2
  541.1 2.1 slice_bitcast_fusion
  543.2 0.6 constant_dynamic-update-slice_fusion.8
  544.4 0.6 constant_dynamic-update-slice_fusion.6
  545.0 0.6 constant_dynamic-update-slice_fusion.5
  545.6 1.7 convert_bitcast_fusion.2
  547.6 1.1 reshape_reshape.7
  548.8 1.1 copy.39
  550.1 1.2 copy.52
  551.4 2.1 fusion.31
  553.5 2.0 fusion.32
  555.5 0.6 constant_dynamic-update-slice_fusion.4
  556.1 0.6 constant_dynamic-update-slice_fusion.3
  556.7 0.6 constant_dynamic-update-slice_fusion.2
  557.3 0.6 constant_dynamic-update-slice_fusion.1
  557.9 0.6 constant_dynamic-update-slice_fusion.vec_ref
  558.5 0.8 fusion.30
  559.3 1.0 pad_maximum_fusion.moments_ref
  560.3 123.0 %shard_map.264 = (bf16[12,64,512]{2,1,0:T(8,128)(2,1)}, f32[12,8,128]{2,1,0:T(8,128)}) custom-call(bf16[12,64,512]{2,1,0:T(8,128)(2,1)} %pad_maximum_fusion.moments_ref, f32[12,8,128]{2,1,0:T(8,128)} %constant_dynamic-update-slice_fusion.vec_ref), custom_call_target="tpu_custom_call" | custom-call | flops 25769803776 | bytes 4194304 | tf_op jit(solution)/shard_map/pallas_call | solution.py:802
  683.4 1.6 bitcast_subtract_fusion.1
  685.0 1.1 convert_bitcast_fusion
  686.2 0.8 pad.26
  687.2 0.7 multiply_subtract_fusion.1
  688.0 0.9 sub.54
  688.8 1.7 multiply_subtract_fusion
  690.5 0.8 bitcast_subtract_fusion
  691.4 3.4 maximum_select_fusion.1
  694.8 4.1 fusion.19
  (128 shorter events, 4.4 us)
Async XLA Ops:
  0.7 9.9 %copy-start = (s32[2,1,2]{2,1,0:T(1,128)S(1)}, s32[2,1,2]{2,1,0:T(1,128)}, u32[]{:S(2)}) copy-start(s32[2,1,2]{2,1,0:T(1,128)} %param.15) | copy-start | bytes 52
  0.7 10.4 %copy-start.8 = (bf16[2,512,1024]{2,1,0:T(8,128)(2,1)S(1)}, bf16[2,512,1024]{2,1,0:T(8,128)(2,1)}, u32[]{:S(2)}) copy-start(bf16[2,512,1024]{2,1,0:T(8,128)(2,1)} %tokens_ref.1) | copy-start | bytes 6291460
  3.8 73.3 %copy-start.31 = (f32[1,1024]{1,0:T(1,128)}, f32[1,1024]{1,0:T(1,128)S(1)}, u32[]{:S(2)}) copy-start(f32[1,1024]{1,0:T(1,128)S(1)} %get-tuple-element.78) | copy-start | bytes 12292
  3.8 211.8 %copy-start.40 = (f32[1,1024]{1,0:T(1,128)}, f32[1,1024]{1,0:T(1,128)S(1)}, u32[]{:S(2)}) copy-start(f32[1,1024]{1,0:T(1,128)S(1)} %get-tuple-element.73) | copy-start | bytes 12292
  13.7 62.6 %copy-start.18 = (bf16[2048,64]{0,1:T(8,128)(2,1)S(1)}, bf16[2048,64]{0,1:T(8,128)(2,1)}, u32[]{:S(2)}) copy-start(bf16[2048,64]{0,1:T(8,128)(2,1)} %convert_element_type.109) | copy-start | bytes 786436
  70.9 6.2 copy-start.2
  73.3 7.3 %copy-start.28 = (f32[1024]{0:T(1024)}, f32[1024]{0:T(1024)S(1)}, u32[]{:S(2)}) copy-start(f32[1024]{0:T(1024)S(1)} %broadcast_multiply_fusion.1) | copy-start | bytes 12292
  75.6 0.6 copy-start.35
  75.7 134.4 %copy-start.33 = (f32[1024]{0:T(1024)}, f32[1024]{0:T(1024)S(1)}, u32[]{:S(2)}) copy-start(f32[1024]{0:T(1024)S(1)} %fusion.22) | copy-start | bytes 12292
  215.0 61.1 %copy-start.3 = (f32[1024,1024]{1,0:T(8,128)}, f32[1024,1024]{1,0:T(8,128)S(1)}, u32[]{:S(2)}) copy-start(f32[1024,1024]{1,0:T(8,128)S(1)} %get-tuple-element.81) | copy-start | bytes 12582916
  215.6 16.1 %copy-start.9 = (bf16[512,1024]{1,0:T(8,128)(2,1)S(1)}, bf16[512,1024]{1,0:T(8,128)(2,1)}, u32[]{:S(2)}) copy-start(bf16[512,1024]{1,0:T(8,128)(2,1)} %get-tuple-element.86) | copy-start | bytes 3145732
  215.6 16.1 %copy-start.19 = (bf16[512,1024]{1,0:T(8,128)(2,1)S(1)}, bf16[512,1024]{1,0:T(8,128)(2,1)}, u32[]{:S(2)}) copy-start(bf16[512,1024]{1,0:T(8,128)(2,1)} %get-tuple-element.35) | copy-start | bytes 3145732
  279.6 4.5 copy-start.45
  284.1 3.7 copy-start.5
  287.8 33.0 %copy-start.29 = (f32[1024]{0:T(1024)S(1)}, f32[1024]{0:T(1024)}, u32[]{:S(2)}) copy-start(f32[1024]{0:T(1024)} %copy-done.28) | copy-start | bytes 12292
  287.8 33.0 %copy-start.32 = (f32[1,1024]{1,0:T(1,128)S(1)}, f32[1,1024]{1,0:T(1,128)}, u32[]{:S(2)}) copy-start(f32[1,1024]{1,0:T(1,128)} %copy-done.31) | copy-start | bytes 12292
  320.8 11.5 %copy-start.36 = (f32[1024]{0:T(1024)S(1)}, f32[1024]{0:T(1024)}, u32[]{:S(2)}) copy-start(f32[1024]{0:T(1024)} %copy-done.35) | copy-start | bytes 12292
  320.8 11.5 %copy-start.34 = (f32[1024]{0:T(1024)S(1)}, f32[1024]{0:T(1024)}, u32[]{:S(2)}) copy-start(f32[1024]{0:T(1024)} %copy-done.33) | copy-start | bytes 12292
  332.3 4.1 copy-start.6
  339.7 1.2 copy-start.42
  340.9 353.9 %collective-permute-start.1 = (bf16[512,1024]{1,0:T(8,128)(2,1)}, bf16[512,1024]{1,0:T(8,128)(2,1)}, u32[]{:S(2)}, u32[]{:S(2)}) collective-permute-start(bf16[512,1024]{1,0:T(8,128)(2,1)} %get-tuple-element.65), channel_id=1, source_target_pairs={{0,1},{1,0},{2,3},{3,2},{4,5},{5,4},{6,7},{7,6},{8,9},{9,8},{10,11... | collective-permute-start | bytes 3145736 | tf_op jit(solution)/shard_map/ppermute | solution.py:1328
  359.4 4.3 copy-start.10
  359.4 4.3 copy-start.20
  362.2 17.1 %copy-start.4 = (f32[1024,1024]{1,0:T(8,128)S(1)}, f32[1024,1024]{1,0:T(8,128)}, u32[]{:S(2)}) copy-start(f32[1024,1024]{1,0:T(8,128)} %copy-done.3) | copy-start | bytes 12582916
  362.2 17.1 %copy-start.41 = (f32[1,1024]{1,0:T(1,128)S(1)}, f32[1,1024]{1,0:T(1,128)}, u32[]{:S(2)}) copy-start(f32[1,1024]{1,0:T(1,128)} %copy-done.40) | copy-start | bytes 12292
  362.2 329.2 %collective-permute-start = (bf16[512,1024]{1,0:T(8,128)(2,1)}, bf16[512,1024]{1,0:T(8,128)(2,1)}, u32[]{:S(2)}, u32[]{:S(2)}) collective-permute-start(bf16[512,1024]{1,0:T(8,128)(2,1)} %get-tuple-element.67), channel_id=1, source_target_pairs={{0,1},{1,0},{2,3},{3,2},{4,5},{5,4},{6,7},{7,6},{8,9},{9,8},{10,11... | collective-permute-start | bytes 3145736 | tf_op jit(solution)/shard_map/ppermute | solution.py:1328
  379.3 15.2 %copy-start.7 = (f32[1024,1024]{1,0:T(8,128)S(1)}, f32[1024,1024]{1,0:T(8,128)}, u32[]{:S(2)}) copy-start(f32[1024,1024]{1,0:T(8,128)} %copy-done.5) | copy-start | bytes 12582916
  379.3 15.2 %copy-start.46 = (bf16[1024,1024]{1,0:T(8,128)(2,1)S(1)}, bf16[1024,1024]{1,0:T(8,128)(2,1)}, u32[]{:S(2)}) copy-start(bf16[1024,1024]{1,0:T(8,128)(2,1)} %get-tuple-element.31.ctx_ref) | copy-start | bytes 6291460
  398.3 3.8 copy-start.15
  413.7 131.9 %copy-start.27 = (f32[512,64]{0,1:T(8,128)S(1)}, f32[512,64]{0,1:T(8,128)}, u32[]{:S(2)}) copy-start(f32[512,64]{0,1:T(8,128)} %param.22) | copy-start | bytes 393220
  547.3 8.2 %copy-start.13 = (f32[4,8,8,512]{3,2,0,1:T(8,128)}, f32[4,8,8,512]{3,2,0,1:T(8,128)S(1)}, u32[]{:S(2)}) copy-start(f32[4,8,8,512]{3,2,0,1:T(8,128)S(1)} %copy.53) | copy-start | bytes 1572868
  547.6 7.9 %copy-start.38 = (f32[1024]{0:T(1024)S(1)}, f32[1024]{0:T(1024)}, u32[]{:S(2)}) copy-start(f32[1024]{0:T(1024)} %get-tuple-element.50) | copy-start | bytes 12292
  547.6 8.5 %copy-start.44 = (f32[1024]{0:T(1024)S(1)}, f32[1024]{0:T(1024)}, u32[]{:S(2)}) copy-start(f32[1024]{0:T(1024)} %get-tuple-element.41) | copy-start | bytes 12292
  547.6 9.1 %copy-start.43 = (f32[1024]{0:T(1024)S(1)}, f32[1024]{0:T(1024)}, u32[]{:S(2)}) copy-start(f32[1024]{0:T(1024)} %get-tuple-element.45) | copy-start | bytes 12292
  547.6 9.7 %copy-start.39 = (f32[4096]{0:T(1024)S(1)}, f32[4096]{0:T(1024)}, u32[]{:S(2)}) copy-start(f32[4096]{0:T(1024)} %get-tuple-element.84) | copy-start | bytes 49156
  547.6 10.3 %copy-start.37 = (f32[1024]{0:T(1024)S(1)}, f32[1024]{0:T(1024)}, u32[]{:S(2)}) copy-start(f32[1024]{0:T(1024)} %get-tuple-element.63) | copy-start | bytes 12292
  549.9 9.4 %copy-start.24 = (bf16[1,64,512]{2,1,0:T(8,128)(2,1)S(1)}, bf16[1,64,512]{2,1,0:T(8,128)(2,1)}, u32[]{:S(2)}) copy-start(bf16[1,64,512]{2,1,0:T(8,128)(2,1)} %get-tuple-element.54) | copy-start | bytes 196612
  550.1 10.2 %copy-start.17 = (f32[3,64,512]{2,1,0:T(8,128)}, f32[3,64,512]{2,1,0:T(8,128)S(1)}, u32[]{:S(2)}) copy-start(f32[3,64,512]{2,1,0:T(8,128)S(1)} %reshape.202) | copy-start | bytes 1179652
  550.1 8.4 %copy-start.22 = (f32[3,64,512]{2,1,0:T(8,128)S(1)}, f32[3,64,512]{2,1,0:T(8,128)}, u32[]{:S(2)}) copy-start(f32[3,64,512]{2,1,0:T(8,128)} %param.21) | copy-start | bytes 1179652
  551.3 132.0 %copy-start.14 = (f32[4,8,8,512]{3,2,0,1:T(8,128)}, f32[4,8,8,512]{3,2,0,1:T(8,128)S(1)}, u32[]{:S(2)}) copy-start(f32[4,8,8,512]{3,2,0,1:T(8,128)S(1)} %copy.52) | copy-start | bytes 1572868
  560.3 123.1 %copy-start.21 = (f32[512,64]{0,1:T(8,128)S(1)}, f32[512,64]{0,1:T(8,128)}, u32[]{:S(2)}) copy-start(f32[512,64]{0,1:T(8,128)} %param.17) | copy-start | bytes 393220
  560.3 126.7 %copy-start.30 = (f32[12,1024]{1,0:T(8,128)S(1)}, f32[12,1024]{1,0:T(8,128)}, u32[]{:S(2)}) copy-start(f32[12,1024]{1,0:T(8,128)} %param.25) | copy-start | bytes 147460
  560.3 126.8 %copy-start.26 = (f32[12,1024]{1,0:T(8,128)S(1)}, f32[12,1024]{1,0:T(8,128)}, u32[]{:S(2)}) copy-start(f32[12,1024]{1,0:T(8,128)} %param.20) | copy-start | bytes 147460
  683.3 4.6 copy-start.11
  683.3 5.5 copy-start.16
  683.4 7.2 %copy-start.12 = (f32[2048,64]{0,1:T(8,128)S(1)}, f32[2048,64]{0,1:T(8,128)}, u32[]{:S(2)}) copy-start(f32[2048,64]{0,1:T(8,128)} %param.19) | copy-start | bytes 1572868
  687.0 7.8 %copy-start.25 = (f32[2,8,8,128]{3,1,2,0:T(8,128)}, f32[2,8,8,128]{3,1,2,0:T(8,128)S(1)}, u32[]{:S(2)}) copy-start(f32[2,8,8,128]{3,1,2,0:T(8,128)S(1)} %copy.57) | copy-start | bytes 196612
  687.1 7.7 %copy-start.23 = (f32[12,1024]{1,0:T(8,128)}, f32[12,1024]{1,0:T(8,128)S(1)}, u32[]{:S(2)}) copy-start(f32[12,1024]{1,0:T(8,128)S(1)} %get-tuple-element.49) | copy-start | bytes 147460
  691.4 7.5 %copy-start.1 = (s32[2,1,2]{2,1,0:T(1,128)S(1)}, s32[2,1,2]{2,1,0:T(1,128)}, u32[]{:S(2)}) copy-start(s32[2,1,2]{2,1,0:T(1,128)} %param.15) | copy-start | bytes 52

commit v5 on v4

--- a/solution.py
+++ b/solution.py
@@ -471,42 +471,6 @@
     ctx_ref[...] = ctx_t[...].T.astype(jnp.bfloat16)
 
 
-def attend_bwd_kernel(packed_ref, ctx_ref, grad_ref, exps_ref, stat_ref, out_ref, dq_t, dk_sum, dv_sum):
-    scale = 1.0 / math.sqrt(HD)
-    queries = packed_ref[:, :PAIR]
-    keys_t = packed_ref[:, PAIR : 2 * PAIR].T
-    values = packed_ref[:, 2 * PAIR :]
-    grads_t = grad_ref[...].T.astype(jnp.float32)
-    context_t = ctx_ref[...].T.astype(jnp.float32)
-    scaled = []
-    inner_rows = []
-    for half in (0, 1):
-        heads = slice(half * HD, half * HD + HD)
-        scaled.append(grads_t[heads] * stat_ref[0, half : half + 1, :])
-        inner_rows.append(jnp.sum(scaled[half] * context_t[heads], axis=0, keepdims=True))
-    scaled_t = jnp.concatenate(scaled, axis=0).astype(jnp.bfloat16)
-    scaled_rows = scaled_t.T
-    dk_sum[...] = jnp.zeros_like(dk_sum)
-    dv_sum[...] = jnp.zeros_like(dv_sum)
-    for half in (0, 1):
-        heads = slice(half * HD, half * HD + HD)
-        half_t = only_rows(scaled_t, half)
-        half_rows = only_cols(scaled_rows, half)
-        half_queries = only_cols(queries, half)
-        for block in range(LEN // QB):
-            span = min(LEN, QB * block + QB + PIECE)
-            cols = slice(block * QB, block * QB + QB)
-            exps = exps_ref[half, :span, cols]
-            grad_probs = mul(values[:span], half_t[:, cols])
-            grad_scores = (exps.astype(jnp.float32) * (grad_probs - inner_rows[half][:, cols])).astype(jnp.bfloat16)
-            dv_sum[:span, :] += mul(exps, half_rows[cols])
-            dk_sum[:span, :] += mul(grad_scores, half_queries[cols])
-            dq_t[heads, cols] = mul(keys_t[heads, :span], grad_scores)
-    out_ref[:, :PAIR] = (dq_t[...] * scale).T.astype(jnp.bfloat16)
-    out_ref[:, PAIR : 2 * PAIR] = (dk_sum[...] * scale).astype(jnp.bfloat16)
-    out_ref[:, 2 * PAIR :] = dv_sum[...].astype(jnp.bfloat16)
-
-
 PACKED_COLS = pl.BlockSpec((LEN, 3 * PAIR), lambda p: (0, p))
 PAIR_COLS = pl.BlockSpec((LEN, PAIR), lambda p: (0, p))
 PAIR_GRID = pl.BlockSpec((2, LEN, LEN), lambda p: (p, 0, 0))
@@ -514,21 +478,135 @@
 SCALARS = pl.BlockSpec(memory_space=pltpu.SMEM)
 
 
-def attention_backward(packed, context, grad_context, exps, stats):
+HIDDEN = 512
+CHUNK = 256
+HIDDEN_STEPS = FF // HIDDEN
+GELU_SLOPE = math.sqrt(2.0 / math.pi)
+GELU_CUBE = 0.044715
+
+
+def dot_last(left, right):
+    return lax.dot_general(left, right, (((1,), (1,)), ((), ())), preferred_element_type=jnp.float32)
+
+
+def gelu_both(rows):
+    square = rows * rows
+    bent = jnp.tanh(rows * (GELU_SLOPE + GELU_SLOPE * GELU_CUBE * square))
+    half = 0.5 + 0.5 * bent
+    slope = half + 0.5 * rows * (1.0 - bent * bent) * (GELU_SLOPE + 3.0 * GELU_SLOPE * GELU_CUBE * square)
+    return rows * half, slope
+
+
+def hidden_block(step):
+    return (step % 2) * (HIDDEN_STEPS // 2) + step // 2
+
+
+def mlp_kernel(
+    rows_ref,
+    cot_ref,
+    base_ref,
+    bias_ref,
+    up_ref,
+    down_ref,
+    block_ref,
+    grad_rows_ref,
+    grad_up_ref,
+    grad_down_ref,
+    bias_sum_ref,
+    rows_t,
+    cot_t,
+    total,
+    up_part,
+    down_part,
+    active,
+    grad_before,
+    load_sem,
+):
+    step = pl.program_id(0)
+
+    def loads(at):
+        cols = pl.ds(pl.multiple_of(hidden_block(at) * HIDDEN, HIDDEN), HIDDEN)
+        place = lax.rem(at, 2)
+        return (
+            pltpu.make_async_copy(up_ref.at[:, cols], up_part.at[place], load_sem.at[0, place]),
+            pltpu.make_async_copy(down_ref.at[:, cols], down_part.at[place], load_sem.at[1, place]),
+        )
+
+    @pl.when(step == 0)
+    def _():
+        for copy in loads(step):
+            copy.start()
+        rows_t[...] = rows_ref[...].T
+        cot_t[...] = cot_ref[...].T
+        total[...] = base_ref[...]
+        grad_rows_ref[...] = jnp.zeros_like(grad_rows_ref)
+
+    for copy in loads(step):
+        copy.wait()
+
+    @pl.when(step < HIDDEN_STEPS - 1)
+    def _():
+        for copy in loads(step + 1):
+            copy.start()
+
+    place = lax.rem(step, 2)
+    up = up_part[place]
+    down = down_part[place]
+    bias = bias_ref[...]
+    bias_sum = jnp.zeros((1, HIDDEN), jnp.float32)
+    for index in range(LEN // CHUNK):
+        here = slice(index * CHUNK, index * CHUNK + CHUNK)
+        value, slope = gelu_both(mul(rows_ref[here], up) + bias)
+        value = value.astype(jnp.bfloat16)
+        grads = (slope * mul(cot_ref[here], down)).astype(jnp.bfloat16)
+        active[here] = value
+        grad_before[here] = grads
+        bias_sum += jnp.sum(grads.astype(jnp.float32), axis=0, keepdims=True)
+        total[here] += dot_last(value, down)
+        grad_rows_ref[here] += dot_last(grads, up)
+    bias_sum_ref[...] = bias_sum
+    grad_down_ref[...] = mul(cot_t[...], active[...]).astype(jnp.bfloat16)
+    grad_up_ref[...] = mul(rows_t[...], grad_before[...]).astype(jnp.bfloat16)
+
+    @pl.when(step == HIDDEN_STEPS - 1)
+    def _():
+        block_ref[...] = total[...].astype(jnp.bfloat16)
+
+
+def mlp_both(rows, cot, base, bias, up, down):
+    anywhere = pl.BlockSpec(memory_space=pl.ANY)
+    whole = pl.BlockSpec((LEN, D), lambda s: (0, 0))
+    hidden = pl.BlockSpec((D, HIDDEN), lambda s: (0, hidden_block(s)))
+    hidden_row = pl.BlockSpec((1, HIDDEN), lambda s: (0, hidden_block(s)))
+    part = pltpu.VMEM((2, D, HIDDEN), jnp.bfloat16)
+    low = jnp.bfloat16
     return pl.pallas_call(
-        attend_bwd_kernel,
-        grid=(PAIRS,),
-        in_specs=[PACKED_COLS, PAIR_COLS, PAIR_COLS, PAIR_GRID, PAIR_STAT],
-        out_specs=PACKED_COLS,
-        out_shape=jax.ShapeDtypeStruct((LEN, 3 * D), jnp.bfloat16),
+        mlp_kernel,
+        grid=(HIDDEN_STEPS,),
+        in_specs=[whole, whole, whole, hidden_row, anywhere, anywhere],
+        out_specs=[whole, whole, hidden, hidden, hidden_row],
+        out_shape=[
+            jax.ShapeDtypeStruct((LEN, D), low),
+            jax.ShapeDtypeStruct((LEN, D), jnp.float32),
+            jax.ShapeDtypeStruct((D, FF), low),
+            jax.ShapeDtypeStruct((D, FF), low),
+            jax.ShapeDtypeStruct((1, FF), jnp.float32),
+        ],
         scratch_shapes=[
-            pltpu.VMEM((PAIR, LEN), jnp.float32),
-            pltpu.VMEM((LEN, PAIR), jnp.float32),
-            pltpu.VMEM((LEN, PAIR), jnp.float32),
+            pltpu.VMEM((D, LEN), low),
+            pltpu.VMEM((D, LEN), low),
+            pltpu.VMEM((LEN, D), jnp.float32),
+            part,
+            part,
+            pltpu.VMEM((LEN, HIDDEN), low),
+            pltpu.VMEM((LEN, HIDDEN), low),
+            pltpu.SemaphoreType.DMA((2, 2)),
         ],
         compiler_params=pltpu.CompilerParams(vmem_limit_bytes=VMEM_LIMIT),
-        cost_estimate=pl.CostEstimate(flops=32 * LEN * LEN * D, bytes_accessed=50 * 1024 * 1024, transcendentals=0),
-    )(packed, context, grad_context, exps, stats)
+        cost_estimate=pl.CostEstimate(
+            flops=12 * LEN * D * FF, bytes_accessed=60 * 1024 * 1024, transcendentals=LEN * FF
+        ),
+    )(rows, cot, base, bias, up, down)
 
 
 SLOTS = 12
@@ -1052,6 +1130,7 @@
     ctx_ref,
     exps_ref,
     stat_ref,
+    normed_t_ref,
     out_ref,
     up_ref,
     down_ref,
@@ -1081,6 +1160,7 @@
     def _():
         greet_neighbours([spread.sibling, spread.beside, spread.across] + spread.stations)
         spread.begin()
+        normed_t_ref[...] = normed_ref[...].T
         layout_grid(starts_ref, dist_ref)
 
     for index in range(1, PAIRS):
@@ -1122,7 +1202,7 @@
 
 def attend_spread(starts, slopes, normed, weights, shifts, slots, cotangent):
     anywhere = pl.BlockSpec(memory_space=pl.ANY)
-    packed, context, exps, stats, out, up, down, got = pl.pallas_call(
+    packed, context, exps, stats, normed_t, out, up, down, got = pl.pallas_call(
         attend_spread_kernel,
         grid=(PAIRS,),
         in_specs=[
@@ -1134,12 +1214,14 @@
             anywhere,
             anywhere,
         ],
-        out_specs=[PACKED_COLS, PAIR_COLS, PAIR_GRID, PAIR_STAT] + [anywhere] * 4,
+        out_specs=[PACKED_COLS, PAIR_COLS, PAIR_GRID, PAIR_STAT, pl.BlockSpec((D, LEN), lambda p: (0, 0))]
+        + [anywhere] * 4,
         out_shape=[
             jax.ShapeDtypeStruct((LEN, 3 * D), jnp.bfloat16),
             jax.ShapeDtypeStruct((LEN, D), jnp.bfloat16),
             jax.ShapeDtypeStruct((H, LEN, LEN), jnp.bfloat16),
             jax.ShapeDtypeStruct((PAIRS, 2, LEN), jnp.float32),
+            jax.ShapeDtypeStruct((D, LEN), jnp.bfloat16),
             whole_shape(D),
             whole_shape(FF),
             whole_shape(FF),
@@ -1156,34 +1238,64 @@
         ),
     )(starts, slopes, normed, weights, shifts, slots, cotangent)
     wholes = out.reshape(D, D), up.reshape(D, FF), down.reshape(D, FF)
-    return packed, context, exps, stats, wholes, got
-
-
-GROUP_SLOTS = (3, 1, 4, 4)
+    return packed, context, exps, stats, normed_t, wholes, got
+
+
 LAG = 2
-
-
-def sum_kernel(
-    qkv_ref,
-    out_ref,
+ORDER = (4, 8, 5, 9, 6, 10, 7, 11, 3, 0, 1, 2)
+READY = 9
+RING = 4
+
+
+def attend_bwd_half(half, scale, values, keys_t, parts, exps, sums):
+    half_t, half_rows, half_queries, inner = parts
+    dq_t, dk_sum, dv_sum = sums
+    heads = slice(half * HD, half * HD + HD)
+    for block in range(LEN // QB):
+        span = min(LEN, QB * block + QB + PIECE)
+        cols = slice(block * QB, block * QB + QB)
+        weights = exps[:span, cols]
+        grad_probs = mul(values[:span], half_t[:, cols])
+        grad_scores = (weights.astype(jnp.float32) * (grad_probs - inner[:, cols])).astype(jnp.bfloat16)
+        dv_sum[:span, :] += mul(weights, half_rows[cols])
+        dk_sum[:span, :] += mul(grad_scores, half_queries[cols])
+        dq_t[heads, cols] = mul(keys_t[heads, :span], grad_scores) * scale
+
+
+def attend_sum_kernel(
+    packed_ref,
+    ctx_ref,
+    grad_ref,
+    stat_ref,
+    weights_ref,
+    normed_t_ref,
+    exps_ref,
     up_ref,
     down_ref,
+    out_ref,
     total_ref,
+    grad_normed_ref,
+    packed_sum_ref,
+    exps,
+    dq_t,
+    dk_sum,
+    dv_sum,
+    grad_qkv,
     mine,
     first,
     second_y,
     second_x,
     third,
     fourth,
+    exps_sem,
     load_sem,
     send_sem,
     recv_sem,
 ):
+    pair = pl.program_id(0)
     (z, x, core, y), sibling, beside, across, stations = neighbours()
     low_cols = pl.ds(0, HALF_SLOT)
     high_cols = pl.ds(HALF_SLOT, HALF_SLOT)
-
-    greet_neighbours([sibling, beside, across] + stations)
 
     def remote(source, target, stage, slot, place):
         return pltpu.make_async_remote_copy(
@@ -1195,16 +1307,26 @@
             device_id_type=MESH_IDS,
         )
 
-    slot = 0
-    for ref, number in zip((qkv_ref, out_ref, up_ref, down_ref), GROUP_SLOTS):
-        for index in range(number):
-            for part in (0, 1):
-                cols = pl.ds((part * number + index) * SLOT, SLOT)
-                remote(ref.at[:, :, 1 - core, :, cols], first.at[slot, part], 0, slot, sibling).start()
-                pltpu.make_async_copy(
-                    ref.at[:, :, core, :, cols], mine.at[slot, part], load_sem.at[slot]
-                ).start()
-            slot += 1
+    def source(slot, part):
+        kind = ORDER[slot]
+        if kind < 3:
+            ref, column = grad_qkv, (part * 3 + kind) * SLOT
+        elif kind == 3:
+            ref, column = out_ref, part * SLOT
+        else:
+            ref = up_ref if kind < 8 else down_ref
+            column = (part * 4 + kind % 4) * SLOT
+        return ref, pl.ds(column, SLOT)
+
+    def load(slot, part):
+        ref, cols = source(slot, part)
+        place = slot % RING
+        return pltpu.make_async_copy(ref.at[:, :, core, :, cols], mine.at[place, part], load_sem.at[place])
+
+    def send_first(slot):
+        for part in (0, 1):
+            ref, cols = source(slot, part)
+            remote(ref.at[:, :, 1 - core, :, cols], first.at[slot, part], 0, slot, sibling).start()
 
     def second_copies(slot):
         return (
@@ -1219,23 +1341,33 @@
         )
 
     def fourth_copies(slot):
-        return [
+        return tuple(
             remote(third.at[slot, lax.rem(z + hop, 4)], fourth.at[slot, hop - 1], 4 + hop, slot, place)
             for hop, place in zip((1, 2, 3), stations)
-        ]
+        )
 
     def landed(ref, stage, slot):
         pltpu.make_async_copy(ref, ref, recv_sem.at[stage, slot]).wait()
 
-    def step(index, carry):
-        @pl.when(index < SLOTS)
-        def _():
-            slot = index
-            pltpu.make_async_copy(mine.at[slot], mine.at[slot], load_sem.at[slot]).wait()
-            landed(first.at[slot], 0, slot)
-            first[slot] = first[slot] + mine[slot]
-            for copy in second_copies(slot):
-                copy.start()
+    def tick(index):
+        for slot in range(SLOTS):
+
+            @pl.when(index == slot)
+            def _(slot=slot):
+                landed(first.at[slot], 0, slot)
+                if slot < READY:
+                    place = slot % RING
+                    pltpu.make_async_copy(mine.at[place], mine.at[place], load_sem.at[place]).wait()
+                    first[slot] = first[slot] + mine[place]
+                    if slot + RING < READY:
+                        for part in (0, 1):
+                            load(slot + RING, part).start()
+                else:
+                    for part in (0, 1):
+                        _, cols = source(slot, part)
+                        first[slot, part] = first[slot, part] + grad_qkv[:, :, core, :, cols]
+                for copy in second_copies(slot):
+                    copy.start()
 
         @pl.when((index >= LAG) & (index < SLOTS + LAG))
         def _():
@@ -1266,45 +1398,125 @@
                 total = total + fourth[slot, hop - 1].astype(jnp.float32)
             total_ref[slot] = total
 
-        return carry
-
-    lax.fori_loop(0, SLOTS + 3 * LAG, step, 0)
-
-    def sent(slot, carry):
-        pltpu.make_async_copy(mine.at[slot], mine.at[slot], send_sem.at[0, slot]).wait()
-        for copy in second_copies(slot) + third_copies(slot) + tuple(fourth_copies(slot)):
-            copy.wait_send()
-        return carry
-
-    lax.fori_loop(0, SLOTS, sent, 0)
-
-
-def sum_over_devices(grads):
+    def exps_load(head, half):
+        return pltpu.make_async_copy(exps_ref.at[head], exps.at[half], exps_sem.at[half])
+
+    @pl.when(pair == 0)
+    def _():
+        for half in (0, 1):
+            exps_load(half, half).start()
+        for slot in range(RING):
+            for part in (0, 1):
+                load(slot, part).start()
+        greet_neighbours([sibling, beside, across] + stations)
+        for slot in range(READY):
+            send_first(slot)
+        grad_normed_ref[...] = jnp.zeros_like(grad_normed_ref)
+
+    scale = 1.0 / math.sqrt(HD)
+    queries = packed_ref[:, :PAIR]
+    keys_t = packed_ref[:, PAIR : 2 * PAIR].T
+    values = packed_ref[:, 2 * PAIR :]
+    grads_t = grad_ref[...].T.astype(jnp.float32)
+    context_t = ctx_ref[...].T.astype(jnp.float32)
+    scaled = []
+    inner_rows = []
+    for half in (0, 1):
+        heads = slice(half * HD, half * HD + HD)
+        scaled.append(grads_t[heads] * stat_ref[0, half : half + 1, :])
+        inner_rows.append(jnp.sum(scaled[half] * context_t[heads], axis=0, keepdims=True))
+    scaled_t = jnp.concatenate(scaled, axis=0).astype(jnp.bfloat16)
+    scaled_rows = scaled_t.T
+    dk_sum[...] = jnp.zeros_like(dk_sum)
+    dv_sum[...] = jnp.zeros_like(dv_sum)
+    for half in (0, 1):
+        exps_load(2 * pair + half, half).wait()
+        parts = (
+            only_rows(scaled_t, half),
+            only_cols(scaled_rows, half),
+            only_cols(queries, half),
+            inner_rows[half],
+        )
+        attend_bwd_half(half, scale, values, keys_t, parts, exps.at[half], (dq_t, dk_sum, dv_sum))
+
+        @pl.when(pair < PAIRS - 1)
+        def _(half=half):
+            exps_load(2 * pair + 2 + half, half).start()
+
+        if half == 0:
+            tick(pair)
+    grads = jnp.concatenate([dq_t[...].T, dk_sum[...] * scale, dv_sum[...]], axis=1).astype(jnp.bfloat16)
+    packed_sum_ref[...] = jnp.sum(grads.astype(jnp.float32), axis=0, keepdims=True)
+    cols = pl.ds(pl.multiple_of(pair * (3 * PAIR), PAIR), 3 * PAIR)
+    grad_weights = mul(normed_t_ref[...], grads).astype(jnp.bfloat16)
+    grad_qkv[:, :, :, :, cols] = grad_weights.reshape(4, 2, 2, 64, 3 * PAIR)
+    grad_normed_ref[...] += dot_last(grads, weights_ref[...])
+
+    @pl.when(pair == PAIRS - 1)
+    def _():
+        for slot in range(READY, SLOTS):
+            send_first(slot)
+
+        def late(index, carry):
+            tick(index)
+            return carry
+
+        lax.fori_loop(PAIRS, SLOTS + 3 * LAG, late, 0)
+
+        def sent(slot, carry):
+            pltpu.make_async_copy(first.at[slot], first.at[slot], send_sem.at[0, slot]).wait()
+            for copy in second_copies(slot) + third_copies(slot) + fourth_copies(slot):
+                copy.wait_send()
+            return carry
+
+        lax.fori_loop(0, SLOTS, sent, 0)
+
+
+def attend_sum(packed, context, grad_context, stats, weights, normed_t, exps, grad_up, grad_down, grad_out):
+    anywhere = pl.BlockSpec(memory_space=pl.ANY)
     rows = 64
-    refs = [grad.reshape(4, 2, 2, rows, grad.shape[-1]) for grad in grads]
-    part = (SLOTS, 2, 4, 2, rows, SLOT)
-    anywhere = pl.BlockSpec(memory_space=pl.ANY)
+    low = jnp.bfloat16
+    once = pl.Buffered(1)
+    tall = pl.BlockSpec((LEN, D), lambda p: (0, 0), pipeline_mode=once)
+    split = [grad.reshape(4, 2, 2, rows, grad.shape[-1]) for grad in (grad_up, grad_down, grad_out)]
     return pl.pallas_call(
-        sum_kernel,
-        in_specs=[anywhere] * 4,
-        out_specs=pl.BlockSpec(memory_space=pltpu.VMEM),
-        out_shape=jax.ShapeDtypeStruct((SLOTS, rows, SLOT), jnp.float32),
+        attend_sum_kernel,
+        grid=(PAIRS,),
+        in_specs=[PACKED_COLS, PAIR_COLS, PAIR_COLS, PAIR_STAT, PACKED_COLS, tall] + [anywhere] * 4,
+        out_specs=[
+            pl.BlockSpec((SLOTS, rows, SLOT), lambda p: (0, 0, 0), pipeline_mode=once),
+            tall,
+            pl.BlockSpec((1, 3 * PAIR), lambda p: (0, p)),
+        ],
+        out_shape=[
+            jax.ShapeDtypeStruct((SLOTS, rows, SLOT), jnp.float32),
+            jax.ShapeDtypeStruct((LEN, D), jnp.float32),
+            jax.ShapeDtypeStruct((1, 3 * D), jnp.float32),
+        ],
         scratch_shapes=[
-            pltpu.VMEM(part, jnp.bfloat16),
-            pltpu.VMEM(part, jnp.bfloat16),
-            pltpu.VMEM((SLOTS, 4, 2, rows, HALF_SLOT), jnp.bfloat16),
-            pltpu.VMEM((SLOTS, 2, 4, rows, HALF_SLOT), jnp.bfloat16),
-            pltpu.VMEM((SLOTS, 4, rows, SLOT), jnp.bfloat16),
-            pltpu.VMEM((SLOTS, 3, rows, SLOT), jnp.bfloat16),
-            pltpu.SemaphoreType.DMA((SLOTS,)),
+            pltpu.VMEM((2, LEN, LEN), low),
+            pltpu.VMEM((PAIR, LEN), jnp.float32),
+            pltpu.VMEM((LEN, PAIR), jnp.float32),
+            pltpu.VMEM((LEN, PAIR), jnp.float32),
+            pltpu.VMEM((4, 2, 2, rows, 3 * D), low),
+            pltpu.VMEM((RING, 2, 4, 2, rows, SLOT), low),
+            pltpu.VMEM((SLOTS, 2, 4, 2, rows, SLOT), low),
+            pltpu.VMEM((SLOTS, 4, 2, rows, HALF_SLOT), low),
+            pltpu.VMEM((SLOTS, 2, 4, rows, HALF_SLOT), low),
+            pltpu.VMEM((SLOTS, 4, rows, SLOT), low),
+            pltpu.VMEM((SLOTS, 3, rows, SLOT), low),
+            pltpu.SemaphoreType.DMA((2,)),
+            pltpu.SemaphoreType.DMA((RING,)),
             pltpu.SemaphoreType.DMA((8, SLOTS)),
             pltpu.SemaphoreType.DMA((8, SLOTS)),
         ],
         compiler_params=pltpu.CompilerParams(
-            collective_id=2, has_side_effects=True, vmem_limit_bytes=VMEM_LIMIT
+            collective_id=2, has_side_effects=True, vmem_limit_bytes=62 * 1024 * 1024
         ),
-        cost_estimate=pl.CostEstimate(flops=0, bytes_accessed=300 * 1024 * 1024, transcendentals=0),
-    )(*refs)
+        cost_estimate=pl.CostEstimate(
+            flops=44 * LEN * LEN * D, bytes_accessed=400 * 1024 * 1024, transcendentals=0
+        ),
+    )(packed, context, grad_context, stats, weights, normed_t, exps, *split)
 
 
 def narrow(rows):
@@ -1367,7 +1579,7 @@
     later_slots = jnp.concatenate(
         [narrow(w_out).T[None], by_slots(narrow(w_up)), by_slots(narrow(w_down).T)]
     )
-    packed, context, exps, stats, wholes, other_cotangent = attend_spread(
+    packed, context, exps, stats, normed_t, wholes, other_cotangent = attend_spread(
         starts, slopes, normed_one, full_qkv, shifts, later_slots, cotangent
     )
     full_out, full_up, full_down = wholes
@@ -1376,30 +1588,25 @@
 
     middle = token_rows + contract(context, full_out, 1, 1) + vectors[4]
     normed_two = narrow(layer_norm(middle, vectors[5], vectors[6]))
-    before = contract(normed_two, full_up, 1, 0) + vectors[7:11].reshape(FF)
-    activated = narrow(gelu_tanh(before))
-    block_rows = narrow(middle + contract(activated, full_down, 1, 1) + vectors[11])
+    block_rows, grad_normed_two, grad_up, grad_down, up_bias = mlp_both(
+        normed_two, cotangent_low, middle + vectors[11], vectors[7:11].reshape(1, FF), full_up, full_down
+    )
     output_pair = swap_halves(block_rows, rank)
-
-    grad_down = narrow(contract(cotangent_low, activated, 0, 0))
-    gelu_pull = jax.vjp(gelu_tanh, before)[1]
-    grad_before = narrow(gelu_pull(contract(cotangent_low, full_down, 1, 0))[0])
-    grad_up = narrow(contract(normed_two, grad_before, 0, 0))
     second_pull = jax.vjp(layer_norm, middle, vectors[5], vectors[6])[1]
-    middle_from_norm, gain_two_grad, shift_two_grad = second_pull(contract(grad_before, full_up, 1, 1))
+    middle_from_norm, gain_two_grad, shift_two_grad = second_pull(grad_normed_two)
     grad_middle = cotangent_rows + middle_from_norm
     grad_middle_low = narrow(grad_middle)
     grad_out = narrow(contract(grad_middle_low, context, 0, 0))
     grad_context = narrow(contract(grad_middle_low, full_out, 1, 0))
-    grad_packed = attention_backward(packed, context, grad_context, exps, stats)
-    grad_qkv = narrow(contract(normed_one, grad_packed, 0, 0))
-    sums = sum_over_devices((grad_qkv, grad_out, grad_up, grad_down))
+    sums, grad_normed_one, packed_grads = attend_sum(
+        packed, context, grad_context, stats, full_qkv, normed_t, exps, grad_up, grad_down, grad_out
+    )
     first_pull = jax.vjp(layer_norm, token_rows, vectors[0], vectors[1])[1]
-    token_from_norm, gain_one_grad, shift_one_grad = first_pull(contract(grad_packed, full_qkv, 1, 1))
+    token_from_norm, gain_one_grad, shift_one_grad = first_pull(grad_normed_one)
     grad_token_rows = grad_middle + token_from_norm
     token_pair = swap_halves(narrow(grad_token_rows), rank).astype(jnp.float32)
 
-    packed_sums = from_pairs(jnp.sum(grad_packed, axis=0, dtype=jnp.float32)[None])[:, 0]
+    packed_sums = from_pairs(packed_grads)[:, 0]
     vector_total = jnp.concatenate(
         [
             jnp.stack(
@@ -1413,15 +1620,15 @@
                     shift_two_grad,
                 ]
             ),
-            jnp.sum(grad_before, axis=0, dtype=jnp.float32).reshape(4, D),
+            up_bias.reshape(4, D),
             jnp.sum(cotangent_rows, axis=0)[None],
         ]
     )
     shards = (
-        from_pairs(from_slots(sums[0:3])),
-        sums[3].T,
-        from_slots(sums[4:8]),
-        from_slots(sums[8:12]).T,
+        from_pairs(from_slots(sums[9:12])),
+        sums[8].T,
+        from_slots(sums[0:8:2]),
+        from_slots(sums[1:8:2]).T,
     )
     outputs = muon_step(shards, vector_total, w_qkv, w_out, w_up, w_down, vectors, m_qkv, m_out, m_up, m_down, m_vec)
     return (output_pair, token_pair) + outputs

time: 710 us -> 650 us (0.915)
  matrix products: 145 us -> 13.3 us
  Pallas kernels: 469 us -> 529 us
  other arithmetic: 56.2 us -> 68.3 us
    dot_general x11 -> x3, matrix products: 145 us -> 13.3 us  [contract(): lax.dot_general(left, right, (((left_dim,), (right_dim,)), ((), ())), pre...]
    pallas_call x2, Pallas kernels: 159 us -> 202 us  [the longest x1 132 us: attend_sum(): pl.pallas_call(attend_sum_kernel, grid=(PAIRS,), in_specs=[PACKED_COLS, P...]
    pallas_call x1, Pallas kernels: 123 us -> 139 us  [muon_call(): pl.pallas_call(muon_kernel, in_specs=[vmem, vmem], out_specs=[vmem, vmem]...]
    reduce_sum x1, other arithmetic: 3.38 us -> 12.8 us  [layer_norm(): centered = inputs - average]
    reduce_sum x1 -> x3, other arithmetic: 4.03 us -> 12 us  [layer_norm(): return centered * lax.rsqrt(variance + NORM_EPSILON) * gain_row + shift_row]
    convert_element_type x8 -> x7, other arithmetic: 15.6 us -> 9.5 us  [narrow(): return rows.astype(jnp.bfloat16)]
  transfers between devices with their start and end apart: 2 -> 2, of which waited for: 0 -> 0; matrix products, arithmetic and copies ran while one was open for 15% -> 5% of each run, Pallas kernels for 36% -> 22%
where the time goes in v5:
time: 650 us; the launch traced here: 638 us
  Pallas kernels  529 us (81%)
  other arithmetic  68.3 us (11%)
  local copies, waits for them, and re-layouts  24.3 us (4%)
  matrix products  13.3 us (2%)
    pallas_call x1, Pallas kernels, muon_call(): pl.pallas_call(muon_kernel, in_specs=[vmem, vmem], out_specs=[vmem, vmem]...  139 us
    pallas_call x1, Pallas kernels, attend_sum(): pl.pallas_call(attend_sum_kernel, grid=(PAIRS,), in_specs=[PACKED_COLS, P...  132 us
    pallas_call x1, Pallas kernels, attend_spread(): pl.pallas_call(attend_spread_kernel, grid=(PAIRS,), in_specs=[SCALARS, SC...  130 us
    pallas_call x1, Pallas kernels, mlp_both(): pl.pallas_call(mlp_kernel, grid=(HIDDEN_STEPS,), in_specs=[whole, whole,...  70.3 us
    pallas_call x1, Pallas kernels, first_spread(): pl.pallas_call(first_spread_kernel, in_specs=[anywhere] * 2, out_specs=[a...  57.3 us
    dot_general x3, matrix products, contract(): lax.dot_general(left, right, (((left_dim,), (right_dim,)), ((), ())), pre...  13.3 us
  transfers between devices with their start and end apart: 2, of which 0 were waited for; matrix products, arithmetic and copies ran while one was open for 5% of the time, Pallas kernels for 22%

profile of v5, /device:TPU:9, one launch (start us, length us, event | category | flops | bytes accessed | tf_op | source)
XLA Modules:
  0.0 638.0 jit_solution(11004746803740220845)
XLA Ops:
  0.7 0.5 multiply_exponential_fusion.slopes_ref
  1.2 1.0 fusion.25
  2.3 0.8 slice_bitcast_fusion.4
  3.1 1.0 convert_element_type.80
  4.6 0.7 copy.68
  5.3 57.3 %shard_map.260 = (bf16[4,2,2,64,3072]{4,3,2,1,0:T(8,128)(2,1)}, bf16[512,1024]{1,0:T(8,128)(2,1)}) custom-call(bf16[3,64,512]{2,1,0:T(8,128)(2,1)} %bitcast.151, bf16[2,512,1024]{2,1,0:T(8,128)(2,1)} %tokens_ref.1), custom_call_target="tpu_custom_call" | custom-call | tf_op jit(solution)/shard_map/pallas_call | solution.py:1192
  62.6 2.8 dynamic-slice_bitcast_fusion.2
  65.4 0.6 convert_reduce_fusion
  66.0 2.5 fusion.9
  68.6 0.5 fusion.17.starts_ref
  69.3 0.6 reshape.194.shifts_ref
  70.0 1.1 convert_element_type.85
  71.1 3.5 fusion.7.normed_ref
  74.6 0.9 pad_maximum_fusion.1.slots_ref
  75.5 130.1 %shard_map.261 = (bf16[1024,3072]{1,0:T(8,128)(2,1)}, bf16[1024,1024]{1,0:T(8,128)(2,1)}, bf16[16,1024,1024]{2,1,0:T(8,128)(2,1)}, f32[8,2,1024]{2,1,0:T(2,128)}...) custom-call(s32[2]{0:T(128)} %fusion.17.starts_ref, ...), custom_call_target="tpu_custom_call" | custom-call | flops 17179869184 | bytes 94371840 | tf_op jit(solution)/shard_map/pallas_call | solution.py:1205
  205.6 5.2 fusion.26
  210.9 0.6 multiply_reduce_fusion.2
  211.4 0.6 copy.56
  212.1 0.3 copy-done.20
  212.4 2.4 maximum_select_fusion.1.cot_ref
  214.7 3.3 broadcast_add_fusion
  218.0 70.3 %shard_map.262 = (bf16[1024,1024]{1,0:T(8,128)(2,1)}, f32[1024,1024]{1,0:T(8,128)}, bf16[1024,4096]{1,0:T(8,128)(2,1)}, bf16[1024,4096]{1,0:T(8,128)(2,1)}, f32[1,4096]{1,0:T(1,128)}) custom-call(bf16[1024,1024]{1,0:T(8,128)(2,1)} %get-tuple-element.83.rows_ref, bf16[1024,1024]{1,0:T(8,128)(2,1)} %maximum_select_fusion.1.cot_ref, ...), custom_call_target="tpu_custom_call" | custom-call | flops 51539607552 | bytes 62914560 | tf_op jit(solution)/shard_map/pallas_call | solution.py:583
  288.4 3.9 multiply_reduce_fusion
  292.3 12.8 %fusion.24 = (f32[1024]{0:T(1024)S(1)}, f32[1024,1024]{1,0:T(8,128)S(1)}) fusion(f32[1024]{0:T(1024)S(1)} %multiply_multiply_fusion.1, f32[1024,1024]{1,0:T(8,128)S(1)} %get-tuple-element.101, f32[1024]{0:T(1024)S(1)} %broadcast_multiply_fusion, f32[1024]{0:T(1024)S(1)} %fusion.16, f32[1024,1024]{1,0:T(8,128)S(1)} %copy-done.7, f32[1024]{0:T(1024)S(1)} %bitcast.161), kind=kLoop, calls=%fused_computation.100 | loop fusion | flops 7339008 | bytes 12603392 | tf_op jit(solution)/shard_map/transpose(jvp())/reduce_sum | solution.py:34
  305.2 4.3 convolution_convert_fusion
  309.5 3.7 convolution_convert_fusion.1.grad_ref
  313.3 131.7 %shard_map.263 = (f32[12,64,512]{2,1,0:T(8,128)}, f32[1024,1024]{1,0:T(8,128)}, f32[1,3072]{1,0:T(1,128)}) custom-call(bf16[1024,3072]{1,0:T(8,128)(2,1)} %get-tuple-element.47.packed_ref, bf16[1024,1024]{1,0:T(8,128)(2,1)} %get-tuple-element.40.ctx_ref, bf16[1024,1024]{1,0:T(8,128)(2,1)} %convolution_convert_fusion.1.grad_ref, ...), custom_call_target="tpu_custom_call" | custom-call | flops 47244640256 | bytes 419430400 | tf_op jit(solution)/shard_map/pallas_call | solution.py:1482
  445.0 3.8 fusion.20
  448.8 0.5 copy-done.4
  449.4 4.3 fusion.8
  453.7 5.4 convert_reduce_fusion.1
  459.1 2.8 dynamic-slice_bitcast_fusion
  461.9 2.7 dynamic-slice_bitcast_fusion.1
  464.6 1.5 collective-permute-start
  466.1 1.0 slice_bitcast_fusion
  467.1 0.6 constant_dynamic-update-slice_fusion.8
  467.7 0.5 broadcast.156
  468.3 0.7 reduce.3
  469.0 0.6 constant_dynamic-update-slice_fusion.7
  469.6 0.6 constant_dynamic-update-slice_fusion.6
  470.2 0.6 constant_dynamic-update-slice_fusion.5
  470.8 0.3 copy.38
  471.0 0.3 reshape_reshape.7
  471.7 1.2 copy.53
  473.0 2.1 fusion.23
  475.2 0.9 fusion.22
  476.2 1.6 convert_bitcast_fusion.2
  477.8 0.6 constant_dynamic-update-slice_fusion.4
  478.4 0.6 constant_dynamic-update-slice_fusion.3
  479.0 0.6 constant_dynamic-update-slice_fusion.2
  479.6 0.6 constant_dynamic-update-slice_fusion.1
  480.2 0.6 constant_dynamic-update-slice_fusion.vec_ref
  480.8 0.8 fusion.21
  481.7 1.0 pad_maximum_fusion.moments_ref
  482.7 139.4 %shard_map.264 = (bf16[12,64,512]{2,1,0:T(8,128)(2,1)}, f32[12,8,128]{2,1,0:T(8,128)}) custom-call(bf16[12,64,512]{2,1,0:T(8,128)(2,1)} %pad_maximum_fusion.moments_ref, f32[12,8,128]{2,1,0:T(8,128)} %constant_dynamic-update-slice_fusion.vec_ref), custom_call_target="tpu_custom_call" | custom-call | flops 25769803776 | bytes 4194304 | tf_op jit(solution)/shard_map/pallas_call | solution.py:880
  622.2 1.3 convert_bitcast_fusion
  623.4 1.5 bitcast_subtract_fusion.1
  624.9 0.8 pad.26
  625.9 0.7 multiply_subtract_fusion.1
  626.7 0.9 sub.50
  627.6 1.7 multiply_subtract_fusion
  629.3 0.8 bitcast_subtract_fusion
  630.2 4.1 fusion.12
  634.3 3.3 maximum_select_fusion.2
  (116 shorter events, 1.5 us)
Async XLA Ops:
  0.7 68.0 %copy-start = (s32[2,1,2]{2,1,0:T(1,128)S(1)}, s32[2,1,2]{2,1,0:T(1,128)}, u32[]{:S(2)}) copy-start(s32[2,1,2]{2,1,0:T(1,128)} %param.15) | copy-start | bytes 52
  2.2 68.9 %copy-start.31 = (f32[1,1024]{1,0:T(1,128)}, f32[1,1024]{1,0:T(1,128)S(1)}, u32[]{:S(2)}) copy-start(f32[1,1024]{1,0:T(1,128)S(1)} %get-tuple-element.99) | copy-start | bytes 12292
  62.6 2.8 copy-start.2
  62.6 7.4 %copy-start.11 = (f32[64,2048]{1,0:T(8,128)S(1)}, f32[64,2048]{1,0:T(8,128)}, u32[]{:S(2)}) copy-start(f32[64,2048]{1,0:T(8,128)} %param.18) | copy-start | bytes 1572868
  62.6 8.5 %copy-start.22 = (f32[512,64]{0,1:T(8,128)S(1)}, f32[512,64]{0,1:T(8,128)}, u32[]{:S(2)}) copy-start(f32[512,64]{0,1:T(8,128)} %param.17) | copy-start | bytes 393220
  66.0 8.6 %copy-start.28 = (f32[1024]{0:T(1024)}, f32[1024]{0:T(1024)S(1)}, u32[]{:S(2)}) copy-start(f32[1024]{0:T(1024)S(1)} %broadcast_multiply_fusion.1) | copy-start | bytes 12292
  68.6 137.0 %copy-start.36 = (f32[1024]{0:T(1024)}, f32[1024]{0:T(1024)S(1)}, u32[]{:S(2)}) copy-start(f32[1024]{0:T(1024)S(1)} %fusion.9) | copy-start | bytes 12292
  68.6 137.0 %copy-start.34 = (f32[1024]{0:T(1024)}, f32[1024]{0:T(1024)S(1)}, u32[]{:S(2)}) copy-start(f32[1024]{0:T(1024)S(1)} %fusion.15) | copy-start | bytes 12292
  210.8 1.2 copy-start.10
  210.8 1.5 copy-start.20
  288.4 3.9 copy-start.7
  292.3 12.9 %copy-start.8 = (bf16[1024,1024]{1,0:T(8,128)(2,1)S(1)}, bf16[1024,1024]{1,0:T(8,128)(2,1)}, u32[]{:S(2)}) copy-start(bf16[1024,1024]{1,0:T(8,128)(2,1)} %maximum_select_fusion.1.cot_ref) | copy-start | bytes 6291460
  292.3 12.9 %copy-start.42 = (bf16[1024,1024]{1,0:T(8,128)(2,1)S(1)}, bf16[1024,1024]{1,0:T(8,128)(2,1)}, u32[]{:S(2)}) copy-start(bf16[1024,1024]{1,0:T(8,128)(2,1)} %get-tuple-element.40.ctx_ref) | copy-start | bytes 6291460
  305.1 4.4 copy-start.5
  305.2 4.4 copy-start.41
  313.3 131.7 %copy-start.29 = (f32[1024]{0:T(1024)S(1)}, f32[1024]{0:T(1024)}, u32[]{:S(2)}) copy-start(f32[1024]{0:T(1024)} %copy-done.28) | copy-start | bytes 12292
  313.3 131.7 %copy-start.32 = (f32[1,1024]{1,0:T(1,128)S(1)}, f32[1,1024]{1,0:T(1,128)}, u32[]{:S(2)}) copy-start(f32[1,1024]{1,0:T(1,128)} %copy-done.31) | copy-start | bytes 12292
  445.0 3.8 copy-start.37
  445.0 3.9 copy-start.3
  445.0 4.4 copy-start.4
  445.0 4.4 copy-start.35
  448.8 4.9 copy-start.6
  448.8 4.9 copy-start.9
  459.1 7.0 %copy-start.17 = (f32[12,64,512]{2,1,0:T(8,128)S(1)}, f32[12,64,512]{2,1,0:T(8,128)}, u32[]{:S(2)}) copy-start(f32[12,64,512]{2,1,0:T(8,128)} %get-tuple-element.54) | copy-start | bytes 4718596
  461.9 6.3 copy-start.40
  461.9 168.2 %collective-permute-start.1 = (bf16[512,1024]{1,0:T(8,128)(2,1)}, bf16[512,1024]{1,0:T(8,128)(2,1)}, u32[]{:S(2)}, u32[]{:S(2)}) collective-permute-start(bf16[512,1024]{1,0:T(8,128)(2,1)} %get-tuple-element.85), channel_id=1, source_target_pairs={{0,1},{1,0},{2,3},{3,2},{4,5},{5,4},{6,7},{7,6},{8,9},{9,8},{10,11... | collective-permute-start | bytes 3145736 | tf_op jit(solution)/shard_map/ppermute | solution.py:1540
  464.6 169.7 %collective-permute-start = (bf16[512,1024]{1,0:T(8,128)(2,1)}, bf16[512,1024]{1,0:T(8,128)(2,1)}, u32[]{:S(2)}, u32[]{:S(2)}) collective-permute-start(bf16[512,1024]{1,0:T(8,128)(2,1)} %get-tuple-element.87), channel_id=1, source_target_pairs={{0,1},{1,0},{2,3},{3,2},{4,5},{5,4},{6,7},{7,6},{8,9},{9,8},{10,11... | collective-permute-start | bytes 3145736 | tf_op jit(solution)/shard_map/ppermute | solution.py:1540
  471.4 3.8 copy-start.16
  471.5 4.7 copy-start.30
  471.5 6.4 copy-start.38
  471.7 10.0 %copy-start.19 = (f32[3,64,512]{2,1,0:T(8,128)}, f32[3,64,512]{2,1,0:T(8,128)S(1)}, u32[]{:S(2)}) copy-start(f32[3,64,512]{2,1,0:T(8,128)S(1)} %reshape.204) | copy-start | bytes 1179652
  471.7 3.5 copy-start.21
  471.7 7.9 %copy-start.39 = (f32[1,4096]{1,0:T(1,128)S(1)}, f32[1,4096]{1,0:T(1,128)}, u32[]{:S(2)}) copy-start(f32[1,4096]{1,0:T(1,128)} %get-tuple-element.56) | copy-start | bytes 49156
  471.7 9.1 %copy-start.24 = (f32[3,64,512]{2,1,0:T(8,128)S(1)}, f32[3,64,512]{2,1,0:T(8,128)}, u32[]{:S(2)}) copy-start(f32[3,64,512]{2,1,0:T(8,128)} %param.21) | copy-start | bytes 1179652
  473.0 9.7 %copy-start.14 = (f32[4,8,8,512]{3,2,0,1:T(8,128)}, f32[4,8,8,512]{3,2,0,1:T(8,128)S(1)}, u32[]{:S(2)}) copy-start(f32[4,8,8,512]{3,2,0,1:T(8,128)S(1)} %copy.53) | copy-start | bytes 1572868
  475.2 146.9 %copy-start.15 = (f32[4,8,8,512]{3,2,0,1:T(8,128)}, f32[4,8,8,512]{3,2,0,1:T(8,128)S(1)}, u32[]{:S(2)}) copy-start(f32[4,8,8,512]{3,2,0,1:T(8,128)S(1)} %copy.52) | copy-start | bytes 1572868
  482.7 140.8 %copy-start.23 = (f32[512,64]{0,1:T(8,128)S(1)}, f32[512,64]{0,1:T(8,128)}, u32[]{:S(2)}) copy-start(f32[512,64]{0,1:T(8,128)} %param.17) | copy-start | bytes 393220
  482.7 143.1 %copy-start.33 = (f32[12,1024]{1,0:T(8,128)S(1)}, f32[12,1024]{1,0:T(8,128)}, u32[]{:S(2)}) copy-start(f32[12,1024]{1,0:T(8,128)} %param.25) | copy-start | bytes 147460
  482.7 143.3 %copy-start.27 = (f32[12,1024]{1,0:T(8,128)S(1)}, f32[12,1024]{1,0:T(8,128)}, u32[]{:S(2)}) copy-start(f32[12,1024]{1,0:T(8,128)} %param.20) | copy-start | bytes 147460
  622.1 4.6 copy-start.12
  622.1 5.5 copy-start.18
  622.1 7.2 %copy-start.13 = (f32[2048,64]{0,1:T(8,128)S(1)}, f32[2048,64]{0,1:T(8,128)}, u32[]{:S(2)}) copy-start(f32[2048,64]{0,1:T(8,128)} %param.19) | copy-start | bytes 1572868
  625.8 8.6 %copy-start.26 = (f32[2,8,8,128]{3,1,2,0:T(8,128)}, f32[2,8,8,128]{3,1,2,0:T(8,128)S(1)}, u32[]{:S(2)}) copy-start(f32[2,8,8,128]{3,1,2,0:T(8,128)S(1)} %copy.57) | copy-start | bytes 196612
  625.9 8.4 %copy-start.25 = (f32[12,1024]{1,0:T(8,128)}, f32[12,1024]{1,0:T(8,128)S(1)}, u32[]{:S(2)}) copy-start(f32[12,1024]{1,0:T(8,128)S(1)} %get-tuple-element.69) | copy-start | bytes 147460
  630.2 7.4 %copy-start.1 = (s32[2,1,2]{2,1,0:T(1,128)S(1)}, s32[2,1,2]{2,1,0:T(1,128)}, u32[]{:S(2)}) copy-start(s32[2,1,2]{2,1,0:T(1,128)} %param.15) | copy-start | bytes 52

commit v6 on v5

--- a/solution.py
+++ b/solution.py
@@ -449,7 +449,7 @@
     return jnp.dot(left, right, preferred_element_type=jnp.float32)
 
 
-def attend_pair(pair, slopes_ref, packed, dist_ref, ctx_ref, exps_ref, stat_ref, ctx_t):
+def attend_pair(pair, slopes_ref, packed, dist_ref, ctx_ref, exps_ref, stat_ref, ctx_t, between):
     keys = packed[:, PAIR : 2 * PAIR]
     values_t = packed[:, 2 * PAIR :].T
     queries_t = (packed[:, :PAIR] * (1.0 / math.sqrt(HD))).T
@@ -468,6 +468,8 @@
             exps_ref[half, :span, cols] = low
             ctx_t[heads, cols] = mul(values_t[heads, :span], low) * inverse
             stat_ref[0, half : half + 1, cols] = inverse
+        if half == 0:
+            between()
     ctx_ref[...] = ctx_t[...].T.astype(jnp.bfloat16)
 
 
@@ -478,141 +480,11 @@
 SCALARS = pl.BlockSpec(memory_space=pltpu.SMEM)
 
 
-HIDDEN = 512
-CHUNK = 256
-HIDDEN_STEPS = FF // HIDDEN
-GELU_SLOPE = math.sqrt(2.0 / math.pi)
-GELU_CUBE = 0.044715
-
-
-def dot_last(left, right):
-    return lax.dot_general(left, right, (((1,), (1,)), ((), ())), preferred_element_type=jnp.float32)
-
-
-def gelu_both(rows):
-    square = rows * rows
-    bent = jnp.tanh(rows * (GELU_SLOPE + GELU_SLOPE * GELU_CUBE * square))
-    half = 0.5 + 0.5 * bent
-    slope = half + 0.5 * rows * (1.0 - bent * bent) * (GELU_SLOPE + 3.0 * GELU_SLOPE * GELU_CUBE * square)
-    return rows * half, slope
-
-
-def hidden_block(step):
-    return (step % 2) * (HIDDEN_STEPS // 2) + step // 2
-
-
-def mlp_kernel(
-    rows_ref,
-    cot_ref,
-    base_ref,
-    bias_ref,
-    up_ref,
-    down_ref,
-    block_ref,
-    grad_rows_ref,
-    grad_up_ref,
-    grad_down_ref,
-    bias_sum_ref,
-    rows_t,
-    cot_t,
-    total,
-    up_part,
-    down_part,
-    active,
-    grad_before,
-    load_sem,
-):
-    step = pl.program_id(0)
-
-    def loads(at):
-        cols = pl.ds(pl.multiple_of(hidden_block(at) * HIDDEN, HIDDEN), HIDDEN)
-        place = lax.rem(at, 2)
-        return (
-            pltpu.make_async_copy(up_ref.at[:, cols], up_part.at[place], load_sem.at[0, place]),
-            pltpu.make_async_copy(down_ref.at[:, cols], down_part.at[place], load_sem.at[1, place]),
-        )
-
-    @pl.when(step == 0)
-    def _():
-        for copy in loads(step):
-            copy.start()
-        rows_t[...] = rows_ref[...].T
-        cot_t[...] = cot_ref[...].T
-        total[...] = base_ref[...]
-        grad_rows_ref[...] = jnp.zeros_like(grad_rows_ref)
-
-    for copy in loads(step):
-        copy.wait()
-
-    @pl.when(step < HIDDEN_STEPS - 1)
-    def _():
-        for copy in loads(step + 1):
-            copy.start()
-
-    place = lax.rem(step, 2)
-    up = up_part[place]
-    down = down_part[place]
-    bias = bias_ref[...]
-    bias_sum = jnp.zeros((1, HIDDEN), jnp.float32)
-    for index in range(LEN // CHUNK):
-        here = slice(index * CHUNK, index * CHUNK + CHUNK)
-        value, slope = gelu_both(mul(rows_ref[here], up) + bias)
-        value = value.astype(jnp.bfloat16)
-        grads = (slope * mul(cot_ref[here], down)).astype(jnp.bfloat16)
-        active[here] = value
-        grad_before[here] = grads
-        bias_sum += jnp.sum(grads.astype(jnp.float32), axis=0, keepdims=True)
-        total[here] += dot_last(value, down)
-        grad_rows_ref[here] += dot_last(grads, up)
-    bias_sum_ref[...] = bias_sum
-    grad_down_ref[...] = mul(cot_t[...], active[...]).astype(jnp.bfloat16)
-    grad_up_ref[...] = mul(rows_t[...], grad_before[...]).astype(jnp.bfloat16)
-
-    @pl.when(step == HIDDEN_STEPS - 1)
-    def _():
-        block_ref[...] = total[...].astype(jnp.bfloat16)
-
-
-def mlp_both(rows, cot, base, bias, up, down):
-    anywhere = pl.BlockSpec(memory_space=pl.ANY)
-    whole = pl.BlockSpec((LEN, D), lambda s: (0, 0))
-    hidden = pl.BlockSpec((D, HIDDEN), lambda s: (0, hidden_block(s)))
-    hidden_row = pl.BlockSpec((1, HIDDEN), lambda s: (0, hidden_block(s)))
-    part = pltpu.VMEM((2, D, HIDDEN), jnp.bfloat16)
-    low = jnp.bfloat16
-    return pl.pallas_call(
-        mlp_kernel,
-        grid=(HIDDEN_STEPS,),
-        in_specs=[whole, whole, whole, hidden_row, anywhere, anywhere],
-        out_specs=[whole, whole, hidden, hidden, hidden_row],
-        out_shape=[
-            jax.ShapeDtypeStruct((LEN, D), low),
-            jax.ShapeDtypeStruct((LEN, D), jnp.float32),
-            jax.ShapeDtypeStruct((D, FF), low),
-            jax.ShapeDtypeStruct((D, FF), low),
-            jax.ShapeDtypeStruct((1, FF), jnp.float32),
-        ],
-        scratch_shapes=[
-            pltpu.VMEM((D, LEN), low),
-            pltpu.VMEM((D, LEN), low),
-            pltpu.VMEM((LEN, D), jnp.float32),
-            part,
-            part,
-            pltpu.VMEM((LEN, HIDDEN), low),
-            pltpu.VMEM((LEN, HIDDEN), low),
-            pltpu.SemaphoreType.DMA((2, 2)),
-        ],
-        compiler_params=pltpu.CompilerParams(vmem_limit_bytes=VMEM_LIMIT),
-        cost_estimate=pl.CostEstimate(
-            flops=12 * LEN * D * FF, bytes_accessed=60 * 1024 * 1024, transcendentals=LEN * FF
-        ),
-    )(rows, cot, base, bias, up, down)
-
-
 SLOTS = 12
 SLOT = 512
 HALF_SLOT = SLOT // 2
 TILE = 256
+GRAM_TILES = 5
 MESH_IDS = pl.DeviceIdType.MESH
 
 
@@ -755,33 +627,56 @@
         @pl.when(is_wide)
         def _():
             core = lax.rem(dp_me, 2)
-            half = D // 2
-            mine = pl.ds(pl.multiple_of(core * half, half), half)
-            theirs = pl.ds(pl.multiple_of((1 - core) * half, half), half)
             sibling = (dp_me + 1 - 2 * core, t_me)
             across = (dp_me, 1 - t_me)
 
-            def exchange(stage, place):
-                copy = pltpu.make_async_remote_copy(
-                    src_ref=out_half.at[stage],
-                    dst_ref=in_half.at[stage],
-                    send_sem=half_send.at[stage],
-                    recv_sem=half_recv.at[stage],
+            def tile_at(index, owner):
+                if index == 4:
+                    row, col = jnp.where(owner == 0, 3, 2), 3
+                elif index == 3:
+                    row, col = jnp.where(owner == 0, 0, 2), jnp.where(owner == 0, 3, 2)
+                else:
+                    row, col = owner, owner + index
+                return (
+                    pl.ds(pl.multiple_of(row * TILE, TILE), TILE),
+                    pl.ds(pl.multiple_of(col * TILE, TILE), TILE),
+                )
+
+            def exchange(stage, index, place):
+                return pltpu.make_async_remote_copy(
+                    src_ref=out_half.at[stage, index],
+                    dst_ref=in_half.at[stage, index],
+                    send_sem=half_send.at[stage, index],
+                    recv_sem=half_recv.at[stage, index],
                     device_id=place,
                     device_id_type=MESH_IDS,
                 )
-                copy.start()
-                copy.wait()
-
-            out_half[0] = gram[theirs, :].astype(jnp.bfloat16)
-            exchange(0, sibling)
-            out_half[1] = (gram[mine, :] + in_half[0].astype(jnp.float32)).astype(jnp.bfloat16)
-            exchange(1, across)
-            total = out_half[1].astype(jnp.float32) + in_half[1].astype(jnp.float32)
-            out_half[2] = total.astype(jnp.bfloat16)
-            exchange(2, sibling)
-            gram[mine, :] = out_half[2].astype(jnp.float32)
-            gram[theirs, :] = in_half[2].astype(jnp.float32)
+
+            for index in range(GRAM_TILES):
+                out_half[0, index] = gram[tile_at(index, 1 - core)].astype(jnp.bfloat16)
+                exchange(0, index, sibling).start()
+            for index in range(GRAM_TILES):
+                exchange(0, index, sibling).wait_recv()
+                total = gram[tile_at(index, core)] + in_half[0, index].astype(jnp.float32)
+                out_half[1, index] = total.astype(jnp.bfloat16)
+                exchange(1, index, across).start()
+            for index in range(GRAM_TILES):
+                exchange(1, index, across).wait_recv()
+                total = out_half[1, index].astype(jnp.float32) + in_half[1, index].astype(jnp.float32)
+                out_half[2, index] = total.astype(jnp.bfloat16)
+                exchange(2, index, sibling).start()
+                rows, cols = tile_at(index, core)
+                gram[cols, rows] = out_half[2, index].astype(jnp.float32).T
+                gram[rows, cols] = out_half[2, index].astype(jnp.float32)
+            for index in range(GRAM_TILES):
+                exchange(2, index, sibling).wait_recv()
+                rows, cols = tile_at(index, 1 - core)
+                gram[cols, rows] = in_half[2, index].astype(jnp.float32).T
+                gram[rows, cols] = in_half[2, index].astype(jnp.float32)
+            for index in range(GRAM_TILES):
+                exchange(0, index, sibling).wait_send()
+                exchange(1, index, across).wait_send()
+                exchange(2, index, sibling).wait_send()
 
         def trace_tile(tile, total):
             rows = pl.ds(pl.multiple_of(tile * TILE, TILE), TILE)
@@ -896,13 +791,13 @@
             low,
             low,
             low,
-            pltpu.VMEM((3, D // 2, D), jnp.bfloat16),
-            pltpu.VMEM((3, D // 2, D), jnp.bfloat16),
+            pltpu.VMEM((3, GRAM_TILES, TILE, TILE), jnp.bfloat16),
+            pltpu.VMEM((3, GRAM_TILES, TILE, TILE), jnp.bfloat16),
             pltpu.SemaphoreType.DMA((2,)),
             pltpu.SemaphoreType.DMA((4,)),
             pltpu.SemaphoreType.DMA((4,)),
-            pltpu.SemaphoreType.DMA((3,)),
-            pltpu.SemaphoreType.DMA((3,)),
+            pltpu.SemaphoreType.DMA((3, GRAM_TILES)),
+            pltpu.SemaphoreType.DMA((3, GRAM_TILES)),
         ],
         compiler_params=pltpu.CompilerParams(
             collective_id=1, has_side_effects=True, vmem_limit_bytes=VMEM_LIMIT
@@ -986,6 +881,8 @@
 
 
 SWAP_AT = 2
+EARLY = 2
+AHEAD = 2
 SPREAD_LAG = 1
 
 
@@ -1005,62 +902,61 @@
             device_id_type=MESH_IDS,
         )
 
-    def cols(self, slot, part, start=0, size=SLOT):
-        _, column, distance, _ = self.table[slot]
-        if isinstance(part, int):
-            return pl.ds(column + part * distance + start, size)
-        return pl.ds(pl.multiple_of(column + part * distance + start, 128), size)
-
     def own(self, slot):
-        here = self.table[slot][0].at[self.z, self.x, self.core, :, self.cols(slot, self.y)]
+        here = self.table[slot][0](self.y, 0, SLOT).at[self.z, self.x, self.core]
         return pltpu.make_async_copy(self.slots_ref.at[slot], here, self.local_sem.at[slot])
 
     def along_z(self, slot):
-        here = self.table[slot][0].at[self.z, self.x, self.core, :, self.cols(slot, self.y)]
+        here = self.table[slot][0](self.y, 0, SLOT).at[self.z, self.x, self.core]
         return [
             self.remote(self.slots_ref.at[slot], here, hop, slot, place)
             for hop, place in enumerate(self.stations)
         ]
 
     def second(self, slot):
-        whole, _, _, size = self.table[slot]
+        view, size = self.table[slot]
         copies = []
         if size:
-            part = whole.at[:, self.x, self.core, :, self.cols(slot, self.y, 0, size)]
+            part = view(self.y, 0, size).at[:, self.x, self.core]
             copies.append(self.remote(part, part, 3, slot, self.beside))
         if size < SLOT:
-            part = whole.at[:, self.x, self.core, :, self.cols(slot, self.y, size, SLOT - size)]
+            part = view(self.y, size, SLOT - size).at[:, self.x, self.core]
             copies.append(self.remote(part, part, 4, slot, self.across))
         return copies
 
     def third(self, slot):
-        whole, _, _, size = self.table[slot]
+        view, size = self.table[slot]
         copies = []
         if size:
-            part = whole.at[:, :, self.core, :, self.cols(slot, self.y, 0, size)]
+            part = view(self.y, 0, size).at[:, :, self.core]
             copies.append(self.remote(part, part, 5, slot, self.across))
         if size < SLOT:
             for index in (0, 1):
-                part = whole.at[:, self.x, self.core, :, self.cols(slot, index, size, SLOT - size)]
+                part = view(index, size, SLOT - size).at[:, self.x, self.core]
                 copies.append(self.remote(part, part, 6 + index, slot, self.beside))
         return copies
 
     def fourth(self, slot):
-        whole = self.table[slot][0]
+        view, _ = self.table[slot]
         copies = []
         for index in (0, 1):
-            part = whole.at[:, :, self.core, :, self.cols(slot, index)]
+            part = view(index, 0, SLOT).at[:, :, self.core]
             copies.append(self.remote(part, part, 8 + index, slot, self.sibling))
         return copies
 
-    def begin(self):
-        for slot in range(len(self.table)):
+    def launch(self, slot):
+        if slot < len(self.table):
             self.own(slot).start()
             for copy in self.along_z(slot):
                 copy.start()
 
+    def begin(self):
+        for slot in range(AHEAD):
+            self.launch(slot)
+
     def tick(self, index):
         count = len(self.table)
+        self.launch(index + AHEAD)
         if index < count:
             self.own(index).wait()
             for copy in self.along_z(index):
@@ -1081,12 +977,36 @@
     def ticks(self):
         return len(self.table) + 2 * SPREAD_LAG
 
+    def arrived(self, slot):
+        for copy in self.fourth(slot):
+            copy.wait_recv()
+
+    def sent(self):
+        for slot in range(len(self.table)):
+            for copy in self.along_z(slot) + self.second(slot) + self.third(slot) + self.fourth(slot):
+                copy.wait_send()
+
     def finish(self):
         for slot in range(len(self.table)):
-            for copy in self.along_z(slot) + self.second(slot) + self.third(slot):
-                copy.wait_send()
-            for copy in self.fourth(slot):
-                copy.wait()
+            self.arrived(slot)
+        self.sent()
+
+
+def column_view(ref, column, distance):
+    def view(part, start, size):
+        first = column + part * distance + start
+        if not isinstance(part, int):
+            first = pl.multiple_of(first, 128)
+        return ref.at[:, :, :, :, pl.ds(first, size)]
+
+    return view
+
+
+def place_view(ref, place):
+    def view(part, start, size):
+        return ref.at[place + part, :, :, :, :, pl.ds(start, size)]
+
+    return view
 
 
 def spread_semaphores(count):
@@ -1098,7 +1018,7 @@
 
 
 def first_spread_kernel(slots_ref, tokens_ref, whole_ref, got_ref, local_sem, send_sem, recv_sem, token_sem):
-    table = [(whole_ref, index * SLOT, 3 * SLOT, 0) for index in range(3)]
+    table = [(column_view(whole_ref, index * SLOT, 3 * SLOT), 0) for index in range(3)]
     spread = Spread(slots_ref, table, local_sem, send_sem, recv_sem)
     greet_neighbours([spread.sibling, spread.beside, spread.across] + spread.stations)
     swap = pltpu.make_async_remote_copy(
@@ -1143,9 +1063,10 @@
     token_sem,
 ):
     pair = pl.program_id(0)
-    table = [(out_ref, 0, SLOT, 0)]
-    table += [(up_ref, index * SLOT, 4 * SLOT, HALF_SLOT if index % 2 else 0) for index in range(4)]
-    table += [(down_ref, index * SLOT, 4 * SLOT, HALF_SLOT if index % 2 else 0) for index in range(4)]
+    table = [(column_view(out_ref, 0, SLOT), HALF_SLOT)]
+    for index in range(EARLY):
+        over_x = HALF_SLOT if index == EARLY - 1 else 0
+        table += [(column_view(ref, index * SLOT, EARLY * SLOT), over_x) for ref in (up_ref, down_ref)]
     spread = Spread(slots_ref, table, local_sem, send_sem, recv_sem)
     swap = pltpu.make_async_remote_copy(
         src_ref=cotangent_ref.at[1 - spread.y],
@@ -1163,22 +1084,21 @@
         normed_t_ref[...] = normed_ref[...].T
         layout_grid(starts_ref, dist_ref)
 
-    for index in range(1, PAIRS):
-
-        @pl.when(pair == index)
-        def _(index=index):
-            spread.tick(index - 1)
-            if index == 5:
-                swap.start()
+    def between():
+        for index in range(spread.ticks()):
+
+            @pl.when(pair == index)
+            def _(index=index):
+                spread.tick(index)
+                if index == len(table) - 1:
+                    swap.start()
 
     packed = (mul(normed_ref[...], weights_ref[...]) + shifts_ref[...]).astype(jnp.bfloat16)
     packed_ref[...] = packed
-    attend_pair(pair, slopes_ref, packed, dist_ref, ctx_ref, exps_ref, stat_ref, ctx_t)
+    attend_pair(pair, slopes_ref, packed, dist_ref, ctx_ref, exps_ref, stat_ref, ctx_t, between)
 
     @pl.when(pair == PAIRS - 1)
     def _():
-        for index in range(PAIRS - 1, spread.ticks()):
-            spread.tick(index)
         spread.finish()
         swap.wait()
 
@@ -1223,12 +1143,12 @@
             jax.ShapeDtypeStruct((PAIRS, 2, LEN), jnp.float32),
             jax.ShapeDtypeStruct((D, LEN), jnp.bfloat16),
             whole_shape(D),
-            whole_shape(FF),
-            whole_shape(FF),
+            whole_shape(2 * EARLY * SLOT),
+            whole_shape(2 * EARLY * SLOT),
             jax.ShapeDtypeStruct(cotangent.shape[1:], cotangent.dtype),
         ],
         scratch_shapes=[pltpu.VMEM((LEN, LEN), jnp.float32), pltpu.VMEM((PAIR, LEN), jnp.float32)]
-        + spread_semaphores(9)
+        + spread_semaphores(1 + 2 * EARLY)
         + [pltpu.SemaphoreType.DMA((2,))],
         compiler_params=pltpu.CompilerParams(
             collective_id=4, has_side_effects=True, vmem_limit_bytes=VMEM_LIMIT
@@ -1237,14 +1157,367 @@
             flops=16 * LEN * LEN * D, bytes_accessed=90 * 1024 * 1024, transcendentals=H * LEN * LEN
         ),
     )(starts, slopes, normed, weights, shifts, slots, cotangent)
-    wholes = out.reshape(D, D), up.reshape(D, FF), down.reshape(D, FF)
+    wholes = out.reshape(D, D), up.reshape(D, -1), down.reshape(D, -1)
     return packed, context, exps, stats, normed_t, wholes, got
 
 
+class Summing:
+    def __init__(self, sources, add_own, buffers, total_ref, sems, lag, ready=0, hold=0):
+        self.sources, self.add_own, self.total_ref, self.lag = sources, add_own, total_ref, lag
+        self.ready, self.hold = ready, hold
+        self.first, self.second_y, self.second_x, self.third, self.fourth = buffers
+        self.send_sem, self.recv_sem = sems
+        (self.z, self.x, self.core, self.y), self.sibling, self.beside, self.across, self.stations = neighbours()
+        self.low_cols = pl.ds(0, HALF_SLOT)
+        self.high_cols = pl.ds(HALF_SLOT, HALF_SLOT)
+
+    def count(self):
+        return len(self.sources)
+
+    def remote(self, source, target, stage, slot, place):
+        return pltpu.make_async_remote_copy(
+            src_ref=source,
+            dst_ref=target,
+            send_sem=self.send_sem.at[stage, slot],
+            recv_sem=self.recv_sem.at[stage, slot],
+            device_id=place,
+            device_id_type=MESH_IDS,
+        )
+
+    def landed(self, ref, stage, slot):
+        pltpu.make_async_copy(ref, ref, self.recv_sem.at[stage, slot]).wait()
+
+    def send_first(self, slot):
+        for part in (0, 1):
+            source = self.sources[slot](part).at[:, :, 1 - self.core]
+            self.remote(source, self.first.at[slot, part], 0, slot, self.sibling).start()
+
+    def second_copies(self, slot):
+        for_y = self.first.at[slot, 1 - self.y, :, :, :, self.low_cols]
+        for_x = self.first.at[slot, :, :, 1 - self.x, :, self.high_cols]
+        return (
+            self.remote(for_y, self.second_y.at[slot], 1, slot, self.across),
+            self.remote(for_x, self.second_x.at[slot], 2, slot, self.beside),
+        )
+
+    def third_copies(self, slot):
+        for_x = self.second_y.at[slot, :, 1 - self.x]
+        for_y = self.second_x.at[slot, 1 - self.y]
+        return (
+            self.remote(for_x, self.third.at[slot, :, :, self.low_cols], 3, slot, self.beside),
+            self.remote(for_y, self.third.at[slot, :, :, self.high_cols], 4, slot, self.across),
+        )
+
+    def fourth_copies(self, slot):
+        return tuple(
+            self.remote(
+                self.third.at[slot, lax.rem(self.z + hop, 4)], self.fourth.at[slot, hop - 1], 4 + hop, slot, place
+            )
+            for hop, place in zip((1, 2, 3), self.stations)
+        )
+
+    def stage_one(self, slot):
+        self.landed(self.first.at[slot], 0, slot)
+        self.add_own(slot)
+        for copy in self.second_copies(slot):
+            copy.start()
+
+    def stage_two(self, slot):
+        first, second_y, second_x = self.first, self.second_y, self.second_x
+        self.landed(second_y.at[slot], 1, slot)
+        second_y[slot] = second_y[slot] + first[slot, self.y, :, :, :, :HALF_SLOT]
+        self.landed(second_x.at[slot], 2, slot)
+        second_x[slot] = second_x[slot] + first[slot, :, :, self.x, :, HALF_SLOT:]
+        for copy in self.third_copies(slot):
+            copy.start()
+
+    def stage_three(self, slot):
+        third = self.third
+        self.landed(third.at[slot, :, :, self.low_cols], 3, slot)
+        self.landed(third.at[slot, :, :, self.high_cols], 4, slot)
+        third[slot, :, :, :HALF_SLOT] = third[slot, :, :, :HALF_SLOT] + self.second_y[slot, :, self.x]
+        third[slot, :, :, HALF_SLOT:] = third[slot, :, :, HALF_SLOT:] + self.second_x[slot, self.y]
+        for copy in self.fourth_copies(slot):
+            copy.start()
+
+    def stage_four(self, slot):
+        total = self.third[slot, self.z].astype(jnp.float32)
+        for hop in (1, 2, 3):
+            self.landed(self.fourth.at[slot, hop - 1], 4 + hop, slot)
+            total = total + self.fourth[slot, hop - 1].astype(jnp.float32)
+        self.total_ref[slot] = total
+
+    def ticks(self):
+        return self.count() + self.hold + 3 * self.lag
+
+    def tick(self, index):
+        for slot in range(self.count()):
+            entry = slot + (self.hold if slot >= self.ready else 0)
+            pl.when(index == entry)(lambda slot=slot: self.stage_one(slot))
+        for number, stage in enumerate((self.stage_two, self.stage_three, self.stage_four)):
+            entry = index - (number + 1) * self.lag
+            slot = jnp.where(entry < self.ready, entry, entry - self.hold)
+            late = (entry >= self.ready + self.hold) & (slot < self.count())
+            early = (entry >= 0) & (entry < self.ready)
+            pl.when(early | late)(lambda stage=stage, slot=slot: stage(slot))
+
+    def fixed_tick(self, index):
+        for number, stage in enumerate((self.stage_one, self.stage_two, self.stage_three, self.stage_four)):
+            slot = index - number * self.lag
+            if 0 <= slot < self.count():
+                stage(slot)
+
+    def sent(self):
+        def one(slot, carry):
+            pltpu.make_async_copy(self.first.at[slot], self.first.at[slot], self.send_sem.at[0, slot]).wait()
+            for copy in self.second_copies(slot) + self.third_copies(slot) + self.fourth_copies(slot):
+                copy.wait_send()
+            return carry
+
+        lax.fori_loop(0, self.count(), one, 0)
+
+
+def summing_buffers(count):
+    rows, low = 64, jnp.bfloat16
+    return [
+        pltpu.VMEM((count, 2, 4, 2, rows, SLOT), low),
+        pltpu.VMEM((count, 4, 2, rows, HALF_SLOT), low),
+        pltpu.VMEM((count, 2, 4, rows, HALF_SLOT), low),
+        pltpu.VMEM((count, 4, rows, SLOT), low),
+        pltpu.VMEM((count, 3, rows, SLOT), low),
+        pltpu.SemaphoreType.DMA((8, count)),
+        pltpu.SemaphoreType.DMA((8, count)),
+    ]
+
+
+HIDDEN = 512
+CHUNK = 256
+HIDDEN_STEPS = FF // HIDDEN
+GELU_SLOPE = math.sqrt(2.0 / math.pi)
+GELU_CUBE = 0.044715
+
+
+def dot_last(left, right):
+    return lax.dot_general(left, right, (((1,), (1,)), ((), ())), preferred_element_type=jnp.float32)
+
+
+def gelu_both(rows):
+    square = rows * rows
+    bent = jnp.tanh(rows * (GELU_SLOPE + GELU_SLOPE * GELU_CUBE * square))
+    half = 0.5 + 0.5 * bent
+    slope = half + 0.5 * rows * (1.0 - bent * bent) * (GELU_SLOPE + 3.0 * GELU_SLOPE * GELU_CUBE * square)
+    return rows * half, slope
+
+
+def hidden_block(step):
+    return (step % 2) * (HIDDEN_STEPS // 2) + step // 2
+
+
+def mlp_kernel(
+    rows_ref,
+    cot_ref,
+    base_ref,
+    bias_ref,
+    up_ref,
+    down_ref,
+    slots_ref,
+    block_ref,
+    grad_rows_ref,
+    grad_up_ref,
+    grad_down_ref,
+    bias_sum_ref,
+    total_ref,
+    rows_t,
+    cot_t,
+    total,
+    up_part,
+    down_part,
+    active,
+    grad_before,
+    grad_early,
+    first,
+    second_y,
+    second_x,
+    third,
+    fourth,
+    sum_send,
+    sum_recv,
+    local_sem,
+    spread_send,
+    spread_recv,
+    load_sem,
+):
+    step = pl.program_id(0)
+    early_steps = 2 * EARLY
+    table = []
+    for index in range(HIDDEN_STEPS // 2 - EARLY):
+        table += [(place_view(ref, 2 + 2 * index), HALF_SLOT) for ref in (up_part, down_part)]
+    spread = Spread(slots_ref, table, local_sem, spread_send, spread_recv)
+
+    def early_block(slot, part):
+        return grad_early.at[slot % 2, 2 * (slot // 2) + part]
+
+    def add_own(slot):
+        for part in (0, 1):
+            first[slot, part] = first[slot, part] + grad_early[slot % 2, 2 * (slot // 2) + part, :, :, summing.core]
+
+    sources = [lambda part, slot=slot: early_block(slot, part) for slot in range(2 * EARLY)]
+    buffers = (first, second_y, second_x, third, fourth)
+    summing = Summing(sources, add_own, buffers, total_ref, (sum_send, sum_recv), 1)
+
+    def loads(at):
+        column = lax.rem(at, 2) * EARLY + at // 2
+        cols = pl.ds(pl.multiple_of(column * HIDDEN, HIDDEN), HIDDEN)
+        place = lax.rem(at, 2)
+        return (
+            pltpu.make_async_copy(up_ref.at[:, :, :, :, cols], up_part.at[place], load_sem.at[0, place]),
+            pltpu.make_async_copy(down_ref.at[:, :, :, :, cols], down_part.at[place], load_sem.at[1, place]),
+        )
+
+    @pl.when(step == 0)
+    def _():
+        for copy in loads(step):
+            copy.start()
+        greet_neighbours([spread.sibling, spread.beside, spread.across] + spread.stations)
+        spread.begin()
+        rows_t[...] = rows_ref[...].T
+        cot_t[...] = cot_ref[...].T
+        total[...] = base_ref[...]
+        grad_rows_ref[...] = jnp.zeros_like(grad_rows_ref)
+
+    @pl.when(step < early_steps)
+    def _():
+        for copy in loads(step):
+            copy.wait()
+
+    @pl.when(step < early_steps - 1)
+    def _():
+        for copy in loads(step + 1):
+            copy.start()
+
+    for index in range(HIDDEN_STEPS // 2 - EARLY):
+
+        @pl.when(step == early_steps + 2 * index)
+        def _(index=index):
+            spread.arrived(2 * index)
+            spread.arrived(2 * index + 1)
+
+    place = jnp.where(step < early_steps, lax.rem(step, 2), step - early_steps + 2)
+    up = up_part[place].reshape(D, HIDDEN)
+    down = down_part[place].reshape(D, HIDDEN)
+    bias = bias_ref[...]
+    bias_sum = jnp.zeros((1, HIDDEN), jnp.float32)
+    for index in range(LEN // CHUNK):
+        here = slice(index * CHUNK, index * CHUNK + CHUNK)
+        value, slope = gelu_both(mul(rows_ref[here], up) + bias)
+        value = value.astype(jnp.bfloat16)
+        grads = (slope * mul(cot_ref[here], down)).astype(jnp.bfloat16)
+        active[here] = value
+        grad_before[here] = grads
+        bias_sum += jnp.sum(grads.astype(jnp.float32), axis=0, keepdims=True)
+        total[here] += dot_last(value, down)
+        grad_rows_ref[here] += dot_last(grads, up)
+        if index == LEN // CHUNK // 2 - 1:
+            for number in range(spread.ticks()):
+                pl.when(step == number)(lambda number=number: spread.tick(number))
+    bias_sum_ref[...] = bias_sum
+    grad_down = mul(cot_t[...], active[...]).astype(jnp.bfloat16)
+    grad_up = mul(rows_t[...], grad_before[...]).astype(jnp.bfloat16)
+
+    @pl.when(step < early_steps)
+    def _():
+        grad_early[0, step] = grad_up.reshape(grad_early.shape[2:])
+        grad_early[1, step] = grad_down.reshape(grad_early.shape[2:])
+
+    @pl.when(step >= early_steps)
+    def _():
+        grad_up_ref[...] = grad_up
+        grad_down_ref[...] = grad_down
+
+    for number in range(HIDDEN_STEPS):
+
+        @pl.when(step == number)
+        def _(number=number):
+            if number < early_steps and number % 2:
+                summing.send_first(number - 1)
+                summing.send_first(number)
+            if number >= 2:
+                summing.fixed_tick(number - 2)
+
+    @pl.when(step == HIDDEN_STEPS - 1)
+    def _():
+        block_ref[...] = total[...].astype(jnp.bfloat16)
+        for number in range(HIDDEN_STEPS - 2, summing.ticks()):
+            summing.fixed_tick(number)
+        summing.sent()
+        spread.sent()
+
+
+def late_block(step):
+    late = HIDDEN_STEPS // 2 - EARLY
+    return jnp.where(step < 2 * EARLY, 0, (step % 2) * late + step // 2 - EARLY)
+
+
+def mlp_both(rows, cot, base, bias, up, down, slots):
+    anywhere = pl.BlockSpec(memory_space=pl.ANY)
+    once = pl.Buffered(1)
+    whole = pl.BlockSpec((LEN, D), lambda s: (0, 0), pipeline_mode=once)
+    hidden = pl.BlockSpec((D, HIDDEN), lambda s: (0, late_block(s)))
+    hidden_row = pl.BlockSpec((1, HIDDEN), lambda s: (0, hidden_block(s)))
+    low = jnp.bfloat16
+    late = HIDDEN_STEPS // 2 - EARLY
+    part = pltpu.VMEM((2 + 2 * late, 4, 2, 2, 64, HIDDEN), low)
+    split = [weights.reshape(4, 2, 2, 64, -1) for weights in (up, down)]
+    return pl.pallas_call(
+        mlp_kernel,
+        grid=(HIDDEN_STEPS,),
+        in_specs=[whole, whole, whole, hidden_row, anywhere, anywhere, anywhere],
+        out_specs=[
+            whole,
+            whole,
+            hidden,
+            hidden,
+            hidden_row,
+            pl.BlockSpec((2 * EARLY, 64, SLOT), lambda s: (0, 0, 0), pipeline_mode=once),
+        ],
+        out_shape=[
+            jax.ShapeDtypeStruct((LEN, D), low),
+            jax.ShapeDtypeStruct((LEN, D), jnp.float32),
+            jax.ShapeDtypeStruct((D, 2 * late * HIDDEN), low),
+            jax.ShapeDtypeStruct((D, 2 * late * HIDDEN), low),
+            jax.ShapeDtypeStruct((1, FF), jnp.float32),
+            jax.ShapeDtypeStruct((2 * EARLY, 64, SLOT), jnp.float32),
+        ],
+        scratch_shapes=[
+            pltpu.VMEM((D, LEN), low),
+            pltpu.VMEM((D, LEN), low),
+            pltpu.VMEM((LEN, D), jnp.float32),
+            part,
+            part,
+            pltpu.VMEM((LEN, HIDDEN), low),
+            pltpu.VMEM((LEN, HIDDEN), low),
+            pltpu.VMEM((2, 2 * EARLY, 4, 2, 2, 64, HIDDEN), low),
+            *summing_buffers(2 * EARLY),
+            *spread_semaphores(2 * late),
+            pltpu.SemaphoreType.DMA((2, 2)),
+        ],
+        compiler_params=pltpu.CompilerParams(
+            collective_id=5, has_side_effects=True, vmem_limit_bytes=62 * 1024 * 1024
+        ),
+        cost_estimate=pl.CostEstimate(
+            flops=12 * LEN * D * FF, bytes_accessed=60 * 1024 * 1024, transcendentals=LEN * FF
+        ),
+    )(rows, cot, base, bias, *split, slots)
+
+
 LAG = 2
-ORDER = (4, 8, 5, 9, 6, 10, 7, 11, 3, 0, 1, 2)
-READY = 9
+READY = 5
+LATE_SLOTS = 8
 RING = 4
+
+
+def block_view(ref, column):
+    return ref.at[:, :, :, :, pl.ds(column, SLOT)]
 
 
 def attend_bwd_half(half, scale, values, keys_t, parts, exps, sums):
@@ -1287,116 +1560,40 @@
     second_x,
     third,
     fourth,
+    send_sem,
+    recv_sem,
     exps_sem,
     load_sem,
-    send_sem,
-    recv_sem,
 ):
     pair = pl.program_id(0)
-    (z, x, core, y), sibling, beside, across, stations = neighbours()
-    low_cols = pl.ds(0, HALF_SLOT)
-    high_cols = pl.ds(HALF_SLOT, HALF_SLOT)
-
-    def remote(source, target, stage, slot, place):
-        return pltpu.make_async_remote_copy(
-            src_ref=source,
-            dst_ref=target,
-            send_sem=send_sem.at[stage, slot],
-            recv_sem=recv_sem.at[stage, slot],
-            device_id=place,
-            device_id_type=MESH_IDS,
-        )
-
-    def source(slot, part):
-        kind = ORDER[slot]
-        if kind < 3:
-            ref, column = grad_qkv, (part * 3 + kind) * SLOT
-        elif kind == 3:
-            ref, column = out_ref, part * SLOT
+    width = up_ref.shape[-1] // 2
+    sources = []
+    for index in range(width // SLOT):
+        for ref in (up_ref, down_ref):
+            sources.append(lambda part, ref=ref, index=index: block_view(ref, part * width + index * SLOT))
+    sources.append(lambda part: block_view(out_ref, part * SLOT))
+    for index in range(3):
+        sources.append(lambda part, index=index: block_view(grad_qkv, (part * 3 + index) * SLOT))
+
+    def load(slot, part):
+        block = sources[slot](part).at[:, :, summing.core]
+        return pltpu.make_async_copy(block, mine.at[slot % RING, part], load_sem.at[slot % RING])
+
+    def add_own(slot):
+        if slot < READY:
+            place = slot % RING
+            pltpu.make_async_copy(mine.at[place], mine.at[place], load_sem.at[place]).wait()
+            first[slot] = first[slot] + mine[place]
+            if slot + RING < READY:
+                for part in (0, 1):
+                    load(slot + RING, part).start()
         else:
-            ref = up_ref if kind < 8 else down_ref
-            column = (part * 4 + kind % 4) * SLOT
-        return ref, pl.ds(column, SLOT)
-
-    def load(slot, part):
-        ref, cols = source(slot, part)
-        place = slot % RING
-        return pltpu.make_async_copy(ref.at[:, :, core, :, cols], mine.at[place, part], load_sem.at[place])
-
-    def send_first(slot):
-        for part in (0, 1):
-            ref, cols = source(slot, part)
-            remote(ref.at[:, :, 1 - core, :, cols], first.at[slot, part], 0, slot, sibling).start()
-
-    def second_copies(slot):
-        return (
-            remote(first.at[slot, 1 - y, :, :, :, low_cols], second_y.at[slot], 1, slot, across),
-            remote(first.at[slot, :, :, 1 - x, :, high_cols], second_x.at[slot], 2, slot, beside),
-        )
-
-    def third_copies(slot):
-        return (
-            remote(second_y.at[slot, :, 1 - x], third.at[slot, :, :, low_cols], 3, slot, beside),
-            remote(second_x.at[slot, 1 - y], third.at[slot, :, :, high_cols], 4, slot, across),
-        )
-
-    def fourth_copies(slot):
-        return tuple(
-            remote(third.at[slot, lax.rem(z + hop, 4)], fourth.at[slot, hop - 1], 4 + hop, slot, place)
-            for hop, place in zip((1, 2, 3), stations)
-        )
-
-    def landed(ref, stage, slot):
-        pltpu.make_async_copy(ref, ref, recv_sem.at[stage, slot]).wait()
-
-    def tick(index):
-        for slot in range(SLOTS):
-
-            @pl.when(index == slot)
-            def _(slot=slot):
-                landed(first.at[slot], 0, slot)
-                if slot < READY:
-                    place = slot % RING
-                    pltpu.make_async_copy(mine.at[place], mine.at[place], load_sem.at[place]).wait()
-                    first[slot] = first[slot] + mine[place]
-                    if slot + RING < READY:
-                        for part in (0, 1):
-                            load(slot + RING, part).start()
-                else:
-                    for part in (0, 1):
-                        _, cols = source(slot, part)
-                        first[slot, part] = first[slot, part] + grad_qkv[:, :, core, :, cols]
-                for copy in second_copies(slot):
-                    copy.start()
-
-        @pl.when((index >= LAG) & (index < SLOTS + LAG))
-        def _():
-            slot = index - LAG
-            landed(second_y.at[slot], 1, slot)
-            second_y[slot] = second_y[slot] + first[slot, y, :, :, :, :HALF_SLOT]
-            landed(second_x.at[slot], 2, slot)
-            second_x[slot] = second_x[slot] + first[slot, :, :, x, :, HALF_SLOT:]
-            for copy in third_copies(slot):
-                copy.start()
-
-        @pl.when((index >= 2 * LAG) & (index < SLOTS + 2 * LAG))
-        def _():
-            slot = index - 2 * LAG
-            landed(third.at[slot, :, :, low_cols], 3, slot)
-            landed(third.at[slot, :, :, high_cols], 4, slot)
-            third[slot, :, :, :HALF_SLOT] = third[slot, :, :, :HALF_SLOT] + second_y[slot, :, x]
-            third[slot, :, :, HALF_SLOT:] = third[slot, :, :, HALF_SLOT:] + second_x[slot, y]
-            for copy in fourth_copies(slot):
-                copy.start()
-
-        @pl.when(index >= 3 * LAG)
-        def _():
-            slot = index - 3 * LAG
-            total = third[slot, z].astype(jnp.float32)
-            for hop in (1, 2, 3):
-                landed(fourth.at[slot, hop - 1], 4 + hop, slot)
-                total = total + fourth[slot, hop - 1].astype(jnp.float32)
-            total_ref[slot] = total
+            for part in (0, 1):
+                cols = pl.ds((part * 3 + slot - READY) * SLOT, SLOT)
+                first[slot, part] = first[slot, part] + grad_qkv[:, :, summing.core, :, cols]
+
+    buffers = (first, second_y, second_x, third, fourth)
+    summing = Summing(sources, add_own, buffers, total_ref, (send_sem, recv_sem), LAG, READY, 1)
 
     def exps_load(head, half):
         return pltpu.make_async_copy(exps_ref.at[head], exps.at[half], exps_sem.at[half])
@@ -1408,9 +1605,9 @@
         for slot in range(RING):
             for part in (0, 1):
                 load(slot, part).start()
-        greet_neighbours([sibling, beside, across] + stations)
+        greet_neighbours([summing.sibling, summing.beside, summing.across] + summing.stations)
         for slot in range(READY):
-            send_first(slot)
+            summing.send_first(slot)
         grad_normed_ref[...] = jnp.zeros_like(grad_normed_ref)
 
     scale = 1.0 / math.sqrt(HD)
@@ -1444,7 +1641,7 @@
             exps_load(2 * pair + 2 + half, half).start()
 
         if half == 0:
-            tick(pair)
+            summing.tick(pair)
     grads = jnp.concatenate([dq_t[...].T, dk_sum[...] * scale, dv_sum[...]], axis=1).astype(jnp.bfloat16)
     packed_sum_ref[...] = jnp.sum(grads.astype(jnp.float32), axis=0, keepdims=True)
     cols = pl.ds(pl.multiple_of(pair * (3 * PAIR), PAIR), 3 * PAIR)
@@ -1452,24 +1649,17 @@
     grad_qkv[:, :, :, :, cols] = grad_weights.reshape(4, 2, 2, 64, 3 * PAIR)
     grad_normed_ref[...] += dot_last(grads, weights_ref[...])
 
+    for slot in range(READY, LATE_SLOTS):
+        pl.when(pair == PAIRS - LATE_SLOTS + slot)(lambda slot=slot: summing.send_first(slot))
+
     @pl.when(pair == PAIRS - 1)
     def _():
-        for slot in range(READY, SLOTS):
-            send_first(slot)
-
         def late(index, carry):
-            tick(index)
+            summing.tick(index)
             return carry
 
-        lax.fori_loop(PAIRS, SLOTS + 3 * LAG, late, 0)
-
-        def sent(slot, carry):
-            pltpu.make_async_copy(first.at[slot], first.at[slot], send_sem.at[0, slot]).wait()
-            for copy in second_copies(slot) + third_copies(slot) + fourth_copies(slot):
-                copy.wait_send()
-            return carry
-
-        lax.fori_loop(0, SLOTS, sent, 0)
+        lax.fori_loop(PAIRS, summing.ticks(), late, 0)
+        summing.sent()
 
 
 def attend_sum(packed, context, grad_context, stats, weights, normed_t, exps, grad_up, grad_down, grad_out):
@@ -1484,12 +1674,12 @@
         grid=(PAIRS,),
         in_specs=[PACKED_COLS, PAIR_COLS, PAIR_COLS, PAIR_STAT, PACKED_COLS, tall] + [anywhere] * 4,
         out_specs=[
-            pl.BlockSpec((SLOTS, rows, SLOT), lambda p: (0, 0, 0), pipeline_mode=once),
+            pl.BlockSpec((LATE_SLOTS, rows, SLOT), lambda p: (0, 0, 0), pipeline_mode=once),
             tall,
             pl.BlockSpec((1, 3 * PAIR), lambda p: (0, p)),
         ],
         out_shape=[
-            jax.ShapeDtypeStruct((SLOTS, rows, SLOT), jnp.float32),
+            jax.ShapeDtypeStruct((LATE_SLOTS, rows, SLOT), jnp.float32),
             jax.ShapeDtypeStruct((LEN, D), jnp.float32),
             jax.ShapeDtypeStruct((1, 3 * D), jnp.float32),
         ],
@@ -1500,15 +1690,9 @@
             pltpu.VMEM((LEN, PAIR), jnp.float32),
             pltpu.VMEM((4, 2, 2, rows, 3 * D), low),
             pltpu.VMEM((RING, 2, 4, 2, rows, SLOT), low),
-            pltpu.VMEM((SLOTS, 2, 4, 2, rows, SLOT), low),
-            pltpu.VMEM((SLOTS, 4, 2, rows, HALF_SLOT), low),
-            pltpu.VMEM((SLOTS, 2, 4, rows, HALF_SLOT), low),
-            pltpu.VMEM((SLOTS, 4, rows, SLOT), low),
-            pltpu.VMEM((SLOTS, 3, rows, SLOT), low),
+            *summing_buffers(LATE_SLOTS),
             pltpu.SemaphoreType.DMA((2,)),
             pltpu.SemaphoreType.DMA((RING,)),
-            pltpu.SemaphoreType.DMA((8, SLOTS)),
-            pltpu.SemaphoreType.DMA((8, SLOTS)),
         ],
         compiler_params=pltpu.CompilerParams(
             collective_id=2, has_side_effects=True, vmem_limit_bytes=62 * 1024 * 1024
@@ -1517,6 +1701,97 @@
             flops=44 * LEN * LEN * D, bytes_accessed=400 * 1024 * 1024, transcendentals=0
         ),
     )(packed, context, grad_context, stats, weights, normed_t, exps, *split)
+
+
+ROWS = 256
+
+
+def norm_pull(rows, grads, gain):
+    centered = rows - jnp.mean(rows, axis=-1, keepdims=True)
+    inverse = lax.rsqrt(jnp.mean(centered * centered, axis=-1, keepdims=True) + NORM_EPSILON)
+    normed = centered * inverse
+    scaled = grads * gain
+    along = jnp.mean(scaled * normed, axis=-1, keepdims=True)
+    pulled = inverse * (scaled - jnp.mean(scaled, axis=-1, keepdims=True) - normed * along)
+    gain_sum = jnp.sum(grads * normed, axis=0, keepdims=True)
+    return pulled, gain_sum, jnp.sum(grads, axis=0, keepdims=True)
+
+
+def add_rows(sums_ref, rows):
+    for index, row in enumerate(rows):
+        sums_ref[index : index + 1, :] += row
+
+
+def middle_kernel(
+    middle_ref, grad_ref, cot_ref, ctx_ref, gain_ref, weights_ref, grad_middle_ref, grad_ctx_ref, grad_out_ref, sums_ref, total
+):
+    step = pl.program_id(0)
+
+    @pl.when(step == 0)
+    def _():
+        sums_ref[...] = jnp.zeros_like(sums_ref)
+        total[...] = jnp.zeros_like(total)
+
+    cot = cot_ref[...].astype(jnp.float32)
+    pulled, gain_sum, shift_sum = norm_pull(middle_ref[...], grad_ref[...], gain_ref[...])
+    grads = cot + pulled
+    low = grads.astype(jnp.bfloat16)
+    grad_middle_ref[...] = grads
+    grad_ctx_ref[...] = mul(low, weights_ref[...]).astype(jnp.bfloat16)
+    total[...] += mul(low.T, ctx_ref[...])
+    grad_sum = jnp.sum(grads, axis=0, keepdims=True)
+    add_rows(sums_ref, (gain_sum, shift_sum, grad_sum, jnp.sum(cot, axis=0, keepdims=True)))
+
+    @pl.when(step == LEN // ROWS - 1)
+    def _():
+        grad_out_ref[...] = total[...].astype(jnp.bfloat16)
+
+
+def middle_backward(middle, grad_rows, cot, context, gain, weights):
+    rows = pl.BlockSpec((ROWS, D), lambda s: (s, 0))
+    whole = pl.BlockSpec((D, D), lambda s: (0, 0), pipeline_mode=pl.Buffered(1))
+    row = pl.BlockSpec((1, D), lambda s: (0, 0))
+    sums = pl.BlockSpec((8, D), lambda s: (0, 0))
+    return pl.pallas_call(
+        middle_kernel,
+        grid=(LEN // ROWS,),
+        in_specs=[rows, rows, rows, rows, row, whole],
+        out_specs=[rows, rows, whole, sums],
+        out_shape=[
+            jax.ShapeDtypeStruct((LEN, D), jnp.float32),
+            jax.ShapeDtypeStruct((LEN, D), jnp.bfloat16),
+            jax.ShapeDtypeStruct((D, D), jnp.bfloat16),
+            jax.ShapeDtypeStruct((8, D), jnp.float32),
+        ],
+        scratch_shapes=[pltpu.VMEM((D, D), jnp.float32)],
+        compiler_params=pltpu.CompilerParams(vmem_limit_bytes=VMEM_LIMIT),
+        cost_estimate=pl.CostEstimate(flops=4 * LEN * D * D, bytes_accessed=24 * 1024 * 1024, transcendentals=0),
+    )(middle, grad_rows, cot, context, gain, weights)
+
+
+def token_kernel(rows_ref, grad_ref, grad_middle_ref, gain_ref, out_ref, sums_ref):
+    @pl.when(pl.program_id(0) == 0)
+    def _():
+        sums_ref[...] = jnp.zeros_like(sums_ref)
+
+    pulled, gain_sum, shift_sum = norm_pull(rows_ref[...].astype(jnp.float32), grad_ref[...], gain_ref[...])
+    out_ref[...] = (grad_middle_ref[...] + pulled).astype(jnp.bfloat16)
+    add_rows(sums_ref, (gain_sum, shift_sum))
+
+
+def token_backward(rows_low, grad_rows, grad_middle, gain):
+    rows = pl.BlockSpec((ROWS, D), lambda s: (s, 0))
+    row = pl.BlockSpec((1, D), lambda s: (0, 0))
+    sums = pl.BlockSpec((8, D), lambda s: (0, 0))
+    return pl.pallas_call(
+        token_kernel,
+        grid=(LEN // ROWS,),
+        in_specs=[rows, rows, rows, row],
+        out_specs=[rows, sums],
+        out_shape=[jax.ShapeDtypeStruct((LEN, D), jnp.bfloat16), jax.ShapeDtypeStruct((8, D), jnp.float32)],
+        compiler_params=pltpu.CompilerParams(vmem_limit_bytes=VMEM_LIMIT),
+        cost_estimate=pl.CostEstimate(flops=0, bytes_accessed=12 * 1024 * 1024, transcendentals=0),
+    )(rows_low, grad_rows, grad_middle, gain)
 
 
 def narrow(rows):
@@ -1573,62 +1848,58 @@
     own_cotangent = lax.dynamic_index_in_dim(cotangent, rank, 0, keepdims=False)
 
     full_qkv, other_tokens = first_spread(by_slots(by_pairs(narrow(w_qkv))), tokens)
-    token_rows = in_order(rank, own_tokens, other_tokens).astype(jnp.float32)
+    token_low = in_order(rank, own_tokens, other_tokens)
+    token_rows = token_low.astype(jnp.float32)
     normed_one = narrow(layer_norm(token_rows, vectors[0], vectors[1]))
     shifts = by_pairs(jnp.stack([vectors[2], jnp.zeros((D,), jnp.float32), vectors[3]])[:, None])
-    later_slots = jnp.concatenate(
-        [narrow(w_out).T[None], by_slots(narrow(w_up)), by_slots(narrow(w_down).T)]
-    )
+    up_slots = by_slots(narrow(w_up))
+    down_slots = by_slots(narrow(w_down).T)
+    in_turn = jnp.stack([up_slots, down_slots], axis=1).reshape(2 * up_slots.shape[0], *up_slots.shape[1:])
+    later_slots = jnp.concatenate([narrow(w_out).T[None], in_turn[: 2 * EARLY]])
     packed, context, exps, stats, normed_t, wholes, other_cotangent = attend_spread(
         starts, slopes, normed_one, full_qkv, shifts, later_slots, cotangent
     )
     full_out, full_up, full_down = wholes
     cotangent_low = in_order(rank, own_cotangent, other_cotangent)
-    cotangent_rows = cotangent_low.astype(jnp.float32)
 
     middle = token_rows + contract(context, full_out, 1, 1) + vectors[4]
     normed_two = narrow(layer_norm(middle, vectors[5], vectors[6]))
-    block_rows, grad_normed_two, grad_up, grad_down, up_bias = mlp_both(
-        normed_two, cotangent_low, middle + vectors[11], vectors[7:11].reshape(1, FF), full_up, full_down
+    block_rows, grad_normed_two, grad_up, grad_down, up_bias, early_sums = mlp_both(
+        normed_two,
+        cotangent_low,
+        middle + vectors[11],
+        vectors[7:11].reshape(1, FF),
+        full_up,
+        full_down,
+        in_turn[2 * EARLY :],
     )
     output_pair = swap_halves(block_rows, rank)
-    second_pull = jax.vjp(layer_norm, middle, vectors[5], vectors[6])[1]
-    middle_from_norm, gain_two_grad, shift_two_grad = second_pull(grad_normed_two)
-    grad_middle = cotangent_rows + middle_from_norm
-    grad_middle_low = narrow(grad_middle)
-    grad_out = narrow(contract(grad_middle_low, context, 0, 0))
-    grad_context = narrow(contract(grad_middle_low, full_out, 1, 0))
+    grad_middle, grad_context, grad_out, middle_sums = middle_backward(
+        middle, grad_normed_two, cotangent_low, context, vectors[5:6], full_out
+    )
     sums, grad_normed_one, packed_grads = attend_sum(
         packed, context, grad_context, stats, full_qkv, normed_t, exps, grad_up, grad_down, grad_out
     )
-    first_pull = jax.vjp(layer_norm, token_rows, vectors[0], vectors[1])[1]
-    token_from_norm, gain_one_grad, shift_one_grad = first_pull(grad_normed_one)
-    grad_token_rows = grad_middle + token_from_norm
-    token_pair = swap_halves(narrow(grad_token_rows), rank).astype(jnp.float32)
+    grad_token_low, token_sums = token_backward(token_low, grad_normed_one, grad_middle, vectors[0:1])
+    token_pair = swap_halves(grad_token_low, rank).astype(jnp.float32)
 
     packed_sums = from_pairs(packed_grads)[:, 0]
     vector_total = jnp.concatenate(
         [
-            jnp.stack(
-                [
-                    gain_one_grad,
-                    shift_one_grad,
-                    packed_sums[0],
-                    packed_sums[2],
-                    jnp.sum(grad_middle, axis=0),
-                    gain_two_grad,
-                    shift_two_grad,
-                ]
-            ),
+            token_sums[0:2],
+            packed_sums[0:1],
+            packed_sums[2:3],
+            middle_sums[2:3],
+            middle_sums[0:2],
             up_bias.reshape(4, D),
-            jnp.sum(cotangent_rows, axis=0)[None],
+            middle_sums[3:4],
         ]
     )
     shards = (
-        from_pairs(from_slots(sums[9:12])),
-        sums[8].T,
-        from_slots(sums[0:8:2]),
-        from_slots(sums[1:8:2]).T,
+        from_pairs(from_slots(sums[5:8])),
+        sums[4].T,
+        from_slots(jnp.concatenate([early_sums[0::2], sums[0:4:2]])),
+        from_slots(jnp.concatenate([early_sums[1::2], sums[1:4:2]])).T,
     )
     outputs = muon_step(shards, vector_total, w_qkv, w_out, w_up, w_down, vectors, m_qkv, m_out, m_up, m_down, m_vec)
     return (output_pair, token_pair) + outputs

time: 650 us -> 590 us (0.908)
  other arithmetic: 68.3 us -> 42.1 us
  Pallas kernels: 529 us -> 505 us
  matrix products: 13.3 us -> 4.79 us
    pallas_call x1, Pallas kernels: 70.3 us -> 108 us  [mlp_both(): pl.pallas_call(mlp_kernel, grid=(HIDDEN_STEPS,), in_specs=[whole, whole,...]
    pallas_call x1, Pallas kernels: 132 us -> 101 us  [attend_sum(): pl.pallas_call(attend_sum_kernel, grid=(PAIRS,), in_specs=[PACKED_COLS, P...]
    reduce_sum x5 -> x0, other arithmetic: 30.2 us -> none  [the longest x1 12.8 us: layer_norm(): centered = inputs - average]
    pallas_call x1, Pallas kernels: 130 us -> 101 us  [attend_spread(): pl.pallas_call(attend_spread_kernel, grid=(PAIRS,), in_specs=[SCALARS, SC...]
    pallas_call x1, Pallas kernels: 139 us -> 116 us  [muon_call(): pl.pallas_call(muon_kernel, in_specs=[vmem, vmem], out_specs=[vmem, vmem]...]
    pallas_call x0 -> x2, Pallas kernels: none -> 21.7 us  [the longest x1 14.4 us: middle_backward(): pl.pallas_call(middle_kernel, grid=(LEN // ROWS,), in_specs=[rows, rows,...]
    dot_general x3 -> x1, matrix products: 13.3 us -> 4.79 us  [contract(): lax.dot_general(left, right, (((left_dim,), (right_dim,)), ((), ())), pre...]
  transfers between devices with their start and end apart: 2 -> 2, of which waited for: 0 -> 0; matrix products, arithmetic and copies ran while one was open for 5% -> 7% of each run, Pallas kernels for 22% -> 20%
where the time goes in v6:
time: 590 us; the launch traced here: 584 us
  Pallas kernels  505 us (86%)
  other arithmetic  42.1 us (7%)
  local copies, waits for them, and re-layouts  29.3 us (5%)
    pallas_call x1, Pallas kernels, muon_call(): pl.pallas_call(muon_kernel, in_specs=[vmem, vmem], out_specs=[vmem, vmem]...  116 us
    pallas_call x1, Pallas kernels, mlp_both(): pl.pallas_call(mlp_kernel, grid=(HIDDEN_STEPS,), in_specs=[whole, whole,...  108 us
    pallas_call x1, Pallas kernels, attend_sum(): pl.pallas_call(attend_sum_kernel, grid=(PAIRS,), in_specs=[PACKED_COLS, P...  101 us
    pallas_call x1, Pallas kernels, attend_spread(): pl.pallas_call(attend_spread_kernel, grid=(PAIRS,), in_specs=[SCALARS, SC...  101 us
    pallas_call x1, Pallas kernels, first_spread(): pl.pallas_call(first_spread_kernel, in_specs=[anywhere] * 2, out_specs=[a...  57.3 us
    pallas_call x1, Pallas kernels, middle_backward(): pl.pallas_call(middle_kernel, grid=(LEN // ROWS,), in_specs=[rows, rows,...  14.4 us
  transfers between devices with their start and end apart: 2, of which 0 were waited for; matrix products, arithmetic and copies ran while one was open for 7% of the time, Pallas kernels for 20%

profile of v6, /device:TPU:9, one launch (start us, length us, event | category | flops | bytes accessed | tf_op | source)
XLA Modules:
  0.0 584.0 jit_solution(11485598250608990349)
XLA Ops:
  0.7 0.5 multiply_exponential_fusion.slopes_ref
  1.2 1.0 fusion.15
  2.3 0.8 slice_bitcast_fusion.2
  3.1 1.0 convert_element_type.65
  4.6 0.7 copy.74
  5.3 57.3 %shard_map.260 = (bf16[4,2,2,64,3072]{4,3,2,1,0:T(8,128)(2,1)}, bf16[512,1024]{1,0:T(8,128)(2,1)}) custom-call(bf16[3,64,512]{2,1,0:T(8,128)(2,1)} %bitcast.152, bf16[2,512,1024]{2,1,0:T(8,128)(2,1)} %tokens_ref.1), custom_call_target="tpu_custom_call" | custom-call | tf_op jit(solution)/shard_map/pallas_call | solution.py:1112
  62.6 1.6 dynamic-slice_bitcast_fusion.2
  64.2 0.9 convert_reduce_fusion
  65.2 1.3 copy-done.2
  66.5 0.7 fusion.2
  67.2 0.5 fusion.9.starts_ref
  67.8 0.6 reshape.147.shifts_ref
  68.5 1.1 convert_element_type.69
  69.5 1.1 convert_element_type.70
  70.7 0.8 pad_maximum_fusion.2
  71.5 0.8 pad_maximum_fusion.1.slots_ref
  72.2 2.1 fusion.5.normed_ref
  74.3 100.5 %shard_map.261 = (bf16[1024,3072]{1,0:T(8,128)(2,1)}, bf16[1024,1024]{1,0:T(8,128)(2,1)}, bf16[16,1024,1024]{2,1,0:T(8,128)(2,1)}, f32[8,2,1024]{2,1,0:T(2,128)}...) custom-call(s32[2]{0:T(128)} %fusion.9.starts_ref, ...), custom_call_target="tpu_custom_call" | custom-call | flops 17179869184 | bytes 94371840 | tf_op jit(solution)/shard_map/pallas_call | solution.py:1125
  174.9 4.8 fusion.17
  179.7 0.6 multiply_reduce_fusion
  180.3 0.6 copy.58
  180.9 0.8 copy-done.12
  181.7 2.4 maximum_select_fusion.1.cot_ref
  184.1 3.3 broadcast_add_fusion
  187.4 107.8 %shard_map.262 = (bf16[1024,1024]{1,0:T(8,128)(2,1)}, f32[1024,1024]{1,0:T(8,128)}, bf16[1024,2048]{1,0:T(8,128)(2,1)}, bf16[1024,2048]{1,0:T(8,128)(2,1)}, f32[1,4096]{1,0:T(1,128)}, /*index=5*/f32[4,64,512]{2,1,0:T(8,128)}) custom-call(bf16[1024,1024]{1,0:T(8,128)(2,1)} %get-tuple-element.87.rows_ref, bf16[1024,1024]{1,0:T(8,128)(2,1)} %maximum_select_fusion.1.cot_ref, ...), custom_call_target="tpu_custom_call" | custom-call | flops 51539607552 | bytes 62914560 | tf_op jit(solution)/shard_map/pallas_call | solution.py:1471
  295.2 14.4 %shard_map.263 = (f32[1024,1024]{1,0:T(8,128)}, bf16[1024,1024]{1,0:T(8,128)(2,1)}, bf16[1024,1024]{1,0:T(8,128)(2,1)}, f32[8,1024]{1,0:T(8,128)}) custom-call(f32[1024,1024]{1,0:T(8,128)} %copy-done.4, f32[1024,1024]{1,0:T(8,128)} %get-tuple-element.54.grad_ref, bf16[1024,1024]{1,0:T(8,128)(2,1)} %maximum_select_fusion.1.cot_ref, ...), custom_call_target="tpu_custom_call" | custom-call | flops 4294967296 | bytes 25165824 | tf_op jit(solution)/shard_map/pallas_call | solution.py:1755
  309.7 101.5 %shard_map.264 = (f32[8,64,512]{2,1,0:T(8,128)}, f32[1024,1024]{1,0:T(8,128)}, f32[1,3072]{1,0:T(1,128)}) custom-call(bf16[1024,3072]{1,0:T(8,128)(2,1)} %get-tuple-element.53.packed_ref, bf16[1024,1024]{1,0:T(8,128)(2,1)} %get-tuple-element.47.ctx_ref, bf16[1024,1024]{1,0:T(8,128)(2,1)} %get-tuple-element.55.grad_ref, ...), custom_call_target="tpu_custom_call" | custom-call | flops 47244640256 | bytes 419430400 | tf_op jit(solution)/shard_map/pallas_call | solution.py:1672
  411.1 7.3 %shard_map.265 = (bf16[1024,1024]{1,0:T(8,128)(2,1)}, f32[8,1024]{1,0:T(8,128)}) custom-call(bf16[1024,1024]{1,0:T(8,128)(2,1)} %copy-done.2, f32[1024,1024]{1,0:T(8,128)} %get-tuple-element.62.grad_ref, f32[1024,1024]{1,0:T(8,128)} %get-tuple-element.63.grad_middle_ref, f32[1,1024]{1,0:T(1,128)} %copy-done.22), custom_call_target="tpu_custom_call" | custom-call | bytes 12582912 | tf_op jit(solution)/shard_map/pallas_call | solution.py:1786
  418.5 2.8 dynamic-slice_bitcast_fusion
  421.2 2.7 dynamic-slice_bitcast_fusion.1
  423.9 1.5 collective-permute-start
  425.4 0.8 fusion.13
  426.3 0.8 slice_bitcast_fusion.4
  427.1 0.6 constant_dynamic-update-slice_fusion.6
  427.7 0.5 broadcast.106
  428.2 1.4 reduce.3
  429.6 0.6 constant_dynamic-update-slice_fusion.5
  430.2 0.6 constant_dynamic-update-slice_fusion.4
  430.8 1.1 fusion.14
  431.9 1.0 maximum_bitcast_fusion.1
  433.0 2.1 fusion.12
  435.1 0.7 copy.71
  435.9 2.1 fusion.11
  438.1 0.7 copy.72
  438.8 1.1 copy.40
  439.9 2.2 reshape_reshape.7
  442.0 1.1 copy.41
  443.4 1.8 convert_bitcast_fusion.2
  445.2 0.6 constant_dynamic-update-slice_fusion.3
  445.8 0.6 constant_dynamic-update-slice_fusion.2
  446.4 1.3 constant_dynamic-update-slice_fusion.1
  447.7 0.6 constant_dynamic-update-slice_fusion.vec_ref
  448.3 1.8 fusion.10
  450.1 2.0 pad_maximum_fusion.moments_ref
  452.2 116.1 %shard_map.266 = (bf16[12,64,512]{2,1,0:T(8,128)(2,1)}, f32[12,8,128]{2,1,0:T(8,128)}) custom-call(bf16[12,64,512]{2,1,0:T(8,128)(2,1)} %pad_maximum_fusion.moments_ref, f32[12,8,128]{2,1,0:T(8,128)} %constant_dynamic-update-slice_fusion.vec_ref), custom_call_target="tpu_custom_call" | custom-call | flops 25769803776 | bytes 4194304 | tf_op jit(solution)/shard_map/pallas_call | solution.py:775
  568.3 1.3 convert_bitcast_fusion
  569.6 1.5 bitcast_subtract_fusion.1
  571.1 0.8 pad.33
  572.1 0.7 multiply_subtract_fusion.1
  572.9 0.9 sub.42
  573.8 1.7 multiply_subtract_fusion
  575.5 0.8 bitcast_subtract_fusion
  576.4 4.1 fusion.7
  580.5 3.3 maximum_select_fusion.2
  (76 shorter events, 1.3 us)
Async XLA Ops:
  0.7 66.5 %copy-start = (s32[2,1,2]{2,1,0:T(1,128)S(1)}, s32[2,1,2]{2,1,0:T(1,128)}, u32[]{:S(2)}) copy-start(s32[2,1,2]{2,1,0:T(1,128)} %param.15) | copy-start | bytes 52
  0.7 62.0 %copy-start.5 = (bf16[2,512,1024]{2,1,0:T(8,128)(2,1)S(1)}, bf16[2,512,1024]{2,1,0:T(8,128)(2,1)}, u32[]{:S(2)}) copy-start(bf16[2,512,1024]{2,1,0:T(8,128)(2,1)} %tokens_ref.1) | copy-start | bytes 6291460
  2.3 69.9 %copy-start.22 = (f32[1,1024]{1,0:T(1,128)}, f32[1,1024]{1,0:T(1,128)S(1)}, u32[]{:S(2)}) copy-start(f32[1,1024]{1,0:T(1,128)S(1)} %get-tuple-element.107.gain_ref) | copy-start | bytes 12292
  2.3 181.8 %copy-start.23 = (f32[1,1024]{1,0:T(1,128)}, f32[1,1024]{1,0:T(1,128)S(1)}, u32[]{:S(2)}) copy-start(f32[1,1024]{1,0:T(1,128)S(1)} %get-tuple-element.102.gain_ref) | copy-start | bytes 12292
  62.6 1.6 copy-start.13
  64.2 6.4 %copy-start.16 = (f32[512,64]{0,1:T(8,128)S(1)}, f32[512,64]{0,1:T(8,128)}, u32[]{:S(2)}) copy-start(f32[512,64]{0,1:T(8,128)} %param.17) | copy-start | bytes 393220
  65.1 1.3 copy-start.2
  67.7 4.5 copy-start.3
  179.7 4.4 copy-start.4
  179.7 2.0 copy-start.12
  418.4 6.9 %copy-start.24 = (f32[8,1024]{1,0:T(8,128)S(1)}, f32[8,1024]{1,0:T(8,128)}, u32[]{:S(2)}) copy-start(f32[8,1024]{1,0:T(8,128)} %get-tuple-element.69) | copy-start | bytes 98308
  418.4 7.0 %copy-start.14 = (f32[8,64,512]{2,1,0:T(8,128)S(1)}, f32[8,64,512]{2,1,0:T(8,128)}, u32[]{:S(2)}) copy-start(f32[8,64,512]{2,1,0:T(8,128)} %get-tuple-element.65) | copy-start | bytes 3145732
  421.2 155.1 %collective-permute-start.1 = (bf16[512,1024]{1,0:T(8,128)(2,1)}, bf16[512,1024]{1,0:T(8,128)(2,1)}, u32[]{:S(2)}, u32[]{:S(2)}) collective-permute-start(bf16[512,1024]{1,0:T(8,128)(2,1)} %get-tuple-element.89), channel_id=1, source_target_pairs={{0,1},{1,0},{2,3},{3,2},{4,5},{5,4},{6,7},{7,6},{8,9},{9,8},{10,11... | collective-permute-start | bytes 3145736 | tf_op jit(solution)/shard_map/ppermute | solution.py:1815
  423.9 156.6 %collective-permute-start = (bf16[512,1024]{1,0:T(8,128)(2,1)}, bf16[512,1024]{1,0:T(8,128)(2,1)}, u32[]{:S(2)}, u32[]{:S(2)}) collective-permute-start(bf16[512,1024]{1,0:T(8,128)(2,1)} %get-tuple-element.91), channel_id=1, source_target_pairs={{0,1},{1,0},{2,3},{3,2},{4,5},{5,4},{6,7},{7,6},{8,9},{9,8},{10,11... | collective-permute-start | bytes 3145736 | tf_op jit(solution)/shard_map/ppermute | solution.py:1815
  426.3 9.6 %copy-start.15 = (f32[2,64,512]{2,1,0:T(8,128)S(1)}, f32[2,64,512]{2,1,0:T(8,128)}, u32[]{:S(2)}) copy-start(f32[2,64,512]{2,1,0:T(8,128)} %get-tuple-element.93) | copy-start | bytes 786436
  432.9 9.1 %copy-start.8 = (f32[4,8,8,512]{3,2,0,1:T(8,128)}, f32[4,8,8,512]{3,2,0,1:T(8,128)S(1)}, u32[]{:S(2)}) copy-start(f32[4,8,8,512]{3,2,0,1:T(8,128)S(1)} %copy.55) | copy-start | bytes 1572868
  435.9 16.2 %copy-start.9 = (f32[4,8,8,512]{3,2,0,1:T(8,128)}, f32[4,8,8,512]{3,2,0,1:T(8,128)S(1)}, u32[]{:S(2)}) copy-start(f32[4,8,8,512]{3,2,0,1:T(8,128)S(1)} %copy.54) | copy-start | bytes 1572868
  443.3 125.0 %copy-start.11 = (f32[3,64,512]{2,1,0:T(8,128)}, f32[3,64,512]{2,1,0:T(8,128)S(1)}, u32[]{:S(2)}) copy-start(f32[3,64,512]{2,1,0:T(8,128)S(1)} %reshape.155) | copy-start | bytes 1179652
  452.1 117.5 %copy-start.17 = (f32[512,64]{0,1:T(8,128)S(1)}, f32[512,64]{0,1:T(8,128)}, u32[]{:S(2)}) copy-start(f32[512,64]{0,1:T(8,128)} %param.17) | copy-start | bytes 393220
  452.1 119.8 %copy-start.21 = (f32[12,1024]{1,0:T(8,128)S(1)}, f32[12,1024]{1,0:T(8,128)}, u32[]{:S(2)}) copy-start(f32[12,1024]{1,0:T(8,128)} %param.25) | copy-start | bytes 147460
  452.1 120.0 %copy-start.20 = (f32[12,1024]{1,0:T(8,128)S(1)}, f32[12,1024]{1,0:T(8,128)}, u32[]{:S(2)}) copy-start(f32[12,1024]{1,0:T(8,128)} %param.20) | copy-start | bytes 147460
  568.3 4.6 copy-start.6
  568.3 5.5 copy-start.10
  568.3 7.2 %copy-start.7 = (f32[2048,64]{0,1:T(8,128)S(1)}, f32[2048,64]{0,1:T(8,128)}, u32[]{:S(2)}) copy-start(f32[2048,64]{0,1:T(8,128)} %param.19) | copy-start | bytes 1572868
  571.9 8.5 %copy-start.19 = (f32[2,8,8,128]{3,1,2,0:T(8,128)}, f32[2,8,8,128]{3,1,2,0:T(8,128)S(1)}, u32[]{:S(2)}) copy-start(f32[2,8,8,128]{3,1,2,0:T(8,128)S(1)} %copy.61) | copy-start | bytes 196612
  572.1 8.4 %copy-start.18 = (f32[12,1024]{1,0:T(8,128)}, f32[12,1024]{1,0:T(8,128)S(1)}, u32[]{:S(2)}) copy-start(f32[12,1024]{1,0:T(8,128)S(1)} %get-tuple-element.74) | copy-start | bytes 147460
  576.4 7.5 %copy-start.1 = (s32[2,1,2]{2,1,0:T(1,128)S(1)}, s32[2,1,2]{2,1,0:T(1,128)}, u32[]{:S(2)}) copy-start(s32[2,1,2]{2,1,0:T(1,128)} %param.15) | copy-start | bytes 52

commit v7 on v6

--- a/solution.py
+++ b/solution.py
@@ -499,8 +499,12 @@
 def muon_kernel(
     moments_ref,
     vec_ref,
+    block_ref,
+    token_ref,
     updates_ref,
     vec_out_ref,
+    block_pair_ref,
+    token_pair_ref,
     pieces,
     turned,
     vec_pieces,
@@ -518,6 +522,7 @@
     recv_sem,
     half_send,
     half_recv,
+    swap_sem,
 ):
     groups = lax.axis_size("dp")
     parts = lax.axis_size("tensor")
@@ -573,6 +578,29 @@
         return carry
 
     lax.fori_loop(0, SLOTS, give, 0)
+
+    rows = block_ref.shape[0] // 2
+    kept_rows = pl.ds(pl.multiple_of(t_me * rows, rows), rows)
+    sent_rows = pl.ds(pl.multiple_of((1 - t_me) * rows, rows), rows)
+    kept = []
+    swaps = []
+    for index, (whole, pair) in enumerate(((block_ref, block_pair_ref), (token_ref, token_pair_ref))):
+        kept.append(pltpu.make_async_copy(whole.at[kept_rows], pair.at[t_me], swap_sem.at[2, index]))
+        swaps.append(
+            pltpu.make_async_remote_copy(
+                src_ref=whole.at[sent_rows],
+                dst_ref=pair.at[t_me],
+                send_sem=swap_sem.at[0, index],
+                recv_sem=swap_sem.at[1, index],
+                device_id=(dp_me, 1 - t_me),
+                device_id_type=MESH_IDS,
+            )
+        )
+
+    @pl.when(jnp.logical_not(is_wide))
+    def _():
+        for copy in kept + swaps:
+            copy.start()
 
     def give_back(source, sem, target):
         def one(step, carry):
@@ -677,6 +705,8 @@
                 exchange(0, index, sibling).wait_send()
                 exchange(1, index, across).wait_send()
                 exchange(2, index, sibling).wait_send()
+            for copy in kept + swaps:
+                copy.start()
 
         def trace_tile(tile, total):
             rows = pl.ds(pl.multiple_of(tile * TILE, TILE), TILE)
@@ -766,19 +796,26 @@
     def _():
         finish(SLOTS)
 
-
-def muon_call(moments, vec_parts):
+    for copy in kept + swaps:
+        copy.wait()
+
+
+def muon_call(moments, vec_parts, block_rows, token_grads):
     count = lax.axis_size("dp") * lax.axis_size("tensor")
     rows = moments.shape[1]
     vmem = pl.BlockSpec(memory_space=pltpu.VMEM)
+    anywhere = pl.BlockSpec(memory_space=pl.ANY)
+    pair = jax.ShapeDtypeStruct((2, LEN // 2, D), jnp.bfloat16)
     low = pltpu.VMEM((D, D), jnp.bfloat16)
     return pl.pallas_call(
         muon_kernel,
-        in_specs=[vmem, vmem],
-        out_specs=[vmem, vmem],
+        in_specs=[vmem, vmem, anywhere, anywhere],
+        out_specs=[vmem, vmem, anywhere, anywhere],
         out_shape=[
             jax.ShapeDtypeStruct(moments.shape, jnp.bfloat16),
             jax.ShapeDtypeStruct(vec_parts.shape, jnp.float32),
+            pair,
+            pair,
         ],
         scratch_shapes=[
             pltpu.VMEM((count, rows, SLOT), jnp.bfloat16),
@@ -798,66 +835,13 @@
             pltpu.SemaphoreType.DMA((4,)),
             pltpu.SemaphoreType.DMA((3, GRAM_TILES)),
             pltpu.SemaphoreType.DMA((3, GRAM_TILES)),
+            pltpu.SemaphoreType.DMA((3, 2)),
         ],
         compiler_params=pltpu.CompilerParams(
             collective_id=1, has_side_effects=True, vmem_limit_bytes=VMEM_LIMIT
         ),
         cost_estimate=pl.CostEstimate(flops=12 * 2 * D**3, bytes_accessed=4 * 1024 * 1024, transcendentals=0),
-    )(moments, vec_parts)
-
-
-def by_slots(rows):
-    return jnp.swapaxes(rows.reshape(rows.shape[0], -1, SLOT), 0, 1)
-
-
-def from_slots(rows):
-    return jnp.swapaxes(rows, 0, 1).reshape(rows.shape[1], -1)
-
-
-def muon_step(
-    shards, vector_total, w_qkv, w_out, w_up, w_down, vectors, m_qkv, m_out, m_up, m_down, m_vec
-):
-    grad_qkv_shard, grad_out_shard, grad_up_shard, grad_down_shard = shards
-    moment_qkv = MOMENTUM_DECAY * m_qkv + grad_qkv_shard
-    moment_out = MOMENTUM_DECAY * m_out + grad_out_shard
-    moment_up = MOMENTUM_DECAY * m_up + grad_up_shard
-    moment_down = MOMENTUM_DECAY * m_down + grad_down_shard
-    slots = jnp.concatenate(
-        [
-            narrow(moment_qkv),
-            narrow(moment_out).T[None],
-            by_slots(narrow(moment_up)),
-            by_slots(narrow(moment_down).T),
-        ]
-    )
-    updates, vector_rows = muon_call(slots, vector_total.reshape(SLOTS, 8, 128))
-    vector_grad = vector_rows.reshape(12, D)
-    wide_factor = math.sqrt(FF / D)
-    new_qkv = w_qkv - MATRIX_RATE * updates[0:3].astype(jnp.float32)
-    new_out = w_out - MATRIX_RATE * updates[3].T.astype(jnp.float32)
-    new_up = w_up - MATRIX_RATE * wide_factor * from_slots(updates[4:8]).astype(jnp.float32)
-    new_down = w_down - MATRIX_RATE * wide_factor * from_slots(updates[8:12]).T.astype(jnp.float32)
-    moment_vec = MOMENTUM_DECAY * m_vec + vector_grad
-    new_vec = vectors - VECTOR_RATE * moment_vec * lax.rsqrt(
-        jnp.mean(moment_vec * moment_vec, axis=1, keepdims=True) + SQUARE_EPSILON
-    )
-    return (
-        grad_qkv_shard,
-        grad_out_shard,
-        grad_up_shard,
-        grad_down_shard,
-        vector_grad,
-        moment_qkv,
-        moment_out,
-        moment_up,
-        moment_down,
-        moment_vec,
-        new_qkv,
-        new_out,
-        new_up,
-        new_down,
-        new_vec,
-    )
+    )(moments, vec_parts, block_rows, token_grads)
 
 
 def neighbours():
@@ -1723,14 +1707,13 @@
 
 
 def middle_kernel(
-    middle_ref, grad_ref, cot_ref, ctx_ref, gain_ref, weights_ref, grad_middle_ref, grad_ctx_ref, grad_out_ref, sums_ref, total
+    middle_ref, grad_ref, cot_ref, ctx_ref, gain_ref, weights_ref, grad_middle_ref, grad_ctx_ref, grad_out_ref, sums_ref, low_t
 ):
     step = pl.program_id(0)
 
     @pl.when(step == 0)
     def _():
         sums_ref[...] = jnp.zeros_like(sums_ref)
-        total[...] = jnp.zeros_like(total)
 
     cot = cot_ref[...].astype(jnp.float32)
     pulled, gain_sum, shift_sum = norm_pull(middle_ref[...], grad_ref[...], gain_ref[...])
@@ -1738,13 +1721,13 @@
     low = grads.astype(jnp.bfloat16)
     grad_middle_ref[...] = grads
     grad_ctx_ref[...] = mul(low, weights_ref[...]).astype(jnp.bfloat16)
-    total[...] += mul(low.T, ctx_ref[...])
+    low_t[:, pl.ds(pl.multiple_of(step * ROWS, ROWS), ROWS)] = low.T
     grad_sum = jnp.sum(grads, axis=0, keepdims=True)
     add_rows(sums_ref, (gain_sum, shift_sum, grad_sum, jnp.sum(cot, axis=0, keepdims=True)))
 
     @pl.when(step == LEN // ROWS - 1)
     def _():
-        grad_out_ref[...] = total[...].astype(jnp.bfloat16)
+        grad_out_ref[...] = mul(low_t[...], ctx_ref[...]).astype(jnp.bfloat16)
 
 
 def middle_backward(middle, grad_rows, cot, context, gain, weights):
@@ -1755,7 +1738,7 @@
     return pl.pallas_call(
         middle_kernel,
         grid=(LEN // ROWS,),
-        in_specs=[rows, rows, rows, rows, row, whole],
+        in_specs=[rows, rows, rows, whole, row, whole],
         out_specs=[rows, rows, whole, sums],
         out_shape=[
             jax.ShapeDtypeStruct((LEN, D), jnp.float32),
@@ -1763,7 +1746,7 @@
             jax.ShapeDtypeStruct((D, D), jnp.bfloat16),
             jax.ShapeDtypeStruct((8, D), jnp.float32),
         ],
-        scratch_shapes=[pltpu.VMEM((D, D), jnp.float32)],
+        scratch_shapes=[pltpu.VMEM((D, LEN), jnp.bfloat16)],
         compiler_params=pltpu.CompilerParams(vmem_limit_bytes=VMEM_LIMIT),
         cost_estimate=pl.CostEstimate(flops=4 * LEN * D * D, bytes_accessed=24 * 1024 * 1024, transcendentals=0),
     )(middle, grad_rows, cot, context, gain, weights)
@@ -1794,6 +1777,120 @@
     )(rows_low, grad_rows, grad_middle, gain)
 
 
+def slot_rows(early_ref, late_ref, slot):
+    index, kind = slot % 4, slot // 4
+    if index < EARLY:
+        return early_ref[2 * index + kind]
+    return late_ref[2 * (index - EARLY) + kind]
+
+
+def moment_kernel(
+    early_ref,
+    late_ref,
+    m_qkv_ref,
+    m_out_ref,
+    m_up_ref,
+    m_down_ref,
+    g_qkv_ref,
+    g_out_ref,
+    g_up_ref,
+    g_down_ref,
+    n_qkv_ref,
+    n_out_ref,
+    n_up_ref,
+    n_down_ref,
+    slots_ref,
+):
+    first_packed = LATE_SLOTS - 3
+    for pair in range(SLOT // PAIR):
+        for part in range(3):
+            column = (pair * 3 + part) * PAIR
+            source = late_ref[first_packed + column // SLOT, :, column % SLOT : column % SLOT + PAIR]
+            g_qkv_ref[part, :, pair * PAIR : (pair + 1) * PAIR] = source
+    for part in range(3):
+        moment = MOMENTUM_DECAY * m_qkv_ref[part] + g_qkv_ref[part]
+        n_qkv_ref[part] = moment
+        slots_ref[part] = moment.astype(jnp.bfloat16)
+    grads = late_ref[first_packed - 1]
+    g_out_ref[...] = grads
+    moment = MOMENTUM_DECAY * m_out_ref[...] + grads
+    n_out_ref[...] = moment
+    slots_ref[3] = moment.astype(jnp.bfloat16)
+    for kind, refs in enumerate(((m_up_ref, g_up_ref, n_up_ref), (m_down_ref, g_down_ref, n_down_ref))):
+        old_ref, grads_ref, new_ref = refs
+        for index in range(4):
+            here = slice(index * SLOT, (index + 1) * SLOT)
+            grads = slot_rows(early_ref, late_ref, 4 * kind + index)
+            grads_ref[:, here] = grads
+            moment = MOMENTUM_DECAY * old_ref[:, here] + grads
+            new_ref[:, here] = moment
+            slots_ref[4 + 4 * kind + index] = moment.astype(jnp.bfloat16)
+
+
+def update_kernel(
+    updates_ref,
+    vec_sum_ref,
+    w_qkv_ref,
+    w_out_ref,
+    w_up_ref,
+    w_down_ref,
+    vectors_ref,
+    m_vec_ref,
+    o_qkv_ref,
+    o_out_ref,
+    o_up_ref,
+    o_down_ref,
+    g_vec_ref,
+    n_vec_ref,
+    o_vec_ref,
+):
+    wide_rate = MATRIX_RATE * math.sqrt(FF / D)
+    for part in range(3):
+        o_qkv_ref[part] = w_qkv_ref[part] - MATRIX_RATE * updates_ref[part].astype(jnp.float32)
+    o_out_ref[...] = w_out_ref[...] - MATRIX_RATE * updates_ref[3].astype(jnp.float32)
+    for index in range(4):
+        here = slice(index * SLOT, (index + 1) * SLOT)
+        o_up_ref[:, here] = w_up_ref[:, here] - wide_rate * updates_ref[4 + index].astype(jnp.float32)
+        o_down_ref[:, here] = w_down_ref[:, here] - wide_rate * updates_ref[8 + index].astype(jnp.float32)
+    grads = vec_sum_ref[...]
+    moment = MOMENTUM_DECAY * m_vec_ref[...] + grads
+    square = jnp.mean(moment * moment, axis=1, keepdims=True)
+    g_vec_ref[...] = grads
+    n_vec_ref[...] = moment
+    o_vec_ref[...] = vectors_ref[...] - VECTOR_RATE * moment * lax.rsqrt(square + SQUARE_EPSILON)
+
+
+def like(arrays):
+    return [jax.ShapeDtypeStruct(array.shape, jnp.float32) for array in arrays]
+
+
+def features_first(arrays):
+    qkv, out, up, down = arrays
+    return qkv, out.T, up, down.T
+
+
+def muon_step(early, late, vector_total, block_rows, token_grads, weights, vectors, momenta, m_vec):
+    limit = pltpu.CompilerParams(vmem_limit_bytes=VMEM_LIMIT)
+    weights, momenta = features_first(weights), features_first(momenta)
+    slots_shape = jax.ShapeDtypeStruct((SLOTS,) + late.shape[1:], jnp.bfloat16)
+    *stored, slots = pl.pallas_call(
+        moment_kernel, out_shape=like(momenta) + like(momenta) + [slots_shape], compiler_params=limit
+    )(early, late, *momenta)
+    updates, vector_rows, output_pair, token_pair = muon_call(
+        slots, vector_total.reshape(SLOTS, 8, 128), block_rows, token_grads
+    )
+    fresh = pl.pallas_call(
+        update_kernel, out_shape=like(weights) + like([vectors] * 3), compiler_params=limit
+    )(updates, vector_rows.reshape(12, D), *weights, vectors, m_vec)
+    vector_grad, moment_vec, new_vec = fresh[4:]
+    grads, moments, new = features_first(stored[:4]), features_first(stored[4:]), features_first(fresh[:4])
+    return (output_pair, token_pair.astype(jnp.float32), *grads, vector_grad, *moments, moment_vec, *new, new_vec)
+
+
+def by_slots(rows):
+    return jnp.swapaxes(rows.reshape(rows.shape[0], -1, SLOT), 0, 1)
+
+
 def narrow(rows):
     return rows.astype(jnp.bfloat16)
 
@@ -1806,14 +1903,6 @@
 
 def in_order(rank, own, got):
     return jnp.where(rank == 0, jnp.concatenate([own, got]), jnp.concatenate([got, own]))
-
-
-def swap_halves(mine, rank):
-    rows = mine.shape[0] // 2
-    kept = lax.dynamic_slice_in_dim(mine, rank * rows, rows, 0)
-    sent = lax.dynamic_slice_in_dim(mine, (1 - rank) * rows, rows, 0)
-    got = lax.ppermute(sent, "tensor", [(0, 1), (1, 0)])
-    return jnp.where(rank == 0, jnp.stack([kept, got]), jnp.stack([got, kept]))
 
 
 def by_pairs(rows):
@@ -1873,7 +1962,6 @@
         full_down,
         in_turn[2 * EARLY :],
     )
-    output_pair = swap_halves(block_rows, rank)
     grad_middle, grad_context, grad_out, middle_sums = middle_backward(
         middle, grad_normed_two, cotangent_low, context, vectors[5:6], full_out
     )
@@ -1881,8 +1969,6 @@
         packed, context, grad_context, stats, full_qkv, normed_t, exps, grad_up, grad_down, grad_out
     )
     grad_token_low, token_sums = token_backward(token_low, grad_normed_one, grad_middle, vectors[0:1])
-    token_pair = swap_halves(grad_token_low, rank).astype(jnp.float32)
-
     packed_sums = from_pairs(packed_grads)[:, 0]
     vector_total = jnp.concatenate(
         [
@@ -1895,14 +1981,11 @@
             middle_sums[3:4],
         ]
     )
-    shards = (
-        from_pairs(from_slots(sums[5:8])),
-        sums[4].T,
-        from_slots(jnp.concatenate([early_sums[0::2], sums[0:4:2]])),
-        from_slots(jnp.concatenate([early_sums[1::2], sums[1:4:2]])).T,
-    )
-    outputs = muon_step(shards, vector_total, w_qkv, w_out, w_up, w_down, vectors, m_qkv, m_out, m_up, m_down, m_vec)
-    return (output_pair, token_pair) + outputs
+    weights = (w_qkv, w_out, w_up, w_down)
+    momenta = (m_qkv, m_out, m_up, m_down)
+    return muon_step(
+        early_sums, sums, vector_total, block_rows, grad_token_low, weights, vectors, momenta, m_vec
+    )
 
 
 def solution(mesh):

time: 590 us -> 549 us (0.931)
  other arithmetic: 42.1 us -> 16.5 us
  local copies, waits for them, and re-layouts: 29.3 us -> 9.66 us
    pallas_call x1 -> x3, Pallas kernels: 116 us -> 128 us  [the longest x1 121 us: muon_call(): pl.pallas_call(muon_kernel, in_specs=[vmem, vmem, anywhere, anywhere], ou...]
    pallas_call x1, Pallas kernels: 101 us -> 90.8 us  [attend_spread(): pl.pallas_call(attend_spread_kernel, grid=(PAIRS,), in_specs=[SCALARS, SC...]
    convert_element_type x7 -> x4, other arithmetic: 11.4 us -> 2.22 us  [narrow(): return rows.astype(jnp.bfloat16)]
    another operation x3 -> x0, local copies, waits for them, and re-layouts: 7.62 us -> none  [the longest x2 5.46 us: swap_halves(): return jnp.where(rank == 0, jnp.stack([kept, got]), jnp.stack([got, kept]))]
  transfers between devices with their start and end apart: 2 -> 0, of which waited for: 0 -> 0; matrix products, arithmetic and copies ran while one was open for 7% -> 0% of each run, Pallas kernels for 20% -> 0%
where the time goes in v7:
time: 549 us; the launch traced here: 540 us
  Pallas kernels  508 us (93%)
  other arithmetic  16.5 us (3%)
  local copies, waits for them, and re-layouts  9.66 us (2%)
    pallas_call x1, Pallas kernels, muon_call(): pl.pallas_call(muon_kernel, in_specs=[vmem, vmem, anywhere, anywhere], ou...  121 us
    pallas_call x1, Pallas kernels, mlp_both(): pl.pallas_call(mlp_kernel, grid=(HIDDEN_STEPS,), in_specs=[whole, whole,...  108 us
    pallas_call x1, Pallas kernels, attend_sum(): pl.pallas_call(attend_sum_kernel, grid=(PAIRS,), in_specs=[PACKED_COLS, P...  101 us
    pallas_call x1, Pallas kernels, attend_spread(): pl.pallas_call(attend_spread_kernel, grid=(PAIRS,), in_specs=[SCALARS, SC...  90.8 us
    pallas_call x1, Pallas kernels, first_spread(): pl.pallas_call(first_spread_kernel, in_specs=[anywhere] * 2, out_specs=[a...  57.3 us
    pallas_call x1, Pallas kernels, middle_backward(): pl.pallas_call(middle_kernel, grid=(LEN // ROWS,), in_specs=[rows, rows,...  15.2 us

profile of v7, /device:TPU:9, one launch (start us, length us, event | category | flops | bytes accessed | tf_op | source)
XLA Modules:
  0.0 540.4 jit_solution(5757063270365406354)
XLA Ops:
  0.7 0.0 copy-start
  0.7 0.0 copy-start.9
  0.7 1.8 dynamic-slice_bitcast_fusion
  2.5 0.0 copy-done.9
  2.5 0.1 reshape.113
  2.6 0.2 copy.55
  2.7 0.2 reshape_reshape.3
  2.9 0.7 copy.56
  3.7 57.3 %shard_map.260 = (bf16[4,2,2,64,3072]{4,3,2,1,0:T(8,128)(2,1)}, bf16[512,1024]{1,0:T(8,128)(2,1)}) custom-call(bf16[3,64,512]{2,1,0:T(8,128)(2,1)} %bitcast.95, bf16[2,512,1024]{2,1,0:T(8,128)(2,1)} %tokens_ref.1), custom_call_target="tpu_custom_call" | custom-call | tf_op jit(solution)/shard_map/pallas_call | solution.py:1096
  61.0 2.1 convert_reduce_fusion
  63.1 0.0 copy-start.2
  63.1 0.0 copy-start.7
  63.1 0.0 copy-start.6
  63.1 0.7 fusion.2
  63.8 0.0 copy-start.11
  63.8 0.0 copy-done.12
  63.9 0.0 copy-start.13
  63.9 0.0 copy-start.14
  63.9 0.5 copy-done.2
  64.4 2.1 fusion.5.normed_ref
  66.5 0.1 pad.9.clone
  66.6 0.1 maximum_bitcast_fusion
  66.7 0.6 reshape.115.shifts_ref
  67.3 0.0 copy-done
  67.3 0.5 fusion.8.starts_ref
  67.8 0.0 copy-done.7
  67.9 0.0 copy-done.6
  68.0 0.8 pad_maximum_fusion.1
  68.7 0.0 copy-done.11
  68.7 0.8 pad_maximum_fusion.slots_ref
  69.5 0.0 copy-done.13
  69.5 0.5 multiply_exponential_fusion.slopes_ref
  70.0 90.8 %shard_map.261 = (bf16[1024,3072]{1,0:T(8,128)(2,1)}, bf16[1024,1024]{1,0:T(8,128)(2,1)}, bf16[16,1024,1024]{2,1,0:T(8,128)(2,1)}, f32[8,2,1024]{2,1,0:T(2,128)}...) custom-call(s32[2]{0:T(128)} %fusion.8.starts_ref, ...), custom_call_target="tpu_custom_call" | custom-call | flops 17179869184 | bytes 94371840 | tf_op jit(solution)/shard_map/pallas_call | solution.py:1109
  160.8 0.0 copy-done.3
  160.8 4.8 fusion.11
  165.6 0.6 multiply_reduce_fusion
  166.2 0.0 copy-done.14
  166.2 0.0 copy-start.10
  166.2 3.3 broadcast_add_fusion
  169.5 0.0 copy-done.4
  169.5 0.0 copy-done.10
  169.6 2.3 maximum_select_fusion.1.cot_ref
  171.9 0.6 copy.44
  172.5 107.9 %shard_map.262 = (bf16[1024,1024]{1,0:T(8,128)(2,1)}, f32[1024,1024]{1,0:T(8,128)}, bf16[1024,2048]{1,0:T(8,128)(2,1)}, bf16[1024,2048]{1,0:T(8,128)(2,1)}, f32[1,4096]{1,0:T(1,128)}, /*index=5*/f32[4,64,512]{2,1,0:T(8,128)}) custom-call(bf16[1024,1024]{1,0:T(8,128)(2,1)} %get-tuple-element.112.rows_ref, bf16[1024,1024]{1,0:T(8,128)(2,1)} %maximum_select_fusion.1.cot_ref, ...), custom_call_target="tpu_custom_call" | custom-call | flops 51539607552 | bytes 62914560 | tf_op jit(solution)/shard_map/pallas_call | solution.py:1455
  280.4 15.2 %shard_map.263 = (f32[1024,1024]{1,0:T(8,128)}, bf16[1024,1024]{1,0:T(8,128)(2,1)}, bf16[1024,1024]{1,0:T(8,128)(2,1)}, f32[8,1024]{1,0:T(8,128)}) custom-call(f32[1024,1024]{1,0:T(8,128)} %copy-done.4, f32[1024,1024]{1,0:T(8,128)} %get-tuple-element.72.grad_ref, bf16[1024,1024]{1,0:T(8,128)(2,1)} %maximum_select_fusion.1.cot_ref, ...), custom_call_target="tpu_custom_call" | custom-call | flops 4294967296 | bytes 25165824 | tf_op jit(solution)/shard_map/pallas_call | solution.py:1738
  295.5 101.4 %shard_map.264 = (f32[8,64,512]{2,1,0:T(8,128)}, f32[1024,1024]{1,0:T(8,128)}, f32[1,3072]{1,0:T(1,128)}) custom-call(bf16[1024,3072]{1,0:T(8,128)(2,1)} %get-tuple-element.71.packed_ref, bf16[1024,1024]{1,0:T(8,128)(2,1)} %get-tuple-element.65.ctx_ref, bf16[1024,1024]{1,0:T(8,128)(2,1)} %get-tuple-element.73.grad_ref, ...), custom_call_target="tpu_custom_call" | custom-call | flops 47244640256 | bytes 419430400 | tf_op jit(solution)/shard_map/pallas_call | solution.py:1656
  397.0 0.0 copy-start.16
  397.0 0.0 copy-start.17
  397.0 0.0 copy-start.15
  397.0 7.4 %shard_map.266 = (bf16[1024,1024]{1,0:T(8,128)(2,1)}, f32[8,1024]{1,0:T(8,128)}) custom-call(bf16[1024,1024]{1,0:T(8,128)(2,1)} %copy-done.2, f32[1024,1024]{1,0:T(8,128)} %get-tuple-element.82.grad_ref, f32[1024,1024]{1,0:T(8,128)} %get-tuple-element.83.grad_middle_ref, f32[1,1024]{1,0:T(1,128)} %copy-done.13), custom_call_target="tpu_custom_call" | custom-call | bytes 12582912 | tf_op jit(solution)/shard_map/pallas_call | solution.py:1769
  404.4 0.8 slice_bitcast_fusion.2
  405.1 0.5 broadcast.64
  405.6 0.0 copy-done.16
  405.6 0.7 reduce.3
  406.5 0.0 copy-start.18
  406.5 3.8 shard_map.265
  410.3 121.5 %shard_map.267 = (bf16[12,64,512]{2,1,0:T(8,128)(2,1)}, f32[12,8,128]{2,1,0:T(8,128)}, bf16[2,512,1024]{2,1,0:T(8,128)(2,1)}, bf16[2,512,1024]{2,1,0:T(8,128)(2,1)}) custom-call(bf16[12,64,512]{2,1,0:T(8,128)(2,1)} %get-tuple-element.81.moments_ref, f32[12,8,128]{2,1,0:T(8,128)} %copy-done.18, bf16[1024,1024]{1,0:T(8,128)(2,1)} %get-tuple-element.88.block_ref, ...), custom_call_target="tpu_custom_call" | custom-call | flops 25769803776 | bytes 4194304 | tf_op jit(solution)/shard_map/pallas_call | solution.py:810
  531.8 0.0 copy-start.5
  531.8 1.0 pad.17
  532.7 0.6 copy.47
  533.4 3.0 shard_map.268
  536.4 0.0 copy-done.5
  536.4 2.5 convert_element_type.31
  538.9 1.3 copy.65
  (32 shorter events, 0.3 us)
Async XLA Ops:
  0.7 66.7 %copy-start = (s32[2,1,2]{2,1,0:T(1,128)S(1)}, s32[2,1,2]{2,1,0:T(1,128)}, u32[]{:S(2)}) copy-start(s32[2,1,2]{2,1,0:T(1,128)} %param.15) | copy-start | bytes 52
  0.7 1.8 copy-start.9
  3.7 60.2 %copy-start.12 = (f32[12,1024]{1,0:T(8,128)S(1)}, f32[12,1024]{1,0:T(8,128)}, u32[]{:S(2)}) copy-start(f32[12,1024]{1,0:T(8,128)} %vectors_ref.1) | copy-start | bytes 147460
  63.1 1.3 copy-start.2
  63.1 4.8 copy-start.7
  63.1 4.8 copy-start.6
  63.8 4.9 copy-start.11
  63.9 5.6 %copy-start.13 = (f32[1,1024]{1,0:T(1,128)}, f32[1,1024]{1,0:T(1,128)S(1)}, u32[]{:S(2)}) copy-start(f32[1,1024]{1,0:T(1,128)S(1)} %get-tuple-element.122.gain_ref) | copy-start | bytes 12292
  63.9 102.3 %copy-start.14 = (f32[1,1024]{1,0:T(1,128)}, f32[1,1024]{1,0:T(1,128)S(1)}, u32[]{:S(2)}) copy-start(f32[1,1024]{1,0:T(1,128)S(1)} %get-tuple-element.117.gain_ref) | copy-start | bytes 12292
  70.0 90.8 %copy-start.3 = (bf16[1024,1024]{1,0:T(8,128)(2,1)S(1)}, bf16[1024,1024]{1,0:T(8,128)(2,1)}, u32[]{:S(2)}) copy-start(bf16[1024,1024]{1,0:T(8,128)(2,1)} %copy-done.2) | copy-start | bytes 6291460
  165.6 3.9 copy-start.4
  166.2 3.3 copy-start.10
  397.0 8.7 %copy-start.16 = (f32[1,3072]{1,0:T(1,128)S(1)}, f32[1,3072]{1,0:T(1,128)}, u32[]{:S(2)}) copy-start(f32[1,3072]{1,0:T(1,128)} %get-tuple-element.85) | copy-start | bytes 36868
  397.0 9.4 %copy-start.17 = (f32[8,1024]{1,0:T(8,128)S(1)}, f32[8,1024]{1,0:T(8,128)}, u32[]{:S(2)}) copy-start(f32[8,1024]{1,0:T(8,128)} %get-tuple-element.86) | copy-start | bytes 98308
  397.0 9.4 %copy-start.15 = (f32[1,4096]{1,0:T(1,128)S(1)}, f32[1,4096]{1,0:T(1,128)}, u32[]{:S(2)}) copy-start(f32[1,4096]{1,0:T(1,128)} %get-tuple-element.87) | copy-start | bytes 49156
  406.5 3.8 copy-start.18
  531.8 4.6 copy-start.5
  533.4 5.5 %copy-start.8 = (bf16[2,512,1024]{2,1,0:T(8,128)(2,1)S(1)}, bf16[2,512,1024]{2,1,0:T(8,128)(2,1)}, u32[]{:S(2)}) copy-start(bf16[2,512,1024]{2,1,0:T(8,128)(2,1)} %get-tuple-element.148) | copy-start | bytes 6291460
  536.4 3.8 copy-start.1

commit v8 on v7

--- a/solution.py
+++ b/solution.py
@@ -478,800 +478,6 @@
 PAIR_GRID = pl.BlockSpec((2, LEN, LEN), lambda p: (p, 0, 0))
 PAIR_STAT = pl.BlockSpec((1, 2, LEN), lambda p: (p, 0, 0))
 SCALARS = pl.BlockSpec(memory_space=pltpu.SMEM)
-
-
-SLOTS = 12
-SLOT = 512
-HALF_SLOT = SLOT // 2
-TILE = 256
-GRAM_TILES = 5
-MESH_IDS = pl.DeviceIdType.MESH
-
-
-def handler_of(slot):
-    wide = slot - 4
-    square = slot < 4
-    dp_index = jnp.where(square, jnp.where(slot < 2, 2, 12), 4 + 6 * (wide // 4) + wide % 2)
-    tensor_index = jnp.where(square, slot % 2, (wide // 2) % 2)
-    return dp_index, tensor_index
-
-
-def muon_kernel(
-    moments_ref,
-    vec_ref,
-    block_ref,
-    token_ref,
-    updates_ref,
-    vec_out_ref,
-    block_pair_ref,
-    token_pair_ref,
-    pieces,
-    turned,
-    vec_pieces,
-    vec_sum,
-    gram,
-    gram_low,
-    poly_low,
-    half_low,
-    chain_low,
-    chain_next,
-    out_half,
-    in_half,
-    local_sem,
-    send_sem,
-    recv_sem,
-    half_send,
-    half_recv,
-    swap_sem,
-):
-    groups = lax.axis_size("dp")
-    parts = lax.axis_size("tensor")
-    count = groups * parts
-    dp_me = lax.axis_index("dp")
-    t_me = lax.axis_index("tensor")
-    me = t_me * groups + dp_me
-    is_square = (dp_me == 2) | (dp_me == 12)
-    is_up = (dp_me == 4) | (dp_me == 5)
-    is_down = (dp_me == 10) | (dp_me == 11)
-    is_wide = is_up | is_down
-    is_handler = is_square | is_wide
-    wide_slot = jnp.where(is_up, 4 + (dp_me - 4), 8 + (dp_me - 10)) + 2 * t_me
-    slot_me = jnp.where(is_square, t_me + jnp.where(dp_me == 12, 2, 0), wide_slot)
-    slot_me = jnp.where(is_handler, slot_me, 0)
-
-    barrier = pltpu.get_barrier_semaphore()
-
-    def greet(step, carry):
-        other = lax.rem(me + step, count)
-        pl.semaphore_signal(
-            barrier, inc=1, device_id=(lax.rem(other, groups), other // groups), device_id_type=MESH_IDS
-        )
-        return carry
-
-    lax.fori_loop(1, count, greet, 0)
-    pl.semaphore_wait(barrier, count - 1)
-
-    def give(step, carry):
-        slot = lax.rem(me + step, SLOTS)
-        dp_to, t_to = handler_of(slot)
-        away = (dp_to != dp_me) | (t_to != t_me)
-
-        @pl.when(away)
-        def _():
-            pltpu.make_async_remote_copy(
-                src_ref=vec_ref.at[slot],
-                dst_ref=vec_pieces.at[me],
-                send_sem=send_sem.at[1],
-                recv_sem=recv_sem.at[1],
-                device_id=(dp_to, t_to),
-                device_id_type=MESH_IDS,
-            ).start()
-            pltpu.make_async_remote_copy(
-                src_ref=moments_ref.at[slot],
-                dst_ref=pieces.at[me],
-                send_sem=send_sem.at[0],
-                recv_sem=recv_sem.at[0],
-                device_id=(dp_to, t_to),
-                device_id_type=MESH_IDS,
-            ).start()
-
-        return carry
-
-    lax.fori_loop(0, SLOTS, give, 0)
-
-    rows = block_ref.shape[0] // 2
-    kept_rows = pl.ds(pl.multiple_of(t_me * rows, rows), rows)
-    sent_rows = pl.ds(pl.multiple_of((1 - t_me) * rows, rows), rows)
-    kept = []
-    swaps = []
-    for index, (whole, pair) in enumerate(((block_ref, block_pair_ref), (token_ref, token_pair_ref))):
-        kept.append(pltpu.make_async_copy(whole.at[kept_rows], pair.at[t_me], swap_sem.at[2, index]))
-        swaps.append(
-            pltpu.make_async_remote_copy(
-                src_ref=whole.at[sent_rows],
-                dst_ref=pair.at[t_me],
-                send_sem=swap_sem.at[0, index],
-                recv_sem=swap_sem.at[1, index],
-                device_id=(dp_me, 1 - t_me),
-                device_id_type=MESH_IDS,
-            )
-        )
-
-    @pl.when(jnp.logical_not(is_wide))
-    def _():
-        for copy in kept + swaps:
-            copy.start()
-
-    def give_back(source, sem, target):
-        def one(step, carry):
-            other = lax.rem(me + step, count)
-            pltpu.make_async_remote_copy(
-                src_ref=source.at[other] if source is turned else source,
-                dst_ref=target.at[slot_me],
-                send_sem=send_sem.at[sem],
-                recv_sem=recv_sem.at[sem],
-                device_id=(lax.rem(other, groups), other // groups),
-                device_id_type=MESH_IDS,
-            ).start()
-            return carry
-
-        lax.fori_loop(1, count, one, 0)
-
-    @pl.when(is_handler)
-    def _():
-        own = [
-            pltpu.make_async_copy(vec_ref.at[slot_me], vec_pieces.at[me], local_sem.at[0]),
-            pltpu.make_async_copy(moments_ref.at[slot_me], pieces.at[me], local_sem.at[1]),
-        ]
-        for copy in own:
-            copy.start()
-        for copy in own:
-            copy.wait()
-        rest = pl.ds(0, count - 1)
-        pltpu.make_async_copy(vec_pieces.at[rest], vec_pieces.at[rest], recv_sem.at[1]).wait()
-        vec_sum[...] = jnp.sum(vec_pieces[...], axis=0)
-        give_back(vec_sum, 2, vec_out_ref)
-        own_vec = pltpu.make_async_copy(vec_sum, vec_out_ref.at[slot_me], local_sem.at[0])
-        own_vec.start()
-        own_vec.wait()
-        pltpu.make_async_copy(pieces.at[rest], pieces.at[rest], recv_sem.at[0]).wait()
-
-        rows_of = TILE // 64
-
-        def gram_tile(tile, carry):
-            rows = pl.ds(pl.multiple_of(tile * TILE, TILE), TILE)
-            total = jnp.zeros((TILE, D), jnp.float32)
-            for part in range(parts):
-                left = pieces[pl.ds(part * groups + tile * rows_of, rows_of)].reshape(TILE, SLOT)
-                right = pieces[part * groups : (part + 1) * groups].reshape(D, SLOT)
-                total += lax.dot_general(
-                    left, right, (((1,), (1,)), ((), ())), preferred_element_type=jnp.float32
-                )
-            gram[rows, :] = total
-            return carry
-
-        lax.fori_loop(0, D // TILE, gram_tile, 0)
-
-        @pl.when(is_wide)
-        def _():
-            core = lax.rem(dp_me, 2)
-            sibling = (dp_me + 1 - 2 * core, t_me)
-            across = (dp_me, 1 - t_me)
-
-            def tile_at(index, owner):
-                if index == 4:
-                    row, col = jnp.where(owner == 0, 3, 2), 3
-                elif index == 3:
-                    row, col = jnp.where(owner == 0, 0, 2), jnp.where(owner == 0, 3, 2)
-                else:
-                    row, col = owner, owner + index
-                return (
-                    pl.ds(pl.multiple_of(row * TILE, TILE), TILE),
-                    pl.ds(pl.multiple_of(col * TILE, TILE), TILE),
-                )
-
-            def exchange(stage, index, place):
-                return pltpu.make_async_remote_copy(
-                    src_ref=out_half.at[stage, index],
-                    dst_ref=in_half.at[stage, index],
-                    send_sem=half_send.at[stage, index],
-                    recv_sem=half_recv.at[stage, index],
-                    device_id=place,
-                    device_id_type=MESH_IDS,
-                )
-
-            for index in range(GRAM_TILES):
-                out_half[0, index] = gram[tile_at(index, 1 - core)].astype(jnp.bfloat16)
-                exchange(0, index, sibling).start()
-            for index in range(GRAM_TILES):
-                exchange(0, index, sibling).wait_recv()
-                total = gram[tile_at(index, core)] + in_half[0, index].astype(jnp.float32)
-                out_half[1, index] = total.astype(jnp.bfloat16)
-                exchange(1, index, across).start()
-            for index in range(GRAM_TILES):
-                exchange(1, index, across).wait_recv()
-                total = out_half[1, index].astype(jnp.float32) + in_half[1, index].astype(jnp.float32)
-                out_half[2, index] = total.astype(jnp.bfloat16)
-                exchange(2, index, sibling).start()
-                rows, cols = tile_at(index, core)
-                gram[cols, rows] = out_half[2, index].astype(jnp.float32).T
-                gram[rows, cols] = out_half[2, index].astype(jnp.float32)
-            for index in range(GRAM_TILES):
-                exchange(2, index, sibling).wait_recv()
-                rows, cols = tile_at(index, 1 - core)
-                gram[cols, rows] = in_half[2, index].astype(jnp.float32).T
-                gram[rows, cols] = in_half[2, index].astype(jnp.float32)
-            for index in range(GRAM_TILES):
-                exchange(0, index, sibling).wait_send()
-                exchange(1, index, across).wait_send()
-                exchange(2, index, sibling).wait_send()
-            for copy in kept + swaps:
-                copy.start()
-
-        def trace_tile(tile, total):
-            rows = pl.ds(pl.multiple_of(tile * TILE, TILE), TILE)
-            row_ids = lax.broadcasted_iota(jnp.int32, (TILE, D), 0) + tile * TILE
-            col_ids = lax.broadcasted_iota(jnp.int32, (TILE, D), 1)
-            diagonal = jnp.where(row_ids == col_ids, gram[rows, :], 0.0)
-            return total + jnp.sum(jnp.sum(diagonal, axis=0, keepdims=True), axis=1, keepdims=True)
-
-        square_total = lax.fori_loop(0, D // TILE, trace_tile, jnp.zeros((1, 1), jnp.float32))
-        factor = lax.rsqrt(square_total + SQUARE_EPSILON)
-        gram_low[...] = (gram[...] * (factor * factor)).astype(jnp.bfloat16)
-
-        first, second, third = SCHULZ_FIRST, SCHULZ_SECOND, SCHULZ_THIRD
-
-        def tiles(body):
-            def one(tile, carry):
-                body(pl.ds(pl.multiple_of(tile * TILE, TILE), TILE))
-                return carry
-
-            lax.fori_loop(0, D // TILE, one, 0)
-
-        chain = chain_low
-        other = chain_next
-        for sweep in range(NS_ITERS):
-            target = chain if sweep == 0 else poly_low
-
-            def poly(rows):
-                square = mul(gram_low[rows, :], gram_low[...])
-                grown = (second / first) * gram_low[rows, :].astype(jnp.float32) + (third / first) * square
-                target[rows, :] = grown.astype(jnp.bfloat16)
-
-            tiles(poly)
-            if sweep > 0:
-
-                def join(rows, chain=chain, other=other):
-                    total = chain[rows, :].astype(jnp.float32) + poly_low[rows, :].astype(jnp.float32)
-                    other[rows, :] = (total + mul(chain[rows, :], poly_low[...])).astype(jnp.bfloat16)
-
-                tiles(join)
-                chain, other = other, chain
-            if sweep < NS_ITERS - 1:
-
-                def half(rows):
-                    grown = gram_low[rows, :].astype(jnp.float32) + mul(gram_low[rows, :], target[...])
-                    half_low[rows, :] = grown.astype(jnp.bfloat16)
-
-                def full(rows):
-                    grown = half_low[rows, :].astype(jnp.float32) + mul(half_low[rows, :], target[...])
-                    gram_low[rows, :] = (grown * (first * first)).astype(jnp.bfloat16)
-
-                tiles(half)
-                tiles(full)
-
-        scale = factor * (first**NS_ITERS)
-
-        def turn_tile(tile, carry):
-            rows = pl.ds(pl.multiple_of(tile * TILE, TILE), TILE)
-            for part in range(parts):
-                at = pl.ds(part * groups + tile * rows_of, rows_of)
-                whole = pieces[part * groups : (part + 1) * groups].reshape(D, SLOT)
-                kept = pieces[at].reshape(TILE, SLOT).astype(jnp.float32)
-                fresh = (kept + mul(chain[rows, :], whole)) * scale
-                turned[at] = fresh.astype(jnp.bfloat16).reshape(rows_of, 64, SLOT)
-            return carry
-
-        lax.fori_loop(0, D // TILE, turn_tile, 0)
-        give_back(turned, 3, updates_ref)
-        own_turned = pltpu.make_async_copy(turned.at[me], updates_ref.at[slot_me], local_sem.at[1])
-        own_turned.start()
-        own_turned.wait()
-
-    def finish(length):
-        here = pl.ds(0, length)
-        pltpu.make_async_copy(vec_ref.at[here], vec_ref.at[here], send_sem.at[1]).wait()
-        pltpu.make_async_copy(moments_ref.at[here], moments_ref.at[here], send_sem.at[0]).wait()
-        pltpu.make_async_copy(vec_out_ref.at[here], vec_out_ref.at[here], recv_sem.at[2]).wait()
-        pltpu.make_async_copy(updates_ref.at[here], updates_ref.at[here], recv_sem.at[3]).wait()
-
-    @pl.when(is_handler)
-    def _():
-        finish(SLOTS - 1)
-        rest = pl.ds(0, count - 1)
-        pltpu.make_async_copy(vec_pieces.at[rest], vec_pieces.at[rest], send_sem.at[2]).wait()
-        pltpu.make_async_copy(turned.at[rest], turned.at[rest], send_sem.at[3]).wait()
-
-    @pl.when(jnp.logical_not(is_handler))
-    def _():
-        finish(SLOTS)
-
-    for copy in kept + swaps:
-        copy.wait()
-
-
-def muon_call(moments, vec_parts, block_rows, token_grads):
-    count = lax.axis_size("dp") * lax.axis_size("tensor")
-    rows = moments.shape[1]
-    vmem = pl.BlockSpec(memory_space=pltpu.VMEM)
-    anywhere = pl.BlockSpec(memory_space=pl.ANY)
-    pair = jax.ShapeDtypeStruct((2, LEN // 2, D), jnp.bfloat16)
-    low = pltpu.VMEM((D, D), jnp.bfloat16)
-    return pl.pallas_call(
-        muon_kernel,
-        in_specs=[vmem, vmem, anywhere, anywhere],
-        out_specs=[vmem, vmem, anywhere, anywhere],
-        out_shape=[
-            jax.ShapeDtypeStruct(moments.shape, jnp.bfloat16),
-            jax.ShapeDtypeStruct(vec_parts.shape, jnp.float32),
-            pair,
-            pair,
-        ],
-        scratch_shapes=[
-            pltpu.VMEM((count, rows, SLOT), jnp.bfloat16),
-            pltpu.VMEM((count, rows, SLOT), jnp.bfloat16),
-            pltpu.VMEM((count,) + vec_parts.shape[1:], jnp.float32),
-            pltpu.VMEM(vec_parts.shape[1:], jnp.float32),
-            pltpu.VMEM((D, D), jnp.float32),
-            low,
-            low,
-            low,
-            low,
-            low,
-            pltpu.VMEM((3, GRAM_TILES, TILE, TILE), jnp.bfloat16),
-            pltpu.VMEM((3, GRAM_TILES, TILE, TILE), jnp.bfloat16),
-            pltpu.SemaphoreType.DMA((2,)),
-            pltpu.SemaphoreType.DMA((4,)),
-            pltpu.SemaphoreType.DMA((4,)),
-            pltpu.SemaphoreType.DMA((3, GRAM_TILES)),
-            pltpu.SemaphoreType.DMA((3, GRAM_TILES)),
-            pltpu.SemaphoreType.DMA((3, 2)),
-        ],
-        compiler_params=pltpu.CompilerParams(
-            collective_id=1, has_side_effects=True, vmem_limit_bytes=VMEM_LIMIT
-        ),
-        cost_estimate=pl.CostEstimate(flops=12 * 2 * D**3, bytes_accessed=4 * 1024 * 1024, transcendentals=0),
-    )(moments, vec_parts, block_rows, token_grads)
-
-
-def neighbours():
-    dp_me = lax.axis_index("dp")
-    y = lax.axis_index("tensor")
-    core = lax.rem(dp_me, 2)
-    x = lax.rem(dp_me // 2, 2)
-    z = dp_me // 4
-    sibling = (dp_me + 1 - 2 * core, y)
-    beside = (dp_me + 2 - 4 * x, y)
-    across = (dp_me, 1 - y)
-    stations = [(lax.rem(dp_me + 4 * hop, 16), y) for hop in (1, 2, 3)]
-    return (z, x, core, y), sibling, beside, across, stations
-
-
-def greet_neighbours(places):
-    barrier = pltpu.get_barrier_semaphore()
-    for place in places:
-        pl.semaphore_signal(barrier, inc=1, device_id=place, device_id_type=MESH_IDS)
-    pl.semaphore_wait(barrier, len(places))
-
-
-SWAP_AT = 2
-EARLY = 2
-AHEAD = 2
-SPREAD_LAG = 1
-
-
-class Spread:
-    def __init__(self, slots_ref, table, local_sem, send_sem, recv_sem):
-        self.slots_ref, self.table = slots_ref, table
-        self.local_sem, self.send_sem, self.recv_sem = local_sem, send_sem, recv_sem
-        (self.z, self.x, self.core, self.y), self.sibling, self.beside, self.across, self.stations = neighbours()
-
-    def remote(self, source, target, stage, slot, place):
-        return pltpu.make_async_remote_copy(
-            src_ref=source,
-            dst_ref=target,
-            send_sem=self.send_sem.at[stage, slot],
-            recv_sem=self.recv_sem.at[stage, slot],
-            device_id=place,
-            device_id_type=MESH_IDS,
-        )
-
-    def own(self, slot):
-        here = self.table[slot][0](self.y, 0, SLOT).at[self.z, self.x, self.core]
-        return pltpu.make_async_copy(self.slots_ref.at[slot], here, self.local_sem.at[slot])
-
-    def along_z(self, slot):
-        here = self.table[slot][0](self.y, 0, SLOT).at[self.z, self.x, self.core]
-        return [
-            self.remote(self.slots_ref.at[slot], here, hop, slot, place)
-            for hop, place in enumerate(self.stations)
-        ]
-
-    def second(self, slot):
-        view, size = self.table[slot]
-        copies = []
-        if size:
-            part = view(self.y, 0, size).at[:, self.x, self.core]
-            copies.append(self.remote(part, part, 3, slot, self.beside))
-        if size < SLOT:
-            part = view(self.y, size, SLOT - size).at[:, self.x, self.core]
-            copies.append(self.remote(part, part, 4, slot, self.across))
-        return copies
-
-    def third(self, slot):
-        view, size = self.table[slot]
-        copies = []
-        if size:
-            part = view(self.y, 0, size).at[:, :, self.core]
-            copies.append(self.remote(part, part, 5, slot, self.across))
-        if size < SLOT:
-            for index in (0, 1):
-                part = view(index, size, SLOT - size).at[:, self.x, self.core]
-                copies.append(self.remote(part, part, 6 + index, slot, self.beside))
-        return copies
-
-    def fourth(self, slot):
-        view, _ = self.table[slot]
-        copies = []
-        for index in (0, 1):
-            part = view(index, 0, SLOT).at[:, :, self.core]
-            copies.append(self.remote(part, part, 8 + index, slot, self.sibling))
-        return copies
-
-    def launch(self, slot):
-        if slot < len(self.table):
-            self.own(slot).start()
-            for copy in self.along_z(slot):
-                copy.start()
-
-    def begin(self):
-        for slot in range(AHEAD):
-            self.launch(slot)
-
-    def tick(self, index):
-        count = len(self.table)
-        self.launch(index + AHEAD)
-        if index < count:
-            self.own(index).wait()
-            for copy in self.along_z(index):
-                copy.wait_recv()
-            for copy in self.second(index):
-                copy.start()
-        if 0 <= index - SPREAD_LAG < count:
-            for copy in self.second(index - SPREAD_LAG):
-                copy.wait_recv()
-            for copy in self.third(index - SPREAD_LAG):
-                copy.start()
-        if 0 <= index - 2 * SPREAD_LAG < count:
-            for copy in self.third(index - 2 * SPREAD_LAG):
-                copy.wait_recv()
-            for copy in self.fourth(index - 2 * SPREAD_LAG):
-                copy.start()
-
-    def ticks(self):
-        return len(self.table) + 2 * SPREAD_LAG
-
-    def arrived(self, slot):
-        for copy in self.fourth(slot):
-            copy.wait_recv()
-
-    def sent(self):
-        for slot in range(len(self.table)):
-            for copy in self.along_z(slot) + self.second(slot) + self.third(slot) + self.fourth(slot):
-                copy.wait_send()
-
-    def finish(self):
-        for slot in range(len(self.table)):
-            self.arrived(slot)
-        self.sent()
-
-
-def column_view(ref, column, distance):
-    def view(part, start, size):
-        first = column + part * distance + start
-        if not isinstance(part, int):
-            first = pl.multiple_of(first, 128)
-        return ref.at[:, :, :, :, pl.ds(first, size)]
-
-    return view
-
-
-def place_view(ref, place):
-    def view(part, start, size):
-        return ref.at[place + part, :, :, :, :, pl.ds(start, size)]
-
-    return view
-
-
-def spread_semaphores(count):
-    return [
-        pltpu.SemaphoreType.DMA((count,)),
-        pltpu.SemaphoreType.DMA((10, count)),
-        pltpu.SemaphoreType.DMA((10, count)),
-    ]
-
-
-def first_spread_kernel(slots_ref, tokens_ref, whole_ref, got_ref, local_sem, send_sem, recv_sem, token_sem):
-    table = [(column_view(whole_ref, index * SLOT, 3 * SLOT), 0) for index in range(3)]
-    spread = Spread(slots_ref, table, local_sem, send_sem, recv_sem)
-    greet_neighbours([spread.sibling, spread.beside, spread.across] + spread.stations)
-    swap = pltpu.make_async_remote_copy(
-        src_ref=tokens_ref.at[1 - spread.y],
-        dst_ref=got_ref,
-        send_sem=token_sem.at[0],
-        recv_sem=token_sem.at[1],
-        device_id=spread.across,
-        device_id_type=MESH_IDS,
-    )
-    spread.begin()
-    for index in range(spread.ticks()):
-        spread.tick(index)
-        if index == SWAP_AT:
-            swap.start()
-    spread.finish()
-    swap.wait()
-
-
-def attend_spread_kernel(
-    starts_ref,
-    slopes_ref,
-    normed_ref,
-    weights_ref,
-    shifts_ref,
-    slots_ref,
-    cotangent_ref,
-    packed_ref,
-    ctx_ref,
-    exps_ref,
-    stat_ref,
-    normed_t_ref,
-    out_ref,
-    up_ref,
-    down_ref,
-    got_ref,
-    dist_ref,
-    ctx_t,
-    local_sem,
-    send_sem,
-    recv_sem,
-    token_sem,
-):
-    pair = pl.program_id(0)
-    table = [(column_view(out_ref, 0, SLOT), HALF_SLOT)]
-    for index in range(EARLY):
-        over_x = HALF_SLOT if index == EARLY - 1 else 0
-        table += [(column_view(ref, index * SLOT, EARLY * SLOT), over_x) for ref in (up_ref, down_ref)]
-    spread = Spread(slots_ref, table, local_sem, send_sem, recv_sem)
-    swap = pltpu.make_async_remote_copy(
-        src_ref=cotangent_ref.at[1 - spread.y],
-        dst_ref=got_ref,
-        send_sem=token_sem.at[0],
-        recv_sem=token_sem.at[1],
-        device_id=spread.across,
-        device_id_type=MESH_IDS,
-    )
-
-    @pl.when(pair == 0)
-    def _():
-        greet_neighbours([spread.sibling, spread.beside, spread.across] + spread.stations)
-        spread.begin()
-        normed_t_ref[...] = normed_ref[...].T
-        layout_grid(starts_ref, dist_ref)
-
-    def between():
-        for index in range(spread.ticks()):
-
-            @pl.when(pair == index)
-            def _(index=index):
-                spread.tick(index)
-                if index == len(table) - 1:
-                    swap.start()
-
-    packed = (mul(normed_ref[...], weights_ref[...]) + shifts_ref[...]).astype(jnp.bfloat16)
-    packed_ref[...] = packed
-    attend_pair(pair, slopes_ref, packed, dist_ref, ctx_ref, exps_ref, stat_ref, ctx_t, between)
-
-    @pl.when(pair == PAIRS - 1)
-    def _():
-        spread.finish()
-        swap.wait()
-
-
-def whole_shape(columns):
-    return jax.ShapeDtypeStruct((4, 2, 2, 64, columns), jnp.bfloat16)
-
-
-def first_spread(slots, tokens):
-    anywhere = pl.BlockSpec(memory_space=pl.ANY)
-    whole, got = pl.pallas_call(
-        first_spread_kernel,
-        in_specs=[anywhere] * 2,
-        out_specs=[anywhere] * 2,
-        out_shape=[whole_shape(3 * D), jax.ShapeDtypeStruct(tokens.shape[1:], tokens.dtype)],
-        scratch_shapes=spread_semaphores(3) + [pltpu.SemaphoreType.DMA((2,))],
-        compiler_params=pltpu.CompilerParams(collective_id=3, has_side_effects=True),
-    )(slots, tokens)
-    return whole.reshape(D, 3 * D), got
-
-
-def attend_spread(starts, slopes, normed, weights, shifts, slots, cotangent):
-    anywhere = pl.BlockSpec(memory_space=pl.ANY)
-    packed, context, exps, stats, normed_t, out, up, down, got = pl.pallas_call(
-        attend_spread_kernel,
-        grid=(PAIRS,),
-        in_specs=[
-            SCALARS,
-            SCALARS,
-            pl.BlockSpec((LEN, D), lambda p: (0, 0)),
-            PACKED_COLS,
-            pl.BlockSpec((1, 3 * PAIR), lambda p: (0, p)),
-            anywhere,
-            anywhere,
-        ],
-        out_specs=[PACKED_COLS, PAIR_COLS, PAIR_GRID, PAIR_STAT, pl.BlockSpec((D, LEN), lambda p: (0, 0))]
-        + [anywhere] * 4,
-        out_shape=[
-            jax.ShapeDtypeStruct((LEN, 3 * D), jnp.bfloat16),
-            jax.ShapeDtypeStruct((LEN, D), jnp.bfloat16),
-            jax.ShapeDtypeStruct((H, LEN, LEN), jnp.bfloat16),
-            jax.ShapeDtypeStruct((PAIRS, 2, LEN), jnp.float32),
-            jax.ShapeDtypeStruct((D, LEN), jnp.bfloat16),
-            whole_shape(D),
-            whole_shape(2 * EARLY * SLOT),
-            whole_shape(2 * EARLY * SLOT),
-            jax.ShapeDtypeStruct(cotangent.shape[1:], cotangent.dtype),
-        ],
-        scratch_shapes=[pltpu.VMEM((LEN, LEN), jnp.float32), pltpu.VMEM((PAIR, LEN), jnp.float32)]
-        + spread_semaphores(1 + 2 * EARLY)
-        + [pltpu.SemaphoreType.DMA((2,))],
-        compiler_params=pltpu.CompilerParams(
-            collective_id=4, has_side_effects=True, vmem_limit_bytes=VMEM_LIMIT
-        ),
-        cost_estimate=pl.CostEstimate(
-            flops=16 * LEN * LEN * D, bytes_accessed=90 * 1024 * 1024, transcendentals=H * LEN * LEN
-        ),
-    )(starts, slopes, normed, weights, shifts, slots, cotangent)
-    wholes = out.reshape(D, D), up.reshape(D, -1), down.reshape(D, -1)
-    return packed, context, exps, stats, normed_t, wholes, got
-
-
-class Summing:
-    def __init__(self, sources, add_own, buffers, total_ref, sems, lag, ready=0, hold=0):
-        self.sources, self.add_own, self.total_ref, self.lag = sources, add_own, total_ref, lag
-        self.ready, self.hold = ready, hold
-        self.first, self.second_y, self.second_x, self.third, self.fourth = buffers
-        self.send_sem, self.recv_sem = sems
-        (self.z, self.x, self.core, self.y), self.sibling, self.beside, self.across, self.stations = neighbours()
-        self.low_cols = pl.ds(0, HALF_SLOT)
-        self.high_cols = pl.ds(HALF_SLOT, HALF_SLOT)
-
-    def count(self):
-        return len(self.sources)
-
-    def remote(self, source, target, stage, slot, place):
-        return pltpu.make_async_remote_copy(
-            src_ref=source,
-            dst_ref=target,
-            send_sem=self.send_sem.at[stage, slot],
-            recv_sem=self.recv_sem.at[stage, slot],
-            device_id=place,
-            device_id_type=MESH_IDS,
-        )
-
-    def landed(self, ref, stage, slot):
-        pltpu.make_async_copy(ref, ref, self.recv_sem.at[stage, slot]).wait()
-
-    def send_first(self, slot):
-        for part in (0, 1):
-            source = self.sources[slot](part).at[:, :, 1 - self.core]
-            self.remote(source, self.first.at[slot, part], 0, slot, self.sibling).start()
-
-    def second_copies(self, slot):
-        for_y = self.first.at[slot, 1 - self.y, :, :, :, self.low_cols]
-        for_x = self.first.at[slot, :, :, 1 - self.x, :, self.high_cols]
-        return (
-            self.remote(for_y, self.second_y.at[slot], 1, slot, self.across),
-            self.remote(for_x, self.second_x.at[slot], 2, slot, self.beside),
-        )
-
-    def third_copies(self, slot):
-        for_x = self.second_y.at[slot, :, 1 - self.x]
-        for_y = self.second_x.at[slot, 1 - self.y]
-        return (
-            self.remote(for_x, self.third.at[slot, :, :, self.low_cols], 3, slot, self.beside),
-            self.remote(for_y, self.third.at[slot, :, :, self.high_cols], 4, slot, self.across),
-        )
-
-    def fourth_copies(self, slot):
-        return tuple(
-            self.remote(
-                self.third.at[slot, lax.rem(self.z + hop, 4)], self.fourth.at[slot, hop - 1], 4 + hop, slot, place
-            )
-            for hop, place in zip((1, 2, 3), self.stations)
-        )
-
-    def stage_one(self, slot):
-        self.landed(self.first.at[slot], 0, slot)
-        self.add_own(slot)
-        for copy in self.second_copies(slot):
-            copy.start()
-
-    def stage_two(self, slot):
-        first, second_y, second_x = self.first, self.second_y, self.second_x
-        self.landed(second_y.at[slot], 1, slot)
-        second_y[slot] = second_y[slot] + first[slot, self.y, :, :, :, :HALF_SLOT]
-        self.landed(second_x.at[slot], 2, slot)
-        second_x[slot] = second_x[slot] + first[slot, :, :, self.x, :, HALF_SLOT:]
-        for copy in self.third_copies(slot):
-            copy.start()
-
-    def stage_three(self, slot):
-        third = self.third
-        self.landed(third.at[slot, :, :, self.low_cols], 3, slot)
-        self.landed(third.at[slot, :, :, self.high_cols], 4, slot)
-        third[slot, :, :, :HALF_SLOT] = third[slot, :, :, :HALF_SLOT] + self.second_y[slot, :, self.x]
-        third[slot, :, :, HALF_SLOT:] = third[slot, :, :, HALF_SLOT:] + self.second_x[slot, self.y]
-        for copy in self.fourth_copies(slot):
-            copy.start()
-
-    def stage_four(self, slot):
-        total = self.third[slot, self.z].astype(jnp.float32)
-        for hop in (1, 2, 3):
-            self.landed(self.fourth.at[slot, hop - 1], 4 + hop, slot)
-            total = total + self.fourth[slot, hop - 1].astype(jnp.float32)
-        self.total_ref[slot] = total
-
-    def ticks(self):
-        return self.count() + self.hold + 3 * self.lag
-
-    def tick(self, index):
-        for slot in range(self.count()):
-            entry = slot + (self.hold if slot >= self.ready else 0)
-            pl.when(index == entry)(lambda slot=slot: self.stage_one(slot))
-        for number, stage in enumerate((self.stage_two, self.stage_three, self.stage_four)):
-            entry = index - (number + 1) * self.lag
-            slot = jnp.where(entry < self.ready, entry, entry - self.hold)
-            late = (entry >= self.ready + self.hold) & (slot < self.count())
-            early = (entry >= 0) & (entry < self.ready)
-            pl.when(early | late)(lambda stage=stage, slot=slot: stage(slot))
-
-    def fixed_tick(self, index):
-        for number, stage in enumerate((self.stage_one, self.stage_two, self.stage_three, self.stage_four)):
-            slot = index - number * self.lag
-            if 0 <= slot < self.count():
-                stage(slot)
-
-    def sent(self):
-        def one(slot, carry):
-            pltpu.make_async_copy(self.first.at[slot], self.first.at[slot], self.send_sem.at[0, slot]).wait()
-            for copy in self.second_copies(slot) + self.third_copies(slot) + self.fourth_copies(slot):
-                copy.wait_send()
-            return carry
-
-        lax.fori_loop(0, self.count(), one, 0)
-
-
-def summing_buffers(count):
-    rows, low = 64, jnp.bfloat16
-    return [
-        pltpu.VMEM((count, 2, 4, 2, rows, SLOT), low),
-        pltpu.VMEM((count, 4, 2, rows, HALF_SLOT), low),
-        pltpu.VMEM((count, 2, 4, rows, HALF_SLOT), low),
-        pltpu.VMEM((count, 4, rows, SLOT), low),
-        pltpu.VMEM((count, 3, rows, SLOT), low),
-        pltpu.SemaphoreType.DMA((8, count)),
-        pltpu.SemaphoreType.DMA((8, count)),
-    ]
 
 
 HIDDEN = 512
@@ -1405,18 +611,17 @@
             for number in range(spread.ticks()):
                 pl.when(step == number)(lambda number=number: spread.tick(number))
     bias_sum_ref[...] = bias_sum
-    grad_down = mul(cot_t[...], active[...]).astype(jnp.bfloat16)
-    grad_up = mul(rows_t[...], grad_before[...]).astype(jnp.bfloat16)
 
     @pl.when(step < early_steps)
     def _():
-        grad_early[0, step] = grad_up.reshape(grad_early.shape[2:])
-        grad_early[1, step] = grad_down.reshape(grad_early.shape[2:])
+        for index, (left, right) in enumerate(((rows_t, grad_before), (cot_t, active))):
+            grads = mul(left[...], right[...]).astype(jnp.bfloat16)
+            grad_early[index, step] = grads.reshape(grad_early.shape[2:])
 
     @pl.when(step >= early_steps)
     def _():
-        grad_up_ref[...] = grad_up
-        grad_down_ref[...] = grad_down
+        grad_up_ref[...] = mul(rows_t[...], grad_before[...]).astype(jnp.bfloat16)
+        grad_down_ref[...] = mul(cot_t[...], active[...]).astype(jnp.bfloat16)
 
     for number in range(HIDDEN_STEPS):
 
@@ -1494,6 +699,865 @@
     )(rows, cot, base, bias, *split, slots)
 
 
+SLOTS = 12
+SLOT = 512
+HALF_SLOT = SLOT // 2
+TILE = 256
+GRAM_TILES = 5
+MESH_IDS = pl.DeviceIdType.MESH
+
+
+def handler_of(slot):
+    wide = slot - 4
+    square = slot < 4
+    dp_index = jnp.where(square, jnp.where(slot < 2, 2, 12), 4 + 6 * (wide // 4) + wide % 2)
+    tensor_index = jnp.where(square, slot % 2, (wide // 2) % 2)
+    return dp_index, tensor_index
+
+
+def muon_kernel(
+    moments_ref,
+    vec_ref,
+    block_ref,
+    token_ref,
+    updates_ref,
+    vec_out_ref,
+    block_pair_ref,
+    token_pair_ref,
+    pieces,
+    turned,
+    vec_pieces,
+    vec_sum,
+    gram,
+    gram_low,
+    poly_low,
+    half_low,
+    chain_low,
+    chain_next,
+    out_half,
+    in_half,
+    local_sem,
+    send_sem,
+    recv_sem,
+    half_send,
+    half_recv,
+    swap_sem,
+):
+    groups = lax.axis_size("dp")
+    parts = lax.axis_size("tensor")
+    count = groups * parts
+    dp_me = lax.axis_index("dp")
+    t_me = lax.axis_index("tensor")
+    me = t_me * groups + dp_me
+    is_square = (dp_me == 2) | (dp_me == 12)
+    is_up = (dp_me == 4) | (dp_me == 5)
+    is_down = (dp_me == 10) | (dp_me == 11)
+    is_wide = is_up | is_down
+    is_handler = is_square | is_wide
+    wide_slot = jnp.where(is_up, 4 + (dp_me - 4), 8 + (dp_me - 10)) + 2 * t_me
+    slot_me = jnp.where(is_square, t_me + jnp.where(dp_me == 12, 2, 0), wide_slot)
+    slot_me = jnp.where(is_handler, slot_me, 0)
+
+    barrier = pltpu.get_barrier_semaphore()
+
+    def greet(step, carry):
+        other = lax.rem(me + step, count)
+        pl.semaphore_signal(
+            barrier, inc=1, device_id=(lax.rem(other, groups), other // groups), device_id_type=MESH_IDS
+        )
+        return carry
+
+    lax.fori_loop(1, count, greet, 0)
+    pl.semaphore_wait(barrier, count - 1)
+
+    def give(step, carry):
+        slot = lax.rem(me + step, SLOTS)
+        dp_to, t_to = handler_of(slot)
+        away = (dp_to != dp_me) | (t_to != t_me)
+
+        @pl.when(away)
+        def _():
+            pltpu.make_async_remote_copy(
+                src_ref=vec_ref.at[slot],
+                dst_ref=vec_pieces.at[me],
+                send_sem=send_sem.at[1],
+                recv_sem=recv_sem.at[1],
+                device_id=(dp_to, t_to),
+                device_id_type=MESH_IDS,
+            ).start()
+            pltpu.make_async_remote_copy(
+                src_ref=moments_ref.at[slot],
+                dst_ref=pieces.at[me],
+                send_sem=send_sem.at[0],
+                recv_sem=recv_sem.at[0],
+                device_id=(dp_to, t_to),
+                device_id_type=MESH_IDS,
+            ).start()
+
+        return carry
+
+    lax.fori_loop(0, SLOTS, give, 0)
+
+    rows = block_ref.shape[0] // 2
+    kept_rows = pl.ds(pl.multiple_of(t_me * rows, rows), rows)
+    sent_rows = pl.ds(pl.multiple_of((1 - t_me) * rows, rows), rows)
+    kept = []
+    swaps = []
+    for index, (whole, pair) in enumerate(((block_ref, block_pair_ref), (token_ref, token_pair_ref))):
+        kept.append(pltpu.make_async_copy(whole.at[kept_rows], pair.at[t_me], swap_sem.at[2, index]))
+        swaps.append(
+            pltpu.make_async_remote_copy(
+                src_ref=whole.at[sent_rows],
+                dst_ref=pair.at[t_me],
+                send_sem=swap_sem.at[0, index],
+                recv_sem=swap_sem.at[1, index],
+                device_id=(dp_me, 1 - t_me),
+                device_id_type=MESH_IDS,
+            )
+        )
+
+    @pl.when(jnp.logical_not(is_wide))
+    def _():
+        for copy in kept + swaps:
+            copy.start()
+
+    def give_back(source, sem, target):
+        def one(step, carry):
+            other = lax.rem(me + step, count)
+            pltpu.make_async_remote_copy(
+                src_ref=source.at[other] if source is turned else source,
+                dst_ref=target.at[slot_me],
+                send_sem=send_sem.at[sem],
+                recv_sem=recv_sem.at[sem],
+                device_id=(lax.rem(other, groups), other // groups),
+                device_id_type=MESH_IDS,
+            ).start()
+            return carry
+
+        lax.fori_loop(1, count, one, 0)
+
+    @pl.when(is_handler)
+    def _():
+        own = [
+            pltpu.make_async_copy(vec_ref.at[slot_me], vec_pieces.at[me], local_sem.at[0]),
+            pltpu.make_async_copy(moments_ref.at[slot_me], pieces.at[me], local_sem.at[1]),
+        ]
+        for copy in own:
+            copy.start()
+        for copy in own:
+            copy.wait()
+        rest = pl.ds(0, count - 1)
+        pltpu.make_async_copy(vec_pieces.at[rest], vec_pieces.at[rest], recv_sem.at[1]).wait()
+        vec_sum[...] = jnp.sum(vec_pieces[...], axis=0)
+        give_back(vec_sum, 2, vec_out_ref)
+        own_vec = pltpu.make_async_copy(vec_sum, vec_out_ref.at[slot_me], local_sem.at[0])
+        own_vec.start()
+        own_vec.wait()
+        pltpu.make_async_copy(pieces.at[rest], pieces.at[rest], recv_sem.at[0]).wait()
+
+        rows_of = TILE // 64
+
+        def gram_tile(tile, carry):
+            rows = pl.ds(pl.multiple_of(tile * TILE, TILE), TILE)
+            total = jnp.zeros((TILE, D), jnp.float32)
+            for part in range(parts):
+                left = pieces[pl.ds(part * groups + tile * rows_of, rows_of)].reshape(TILE, SLOT)
+                right = pieces[part * groups : (part + 1) * groups].reshape(D, SLOT)
+                total += lax.dot_general(
+                    left, right, (((1,), (1,)), ((), ())), preferred_element_type=jnp.float32
+                )
+            gram[rows, :] = total
+            return carry
+
+        lax.fori_loop(0, D // TILE, gram_tile, 0)
+
+        @pl.when(is_wide)
+        def _():
+            core = lax.rem(dp_me, 2)
+            sibling = (dp_me + 1 - 2 * core, t_me)
+            across = (dp_me, 1 - t_me)
+
+            def tile_at(index, owner):
+                if index == 4:
+                    row, col = jnp.where(owner == 0, 3, 2), 3
+                elif index == 3:
+                    row, col = jnp.where(owner == 0, 0, 2), jnp.where(owner == 0, 3, 2)
+                else:
+                    row, col = owner, owner + index
+                return (
+                    pl.ds(pl.multiple_of(row * TILE, TILE), TILE),
+                    pl.ds(pl.multiple_of(col * TILE, TILE), TILE),
+                )
+
+            def exchange(stage, index, place):
+                return pltpu.make_async_remote_copy(
+                    src_ref=out_half.at[stage, index],
+                    dst_ref=in_half.at[stage, index],
+                    send_sem=half_send.at[stage, index],
+                    recv_sem=half_recv.at[stage, index],
+                    device_id=place,
+                    device_id_type=MESH_IDS,
+                )
+
+            for index in range(GRAM_TILES):
+                out_half[0, index] = gram[tile_at(index, 1 - core)].astype(jnp.bfloat16)
+                exchange(0, index, sibling).start()
+            for index in range(GRAM_TILES):
+                exchange(0, index, sibling).wait_recv()
+                total = gram[tile_at(index, core)] + in_half[0, index].astype(jnp.float32)
+                out_half[1, index] = total.astype(jnp.bfloat16)
+                exchange(1, index, across).start()
+            for index in range(GRAM_TILES):
+                exchange(1, index, across).wait_recv()
+                total = out_half[1, index].astype(jnp.float32) + in_half[1, index].astype(jnp.float32)
+                out_half[2, index] = total.astype(jnp.bfloat16)
+                exchange(2, index, sibling).start()
+                rows, cols = tile_at(index, core)
+                gram[cols, rows] = out_half[2, index].astype(jnp.float32).T
+                gram[rows, cols] = out_half[2, index].astype(jnp.float32)
+            for index in range(GRAM_TILES):
+                exchange(2, index, sibling).wait_recv()
+                rows, cols = tile_at(index, 1 - core)
+                gram[cols, rows] = in_half[2, index].astype(jnp.float32).T
+                gram[rows, cols] = in_half[2, index].astype(jnp.float32)
+            for index in range(GRAM_TILES):
+                exchange(0, index, sibling).wait_send()
+                exchange(1, index, across).wait_send()
+                exchange(2, index, sibling).wait_send()
+            for copy in kept + swaps:
+                copy.start()
+
+        def trace_tile(tile, total):
+            rows = pl.ds(pl.multiple_of(tile * TILE, TILE), TILE)
+            row_ids = lax.broadcasted_iota(jnp.int32, (TILE, D), 0) + tile * TILE
+            col_ids = lax.broadcasted_iota(jnp.int32, (TILE, D), 1)
+            diagonal = jnp.where(row_ids == col_ids, gram[rows, :], 0.0)
+            return total + jnp.sum(jnp.sum(diagonal, axis=0, keepdims=True), axis=1, keepdims=True)
+
+        square_total = lax.fori_loop(0, D // TILE, trace_tile, jnp.zeros((1, 1), jnp.float32))
+        factor = lax.rsqrt(square_total + SQUARE_EPSILON)
+        gram_low[...] = (gram[...] * (factor * factor)).astype(jnp.bfloat16)
+
+        first, second, third = SCHULZ_FIRST, SCHULZ_SECOND, SCHULZ_THIRD
+
+        def tiles(body):
+            def one(tile, carry):
+                body(pl.ds(pl.multiple_of(tile * TILE, TILE), TILE))
+                return carry
+
+            lax.fori_loop(0, D // TILE, one, 0)
+
+        chain = chain_low
+        other = chain_next
+        for sweep in range(NS_ITERS):
+            target = chain if sweep == 0 else poly_low
+
+            def poly(rows):
+                square = mul(gram_low[rows, :], gram_low[...])
+                grown = (second / first) * gram_low[rows, :].astype(jnp.float32) + (third / first) * square
+                target[rows, :] = grown.astype(jnp.bfloat16)
+
+            tiles(poly)
+            if sweep > 0:
+
+                def join(rows, chain=chain, other=other):
+                    total = chain[rows, :].astype(jnp.float32) + poly_low[rows, :].astype(jnp.float32)
+                    other[rows, :] = (total + mul(chain[rows, :], poly_low[...])).astype(jnp.bfloat16)
+
+                tiles(join)
+                chain, other = other, chain
+            if sweep < NS_ITERS - 1:
+
+                def half(rows):
+                    grown = gram_low[rows, :].astype(jnp.float32) + mul(gram_low[rows, :], target[...])
+                    half_low[rows, :] = grown.astype(jnp.bfloat16)
+
+                def full(rows):
+                    grown = half_low[rows, :].astype(jnp.float32) + mul(half_low[rows, :], target[...])
+                    gram_low[rows, :] = (grown * (first * first)).astype(jnp.bfloat16)
+
+                tiles(half)
+                tiles(full)
+
+        scale = factor * (first**NS_ITERS)
+
+        def turn_tile(tile, carry):
+            rows = pl.ds(pl.multiple_of(tile * TILE, TILE), TILE)
+            for part in range(parts):
+                at = pl.ds(part * groups + tile * rows_of, rows_of)
+                whole = pieces[part * groups : (part + 1) * groups].reshape(D, SLOT)
+                kept = pieces[at].reshape(TILE, SLOT).astype(jnp.float32)
+                fresh = (kept + mul(chain[rows, :], whole)) * scale
+                turned[at] = fresh.astype(jnp.bfloat16).reshape(rows_of, 64, SLOT)
+            return carry
+
+        lax.fori_loop(0, D // TILE, turn_tile, 0)
+        give_back(turned, 3, updates_ref)
+        own_turned = pltpu.make_async_copy(turned.at[me], updates_ref.at[slot_me], local_sem.at[1])
+        own_turned.start()
+        own_turned.wait()
+
+    def finish(length):
+        here = pl.ds(0, length)
+        pltpu.make_async_copy(vec_ref.at[here], vec_ref.at[here], send_sem.at[1]).wait()
+        pltpu.make_async_copy(moments_ref.at[here], moments_ref.at[here], send_sem.at[0]).wait()
+        pltpu.make_async_copy(vec_out_ref.at[here], vec_out_ref.at[here], recv_sem.at[2]).wait()
+        pltpu.make_async_copy(updates_ref.at[here], updates_ref.at[here], recv_sem.at[3]).wait()
+
+    @pl.when(is_handler)
+    def _():
+        finish(SLOTS - 1)
+        rest = pl.ds(0, count - 1)
+        pltpu.make_async_copy(vec_pieces.at[rest], vec_pieces.at[rest], send_sem.at[2]).wait()
+        pltpu.make_async_copy(turned.at[rest], turned.at[rest], send_sem.at[3]).wait()
+
+    @pl.when(jnp.logical_not(is_handler))
+    def _():
+        finish(SLOTS)
+
+    for copy in kept + swaps:
+        copy.wait()
+
+
+def muon_call(moments, vec_parts, block_rows, token_grads):
+    count = lax.axis_size("dp") * lax.axis_size("tensor")
+    rows = moments.shape[1]
+    vmem = pl.BlockSpec(memory_space=pltpu.VMEM)
+    anywhere = pl.BlockSpec(memory_space=pl.ANY)
+    pair = jax.ShapeDtypeStruct((2, LEN // 2, D), jnp.bfloat16)
+    low = pltpu.VMEM((D, D), jnp.bfloat16)
+    return pl.pallas_call(
+        muon_kernel,
+        in_specs=[vmem, vmem, anywhere, anywhere],
+        out_specs=[vmem, vmem, anywhere, anywhere],
+        out_shape=[
+            jax.ShapeDtypeStruct(moments.shape, jnp.bfloat16),
+            jax.ShapeDtypeStruct(vec_parts.shape, jnp.float32),
+            pair,
+            pair,
+        ],
+        scratch_shapes=[
+            pltpu.VMEM((count, rows, SLOT), jnp.bfloat16),
+            pltpu.VMEM((count, rows, SLOT), jnp.bfloat16),
+            pltpu.VMEM((count,) + vec_parts.shape[1:], jnp.float32),
+            pltpu.VMEM(vec_parts.shape[1:], jnp.float32),
+            pltpu.VMEM((D, D), jnp.float32),
+            low,
+            low,
+            low,
+            low,
+            low,
+            pltpu.VMEM((3, GRAM_TILES, TILE, TILE), jnp.bfloat16),
+            pltpu.VMEM((3, GRAM_TILES, TILE, TILE), jnp.bfloat16),
+            pltpu.SemaphoreType.DMA((2,)),
+            pltpu.SemaphoreType.DMA((4,)),
+            pltpu.SemaphoreType.DMA((4,)),
+            pltpu.SemaphoreType.DMA((3, GRAM_TILES)),
+            pltpu.SemaphoreType.DMA((3, GRAM_TILES)),
+            pltpu.SemaphoreType.DMA((3, 2)),
+        ],
+        compiler_params=pltpu.CompilerParams(
+            collective_id=1, has_side_effects=True, vmem_limit_bytes=VMEM_LIMIT
+        ),
+        cost_estimate=pl.CostEstimate(flops=12 * 2 * D**3, bytes_accessed=4 * 1024 * 1024, transcendentals=0),
+    )(moments, vec_parts, block_rows, token_grads)
+
+
+def neighbours():
+    dp_me = lax.axis_index("dp")
+    y = lax.axis_index("tensor")
+    core = lax.rem(dp_me, 2)
+    x = lax.rem(dp_me // 2, 2)
+    z = dp_me // 4
+    sibling = (dp_me + 1 - 2 * core, y)
+    beside = (dp_me + 2 - 4 * x, y)
+    across = (dp_me, 1 - y)
+    stations = [(lax.rem(dp_me + 4 * hop, 16), y) for hop in (1, 2, 3)]
+    return (z, x, core, y), sibling, beside, across, stations
+
+
+def greet_neighbours(places):
+    barrier = pltpu.get_barrier_semaphore()
+    for place in places:
+        pl.semaphore_signal(barrier, inc=1, device_id=place, device_id_type=MESH_IDS)
+    pl.semaphore_wait(barrier, len(places))
+
+
+EARLY = 2
+AHEAD = 2
+
+
+class Spread:
+    def __init__(self, slots_ref, table, local_sem, send_sem, recv_sem):
+        self.slots_ref, self.table = slots_ref, table
+        self.local_sem, self.send_sem, self.recv_sem = local_sem, send_sem, recv_sem
+        (self.z, self.x, self.core, self.y), self.sibling, self.beside, self.across, self.stations = neighbours()
+
+    def remote(self, source, target, stage, slot, place):
+        return pltpu.make_async_remote_copy(
+            src_ref=source,
+            dst_ref=target,
+            send_sem=self.send_sem.at[stage, slot],
+            recv_sem=self.recv_sem.at[stage, slot],
+            device_id=place,
+            device_id_type=MESH_IDS,
+        )
+
+    def own(self, slot):
+        here = self.table[slot][0](self.y, 0, SLOT).at[self.z, self.x, self.core]
+        return pltpu.make_async_copy(self.slots_ref.at[slot], here, self.local_sem.at[slot])
+
+    def along_z(self, slot):
+        here = self.table[slot][0](self.y, 0, SLOT).at[self.z, self.x, self.core]
+        return [
+            self.remote(self.slots_ref.at[slot], here, hop, slot, place)
+            for hop, place in enumerate(self.stations)
+        ]
+
+    def second(self, slot):
+        view, size = self.table[slot]
+        copies = []
+        if size:
+            part = view(self.y, 0, size).at[:, self.x, self.core]
+            copies.append(self.remote(part, part, 3, slot, self.beside))
+        if size < SLOT:
+            part = view(self.y, size, SLOT - size).at[:, self.x, self.core]
+            copies.append(self.remote(part, part, 4, slot, self.across))
+        return copies
+
+    def third(self, slot):
+        view, size = self.table[slot]
+        copies = []
+        if size:
+            part = view(self.y, 0, size).at[:, :, self.core]
+            copies.append(self.remote(part, part, 5, slot, self.across))
+        if size < SLOT:
+            for index in (0, 1):
+                part = view(index, size, SLOT - size).at[:, self.x, self.core]
+                copies.append(self.remote(part, part, 6 + index, slot, self.beside))
+        return copies
+
+    def fourth(self, slot):
+        view, _ = self.table[slot]
+        copies = []
+        for index in (0, 1):
+            part = view(index, 0, SLOT).at[:, :, self.core]
+            copies.append(self.remote(part, part, 8 + index, slot, self.sibling))
+        return copies
+
+    def launch(self, slot):
+        if slot < len(self.table):
+            self.own(slot).start()
+            for copy in self.along_z(slot):
+                copy.start()
+
+    def begin(self):
+        for slot in range(AHEAD):
+            self.launch(slot)
+
+    def push_second(self, slot):
+        self.own(slot).wait()
+        for copy in self.along_z(slot):
+            copy.wait_recv()
+        for copy in self.second(slot):
+            copy.start()
+
+    def push_third(self, slot):
+        for copy in self.second(slot):
+            copy.wait_recv()
+        for copy in self.third(slot):
+            copy.start()
+
+    def push_fourth(self, slot):
+        for copy in self.third(slot):
+            copy.wait_recv()
+        for copy in self.fourth(slot):
+            copy.start()
+
+    def tick(self, index):
+        count = len(self.table)
+        self.launch(index + AHEAD)
+        if index < count:
+            self.push_second(index)
+        if 0 <= index - 1 < count:
+            self.push_third(index - 1)
+        if 0 <= index - 2 < count:
+            self.push_fourth(index - 2)
+
+    def ticks(self):
+        return len(self.table) + 2
+
+    def arrived(self, slot):
+        for copy in self.fourth(slot):
+            copy.wait_recv()
+
+    def sent(self):
+        for slot in range(len(self.table)):
+            for copy in self.along_z(slot) + self.second(slot) + self.third(slot) + self.fourth(slot):
+                copy.wait_send()
+
+
+def column_view(ref, column, distance):
+    def view(part, start, size):
+        first = column + part * distance + start
+        if not isinstance(part, int):
+            first = pl.multiple_of(first, 128)
+        return ref.at[:, :, :, :, pl.ds(first, size)]
+
+    return view
+
+
+def place_view(ref, place):
+    def view(part, start, size):
+        return ref.at[place + part, :, :, :, :, pl.ds(start, size)]
+
+    return view
+
+
+def spread_semaphores(count):
+    return [
+        pltpu.SemaphoreType.DMA((count,)),
+        pltpu.SemaphoreType.DMA((10, count)),
+        pltpu.SemaphoreType.DMA((10, count)),
+    ]
+
+
+def pair_of(step):
+    return (step % 2) * (PAIRS // 2) + step // 2
+
+
+def attend_spread_kernel(
+    starts_ref,
+    slopes_ref,
+    norm_ref,
+    shifts_ref,
+    tokens_ref,
+    cotangent_ref,
+    slots_ref,
+    packed_ref,
+    ctx_ref,
+    exps_ref,
+    stat_ref,
+    normed_t_ref,
+    rows_ref,
+    qkv_ref,
+    out_ref,
+    up_ref,
+    down_ref,
+    got_ref,
+    dist_ref,
+    ctx_t,
+    rows,
+    normed,
+    weights,
+    local_sem,
+    send_sem,
+    recv_sem,
+    swap_sem,
+    load_sem,
+):
+    step = pl.program_id(0)
+    pair = pair_of(step)
+    table = [(column_view(qkv_ref, index * SLOT, 3 * SLOT), SLOT if index == 1 else 0) for index in range(3)]
+    table += [(column_view(out_ref, 0, SLOT), 0)]
+    for index in range(EARLY):
+        for ref, over_x in ((up_ref, 0), (down_ref, HALF_SLOT if index else 0)):
+            table += [(column_view(ref, index * SLOT, EARLY * SLOT), over_x)]
+    count = len(table)
+    spread = Spread(slots_ref, table, local_sem, send_sem, recv_sem)
+    half_rows = pl.ds(pl.multiple_of(spread.y * (LEN // 2), LEN // 2), LEN // 2)
+    own_rows = pltpu.make_async_copy(tokens_ref.at[spread.y], rows.at[half_rows], load_sem.at[2])
+
+    def swap(source, target, index):
+        return pltpu.make_async_remote_copy(
+            src_ref=source.at[1 - spread.y],
+            dst_ref=target,
+            send_sem=swap_sem.at[0, index],
+            recv_sem=swap_sem.at[1, index],
+            device_id=spread.across,
+            device_id_type=MESH_IDS,
+        )
+
+    token_swap = swap(tokens_ref, rows.at[half_rows], 0)
+    cotangent_swap = swap(cotangent_ref, got_ref, 1)
+
+    def load(at):
+        cols = pl.ds(pl.multiple_of(pair_of(at) * (3 * PAIR), PAIR), 3 * PAIR)
+        place = lax.rem(at, 2)
+        return pltpu.make_async_copy(qkv_ref.at[:, :, :, :, cols], weights.at[place], load_sem.at[place])
+
+    @pl.when(step == 0)
+    def _():
+        greet_neighbours([spread.sibling, spread.beside, spread.across] + spread.stations)
+        own_rows.start()
+        for slot in range(3):
+            spread.launch(slot)
+        spread.push_second(0)
+        token_swap.start()
+        spread.push_second(1)
+        spread.push_third(0)
+        spread.push_second(2)
+        for slot in range(3, count):
+            spread.launch(slot)
+        layout_grid(starts_ref, dist_ref)
+        spread.push_fourth(0)
+        own_rows.wait()
+        token_swap.wait_recv()
+        spread.push_third(1)
+        for index in range(LEN // CHUNK):
+            here = slice(index * CHUNK, index * CHUNK + CHUNK)
+            block = rows[here].astype(jnp.float32)
+            low = layer_norm(block, norm_ref[0:1], norm_ref[1:2]).astype(jnp.bfloat16)
+            normed[here] = low
+            normed_t_ref[:, here] = low.T
+            rows_ref[here] = rows[here]
+
+    for slot in range(3):
+
+        @pl.when(step == 2 * slot)
+        def _(slot=slot):
+            spread.arrived(slot)
+
+    @pl.when(lax.rem(step, 2) == 0)
+    def _():
+        load(step).start()
+
+    load(step).wait()
+
+    def between():
+        @pl.when(lax.rem(step, 2) == 0)
+        def _():
+            load(step + 1).start()
+
+        moves = (
+            ((), (), 3),
+            ((1,), (2,), 4),
+            ((), (3,), 5),
+            ((2,), (4,), 6),
+            ((3,), (5,), 7),
+            ((4,), (6,), None),
+            ((5,), (7,), None),
+            ((6,), (), None),
+        )
+        for index, (fourth, third, fresh) in enumerate(moves):
+
+            @pl.when(step == index)
+            def _(index=index, fourth=fourth, third=third, fresh=fresh):
+                for slot in fourth:
+                    spread.push_fourth(slot)
+                for slot in third:
+                    spread.push_third(slot)
+                if fresh is not None:
+                    spread.push_second(fresh)
+                if fresh == count - 1:
+                    cotangent_swap.start()
+
+    packed = mul(normed[...], weights[lax.rem(step, 2)].reshape(D, 3 * PAIR)) + shifts_ref[...]
+    packed = packed.astype(jnp.bfloat16)
+    packed_ref[...] = packed
+    attend_pair(pair, slopes_ref, packed, dist_ref, ctx_ref, exps_ref, stat_ref, ctx_t, between)
+
+    @pl.when(step == PAIRS - 1)
+    def _():
+        spread.push_fourth(count - 1)
+        for slot in range(3, count):
+            spread.arrived(slot)
+        spread.sent()
+        token_swap.wait_send()
+        cotangent_swap.wait()
+
+
+def whole_shape(columns):
+    return jax.ShapeDtypeStruct((4, 2, 2, 64, columns), jnp.bfloat16)
+
+
+def attend_spread(starts, slopes, norm_rows, shifts, tokens, cotangent, slots):
+    anywhere = pl.BlockSpec(memory_space=pl.ANY)
+    whole = pl.BlockSpec((LEN, D), lambda s: (0, 0), pipeline_mode=pl.Buffered(1))
+    low = jnp.bfloat16
+    packed, context, exps, stats, normed_t, rows, qkv, out, up, down, got = pl.pallas_call(
+        attend_spread_kernel,
+        grid=(PAIRS,),
+        in_specs=[
+            SCALARS,
+            SCALARS,
+            pl.BlockSpec((2, D), lambda s: (0, 0)),
+            pl.BlockSpec((1, 3 * PAIR), lambda s: (0, pair_of(s))),
+            anywhere,
+            anywhere,
+            anywhere,
+        ],
+        out_specs=[
+            pl.BlockSpec((LEN, 3 * PAIR), lambda s: (0, pair_of(s))),
+            pl.BlockSpec((LEN, PAIR), lambda s: (0, pair_of(s))),
+            pl.BlockSpec((2, LEN, LEN), lambda s: (pair_of(s), 0, 0)),
+            pl.BlockSpec((1, 2, LEN), lambda s: (pair_of(s), 0, 0)),
+            whole,
+            whole,
+        ]
+        + [anywhere] * 5,
+        out_shape=[
+            jax.ShapeDtypeStruct((LEN, 3 * D), low),
+            jax.ShapeDtypeStruct((LEN, D), low),
+            jax.ShapeDtypeStruct((H, LEN, LEN), low),
+            jax.ShapeDtypeStruct((PAIRS, 2, LEN), jnp.float32),
+            jax.ShapeDtypeStruct((D, LEN), low),
+            jax.ShapeDtypeStruct((LEN, D), low),
+            whole_shape(3 * D),
+            whole_shape(D),
+            whole_shape(2 * EARLY * SLOT),
+            whole_shape(2 * EARLY * SLOT),
+            jax.ShapeDtypeStruct(cotangent.shape[1:], low),
+        ],
+        scratch_shapes=[
+            pltpu.VMEM((LEN, LEN), jnp.float32),
+            pltpu.VMEM((PAIR, LEN), jnp.float32),
+            pltpu.VMEM((LEN, D), low),
+            pltpu.VMEM((LEN, D), low),
+            pltpu.VMEM((2, 4, 2, 2, 64, 3 * PAIR), low),
+        ]
+        + spread_semaphores(4 + 2 * EARLY)
+        + [pltpu.SemaphoreType.DMA((2, 2)), pltpu.SemaphoreType.DMA((3,))],
+        compiler_params=pltpu.CompilerParams(
+            collective_id=4, has_side_effects=True, vmem_limit_bytes=VMEM_LIMIT
+        ),
+        cost_estimate=pl.CostEstimate(
+            flops=22 * LEN * LEN * D, bytes_accessed=90 * 1024 * 1024, transcendentals=H * LEN * LEN
+        ),
+    )(starts, slopes, norm_rows, shifts, tokens, cotangent, slots)
+    wholes = [whole.reshape(D, -1) for whole in (qkv, out, up, down)]
+    return packed, context, exps, stats, normed_t, rows, wholes, got
+
+
+class Summing:
+    def __init__(self, sources, add_own, buffers, total_ref, sems, lag, ready=0, hold=0):
+        self.sources, self.add_own, self.total_ref, self.lag = sources, add_own, total_ref, lag
+        self.ready, self.hold = ready, hold
+        self.first, self.second_y, self.second_x, self.third, self.fourth = buffers
+        self.send_sem, self.recv_sem = sems
+        (self.z, self.x, self.core, self.y), self.sibling, self.beside, self.across, self.stations = neighbours()
+        self.low_cols = pl.ds(0, HALF_SLOT)
+        self.high_cols = pl.ds(HALF_SLOT, HALF_SLOT)
+
+    def count(self):
+        return len(self.sources)
+
+    def remote(self, source, target, stage, slot, place):
+        return pltpu.make_async_remote_copy(
+            src_ref=source,
+            dst_ref=target,
+            send_sem=self.send_sem.at[stage, slot],
+            recv_sem=self.recv_sem.at[stage, slot],
+            device_id=place,
+            device_id_type=MESH_IDS,
+        )
+
+    def landed(self, ref, stage, slot):
+        pltpu.make_async_copy(ref, ref, self.recv_sem.at[stage, slot]).wait()
+
+    def send_first(self, slot):
+        for part in (0, 1):
+            source = self.sources[slot](part).at[:, :, 1 - self.core]
+            self.remote(source, self.first.at[slot, part], 0, slot, self.sibling).start()
+
+    def second_copies(self, slot):
+        for_y = self.first.at[slot, 1 - self.y, :, :, :, self.low_cols]
+        for_x = self.first.at[slot, :, :, 1 - self.x, :, self.high_cols]
+        return (
+            self.remote(for_y, self.second_y.at[slot], 1, slot, self.across),
+            self.remote(for_x, self.second_x.at[slot], 2, slot, self.beside),
+        )
+
+    def third_copies(self, slot):
+        for_x = self.second_y.at[slot, :, 1 - self.x]
+        for_y = self.second_x.at[slot, 1 - self.y]
+        return (
+            self.remote(for_x, self.third.at[slot, :, :, self.low_cols], 3, slot, self.beside),
+            self.remote(for_y, self.third.at[slot, :, :, self.high_cols], 4, slot, self.across),
+        )
+
+    def fourth_copies(self, slot):
+        return tuple(
+            self.remote(
+                self.third.at[slot, lax.rem(self.z + hop, 4)], self.fourth.at[slot, hop - 1], 4 + hop, slot, place
+            )
+            for hop, place in zip((1, 2, 3), self.stations)
+        )
+
+    def stage_one(self, slot):
+        self.landed(self.first.at[slot], 0, slot)
+        self.add_own(slot)
+        for copy in self.second_copies(slot):
+            copy.start()
+
+    def stage_two(self, slot):
+        first, second_y, second_x = self.first, self.second_y, self.second_x
+        self.landed(second_y.at[slot], 1, slot)
+        second_y[slot] = second_y[slot] + first[slot, self.y, :, :, :, :HALF_SLOT]
+        self.landed(second_x.at[slot], 2, slot)
+        second_x[slot] = second_x[slot] + first[slot, :, :, self.x, :, HALF_SLOT:]
+        for copy in self.third_copies(slot):
+            copy.start()
+
+    def stage_three(self, slot):
+        third = self.third
+        self.landed(third.at[slot, :, :, self.low_cols], 3, slot)
+        self.landed(third.at[slot, :, :, self.high_cols], 4, slot)
+        third[slot, :, :, :HALF_SLOT] = third[slot, :, :, :HALF_SLOT] + self.second_y[slot, :, self.x]
+        third[slot, :, :, HALF_SLOT:] = third[slot, :, :, HALF_SLOT:] + self.second_x[slot, self.y]
+        for copy in self.fourth_copies(slot):
+            copy.start()
+
+    def stage_four(self, slot):
+        total = self.third[slot, self.z].astype(jnp.float32)
+        for hop in (1, 2, 3):
+            self.landed(self.fourth.at[slot, hop - 1], 4 + hop, slot)
+            total = total + self.fourth[slot, hop - 1].astype(jnp.float32)
+        self.total_ref[slot] = total
+
+    def ticks(self):
+        return self.count() + self.hold + 3 * self.lag
+
+    def tick(self, index):
+        for slot in range(self.count()):
+            entry = slot + (self.hold if slot >= self.ready else 0)
+            pl.when(index == entry)(lambda slot=slot: self.stage_one(slot))
+        for number, stage in enumerate((self.stage_two, self.stage_three, self.stage_four)):
+            entry = index - (number + 1) * self.lag
+            slot = jnp.where(entry < self.ready, entry, entry - self.hold)
+            late = (entry >= self.ready + self.hold) & (slot < self.count())
+            early = (entry >= 0) & (entry < self.ready)
+            pl.when(early | late)(lambda stage=stage, slot=slot: stage(slot))
+
+    def fixed_tick(self, index):
+        for number, stage in enumerate((self.stage_one, self.stage_two, self.stage_three, self.stage_four)):
+            slot = index - number * self.lag
+            if 0 <= slot < self.count():
+                stage(slot)
+
+    def sent(self):
+        def one(slot, carry):
+            pltpu.make_async_copy(self.first.at[slot], self.first.at[slot], self.send_sem.at[0, slot]).wait()
+            for copy in self.second_copies(slot) + self.third_copies(slot) + self.fourth_copies(slot):
+                copy.wait_send()
+            return carry
+
+        lax.fori_loop(0, self.count(), one, 0)
+
+
+def summing_buffers(count):
+    rows, low = 64, jnp.bfloat16
+    return [
+        pltpu.VMEM((count, 2, 4, 2, rows, SLOT), low),
+        pltpu.VMEM((count, 4, 2, rows, HALF_SLOT), low),
+        pltpu.VMEM((count, 2, 4, rows, HALF_SLOT), low),
+        pltpu.VMEM((count, 4, rows, SLOT), low),
+        pltpu.VMEM((count, 3, rows, SLOT), low),
+        pltpu.SemaphoreType.DMA((8, count)),
+        pltpu.SemaphoreType.DMA((8, count)),
+    ]
+
+
 LAG = 2
 READY = 5
 LATE_SLOTS = 8
@@ -1933,22 +1997,18 @@
     rank = lax.axis_index("tensor")
     slopes = jnp.exp2(-8.0 * jnp.arange(1, H + 1, dtype=jnp.float32) / H)
     starts = lax.dynamic_slice_in_dim(piece_starts[:, 0], rank, 1, 0)[0]
-    own_tokens = lax.dynamic_index_in_dim(tokens, rank, 0, keepdims=False)
     own_cotangent = lax.dynamic_index_in_dim(cotangent, rank, 0, keepdims=False)
 
-    full_qkv, other_tokens = first_spread(by_slots(by_pairs(narrow(w_qkv))), tokens)
-    token_low = in_order(rank, own_tokens, other_tokens)
-    token_rows = token_low.astype(jnp.float32)
-    normed_one = narrow(layer_norm(token_rows, vectors[0], vectors[1]))
     shifts = by_pairs(jnp.stack([vectors[2], jnp.zeros((D,), jnp.float32), vectors[3]])[:, None])
     up_slots = by_slots(narrow(w_up))
     down_slots = by_slots(narrow(w_down).T)
     in_turn = jnp.stack([up_slots, down_slots], axis=1).reshape(2 * up_slots.shape[0], *up_slots.shape[1:])
-    later_slots = jnp.concatenate([narrow(w_out).T[None], in_turn[: 2 * EARLY]])
-    packed, context, exps, stats, normed_t, wholes, other_cotangent = attend_spread(
-        starts, slopes, normed_one, full_qkv, shifts, later_slots, cotangent
-    )
-    full_out, full_up, full_down = wholes
+    slots = jnp.concatenate([by_slots(by_pairs(narrow(w_qkv))), narrow(w_out).T[None], in_turn[: 2 * EARLY]])
+    packed, context, exps, stats, normed_t, token_low, wholes, other_cotangent = attend_spread(
+        starts, slopes, vectors[0:2], shifts, tokens, cotangent, slots
+    )
+    full_qkv, full_out, full_up, full_down = wholes
+    token_rows = token_low.astype(jnp.float32)
     cotangent_low = in_order(rank, own_cotangent, other_cotangent)
 
     middle = token_rows + contract(context, full_out, 1, 1) + vectors[4]

time: 549 us -> 528 us (0.962)
  Pallas kernels: 508 us -> 486 us
    pallas_call x1 -> x0, Pallas kernels: 57.3 us -> none  [first_spread(): pl.pallas_call(first_spread_kernel, in_specs=[anywhere] * 2, out_specs=[a...]
    pallas_call x1, Pallas kernels: 90.8 us -> 137 us  [attend_spread(): pl.pallas_call(attend_spread_kernel, grid=(PAIRS,), in_specs=[SCALARS, SC...]
    pallas_call x1, Pallas kernels: 108 us -> 102 us  [mlp_both(): pl.pallas_call(mlp_kernel, grid=(HIDDEN_STEPS,), in_specs=[whole, whole,...]
where the time goes in v8:
time: 528 us; the launch traced here: 518 us
  Pallas kernels  486 us (92%)
  other arithmetic  15.1 us (3%)
  local copies, waits for them, and re-layouts  10.8 us (2%)
  matrix products  5.38 us (1%)
    pallas_call x1, Pallas kernels, attend_spread(): pl.pallas_call(attend_spread_kernel, grid=(PAIRS,), in_specs=[SCALARS, SC...  137 us
    pallas_call x1, Pallas kernels, muon_call(): pl.pallas_call(muon_kernel, in_specs=[vmem, vmem, anywhere, anywhere], ou...  120 us
    pallas_call x1, Pallas kernels, mlp_both(): pl.pallas_call(mlp_kernel, grid=(HIDDEN_STEPS,), in_specs=[whole, whole,...  102 us
    pallas_call x1, Pallas kernels, attend_sum(): pl.pallas_call(attend_sum_kernel, grid=(PAIRS,), in_specs=[PACKED_COLS, P...  97.7 us
    pallas_call x1, Pallas kernels, middle_backward(): pl.pallas_call(middle_kernel, grid=(LEN // ROWS,), in_specs=[rows, rows,...  15.2 us

profile of v8, /device:TPU:9, one launch (start us, length us, event | category | flops | bytes accessed | tf_op | source)
XLA Modules:
  0.0 518.2 jit_solution(12014265907370649383)
XLA Ops:
  0.7 0.0 copy-start
  0.7 0.0 copy-start.7
  0.7 1.6 fusion.1
  2.3 0.0 copy-start.8
  2.3 0.1 pad.10.clone
  2.4 0.1 maximum_bitcast_fusion
  2.4 0.6 reshape.101.shifts_ref
  3.1 0.0 copy-done
  3.1 0.5 dynamic-slice_bitcast_fusion.1.starts_ref
  3.6 1.1 convert_element_type.23
  4.6 1.1 convert_element_type.24
  5.8 0.8 pad_maximum_fusion.1
  6.5 1.0 convert_element_type.21
  7.5 0.1 reshape.102
  7.6 0.2 copy.55
  7.8 0.2 reshape_reshape.3
  8.0 0.0 copy-done.7
  8.1 0.8 pad_maximum_fusion.slots_ref
  8.9 1.4 slice.60.norm_ref
  10.3 0.5 multiply_exponential_fusion.slopes_ref
  10.8 136.7 %shard_map.260 = (bf16[1024,3072]{1,0:T(8,128)(2,1)}, bf16[1024,1024]{1,0:T(8,128)(2,1)}, bf16[16,1024,1024]{2,1,0:T(8,128)(2,1)}, f32[8,2,1024]{2,1,0:T(2,128)}...) custom-call(s32[2]{0:T(128)} %dynamic-slice_bitcast_fusion.1.starts_, ...), custom_call_target="tpu_custom_call" | custom-call | flops 23622320128 | bytes 94371840 | tf_op jit(solution)/shard_map/pallas_call | solution.py:1378
  147.5 5.4 %fusion.3 = (f32[1024]{0:T(1024)S(1)}, f32[1024,1024]{1,0:T(8,128)S(1)}) fusion(f32[1024]{0:T(1024)S(1)} %bitcast.107, bf16[1024,1024]{1,0:T(8,128)(2,1)} %get-tuple-element.64.ctx_ref, bf16[1024,1024]{1,0:T(8,128)(2,1)} %bitcast.117, bf16[1024,1024]{1,0:T(8,128)(2,1)} %get-tuple-element.63.rows_ref), kind=kOutput, calls=%fused_computation.36 | convolution fusion | flops 2151676928 | bytes 10493952 | tf_op jit(solution)/shard_map/dot_general | solution.py:1963
  152.9 0.0 copy-start.2
  152.9 0.6 multiply_reduce_fusion
  153.5 0.0 copy-done.8
  153.5 0.0 copy-start.6
  153.5 0.0 copy-start.5
  153.5 3.7 broadcast_add_fusion
  157.2 0.2 copy-done.2
  157.4 0.0 copy-done.6
  157.4 0.1 dynamic-slice_bitcast_fusion
  157.4 0.2 copy-done.5
  157.6 2.3 maximum_select_fusion.cot_ref
  159.9 0.8 slice_bitcast_fusion
  160.8 0.6 copy.44
  161.4 102.0 %shard_map.261 = (bf16[1024,1024]{1,0:T(8,128)(2,1)}, f32[1024,1024]{1,0:T(8,128)}, bf16[1024,2048]{1,0:T(8,128)(2,1)}, bf16[1024,2048]{1,0:T(8,128)(2,1)}, f32[1,4096]{1,0:T(1,128)}, /*index=5*/f32[4,64,512]{2,1,0:T(8,128)}) custom-call(bf16[1024,1024]{1,0:T(8,128)(2,1)} %get-tuple-element.110.rows_ref, bf16[1024,1024]{1,0:T(8,128)(2,1)} %maximum_select_fusion.cot_ref, ...), custom_call_target="tpu_custom_call" | custom-call | flops 51539607552 | bytes 62914560 | tf_op jit(solution)/shard_map/pallas_call | solution.py:660
  263.4 15.2 %shard_map.262 = (f32[1024,1024]{1,0:T(8,128)}, bf16[1024,1024]{1,0:T(8,128)(2,1)}, bf16[1024,1024]{1,0:T(8,128)(2,1)}, f32[8,1024]{1,0:T(8,128)}) custom-call(f32[1024,1024]{1,0:T(8,128)} %copy-done.2, f32[1024,1024]{1,0:T(8,128)} %get-tuple-element.71.grad_ref, bf16[1024,1024]{1,0:T(8,128)(2,1)} %maximum_select_fusion.cot_ref, ...), custom_call_target="tpu_custom_call" | custom-call | flops 4294967296 | bytes 25165824 | tf_op jit(solution)/shard_map/pallas_call | solution.py:1802
  278.6 97.7 %shard_map.263 = (f32[8,64,512]{2,1,0:T(8,128)}, f32[1024,1024]{1,0:T(8,128)}, f32[1,3072]{1,0:T(1,128)}) custom-call(bf16[1024,3072]{1,0:T(8,128)(2,1)} %get-tuple-element.70.packed_ref, bf16[1024,1024]{1,0:T(8,128)(2,1)} %get-tuple-element.64.ctx_ref, bf16[1024,1024]{1,0:T(8,128)(2,1)} %get-tuple-element.72.grad_ref, ...), custom_call_target="tpu_custom_call" | custom-call | flops 47244640256 | bytes 419430400 | tf_op jit(solution)/shard_map/pallas_call | solution.py:1720
  376.3 0.0 copy-start.10
  376.3 0.0 copy-start.11
  376.3 0.0 copy-start.9
  376.3 7.4 %shard_map.265 = (bf16[1024,1024]{1,0:T(8,128)(2,1)}, f32[8,1024]{1,0:T(8,128)}) custom-call(bf16[1024,1024]{1,0:T(8,128)(2,1)} %get-tuple-element.63.rows_ref, f32[1024,1024]{1,0:T(8,128)} %get-tuple-element.82.grad_ref, f32[1024,1024]{1,0:T(8,128)} %get-tuple-element.83.grad_middle_ref, f32[1,1024]{1,0:T(1,128)} %get-tuple-element.113.gain_ref), custom_call_target="tpu_custom_call" | custom-call | bytes 12582912 | tf_op jit(solution)/shard_map/pallas_call | solution.py:1833
  383.7 0.8 slice_bitcast_fusion.2
  384.4 0.5 broadcast.39
  385.0 0.0 copy-done.10
  385.0 0.7 reduce.3
  385.7 0.0 copy-done.11
  385.8 0.0 copy-done.9
  385.8 0.0 copy-start.12
  385.8 3.8 shard_map.264
  389.6 0.0 copy-done.12
  389.6 119.9 %shard_map.266 = (bf16[12,64,512]{2,1,0:T(8,128)(2,1)}, f32[12,8,128]{2,1,0:T(8,128)}, bf16[2,512,1024]{2,1,0:T(8,128)(2,1)}, bf16[2,512,1024]{2,1,0:T(8,128)(2,1)}) custom-call(bf16[12,64,512]{2,1,0:T(8,128)(2,1)} %get-tuple-element.81.moments_ref, f32[12,8,128]{2,1,0:T(8,128)} %copy-done.12, bf16[1024,1024]{1,0:T(8,128)(2,1)} %get-tuple-element.88.block_ref, ...), custom_call_target="tpu_custom_call" | custom-call | flops 25769803776 | bytes 4194304 | tf_op jit(solution)/shard_map/pallas_call | solution.py:1029
  509.5 0.0 copy-start.3
  509.5 1.0 pad.14
  510.5 0.6 copy.47
  511.1 0.0 copy-start.4
  511.1 3.0 shard_map.267
  514.1 0.0 copy-start.1
  514.1 0.0 copy-done.3
  514.1 2.5 convert_element_type.27
  516.6 0.0 copy-done.4
  516.6 1.3 copy.65
  517.9 0.0 copy-done.1
  (16 shorter events, 0.2 us)
Async XLA Ops:
  0.7 2.4 copy-start
  0.7 7.4 %copy-start.7 = (f32[512,64]{0,1:T(8,128)S(1)}, f32[512,64]{0,1:T(8,128)}, u32[]{:S(2)}) copy-start(f32[512,64]{0,1:T(8,128)} %param.17) | copy-start | bytes 393220
  2.3 151.2 %copy-start.8 = (f32[1,1024]{1,0:T(1,128)}, f32[1,1024]{1,0:T(1,128)S(1)}, u32[]{:S(2)}) copy-start(f32[1,1024]{1,0:T(1,128)S(1)} %get-tuple-element.116.gain_ref) | copy-start | bytes 12292
  152.9 4.5 copy-start.2
  153.5 3.9 copy-start.6
  153.5 4.1 copy-start.5
  376.3 8.7 %copy-start.10 = (f32[1,3072]{1,0:T(1,128)S(1)}, f32[1,3072]{1,0:T(1,128)}, u32[]{:S(2)}) copy-start(f32[1,3072]{1,0:T(1,128)} %get-tuple-element.85) | copy-start | bytes 36868
  376.3 9.4 %copy-start.11 = (f32[8,1024]{1,0:T(8,128)S(1)}, f32[8,1024]{1,0:T(8,128)}, u32[]{:S(2)}) copy-start(f32[8,1024]{1,0:T(8,128)} %get-tuple-element.86) | copy-start | bytes 98308
  376.3 9.4 %copy-start.9 = (f32[1,4096]{1,0:T(1,128)S(1)}, f32[1,4096]{1,0:T(1,128)}, u32[]{:S(2)}) copy-start(f32[1,4096]{1,0:T(1,128)} %get-tuple-element.87) | copy-start | bytes 49156
  385.8 3.8 copy-start.12
  509.5 4.6 copy-start.3
  511.1 5.5 %copy-start.4 = (bf16[2,512,1024]{2,1,0:T(8,128)(2,1)S(1)}, bf16[2,512,1024]{2,1,0:T(8,128)(2,1)}, u32[]{:S(2)}) copy-start(bf16[2,512,1024]{2,1,0:T(8,128)(2,1)} %get-tuple-element.143) | copy-start | bytes 6291460
  514.1 3.8 copy-start.1

commit v9 on v8

--- a/solution.py
+++ b/solution.py
@@ -507,6 +507,7 @@
     rows_ref,
     cot_ref,
     base_ref,
+    last_ref,
     bias_ref,
     up_ref,
     down_ref,
@@ -564,6 +565,14 @@
             pltpu.make_async_copy(down_ref.at[:, :, :, :, cols], down_part.at[place], load_sem.at[1, place]),
         )
 
+    def sum_moves(moment):
+        stages = (summing.stage_one, summing.stage_two, summing.stage_three, summing.stage_four)
+        for slot in range(summing.count()):
+            entry = 4 * (slot // 2 + 1) + slot % 2
+            for number, stage in enumerate(stages):
+                if moment == entry + 2 * number:
+                    stage(slot)
+
     @pl.when(step == 0)
     def _():
         for copy in loads(step):
@@ -572,7 +581,7 @@
         spread.begin()
         rows_t[...] = rows_ref[...].T
         cot_t[...] = cot_ref[...].T
-        total[...] = base_ref[...]
+        total[...] = base_ref[...] + last_ref[...]
         grad_rows_ref[...] = jnp.zeros_like(grad_rows_ref)
 
     @pl.when(step < early_steps)
@@ -610,6 +619,8 @@
         if index == LEN // CHUNK // 2 - 1:
             for number in range(spread.ticks()):
                 pl.when(step == number)(lambda number=number: spread.tick(number))
+            for number in range(HIDDEN_STEPS):
+                pl.when(step == number)(lambda number=number: sum_moves(2 * number))
     bias_sum_ref[...] = bias_sum
 
     @pl.when(step < early_steps)
@@ -630,14 +641,11 @@
             if number < early_steps and number % 2:
                 summing.send_first(number - 1)
                 summing.send_first(number)
-            if number >= 2:
-                summing.fixed_tick(number - 2)
+            sum_moves(2 * number + 1)
 
     @pl.when(step == HIDDEN_STEPS - 1)
     def _():
         block_ref[...] = total[...].astype(jnp.bfloat16)
-        for number in range(HIDDEN_STEPS - 2, summing.ticks()):
-            summing.fixed_tick(number)
         summing.sent()
         spread.sent()
 
@@ -647,7 +655,7 @@
     return jnp.where(step < 2 * EARLY, 0, (step % 2) * late + step // 2 - EARLY)
 
 
-def mlp_both(rows, cot, base, bias, up, down, slots):
+def mlp_both(rows, cot, base, last, bias, up, down, slots):
     anywhere = pl.BlockSpec(memory_space=pl.ANY)
     once = pl.Buffered(1)
     whole = pl.BlockSpec((LEN, D), lambda s: (0, 0), pipeline_mode=once)
@@ -660,7 +668,7 @@
     return pl.pallas_call(
         mlp_kernel,
         grid=(HIDDEN_STEPS,),
-        in_specs=[whole, whole, whole, hidden_row, anywhere, anywhere, anywhere],
+        in_specs=[whole, whole, whole, pl.BlockSpec((1, D), lambda s: (0, 0)), hidden_row, anywhere, anywhere, anywhere],
         out_specs=[
             whole,
             whole,
@@ -696,7 +704,7 @@
         cost_estimate=pl.CostEstimate(
             flops=12 * LEN * D * FF, bytes_accessed=60 * 1024 * 1024, transcendentals=LEN * FF
         ),
-    )(rows, cot, base, bias, *split, slots)
+    )(rows, cot, base, last, bias, *split, slots)
 
 
 SLOTS = 12
@@ -816,9 +824,12 @@
             )
         )
 
+    for copy in kept:
+        copy.start()
+
     @pl.when(jnp.logical_not(is_wide))
     def _():
-        for copy in kept + swaps:
+        for copy in swaps:
             copy.start()
 
     def give_back(source, sem, target):
@@ -924,7 +935,7 @@
                 exchange(0, index, sibling).wait_send()
                 exchange(1, index, across).wait_send()
                 exchange(2, index, sibling).wait_send()
-            for copy in kept + swaps:
+            for copy in swaps:
                 copy.start()
 
         def trace_tile(tile, total):
@@ -1230,6 +1241,7 @@
     starts_ref,
     slopes_ref,
     norm_ref,
+    middle_rows_ref,
     shifts_ref,
     tokens_ref,
     cotangent_ref,
@@ -1240,13 +1252,17 @@
     stat_ref,
     normed_t_ref,
     rows_ref,
+    middle_ref,
+    normed_two_ref,
     qkv_ref,
     out_ref,
     up_ref,
     down_ref,
-    got_ref,
+    cot_ref,
     dist_ref,
     ctx_t,
+    ctx_all,
+    out_weights,
     rows,
     normed,
     weights,
@@ -1279,7 +1295,9 @@
         )
 
     token_swap = swap(tokens_ref, rows.at[half_rows], 0)
-    cotangent_swap = swap(cotangent_ref, got_ref, 1)
+    cotangent_swap = swap(cotangent_ref, cot_ref.at[half_rows], 1)
+    own_cotangent = pltpu.make_async_copy(cotangent_ref.at[spread.y], cot_ref.at[half_rows], load_sem.at[3])
+    out_load = pltpu.make_async_copy(out_ref, out_weights, load_sem.at[4])
 
     def load(at):
         cols = pl.ds(pl.multiple_of(pair_of(at) * (3 * PAIR), PAIR), 3 * PAIR)
@@ -1311,6 +1329,7 @@
             normed[here] = low
             normed_t_ref[:, here] = low.T
             rows_ref[here] = rows[here]
+        own_cotangent.start()
 
     for slot in range(3):
 
@@ -1355,33 +1374,50 @@
     packed = mul(normed[...], weights[lax.rem(step, 2)].reshape(D, 3 * PAIR)) + shifts_ref[...]
     packed = packed.astype(jnp.bfloat16)
     packed_ref[...] = packed
-    attend_pair(pair, slopes_ref, packed, dist_ref, ctx_ref, exps_ref, stat_ref, ctx_t, between)
-
     @pl.when(step == PAIRS - 1)
     def _():
-        spread.push_fourth(count - 1)
-        for slot in range(3, count):
+        spread.arrived(3)
+        out_load.start()
+
+    attend_pair(pair, slopes_ref, packed, dist_ref, ctx_ref, exps_ref, stat_ref, ctx_t, between)
+    ctx_all[:, pl.ds(pl.multiple_of(pair * PAIR, PAIR), PAIR)] = ctx_ref[...]
+
+    @pl.when(step == PAIRS - 1)
+    def _():
+        out_load.wait()
+        for index in range(LEN // CHUNK):
+            here = slice(index * CHUNK, index * CHUNK + CHUNK)
+            attended = dot_last(ctx_all[here], out_weights[...].reshape(D, D))
+            middle = rows[here].astype(jnp.float32) + attended + middle_rows_ref[0:1]
+            middle_ref[here] = middle
+            normed_two = layer_norm(middle, middle_rows_ref[1:2], middle_rows_ref[2:3])
+            normed_two_ref[here] = normed_two.astype(jnp.bfloat16)
+            if index == LEN // CHUNK // 2 - 1:
+                spread.push_fourth(count - 1)
+        for slot in range(4, count):
             spread.arrived(slot)
         spread.sent()
         token_swap.wait_send()
         cotangent_swap.wait()
+        own_cotangent.wait()
 
 
 def whole_shape(columns):
     return jax.ShapeDtypeStruct((4, 2, 2, 64, columns), jnp.bfloat16)
 
 
-def attend_spread(starts, slopes, norm_rows, shifts, tokens, cotangent, slots):
+def attend_spread(starts, slopes, norm_rows, middle_rows, shifts, tokens, cotangent, slots):
     anywhere = pl.BlockSpec(memory_space=pl.ANY)
     whole = pl.BlockSpec((LEN, D), lambda s: (0, 0), pipeline_mode=pl.Buffered(1))
     low = jnp.bfloat16
-    packed, context, exps, stats, normed_t, rows, qkv, out, up, down, got = pl.pallas_call(
+    *local, qkv, out, up, down, cotangent_rows = pl.pallas_call(
         attend_spread_kernel,
         grid=(PAIRS,),
         in_specs=[
             SCALARS,
             SCALARS,
             pl.BlockSpec((2, D), lambda s: (0, 0)),
+            pl.BlockSpec((3, D), lambda s: (0, 0)),
             pl.BlockSpec((1, 3 * PAIR), lambda s: (0, pair_of(s))),
             anywhere,
             anywhere,
@@ -1394,6 +1430,8 @@
             pl.BlockSpec((1, 2, LEN), lambda s: (pair_of(s), 0, 0)),
             whole,
             whole,
+            whole,
+            whole,
         ]
         + [anywhere] * 5,
         out_shape=[
@@ -1403,30 +1441,34 @@
             jax.ShapeDtypeStruct((PAIRS, 2, LEN), jnp.float32),
             jax.ShapeDtypeStruct((D, LEN), low),
             jax.ShapeDtypeStruct((LEN, D), low),
+            jax.ShapeDtypeStruct((LEN, D), jnp.float32),
+            jax.ShapeDtypeStruct((LEN, D), low),
             whole_shape(3 * D),
             whole_shape(D),
             whole_shape(2 * EARLY * SLOT),
             whole_shape(2 * EARLY * SLOT),
-            jax.ShapeDtypeStruct(cotangent.shape[1:], low),
+            jax.ShapeDtypeStruct((LEN, D), low),
         ],
         scratch_shapes=[
             pltpu.VMEM((LEN, LEN), jnp.float32),
             pltpu.VMEM((PAIR, LEN), jnp.float32),
             pltpu.VMEM((LEN, D), low),
+            pltpu.VMEM((4, 2, 2, 64, D), low),
+            pltpu.VMEM((LEN, D), low),
             pltpu.VMEM((LEN, D), low),
             pltpu.VMEM((2, 4, 2, 2, 64, 3 * PAIR), low),
         ]
         + spread_semaphores(4 + 2 * EARLY)
-        + [pltpu.SemaphoreType.DMA((2, 2)), pltpu.SemaphoreType.DMA((3,))],
+        + [pltpu.SemaphoreType.DMA((2, 2)), pltpu.SemaphoreType.DMA((5,))],
         compiler_params=pltpu.CompilerParams(
             collective_id=4, has_side_effects=True, vmem_limit_bytes=VMEM_LIMIT
         ),
         cost_estimate=pl.CostEstimate(
             flops=22 * LEN * LEN * D, bytes_accessed=90 * 1024 * 1024, transcendentals=H * LEN * LEN
         ),
-    )(starts, slopes, norm_rows, shifts, tokens, cotangent, slots)
+    )(starts, slopes, norm_rows, middle_rows, shifts, tokens, cotangent, slots)
     wholes = [whole.reshape(D, -1) for whole in (qkv, out, up, down)]
-    return packed, context, exps, stats, normed_t, rows, wholes, got
+    return *local, wholes, cotangent_rows
 
 
 class Summing:
@@ -1528,12 +1570,6 @@
             late = (entry >= self.ready + self.hold) & (slot < self.count())
             early = (entry >= 0) & (entry < self.ready)
             pl.when(early | late)(lambda stage=stage, slot=slot: stage(slot))
-
-    def fixed_tick(self, index):
-        for number, stage in enumerate((self.stage_one, self.stage_two, self.stage_three, self.stage_four)):
-            slot = index - number * self.lag
-            if 0 <= slot < self.count():
-                stage(slot)
 
     def sent(self):
         def one(slot, carry):
@@ -1590,13 +1626,18 @@
     stat_ref,
     weights_ref,
     normed_t_ref,
+    rows_ref,
+    grad_middle_ref,
+    gain_ref,
     exps_ref,
     up_ref,
     down_ref,
     out_ref,
     total_ref,
-    grad_normed_ref,
+    token_grad_ref,
+    sums_ref,
     packed_sum_ref,
+    grad_normed,
     exps,
     dq_t,
     dk_sum,
@@ -1656,7 +1697,8 @@
         greet_neighbours([summing.sibling, summing.beside, summing.across] + summing.stations)
         for slot in range(READY):
             summing.send_first(slot)
-        grad_normed_ref[...] = jnp.zeros_like(grad_normed_ref)
+        grad_normed[...] = jnp.zeros_like(grad_normed)
+        sums_ref[...] = jnp.zeros_like(sums_ref)
 
     scale = 1.0 / math.sqrt(HD)
     queries = packed_ref[:, :PAIR]
@@ -1695,7 +1737,7 @@
     cols = pl.ds(pl.multiple_of(pair * (3 * PAIR), PAIR), 3 * PAIR)
     grad_weights = mul(normed_t_ref[...], grads).astype(jnp.bfloat16)
     grad_qkv[:, :, :, :, cols] = grad_weights.reshape(4, 2, 2, 64, 3 * PAIR)
-    grad_normed_ref[...] += dot_last(grads, weights_ref[...])
+    grad_normed[...] += dot_last(grads, weights_ref[...])
 
     for slot in range(READY, LATE_SLOTS):
         pl.when(pair == PAIRS - LATE_SLOTS + slot)(lambda slot=slot: summing.send_first(slot))
@@ -1704,13 +1746,25 @@
     def _():
         def late(index, carry):
             summing.tick(index)
+            chunk = index - PAIRS
+
+            @pl.when(chunk < LEN // ROWS)
+            def _():
+                here = pl.ds(pl.multiple_of(chunk * ROWS, ROWS), ROWS)
+                block = rows_ref[here, :].astype(jnp.float32)
+                pulled, gain_sum, shift_sum = norm_pull(block, grad_normed[here, :], gain_ref[...])
+                token_grad_ref[here, :] = (grad_middle_ref[here, :] + pulled).astype(jnp.bfloat16)
+                add_rows(sums_ref, (gain_sum, shift_sum))
+
             return carry
 
         lax.fori_loop(PAIRS, summing.ticks(), late, 0)
         summing.sent()
 
 
-def attend_sum(packed, context, grad_context, stats, weights, normed_t, exps, grad_up, grad_down, grad_out):
+def attend_sum(
+    packed, context, grad_context, stats, weights, normed_t, rows_low, grad_middle, gain, exps, grad_up, grad_down, grad_out
+):
     anywhere = pl.BlockSpec(memory_space=pl.ANY)
     rows = 64
     low = jnp.bfloat16
@@ -1720,18 +1774,23 @@
     return pl.pallas_call(
         attend_sum_kernel,
         grid=(PAIRS,),
-        in_specs=[PACKED_COLS, PAIR_COLS, PAIR_COLS, PAIR_STAT, PACKED_COLS, tall] + [anywhere] * 4,
+        in_specs=[PACKED_COLS, PAIR_COLS, PAIR_COLS, PAIR_STAT, PACKED_COLS, tall, tall, tall]
+        + [pl.BlockSpec((1, D), lambda p: (0, 0))]
+        + [anywhere] * 4,
         out_specs=[
             pl.BlockSpec((LATE_SLOTS, rows, SLOT), lambda p: (0, 0, 0), pipeline_mode=once),
             tall,
+            pl.BlockSpec((8, D), lambda p: (0, 0)),
             pl.BlockSpec((1, 3 * PAIR), lambda p: (0, p)),
         ],
         out_shape=[
             jax.ShapeDtypeStruct((LATE_SLOTS, rows, SLOT), jnp.float32),
-            jax.ShapeDtypeStruct((LEN, D), jnp.float32),
+            jax.ShapeDtypeStruct((LEN, D), low),
+            jax.ShapeDtypeStruct((8, D), jnp.float32),
             jax.ShapeDtypeStruct((1, 3 * D), jnp.float32),
         ],
         scratch_shapes=[
+            pltpu.VMEM((LEN, D), jnp.float32),
             pltpu.VMEM((2, LEN, LEN), low),
             pltpu.VMEM((PAIR, LEN), jnp.float32),
             pltpu.VMEM((LEN, PAIR), jnp.float32),
@@ -1748,7 +1807,7 @@
         cost_estimate=pl.CostEstimate(
             flops=44 * LEN * LEN * D, bytes_accessed=400 * 1024 * 1024, transcendentals=0
         ),
-    )(packed, context, grad_context, stats, weights, normed_t, exps, *split)
+    )(packed, context, grad_context, stats, weights, normed_t, rows_low, grad_middle, gain, exps, *split)
 
 
 ROWS = 256
@@ -1814,31 +1873,6 @@
         compiler_params=pltpu.CompilerParams(vmem_limit_bytes=VMEM_LIMIT),
         cost_estimate=pl.CostEstimate(flops=4 * LEN * D * D, bytes_accessed=24 * 1024 * 1024, transcendentals=0),
     )(middle, grad_rows, cot, context, gain, weights)
-
-
-def token_kernel(rows_ref, grad_ref, grad_middle_ref, gain_ref, out_ref, sums_ref):
-    @pl.when(pl.program_id(0) == 0)
-    def _():
-        sums_ref[...] = jnp.zeros_like(sums_ref)
-
-    pulled, gain_sum, shift_sum = norm_pull(rows_ref[...].astype(jnp.float32), grad_ref[...], gain_ref[...])
-    out_ref[...] = (grad_middle_ref[...] + pulled).astype(jnp.bfloat16)
-    add_rows(sums_ref, (gain_sum, shift_sum))
-
-
-def token_backward(rows_low, grad_rows, grad_middle, gain):
-    rows = pl.BlockSpec((ROWS, D), lambda s: (s, 0))
-    row = pl.BlockSpec((1, D), lambda s: (0, 0))
-    sums = pl.BlockSpec((8, D), lambda s: (0, 0))
-    return pl.pallas_call(
-        token_kernel,
-        grid=(LEN // ROWS,),
-        in_specs=[rows, rows, rows, row],
-        out_specs=[rows, sums],
-        out_shape=[jax.ShapeDtypeStruct((LEN, D), jnp.bfloat16), jax.ShapeDtypeStruct((8, D), jnp.float32)],
-        compiler_params=pltpu.CompilerParams(vmem_limit_bytes=VMEM_LIMIT),
-        cost_estimate=pl.CostEstimate(flops=0, bytes_accessed=12 * 1024 * 1024, transcendentals=0),
-    )(rows_low, grad_rows, grad_middle, gain)
 
 
 def slot_rows(early_ref, late_ref, slot):
@@ -1965,10 +1999,6 @@
     )
 
 
-def in_order(rank, own, got):
-    return jnp.where(rank == 0, jnp.concatenate([own, got]), jnp.concatenate([got, own]))
-
-
 def by_pairs(rows):
     count, height, width = rows.shape
     return jnp.transpose(rows.reshape(count, height, width // PAIR, PAIR), (1, 2, 0, 3)).reshape(height, -1)
@@ -1997,26 +2027,20 @@
     rank = lax.axis_index("tensor")
     slopes = jnp.exp2(-8.0 * jnp.arange(1, H + 1, dtype=jnp.float32) / H)
     starts = lax.dynamic_slice_in_dim(piece_starts[:, 0], rank, 1, 0)[0]
-    own_cotangent = lax.dynamic_index_in_dim(cotangent, rank, 0, keepdims=False)
-
     shifts = by_pairs(jnp.stack([vectors[2], jnp.zeros((D,), jnp.float32), vectors[3]])[:, None])
     up_slots = by_slots(narrow(w_up))
     down_slots = by_slots(narrow(w_down).T)
     in_turn = jnp.stack([up_slots, down_slots], axis=1).reshape(2 * up_slots.shape[0], *up_slots.shape[1:])
     slots = jnp.concatenate([by_slots(by_pairs(narrow(w_qkv))), narrow(w_out).T[None], in_turn[: 2 * EARLY]])
-    packed, context, exps, stats, normed_t, token_low, wholes, other_cotangent = attend_spread(
-        starts, slopes, vectors[0:2], shifts, tokens, cotangent, slots
+    packed, context, exps, stats, normed_t, token_low, middle, normed_two, wholes, cotangent_low = attend_spread(
+        starts, slopes, vectors[0:2], vectors[4:7], shifts, tokens, cotangent, slots
     )
     full_qkv, full_out, full_up, full_down = wholes
-    token_rows = token_low.astype(jnp.float32)
-    cotangent_low = in_order(rank, own_cotangent, other_cotangent)
-
-    middle = token_rows + contract(context, full_out, 1, 1) + vectors[4]
-    normed_two = narrow(layer_norm(middle, vectors[5], vectors[6]))
     block_rows, grad_normed_two, grad_up, grad_down, up_bias, early_sums = mlp_both(
         normed_two,
         cotangent_low,
-        middle + vectors[11],
+        middle,
+        vectors[11:12],
         vectors[7:11].reshape(1, FF),
         full_up,
         full_down,
@@ -2025,10 +2049,21 @@
     grad_middle, grad_context, grad_out, middle_sums = middle_backward(
         middle, grad_normed_two, cotangent_low, context, vectors[5:6], full_out
     )
-    sums, grad_normed_one, packed_grads = attend_sum(
-        packed, context, grad_context, stats, full_qkv, normed_t, exps, grad_up, grad_down, grad_out
-    )
-    grad_token_low, token_sums = token_backward(token_low, grad_normed_one, grad_middle, vectors[0:1])
+    sums, grad_token_low, token_sums, packed_grads = attend_sum(
+        packed,
+        context,
+        grad_context,
+        stats,
+        full_qkv,
+        normed_t,
+        token_low,
+        grad_middle,
+        vectors[0:1],
+        exps,
+        grad_up,
+        grad_down,
+        grad_out,
+    )
     packed_sums = from_pairs(packed_grads)[:, 0]
     vector_total = jnp.concatenate(
         [

time: 528 us -> 503 us (0.953)
  Pallas kernels: 486 us -> 474 us
  other arithmetic: 15.1 us -> 8.24 us
  matrix products: 5.38 us -> 0 us
    pallas_call x1 -> x0, Pallas kernels: 7.35 us -> none  [token_backward(): pl.pallas_call(token_kernel, grid=(LEN // ROWS,), in_specs=[rows, rows, r...]
    pallas_call x1, Pallas kernels: 120 us -> 114 us  [muon_call(): pl.pallas_call(muon_kernel, in_specs=[vmem, vmem, anywhere, anywhere], ou...]
    dot_general x1 -> x0, matrix products: 5.38 us -> none  [contract(): lax.dot_general(left, right, (((left_dim,), (right_dim,)), ((), ())), pre...]
where the time goes in v9:
time: 503 us; the launch traced here: 493 us
  Pallas kernels  474 us (94%)
  local copies, waits for them, and re-layouts  9.38 us (2%)
  other arithmetic  8.24 us (2%)
    pallas_call x1, Pallas kernels, attend_spread(): pl.pallas_call(attend_spread_kernel, grid=(PAIRS,), in_specs=[SCALARS, SC...  139 us
    pallas_call x1, Pallas kernels, muon_call(): pl.pallas_call(muon_kernel, in_specs=[vmem, vmem, anywhere, anywhere], ou...  114 us
    pallas_call x1, Pallas kernels, attend_sum(): pl.pallas_call(attend_sum_kernel, grid=(PAIRS,), in_specs=[PACKED_COLS, P...  99.9 us
    pallas_call x1, Pallas kernels, mlp_both(): pl.pallas_call(mlp_kernel, grid=(HIDDEN_STEPS,), in_specs=[whole, whole,...  99.7 us
    pallas_call x1, Pallas kernels, middle_backward(): pl.pallas_call(middle_kernel, grid=(LEN // ROWS,), in_specs=[rows, rows,...  15.2 us

profile of v9, /device:TPU:9, one launch (start us, length us, event | category | flops | bytes accessed | tf_op | source)
XLA Modules:
  0.0 492.9 jit_solution(4016950735127706872)
XLA Ops:
  0.7 0.0 copy-start
  0.7 0.0 copy-start.4
  0.7 1.5 fusion.1
  2.2 0.1 pad.6.clone
  2.3 0.1 maximum_bitcast_fusion
  2.4 0.6 reshape.89.shifts_ref
  3.0 0.0 copy-done
  3.0 0.5 dynamic-slice_bitcast_fusion.starts_ref
  3.5 1.1 convert_element_type.17
  4.6 1.1 convert_element_type.18
  5.6 0.0 copy-start.5
  5.7 0.8 pad_maximum_fusion.1
  6.5 0.0 copy-start.6
  6.5 0.0 copy-done.4
  6.5 0.1 reshape.90
  6.5 0.2 copy.52
  6.7 0.2 reshape_reshape.3
  7.0 0.0 copy-done.5
  7.0 0.8 pad_maximum_fusion.slots_ref
  7.9 0.0 copy-done.6
  7.9 0.6 slice.57.middle_rows_ref
  8.5 0.6 slice.56.norm_ref
  9.1 0.5 multiply_exponential_fusion.slopes_ref
  9.6 139.2 %shard_map.260 = (bf16[1024,3072]{1,0:T(8,128)(2,1)}, bf16[1024,1024]{1,0:T(8,128)(2,1)}, bf16[16,1024,1024]{2,1,0:T(8,128)(2,1)}, f32[8,2,1024]{2,1,0:T(2,128)}...) custom-call(s32[2]{0:T(128)} %dynamic-slice_bitcast_fusion.starts_re, ...), custom_call_target="tpu_custom_call" | custom-call | flops 23622320128 | bytes 94371840 | tf_op jit(solution)/shard_map/pallas_call | solution.py:1413
  148.8 0.6 copy.41
  149.4 99.7 %shard_map.261 = (bf16[1024,1024]{1,0:T(8,128)(2,1)}, f32[1024,1024]{1,0:T(8,128)}, bf16[1024,2048]{1,0:T(8,128)(2,1)}, bf16[1024,2048]{1,0:T(8,128)(2,1)}, f32[1,4096]{1,0:T(1,128)}, /*index=5*/f32[4,64,512]{2,1,0:T(8,128)}) custom-call(bf16[1024,1024]{1,0:T(8,128)(2,1)} %get-tuple-element.64.rows_ref, bf16[1024,1024]{1,0:T(8,128)(2,1)} %get-tuple-element.65.cot_ref, ...), custom_call_target="tpu_custom_call" | custom-call | flops 51539607552 | bytes 62914560 | tf_op jit(solution)/shard_map/pallas_call | solution.py:668
  249.1 15.2 %shard_map.262 = (f32[1024,1024]{1,0:T(8,128)}, bf16[1024,1024]{1,0:T(8,128)(2,1)}, bf16[1024,1024]{1,0:T(8,128)(2,1)}, f32[8,1024]{1,0:T(8,128)}) custom-call(f32[1024,1024]{1,0:T(8,128)} %get-tuple-element.66.base_ref.middle_ref, f32[1024,1024]{1,0:T(8,128)} %get-tuple-element.72.grad_ref, bf16[1024,1024]{1,0:T(8,128)(2,1)} %get-tuple-element.65.cot_ref, ...), custom_call_target="tpu_custom_call" | custom-call | flops 4294967296 | bytes 25165824 | tf_op jit(solution)/shard_map/pallas_call | solution.py:1861
  264.2 0.0 copy-start.8
  264.3 0.0 copy-start.7
  264.3 99.9 %shard_map.263 = (f32[8,64,512]{2,1,0:T(8,128)}, bf16[1024,1024]{1,0:T(8,128)(2,1)}, f32[8,1024]{1,0:T(8,128)}, f32[1,3072]{1,0:T(1,128)}) custom-call(bf16[1024,3072]{1,0:T(8,128)(2,1)} %get-tuple-element.70.packed_ref, bf16[1024,1024]{1,0:T(8,128)(2,1)} %get-tuple-element.71.ctx_ref, bf16[1024,1024]{1,0:T(8,128)(2,1)} %get-tuple-element.74.grad_ref, ...), custom_call_target="tpu_custom_call" | custom-call | flops 47244640256 | bytes 419430400 | tf_op jit(solution)/shard_map/pallas_call | solution.py:1774
  364.1 0.8 slice_bitcast_fusion.2
  364.9 0.5 broadcast.16
  365.4 1.4 reduce.3
  366.9 0.0 copy-done.8
  366.9 0.0 copy-done.7
  367.0 0.0 copy-start.9
  367.0 3.8 shard_map.264
  370.8 0.0 copy-done.9
  370.8 113.6 %shard_map.265 = (bf16[12,64,512]{2,1,0:T(8,128)(2,1)}, f32[12,8,128]{2,1,0:T(8,128)}, bf16[2,512,1024]{2,1,0:T(8,128)(2,1)}, bf16[2,512,1024]{2,1,0:T(8,128)(2,1)}) custom-call(bf16[12,64,512]{2,1,0:T(8,128)(2,1)} %get-tuple-element.85.moments_ref, f32[12,8,128]{2,1,0:T(8,128)} %copy-done.9, bf16[1024,1024]{1,0:T(8,128)(2,1)} %get-tuple-element.90.block_ref, ...), custom_call_target="tpu_custom_call" | custom-call | flops 25769803776 | bytes 4194304 | tf_op jit(solution)/shard_map/pallas_call | solution.py:1040
  484.4 0.0 copy-start.2
  484.4 1.0 pad.10
  485.4 0.6 copy.44
  486.0 2.9 shard_map.266
  488.9 0.0 copy-done.2
  488.9 0.0 copy-start.3
  488.9 2.5 convert_element_type.19
  491.4 0.0 copy-start.1
  491.4 0.0 copy-done.3
  491.4 1.3 copy.62
  492.7 0.0 copy-done.1
  (16 shorter events, 0.2 us)
Async XLA Ops:
  0.7 2.3 copy-start
  0.7 5.8 %copy-start.4 = (f32[3,64,512]{2,1,0:T(8,128)S(1)}, f32[3,64,512]{2,1,0:T(8,128)}, u32[]{:S(2)}) copy-start(f32[3,64,512]{2,1,0:T(8,128)} %w_qkv_ref.1) | copy-start | bytes 1179652
  5.6 1.3 copy-start.5
  6.5 1.4 copy-start.6
  264.2 102.6 %copy-start.8 = (f32[8,1024]{1,0:T(8,128)S(1)}, f32[8,1024]{1,0:T(8,128)}, u32[]{:S(2)}) copy-start(f32[8,1024]{1,0:T(8,128)} %get-tuple-element.88) | copy-start | bytes 98308
  264.3 102.7 %copy-start.7 = (f32[1,4096]{1,0:T(1,128)S(1)}, f32[1,4096]{1,0:T(1,128)}, u32[]{:S(2)}) copy-start(f32[1,4096]{1,0:T(1,128)} %get-tuple-element.89) | copy-start | bytes 49156
  367.0 3.8 copy-start.9
  484.4 4.5 copy-start.2
  488.9 2.5 copy-start.3
  491.4 1.3 copy-start.1

commit v10 on v9

--- a/solution.py
+++ b/solution.py
@@ -712,6 +712,7 @@
 HALF_SLOT = SLOT // 2
 TILE = 256
 GRAM_TILES = 5
+POLY_TILE = 512
 MESH_IDS = pl.DeviceIdType.MESH
 
 
@@ -953,10 +954,10 @@
 
         def tiles(body):
             def one(tile, carry):
-                body(pl.ds(pl.multiple_of(tile * TILE, TILE), TILE))
+                body(pl.ds(pl.multiple_of(tile * POLY_TILE, POLY_TILE), POLY_TILE))
                 return carry
 
-            lax.fori_loop(0, D // TILE, one, 0)
+            lax.fori_loop(0, D // POLY_TILE, one, 0)
 
         chain = chain_low
         other = chain_next
@@ -1237,15 +1238,32 @@
     return (step % 2) * (PAIRS // 2) + step // 2
 
 
+def fill_slots(w_qkv_ref, w_out_ref, w_up_ref, w_down_ref, slots_ref, later_ref):
+    low = jnp.bfloat16
+    for pair in range(SLOT // PAIR):
+        for part in range(3):
+            column = (pair * 3 + part) * PAIR
+            source = w_qkv_ref[part, :, pair * PAIR : (pair + 1) * PAIR].astype(low)
+            slots_ref[column // SLOT, :, column % SLOT : column % SLOT + PAIR] = source
+    slots_ref[3] = w_out_ref[...].astype(low)
+    for index in range(4):
+        target, place = (slots_ref, 4 + 2 * index) if index < EARLY else (later_ref, 2 * (index - EARLY))
+        for kind, ref in enumerate((w_up_ref, w_down_ref)):
+            target[place + kind] = ref[:, index * SLOT : (index + 1) * SLOT].astype(low)
+
+
 def attend_spread_kernel(
     starts_ref,
     slopes_ref,
     norm_ref,
     middle_rows_ref,
     shifts_ref,
+    w_qkv_ref,
+    w_out_ref,
+    w_up_ref,
+    w_down_ref,
     tokens_ref,
     cotangent_ref,
-    slots_ref,
     packed_ref,
     ctx_ref,
     exps_ref,
@@ -1254,11 +1272,13 @@
     rows_ref,
     middle_ref,
     normed_two_ref,
+    later_ref,
     qkv_ref,
     out_ref,
     up_ref,
     down_ref,
     cot_ref,
+    slots_ref,
     dist_ref,
     ctx_t,
     ctx_all,
@@ -1306,6 +1326,7 @@
 
     @pl.when(step == 0)
     def _():
+        fill_slots(w_qkv_ref, w_out_ref, w_up_ref, w_down_ref, slots_ref, later_ref)
         greet_neighbours([spread.sibling, spread.beside, spread.across] + spread.stations)
         own_rows.start()
         for slot in range(3):
@@ -1406,10 +1427,12 @@
     return jax.ShapeDtypeStruct((4, 2, 2, 64, columns), jnp.bfloat16)
 
 
-def attend_spread(starts, slopes, norm_rows, middle_rows, shifts, tokens, cotangent, slots):
+def attend_spread(starts, slopes, norm_rows, middle_rows, shifts, weights, tokens, cotangent):
     anywhere = pl.BlockSpec(memory_space=pl.ANY)
-    whole = pl.BlockSpec((LEN, D), lambda s: (0, 0), pipeline_mode=pl.Buffered(1))
+    once = pl.Buffered(1)
+    whole = pl.BlockSpec((LEN, D), lambda s: (0, 0), pipeline_mode=once)
     low = jnp.bfloat16
+    later = (2 * (4 - EARLY), 64, SLOT)
     *local, qkv, out, up, down, cotangent_rows = pl.pallas_call(
         attend_spread_kernel,
         grid=(PAIRS,),
@@ -1419,10 +1442,10 @@
             pl.BlockSpec((2, D), lambda s: (0, 0)),
             pl.BlockSpec((3, D), lambda s: (0, 0)),
             pl.BlockSpec((1, 3 * PAIR), lambda s: (0, pair_of(s))),
-            anywhere,
-            anywhere,
-            anywhere,
-        ],
+            pl.BlockSpec(weights[0].shape, lambda s: (0, 0, 0), pipeline_mode=once),
+        ]
+        + [pl.BlockSpec(weight.shape, lambda s: (0, 0), pipeline_mode=once) for weight in weights[1:]]
+        + [anywhere] * 2,
         out_specs=[
             pl.BlockSpec((LEN, 3 * PAIR), lambda s: (0, pair_of(s))),
             pl.BlockSpec((LEN, PAIR), lambda s: (0, pair_of(s))),
@@ -1432,6 +1455,7 @@
             whole,
             whole,
             whole,
+            pl.BlockSpec(later, lambda s: (0, 0, 0), pipeline_mode=once),
         ]
         + [anywhere] * 5,
         out_shape=[
@@ -1443,6 +1467,7 @@
             jax.ShapeDtypeStruct((LEN, D), low),
             jax.ShapeDtypeStruct((LEN, D), jnp.float32),
             jax.ShapeDtypeStruct((LEN, D), low),
+            jax.ShapeDtypeStruct(later, low),
             whole_shape(3 * D),
             whole_shape(D),
             whole_shape(2 * EARLY * SLOT),
@@ -1450,6 +1475,7 @@
             jax.ShapeDtypeStruct((LEN, D), low),
         ],
         scratch_shapes=[
+            pltpu.VMEM((4 + 2 * EARLY, 64, SLOT), low),
             pltpu.VMEM((LEN, LEN), jnp.float32),
             pltpu.VMEM((PAIR, LEN), jnp.float32),
             pltpu.VMEM((LEN, D), low),
@@ -1466,7 +1492,7 @@
         cost_estimate=pl.CostEstimate(
             flops=22 * LEN * LEN * D, bytes_accessed=90 * 1024 * 1024, transcendentals=H * LEN * LEN
         ),
-    )(starts, slopes, norm_rows, middle_rows, shifts, tokens, cotangent, slots)
+    )(starts, slopes, norm_rows, middle_rows, shifts, *weights, tokens, cotangent)
     wholes = [whole.reshape(D, -1) for whole in (qkv, out, up, down)]
     return *local, wholes, cotangent_rows
 
@@ -1985,10 +2011,6 @@
     return (output_pair, token_pair.astype(jnp.float32), *grads, vector_grad, *moments, moment_vec, *new, new_vec)
 
 
-def by_slots(rows):
-    return jnp.swapaxes(rows.reshape(rows.shape[0], -1, SLOT), 0, 1)
-
-
 def narrow(rows):
     return rows.astype(jnp.bfloat16)
 
@@ -2028,12 +2050,9 @@
     slopes = jnp.exp2(-8.0 * jnp.arange(1, H + 1, dtype=jnp.float32) / H)
     starts = lax.dynamic_slice_in_dim(piece_starts[:, 0], rank, 1, 0)[0]
     shifts = by_pairs(jnp.stack([vectors[2], jnp.zeros((D,), jnp.float32), vectors[3]])[:, None])
-    up_slots = by_slots(narrow(w_up))
-    down_slots = by_slots(narrow(w_down).T)
-    in_turn = jnp.stack([up_slots, down_slots], axis=1).reshape(2 * up_slots.shape[0], *up_slots.shape[1:])
-    slots = jnp.concatenate([by_slots(by_pairs(narrow(w_qkv))), narrow(w_out).T[None], in_turn[: 2 * EARLY]])
-    packed, context, exps, stats, normed_t, token_low, middle, normed_two, wholes, cotangent_low = attend_spread(
-        starts, slopes, vectors[0:2], vectors[4:7], shifts, tokens, cotangent, slots
+    weights = (w_qkv, w_out, w_up, w_down)
+    packed, context, exps, stats, normed_t, token_low, middle, normed_two, later, wholes, cotangent_low = attend_spread(
+        starts, slopes, vectors[0:2], vectors[4:7], shifts, features_first(weights), tokens, cotangent
     )
     full_qkv, full_out, full_up, full_down = wholes
     block_rows, grad_normed_two, grad_up, grad_down, up_bias, early_sums = mlp_both(
@@ -2044,7 +2063,7 @@
         vectors[7:11].reshape(1, FF),
         full_up,
         full_down,
-        in_turn[2 * EARLY :],
+        later,
     )
     grad_middle, grad_context, grad_out, middle_sums = middle_backward(
         middle, grad_normed_two, cotangent_low, context, vectors[5:6], full_out
@@ -2076,7 +2095,6 @@
             middle_sums[3:4],
         ]
     )
-    weights = (w_qkv, w_out, w_up, w_down)
     momenta = (m_qkv, m_out, m_up, m_down)
     return muon_step(
         early_sums, sums, vector_total, block_rows, grad_token_low, weights, vectors, momenta, m_vec

time: 503 us -> 501 us (level)
  no operation moved by 1% of the time
where the time goes in v10:
time: 501 us; the launch traced here: 492 us
  Pallas kernels  475 us (95%)
  local copies, waits for them, and re-layouts  11.2 us (2%)
    pallas_call x1, Pallas kernels, attend_spread(): pl.pallas_call(attend_spread_kernel, grid=(PAIRS,), in_specs=[SCALARS, SC...  140 us
    pallas_call x1, Pallas kernels, muon_call(): pl.pallas_call(muon_kernel, in_specs=[vmem, vmem, anywhere, anywhere], ou...  114 us
    pallas_call x1, Pallas kernels, attend_sum(): pl.pallas_call(attend_sum_kernel, grid=(PAIRS,), in_specs=[PACKED_COLS, P...  99.9 us
    pallas_call x1, Pallas kernels, mlp_both(): pl.pallas_call(mlp_kernel, grid=(HIDDEN_STEPS,), in_specs=[whole, whole,...  99.7 us
    pallas_call x1, Pallas kernels, middle_backward(): pl.pallas_call(middle_kernel, grid=(LEN // ROWS,), in_specs=[rows, rows,...  15.4 us

profile of v10, /device:TPU:9, one launch (start us, length us, event | category | flops | bytes accessed | tf_op | source)
XLA Modules:
  0.0 491.8 jit_solution(15872957459213270622)
XLA Ops:
  0.7 0.0 copy-start
  0.7 1.5 fusion
  2.2 0.1 pad.1.clone
  2.3 0.1 maximum_bitcast_fusion
  2.3 0.6 reshape.77.shifts_ref
  3.0 0.0 copy-done
  3.0 0.5 dynamic-slice_bitcast_fusion.starts_ref
  3.5 1.4 slice.45.middle_rows_ref
  4.8 1.4 slice.44.norm_ref
  6.2 0.5 multiply_exponential_fusion.slopes_ref
  6.7 139.8 %shard_map.260 = (bf16[1024,3072]{1,0:T(8,128)(2,1)}, bf16[1024,1024]{1,0:T(8,128)(2,1)}, bf16[16,1024,1024]{2,1,0:T(8,128)(2,1)}, f32[8,2,1024]{2,1,0:T(2,128)}...) custom-call(s32[2]{0:T(128)} %dynamic-slice_bitcast_fusion.starts_re, ...), custom_call_target="tpu_custom_call" | custom-call | flops 23622320128 | bytes 94371840 | tf_op jit(solution)/shard_map/pallas_call | solution.py:1436
  146.6 0.8 slice_bitcast_fusion
  147.4 0.6 copy.33
  148.0 99.7 %shard_map.261 = (bf16[1024,1024]{1,0:T(8,128)(2,1)}, f32[1024,1024]{1,0:T(8,128)}, bf16[1024,2048]{1,0:T(8,128)(2,1)}, bf16[1024,2048]{1,0:T(8,128)(2,1)}, f32[1,4096]{1,0:T(1,128)}, /*index=5*/f32[4,64,512]{2,1,0:T(8,128)}) custom-call(bf16[1024,1024]{1,0:T(8,128)(2,1)} %get-tuple-element.65.rows_ref, bf16[1024,1024]{1,0:T(8,128)(2,1)} %get-tuple-element.66.cot_ref, ...), custom_call_target="tpu_custom_call" | custom-call | flops 51539607552 | bytes 62914560 | tf_op jit(solution)/shard_map/pallas_call | solution.py:668
  247.8 15.4 %shard_map.262 = (f32[1024,1024]{1,0:T(8,128)}, bf16[1024,1024]{1,0:T(8,128)(2,1)}, bf16[1024,1024]{1,0:T(8,128)(2,1)}, f32[8,1024]{1,0:T(8,128)}) custom-call(f32[1024,1024]{1,0:T(8,128)} %get-tuple-element.67.base_ref.middle_ref, f32[1024,1024]{1,0:T(8,128)} %get-tuple-element.74.grad_ref, bf16[1024,1024]{1,0:T(8,128)(2,1)} %get-tuple-element.66.cot_ref, ...), custom_call_target="tpu_custom_call" | custom-call | flops 4294967296 | bytes 25165824 | tf_op jit(solution)/shard_map/pallas_call | solution.py:1887
  263.2 0.0 copy-start.5
  263.2 0.0 copy-start.4
  263.2 99.9 %shard_map.263 = (f32[8,64,512]{2,1,0:T(8,128)}, bf16[1024,1024]{1,0:T(8,128)(2,1)}, f32[8,1024]{1,0:T(8,128)}, f32[1,3072]{1,0:T(1,128)}) custom-call(bf16[1024,3072]{1,0:T(8,128)(2,1)} %get-tuple-element.72.packed_ref, bf16[1024,1024]{1,0:T(8,128)(2,1)} %get-tuple-element.73.ctx_ref, bf16[1024,1024]{1,0:T(8,128)(2,1)} %get-tuple-element.76.grad_ref, ...), custom_call_target="tpu_custom_call" | custom-call | flops 47244640256 | bytes 419430400 | tf_op jit(solution)/shard_map/pallas_call | solution.py:1800
  363.0 0.8 slice_bitcast_fusion.2
  363.8 0.5 broadcast.16
  364.3 1.4 reduce.3
  365.8 0.0 copy-done.5
  365.8 0.0 copy-done.4
  365.9 0.0 copy-start.6
  365.9 3.8 shard_map.264
  369.7 0.0 copy-done.6
  369.7 113.7 %shard_map.265 = (bf16[12,64,512]{2,1,0:T(8,128)(2,1)}, f32[12,8,128]{2,1,0:T(8,128)}, bf16[2,512,1024]{2,1,0:T(8,128)(2,1)}, bf16[2,512,1024]{2,1,0:T(8,128)(2,1)}) custom-call(bf16[12,64,512]{2,1,0:T(8,128)(2,1)} %get-tuple-element.87.moments_ref, f32[12,8,128]{2,1,0:T(8,128)} %copy-done.6, bf16[1024,1024]{1,0:T(8,128)(2,1)} %get-tuple-element.92.block_ref, ...), custom_call_target="tpu_custom_call" | custom-call | flops 25769803776 | bytes 4194304 | tf_op jit(solution)/shard_map/pallas_call | solution.py:1041
  483.4 0.0 copy-start.2
  483.4 1.0 pad.3
  484.3 0.6 copy.36
  485.0 2.9 shard_map.266
  487.8 0.0 copy-done.2
  487.8 0.0 copy-start.3
  487.8 2.5 convert_element_type.3
  490.3 0.0 copy-start.1
  490.3 0.0 copy-done.3
  490.3 1.3 copy.48
  491.6 0.0 copy-done.1
  (11 shorter events, 0.1 us)
Async XLA Ops:
  0.7 2.3 copy-start
  263.2 102.6 %copy-start.5 = (f32[8,1024]{1,0:T(8,128)S(1)}, f32[8,1024]{1,0:T(8,128)}, u32[]{:S(2)}) copy-start(f32[8,1024]{1,0:T(8,128)} %get-tuple-element.90) | copy-start | bytes 98308
  263.2 102.6 %copy-start.4 = (f32[1,4096]{1,0:T(1,128)S(1)}, f32[1,4096]{1,0:T(1,128)}, u32[]{:S(2)}) copy-start(f32[1,4096]{1,0:T(1,128)} %get-tuple-element.91) | copy-start | bytes 49156
  365.9 3.8 copy-start.6
  483.4 4.5 copy-start.2
  487.8 2.5 copy-start.3
  490.3 1.3 copy-start.1

commit v11 on v10

--- a/solution.py
+++ b/solution.py
@@ -1297,7 +1297,7 @@
     table = [(column_view(qkv_ref, index * SLOT, 3 * SLOT), SLOT if index == 1 else 0) for index in range(3)]
     table += [(column_view(out_ref, 0, SLOT), 0)]
     for index in range(EARLY):
-        for ref, over_x in ((up_ref, 0), (down_ref, HALF_SLOT if index else 0)):
+        for ref, over_x in ((up_ref, HALF_SLOT if index else 0), (down_ref, HALF_SLOT if index else 0)):
             table += [(column_view(ref, index * SLOT, EARLY * SLOT), over_x)]
     count = len(table)
     spread = Spread(slots_ref, table, local_sem, send_sem, recv_sem)

time: 501 us -> 501 us (level)
  no operation moved by 1% of the time
where the time goes in v11:
time: 501 us; the launch traced here: 491 us
  Pallas kernels  475 us (95%)
  local copies, waits for them, and re-layouts  11.2 us (2%)
    pallas_call x1, Pallas kernels, attend_spread(): pl.pallas_call(attend_spread_kernel, grid=(PAIRS,), in_specs=[SCALARS, SC...  138 us
    pallas_call x1, Pallas kernels, muon_call(): pl.pallas_call(muon_kernel, in_specs=[vmem, vmem, anywhere, anywhere], ou...  114 us
    pallas_call x1, Pallas kernels, mlp_both(): pl.pallas_call(mlp_kernel, grid=(HIDDEN_STEPS,), in_specs=[whole, whole,...  101 us
    pallas_call x1, Pallas kernels, attend_sum(): pl.pallas_call(attend_sum_kernel, grid=(PAIRS,), in_specs=[PACKED_COLS, P...  99.9 us
    pallas_call x1, Pallas kernels, middle_backward(): pl.pallas_call(middle_kernel, grid=(LEN // ROWS,), in_specs=[rows, rows,...  15.4 us

profile of v11, /device:TPU:9, one launch (start us, length us, event | category | flops | bytes accessed | tf_op | source)
XLA Modules:
  0.0 491.4 jit_solution(16239364899886798731)
XLA Ops:
  0.7 0.0 copy-start
  0.7 1.5 fusion
  2.2 0.1 pad.1.clone
  2.3 0.1 maximum_bitcast_fusion
  2.3 0.6 reshape.77.shifts_ref
  3.0 0.0 copy-done
  3.0 0.5 dynamic-slice_bitcast_fusion.starts_ref
  3.5 1.4 slice.45.middle_rows_ref
  4.8 1.4 slice.44.norm_ref
  6.2 0.5 multiply_exponential_fusion.slopes_ref
  6.7 138.5 %shard_map.260 = (bf16[1024,3072]{1,0:T(8,128)(2,1)}, bf16[1024,1024]{1,0:T(8,128)(2,1)}, bf16[16,1024,1024]{2,1,0:T(8,128)(2,1)}, f32[8,2,1024]{2,1,0:T(2,128)}...) custom-call(s32[2]{0:T(128)} %dynamic-slice_bitcast_fusion.starts_re, ...), custom_call_target="tpu_custom_call" | custom-call | flops 23622320128 | bytes 94371840 | tf_op jit(solution)/shard_map/pallas_call | solution.py:1436
  145.2 0.8 slice_bitcast_fusion
  146.0 0.6 copy.33
  146.7 100.6 %shard_map.261 = (bf16[1024,1024]{1,0:T(8,128)(2,1)}, f32[1024,1024]{1,0:T(8,128)}, bf16[1024,2048]{1,0:T(8,128)(2,1)}, bf16[1024,2048]{1,0:T(8,128)(2,1)}, f32[1,4096]{1,0:T(1,128)}, /*index=5*/f32[4,64,512]{2,1,0:T(8,128)}) custom-call(bf16[1024,1024]{1,0:T(8,128)(2,1)} %get-tuple-element.65.rows_ref, bf16[1024,1024]{1,0:T(8,128)(2,1)} %get-tuple-element.66.cot_ref, ...), custom_call_target="tpu_custom_call" | custom-call | flops 51539607552 | bytes 62914560 | tf_op jit(solution)/shard_map/pallas_call | solution.py:668
  247.3 15.4 %shard_map.262 = (f32[1024,1024]{1,0:T(8,128)}, bf16[1024,1024]{1,0:T(8,128)(2,1)}, bf16[1024,1024]{1,0:T(8,128)(2,1)}, f32[8,1024]{1,0:T(8,128)}) custom-call(f32[1024,1024]{1,0:T(8,128)} %get-tuple-element.67.base_ref.middle_ref, f32[1024,1024]{1,0:T(8,128)} %get-tuple-element.74.grad_ref, bf16[1024,1024]{1,0:T(8,128)(2,1)} %get-tuple-element.66.cot_ref, ...), custom_call_target="tpu_custom_call" | custom-call | flops 4294967296 | bytes 25165824 | tf_op jit(solution)/shard_map/pallas_call | solution.py:1887
  262.7 0.0 copy-start.5
  262.7 0.0 copy-start.4
  262.7 99.9 %shard_map.263 = (f32[8,64,512]{2,1,0:T(8,128)}, bf16[1024,1024]{1,0:T(8,128)(2,1)}, f32[8,1024]{1,0:T(8,128)}, f32[1,3072]{1,0:T(1,128)}) custom-call(bf16[1024,3072]{1,0:T(8,128)(2,1)} %get-tuple-element.72.packed_ref, bf16[1024,1024]{1,0:T(8,128)(2,1)} %get-tuple-element.73.ctx_ref, bf16[1024,1024]{1,0:T(8,128)(2,1)} %get-tuple-element.76.grad_ref, ...), custom_call_target="tpu_custom_call" | custom-call | flops 47244640256 | bytes 419430400 | tf_op jit(solution)/shard_map/pallas_call | solution.py:1800
  362.6 0.8 slice_bitcast_fusion.2
  363.3 0.5 broadcast.16
  363.8 1.4 reduce.3
  365.3 0.0 copy-done.5
  365.3 0.0 copy-done.4
  365.4 0.0 copy-start.6
  365.4 3.8 shard_map.264
  369.2 0.0 copy-done.6
  369.2 113.7 %shard_map.265 = (bf16[12,64,512]{2,1,0:T(8,128)(2,1)}, f32[12,8,128]{2,1,0:T(8,128)}, bf16[2,512,1024]{2,1,0:T(8,128)(2,1)}, bf16[2,512,1024]{2,1,0:T(8,128)(2,1)}) custom-call(bf16[12,64,512]{2,1,0:T(8,128)(2,1)} %get-tuple-element.87.moments_ref, f32[12,8,128]{2,1,0:T(8,128)} %copy-done.6, bf16[1024,1024]{1,0:T(8,128)(2,1)} %get-tuple-element.92.block_ref, ...), custom_call_target="tpu_custom_call" | custom-call | flops 25769803776 | bytes 4194304 | tf_op jit(solution)/shard_map/pallas_call | solution.py:1041
  482.9 0.0 copy-start.2
  482.9 1.0 pad.3
  483.9 0.6 copy.36
  484.5 2.9 shard_map.266
  487.4 0.0 copy-done.2
  487.4 0.0 copy-start.3
  487.4 2.5 convert_element_type.3
  489.9 0.0 copy-start.1
  489.9 0.0 copy-done.3
  489.9 1.3 copy.48
  491.2 0.0 copy-done.1
  (11 shorter events, 0.1 us)
Async XLA Ops:
  0.7 2.3 copy-start
  262.7 102.6 %copy-start.5 = (f32[8,1024]{1,0:T(8,128)S(1)}, f32[8,1024]{1,0:T(8,128)}, u32[]{:S(2)}) copy-start(f32[8,1024]{1,0:T(8,128)} %get-tuple-element.90) | copy-start | bytes 98308
  262.7 102.7 %copy-start.4 = (f32[1,4096]{1,0:T(1,128)S(1)}, f32[1,4096]{1,0:T(1,128)}, u32[]{:S(2)}) copy-start(f32[1,4096]{1,0:T(1,128)} %get-tuple-element.91) | copy-start | bytes 49156
  365.4 3.8 copy-start.6
  482.9 4.5 copy-start.2
  487.4 2.5 copy-start.3
  489.9 1.3 copy-start.1
